TPU v7x, 256 devices: a whole 4x4x8 slice. The times are simulated.
256 devices in a mesh: row: 8 (over z_lo, core), lab: 32 (over y, x, z_hi).
Axes of the slice: x: 4, y: 4, z: 8 (z_hi: 2, z_lo: 4; z = z_hi * 4 + z_lo), core: 2. Of those that a mesh axis runs over, the one named last changes fastest.
Arguments:
- scores: bfloat16 [65536, 8192], P('row', 'lab'), may hold values from -8 to 8
- targets: int32 [65536, 8192], P('row', 'lab'), may hold values 0 or 1
- signs: int32 [8192, 16], P('lab'), may hold values from 0 to 1
- bins: int32 [65536, 512], P('row', 'lab'), may hold values from 0 to 255
- leaves: int32 [65536], P('row'), may hold values from 0 to 3
Outputs:
- histogram: float32 [256, 512, 68], P('row', 'lab')
All inputs are finite; a program needn't handle non-finite values. No bound on the sum of `targets` on one device may be relied on, other than what follows from the above.
Results may differ from a plain program's by a relative error of at most 0.00091.
Values sent between devices are 32-bit elements; how exact they have to be, the bound alone decides.
No kernel may reach another device: no remote copies, remote signals or barrier semaphores. Data moves between devices by JAX's collectives and lax.ppermute only.
A program may use at most 64 MiB of HBM per device.

v0:
```python
import math

import jax
import jax.numpy as jnp
from jax import lax
from jax.sharding import PartitionSpec as P

L = 8192
BINS = 256
K = 16
LEAVES = 4


def per_device(scores, targets, signs, bins, leaves):
    row_count = scores.shape[0]
    sign_matrix = (2 * signs - 1).astype(jnp.float32)
    prob = jax.nn.sigmoid(scores.astype(jnp.float32))
    gradient = prob - targets.astype(jnp.float32)
    hessian = prob * (1.0 - prob)
    sketch = jnp.dot(
        gradient, sign_matrix, precision=lax.Precision.HIGHEST, preferred_element_type=jnp.float32
    ) / math.sqrt(L)
    curvature = jnp.sum(hessian, axis=1) / L
    partial_stats = jnp.concatenate([sketch, curvature[:, None]], axis=1)
    stats = lax.psum(partial_stats, "lab")
    leaf_onehot = (leaves[:, None] == jnp.arange(LEAVES, dtype=jnp.int32)[None, :]).astype(
        jnp.float32
    )
    weights = (
        (leaf_onehot[:, :, None] * stats[:, None, :])
        .reshape(row_count, LEAVES * (K + 1))
        .astype(jnp.bfloat16)
    )
    block_rows = min(512, row_count)
    block_total = row_count // block_rows
    feat_count = bins.shape[1]
    width = LEAVES * (K + 1)
    codes = jnp.arange(BINS, dtype=jnp.int32)

    def add_block(step, total):
        first = step * block_rows
        block_bins = lax.dynamic_slice_in_dim(bins, first, block_rows, 0)
        block_weights = lax.dynamic_slice_in_dim(weights, first, block_rows, 0)
        onehot = (block_bins[:, :, None] == codes[None, None, :]).astype(jnp.bfloat16)
        return total + jnp.einsum(
            "rfb,rc->bfc", onehot, block_weights, preferred_element_type=jnp.float32
        )

    empty = jnp.zeros((BINS, feat_count, width), jnp.float32)
    term = lax.fori_loop(0, block_total, add_block, empty)
    return lax.psum_scatter(term, "row", scatter_dimension=0, tiled=True)


def solution(mesh):
    in_specs = (P("row", "lab"), P("row", "lab"), P("lab", None), P("row", "lab"), P("row"))
    out_specs = P("row", "lab", None)
    return jax.shard_map(
        per_device, mesh=mesh, in_specs=in_specs, out_specs=out_specs, check_vma=False
    )
```

profile of v0, /device:TPU:1, one launch (start us, length us, event | category | flops | bytes accessed | tf_op | source)
XLA Modules:
  0.0 611.3 jit_solution(8129888543109334248)
XLA Ops:
  6.5 0.0 copy-start.2
  6.5 0.0 all-reduce.2.cloned.1.call-start
  6.5 0.0 copy-start
  6.5 4.1 fusion.9
  10.7 0.0 copy-done.2
  10.7 0.0 copy-done
  10.7 0.0 copy-start.1
  10.7 11.4 %convolution_multiply_fusion = f32[8192,16]{0,1:T(8,128)S(1)} fusion(s32[8192,256]{1,0:T(8,128)} %param.8, bf16[8192,256]{1,0:T(8,128)(2,1)S(1)} %copy-done, s32[256,16]{0,1:T(8,128)S(1)} %copy-done.2), kind=kOutput, calls=%fused_computation.11 | convolution fusion | flops 415379456 | bytes 13123584 | tf_op jit(solution)/shard_map/dot_general | solution.py:20
  22.1 0.9 pad_maximum_fusion
  23.1 0.0 all-reduce.2.cloned.1.call-update
  23.1 0.0 reduce-scatter.2.cloned.1.call-start
  23.2 0.0 copy-done.1
  23.2 409.1 %all-reduce.2.cloned.1.call-done = f32[8192,17]{0,1:T(8,128)} async-done(((f32[8192,17]{0,1:T(8,128)}), f32[8192,17]{0,1:T(8,128)}) %all-reduce.2.cloned.1.call-update) | async-done | bytes 557072 | tf_op jit(solution)/shard_map/psum | solution.py:25
  432.4 1.3 multiply_convert_fusion
  433.7 1.4 convert_element_type.30
  435.1 106.2 %while.14 = (s32[]{:T(128)}, f32[256,16,68]{0,2,1:T(8,128)S(1)}, bf16[8192,68]{0,1:T(8,128)(2,1)}, s32[8192,16]{0,1:T(8,128)}, s32[]{:T(128)}, /*index=5*/s32[]{:T(128)}, s32[]{:T(128)}, s32[]{:T(128)}) while((s32[]{:T(128)}, f32[256,16,68]{0,2,1:T(8,128)S(1)}, bf16[8192,68]{0,1:T(8,128)(2,1)}, s32[8192,16]{0,1:T(8,128)}, ...), condition=%wide.region_3.0_spmd.clone, body=%wide.region_2.0_spmd.clone.sunk | while | flops 287866880 | bytes 2400413 | solution.py:50
  435.1 0.8 constant_dynamic-slice_fusion.2
  435.9 5.8 fusion.24
  441.8 0.8 constant_dynamic-slice_fusion.2
  442.5 5.8 fusion.24
  448.4 0.8 constant_dynamic-slice_fusion.2
  449.2 5.8 fusion.24
  455.0 0.8 constant_dynamic-slice_fusion.2
  455.8 5.8 fusion.24
  461.7 0.8 constant_dynamic-slice_fusion.2
  462.4 5.8 fusion.24
  468.3 0.8 constant_dynamic-slice_fusion.2
  469.1 5.8 fusion.24
  475.0 0.8 constant_dynamic-slice_fusion.2
  475.7 5.8 fusion.24
  481.6 0.8 constant_dynamic-slice_fusion.2
  482.4 5.8 fusion.24
  488.2 0.8 constant_dynamic-slice_fusion.2
  489.0 5.8 fusion.24
  494.9 0.8 constant_dynamic-slice_fusion.2
  495.6 5.8 fusion.24
  501.5 0.8 constant_dynamic-slice_fusion.2
  502.3 5.8 fusion.24
  508.1 0.8 constant_dynamic-slice_fusion.2
  508.9 5.8 fusion.24
  514.8 0.8 constant_dynamic-slice_fusion.2
  515.6 5.8 fusion.24
  521.4 0.8 constant_dynamic-slice_fusion.2
  522.2 5.8 fusion.24
  528.1 0.8 constant_dynamic-slice_fusion.2
  528.8 5.8 fusion.24
  534.7 0.8 constant_dynamic-slice_fusion.2
  535.5 5.8 fusion.24
  541.3 2.0 copy.7
  543.3 0.0 reduce-scatter.2.cloned.1.call-update
  543.4 61.1 %reduce-scatter.2.cloned.1.call-done = f32[32,16,68]{2,1,0:T(8,128)} async-done(((f32[256,16,68]{2,1,0:T(8,128)}), f32[32,16,68]{2,1,0:T(8,128)}) %reduce-scatter.2.cloned.1.call-update) | async-done | bytes 139280 | tf_op jit(solution)/shard_map/reduce_scatter | solution.py:51
  (3 shorter events, 0.0 us)
Async XLA Ops:
  6.5 4.1 copy-start.2
  6.5 425.8 %all-reduce.2.cloned.1.call-start = ((), (), s32[]{:S(2)}) async-start(), calls=%async_computation.1 | async-start | bytes 1572864 | tf_op jit(solution)/shard_map/psum | solution.py:25
  6.5 4.1 copy-start
  10.7 12.5 %copy-start.1 = (s32[8192]{0:T(1024)S(1)}, s32[8192]{0:T(1024)}, u32[]{:S(2)}) copy-start(s32[8192]{0:T(1024)} %param.11) | copy-start | bytes 98308
  23.1 581.3 %reduce-scatter.2.cloned.1.call-start = ((), (), s32[]{:S(2)}) async-start(), calls=%async_computation.2 | async-start | bytes 2359296 | tf_op jit(solution)/shard_map/reduce_scatter | solution.py:51
Sparse Core Ops, SparseCore 0:
  23.2 409.0 all-reduce.1
  543.5 60.9 reduce-scatter.1
where the time goes:
time: 615 us; the launch traced here: 611 us
  waiting for transfers between devices  470 us (76%)
  matrix products  105 us (17%)
  local copies, waits for them, and re-layouts  15.7 us (3%)
  between operations  13.5 us (2%)
  other arithmetic  6.42 us (1%)
    psum x1, waiting for transfers between devices, per_device(): stats = lax.psum(partial_stats, 'lab')  409 us
    dot_general x16, matrix products, add_block(): jnp.einsum('rfb,rc->bfc', onehot, block_weights, preferred_element_type=j...  93.5 us
    reduce_scatter x1, waiting for transfers between devices, per_device(): return lax.psum_scatter(term, 'row', scatter_dimension=0, tiled=True)  61.1 us
  transfers between devices with their start and end apart: 2, of which 2 were waited for; matrix products, arithmetic and copies ran while one was open for 0% of the time, Pallas kernels for 0%

commit v1 on v0

v1 whole, which is shorter than its diff:
```python
import functools
import math

import jax
import jax.numpy as jnp
from jax import lax
from jax.experimental import pallas as pl
from jax.experimental.pallas import tpu as pltpu
from jax.sharding import Mesh, PartitionSpec as P

L = 8192
BINS = 256
K = 16
LEAVES = 4
ROWS = 8192
LABS = 256
FEATS = 16
SLAB = 512
LANES = 128
QUADS = SLAB // LANES
SLAB_ROWS = QUADS * (K + 1)
F8 = jnp.float8_e4m3fn
NT = (((1,), (1,)), ((), ()))
SKETCH_SCALES = (4.0, 64.0, 2.0**24, 2.0**29)
CURVE_SCALES = (1024.0, 2.0**14)
TERM_ROWS = LEAVES * K
W_ROWS = 288
OWN_BINS = 32


def sketch_kernel(chunk_ref, scores_ref, targets_ref, signs_ref, out_ref):
    del chunk_ref
    sign_matrix = (2 * signs_ref[...] - 1).astype(jnp.bfloat16)
    left = jnp.concatenate(
        [
            jnp.concatenate([sign_matrix, sign_matrix, jnp.zeros((K, LABS), jnp.bfloat16)], axis=1),
            jnp.concatenate(
                [jnp.zeros((K, 2 * LABS), jnp.bfloat16), jnp.ones((K, LABS), jnp.bfloat16)], axis=1
            ),
        ],
        axis=0,
    )
    prob = jax.nn.sigmoid(scores_ref[...].astype(jnp.float32))
    gradient = prob - targets_ref[...].astype(jnp.float32)
    hessian = prob * (1.0 - prob)
    hessian = hessian[:, :LANES] + hessian[:, LANES:]
    grad_high = gradient.astype(jnp.bfloat16)
    grad_low = (gradient - grad_high.astype(jnp.float32)).astype(jnp.bfloat16)
    hess_high = hessian.astype(jnp.bfloat16)
    hess_low = (hessian - hess_high.astype(jnp.float32)).astype(jnp.bfloat16)
    right = jnp.concatenate([grad_high, grad_low, hess_high, hess_low], axis=1)
    stats = lax.dot_general(left, right, NT, preferred_element_type=jnp.float32)
    for quad in range(QUADS):
        lanes = slice(quad * LANES, (quad + 1) * LANES)
        out_ref[0, quad * K : (quad + 1) * K, :] = stats[:K, lanes] * (1.0 / math.sqrt(L))
        out_ref[0, QUADS * K + quad : QUADS * K + quad + 1, :] = stats[K : K + 1, lanes] * (1.0 / L)


def sketch_call(chunk, scores, targets, signs_t):
    return pl.pallas_call(
        sketch_kernel,
        grid_spec=pltpu.PrefetchScalarGridSpec(
            num_scalar_prefetch=1,
            grid=(4,),
            in_specs=[
                pl.BlockSpec((SLAB, LABS), lambda i, c: (c[0] * 4 + i, 0)),
                pl.BlockSpec((SLAB, LABS), lambda i, c: (c[0] * 4 + i, 0)),
                pl.BlockSpec((K, LABS), lambda i, c: (0, 0)),
            ],
            out_specs=pl.BlockSpec((1, SLAB_ROWS, LANES), lambda i, c: (i, 0, 0)),
        ),
        out_shape=jax.ShapeDtypeStruct((4, SLAB_ROWS, LANES), jnp.float32),
        compiler_params=pltpu.CompilerParams(vmem_limit_bytes=16 << 20),
        cost_estimate=pl.CostEstimate(
            flops=2 * 4 * SLAB * 768 * 32, bytes_accessed=4 * SLAB * LABS * 6, transcendentals=4 * SLAB * LABS
        ),
        name="sketch",
    )(chunk, scores, targets, signs_t)


def split_terms(values, scales):
    terms = []
    for scale in scales:
        term = (values * scale).astype(F8).astype(jnp.float32)
        terms.append(term)
        values = values - term * (1.0 / scale)
    return terms


def weight_kernel(place_ref, s0, s1, s2, s3, leaves_ref, out_ref):
    leaf_iota = lax.broadcasted_iota(jnp.int32, (8, LANES), 0)
    zeros = jnp.zeros((K, LANES), jnp.float32)
    for kx, stats_ref in enumerate((s0, s1, s2, s3)):
        for ky in range(4):
            chunk = place_ref[kx] * 4 + place_ref[4 + ky]
            for quad in range(QUADS):
                leaf = leaves_ref[pl.ds(chunk * QUADS + quad, 1), :]
                sketch = stats_ref[ky, quad * K : (quad + 1) * K, :]
                curve = stats_ref[ky, QUADS * K + quad : QUADS * K + quad + 1, :]
                sketch = sketch.astype(jnp.bfloat16).astype(jnp.float32)
                curve = jnp.broadcast_to(curve, (8, LANES)).astype(jnp.bfloat16).astype(jnp.float32)
                masks = [jnp.broadcast_to(leaf == e, (K, LANES)) for e in range(LEAVES)]
                curve_mask = jnp.broadcast_to(leaf, (8, LANES)) == leaf_iota
                parts = [
                    jnp.where(mask, term, zeros)
                    for term in split_terms(sketch, SKETCH_SCALES)
                    for mask in masks
                ]
                parts += [jnp.where(curve_mask, term, 0.0) for term in split_terms(curve, CURVE_SCALES)]
                parts.append(jnp.zeros((W_ROWS - 4 * TERM_ROWS - 16, LANES), jnp.float32))
                lanes = pl.ds(pl.multiple_of(chunk * SLAB + quad * LANES, LANES), LANES)
                out_ref[:, lanes] = jnp.concatenate(parts, axis=0).astype(F8)


def weight_call(place, stats, leaves):
    return pl.pallas_call(
        weight_kernel,
        grid_spec=pltpu.PrefetchScalarGridSpec(
            num_scalar_prefetch=1,
            grid=(1,),
            in_specs=[pl.BlockSpec((4, SLAB_ROWS, LANES), lambda i, s: (0, 0, 0))] * 4
            + [pl.BlockSpec((ROWS // LANES, LANES), lambda i, s: (0, 0))],
            out_specs=pl.BlockSpec((W_ROWS, ROWS), lambda i, s: (0, 0)),
        ),
        out_shape=jax.ShapeDtypeStruct((W_ROWS, ROWS), F8),
        compiler_params=pltpu.CompilerParams(vmem_limit_bytes=24 << 20),
        cost_estimate=pl.CostEstimate(flops=20_000_000, bytes_accessed=4_000_000, transcendentals=0),
        name="weights",
    )(place, *stats, leaves)


def hist_kernel(base_ref, bins_ref, weights_ref, own_ref, other_ref):
    for which, out_ref in ((0, other_ref), (1, own_ref)):
        codes = bins_ref[...] - base_ref[which]
        codes = jnp.clip(codes, -1, OWN_BINS)
        pair = jnp.concatenate([codes, codes - 1], axis=0).astype(jnp.int8)
        one = jnp.ones(pair.shape, F8)
        zero = jnp.zeros(pair.shape, F8)
        onehot = jnp.concatenate(
            [jnp.where(pair == jnp.int8(b), one, zero) for b in range(0, OWN_BINS, 2)], axis=0
        )
        total = lax.dot_general(weights_ref[...], onehot, NT, preferred_element_type=jnp.float32)
        sketch = sum(
            total[t * TERM_ROWS : (t + 1) * TERM_ROWS] * (1.0 / scale)
            for t, scale in enumerate(SKETCH_SCALES)
        )
        curve = sum(
            total[4 * TERM_ROWS + 8 * t : 4 * TERM_ROWS + 8 * t + 8] * (1.0 / scale)
            for t, scale in enumerate(CURVE_SCALES)
        )
        out_ref[:TERM_ROWS, :] = sketch
        out_ref[TERM_ROWS:, :] = curve[:LEAVES]


def hist_call(base, bins_t, weights):
    cols = OWN_BINS * FEATS
    shape = jax.ShapeDtypeStruct((LEAVES * (K + 1), cols), jnp.float32)
    spec = pl.BlockSpec((LEAVES * (K + 1), cols), lambda i, s: (0, 0))
    return pl.pallas_call(
        hist_kernel,
        grid_spec=pltpu.PrefetchScalarGridSpec(
            num_scalar_prefetch=1,
            grid=(1,),
            in_specs=[
                pl.BlockSpec((FEATS, ROWS), lambda i, s: (0, 0)),
                pl.BlockSpec((W_ROWS, ROWS), lambda i, s: (0, 0)),
            ],
            out_specs=[spec, spec],
        ),
        out_shape=[shape, shape],
        compiler_params=pltpu.CompilerParams(vmem_limit_bytes=40 << 20),
        cost_estimate=pl.CostEstimate(
            flops=2 * 2 * cols * ROWS * W_ROWS, bytes_accessed=3_000_000, transcendentals=0
        ),
        name="hist",
    )(base, bins_t, weights)


def finish_kernel(a_ref, b_ref, c_ref, d_ref, out_ref):
    total = (a_ref[...] + b_ref[...]) + (c_ref[...] + d_ref[...])
    rows = []
    for e in range(LEAVES):
        rows.append(total[e * K : (e + 1) * K])
        rows.append(total[TERM_ROWS + e : TERM_ROWS + e + 1])
    total = jnp.concatenate(rows, axis=0)
    out_ref[...] = total.T.reshape(OWN_BINS, FEATS, LEAVES * (K + 1))


def finish_call(parts):
    return pl.pallas_call(
        finish_kernel,
        out_shape=jax.ShapeDtypeStruct((OWN_BINS, FEATS, LEAVES * (K + 1)), jnp.float32),
        name="finish",
    )(*parts)


def shift(value, axis, step, size):
    return lax.ppermute(value, axis, [(i, (i + step) % size) for i in range(size)])


def swap(value, axis, bit, size):
    return lax.ppermute(value, axis, [(i, i ^ bit) for i in range(size)])


def per_device(scores, targets, signs, bins, leaves):
    x = lax.axis_index("x")
    y = lax.axis_index("y")
    zl = lax.axis_index("zl")
    core = lax.axis_index("c")
    signs_t = signs.T
    bins_t = bins.T
    leaves2 = leaves.reshape(ROWS // LANES, LANES)

    arrived = []
    for k in (2, 1, 3, 0):
        chunk = ((x + k) % 4).astype(jnp.int32).reshape(1)
        part = sketch_call(chunk, scores, targets, signs_t)
        arrived.append(shift(part, "x", k, 4) if k else part)
    mine = (arrived[0] + arrived[1]) + (arrived[2] + arrived[3])
    arrived = [lax.dynamic_index_in_dim(mine, y, 0, keepdims=False)]
    for k in (2, 1, 3):
        arrived.append(shift(lax.dynamic_index_in_dim(mine, (y + k) % 4, 0, keepdims=False), "y", k, 4))
    mine = (arrived[0] + arrived[1]) + (arrived[2] + arrived[3])
    mine = mine + swap(mine, "zh", 1, 2)
    slabs = jnp.stack([mine] + [shift(mine, "y", k, 4) for k in (1, 2, 3)])
    blocks = [slabs] + [shift(slabs, "x", k, 4) for k in (1, 2, 3)]
    place = jnp.stack([(x - k) % 4 for k in range(4)] + [(y - k) % 4 for k in range(4)]).astype(jnp.int32)
    weights = weight_call(place, blocks, leaves2)

    parts = []
    for k in (3, 2, 1, 0):
        first = 2 * OWN_BINS * (zl ^ k)
        base = jnp.stack([first + OWN_BINS * (1 - core), first + OWN_BINS * core]).astype(jnp.int32)
        own, other = hist_call(base, bins_t, weights)
        part = own + swap(other, "c", 1, 2)
        parts.append(swap(part, "zl", k, 4) if k else part)
    return finish_call(parts)


def solution(mesh):
    fine = Mesh(mesh.devices.reshape(4, 2, 4, 4, 2), ("zl", "c", "y", "x", "zh"))
    row, lab = ("zl", "c"), ("y", "x", "zh")
    in_specs = (P(row, lab), P(row, lab), P(lab, None), P(row, lab), P(row))
    out_specs = P(row, lab, None)
    return jax.shard_map(
        per_device, mesh=fine, in_specs=in_specs, out_specs=out_specs, check_vma=False
    )
```

time: 615 us -> 105 us (0.17)
  waiting for transfers between devices: 470 us -> 19.9 us
  matrix products: 105 us -> 0 us
  starting transfers between devices: 0.04 us -> 36.4 us
  Pallas kernels: 0 us -> 22.5 us
  between operations: 13.5 us -> 0.22 us
  local copies, waits for them, and re-layouts: 15.7 us -> 24.4 us
    psum x1 -> x0, waiting for transfers between devices: 409 us -> none  [per_device(): stats = lax.psum(partial_stats, 'lab')]
    dot_general x17 -> x0, matrix products: 105 us -> none  [the longest x16 93.5 us: add_block(): jnp.einsum('rfb,rc->bfc', onehot, block_weights, preferred_element_type=j...]
    reduce_scatter x1 -> x0, waiting for transfers between devices: 61.1 us -> none  [per_device(): return lax.psum_scatter(term, 'row', scatter_dimension=0, tiled=True)]
    ppermute x0 -> x20, starting transfers between devices: none -> 36.4 us  [the longest x8 18.8 us: swap(): return lax.ppermute(value, axis, [(i, i ^ bit) for i in range(size)])]
    unnamed x6 -> x30, local copies, waits for them, and re-layouts: 0.01 us -> 24.3 us
    pallas_call x0 -> x10, Pallas kernels: none -> 22.5 us  [the longest x4 12.5 us: hist_call(): pl.pallas_call(hist_kernel, grid_spec=pltpu.PrefetchScalarGridSpec(num_sc...]
    ppermute x0 -> x20, waiting for transfers between devices: none -> 19.9 us  [the longest x8 11.7 us: swap(): return lax.ppermute(value, axis, [(i, i ^ bit) for i in range(size)])]
    dynamic_slice x16 -> x0, local copies, waits for them, and re-layouts: 12.3 us -> none  [add_block(): block_bins = lax.dynamic_slice_in_dim(bins, first, block_rows, 0)]
  transfers between devices with their start and end apart: 2 -> 20, of which waited for: 2 -> 8; matrix products, arithmetic and copies ran while one was open for 0% -> 1% of each run, Pallas kernels for 0% -> 14%
where the time goes in v1:
time: 105 us; the launch traced here: 104 us
  starting transfers between devices  36.4 us (35%)
  local copies, waits for them, and re-layouts  24.4 us (23%)
  Pallas kernels  22.5 us (21%)
  waiting for transfers between devices  19.9 us (19%)
    unnamed x30, local copies, waits for them, and re-layouts  24.3 us
    ppermute x8, starting transfers between devices, swap(): return lax.ppermute(value, axis, [(i, i ^ bit) for i in range(size)])  18.8 us
    ppermute x12, starting transfers between devices, shift(): lax.ppermute(value, axis, [(i, (i + step) % size) for i in range(size)])  17.6 us
    pallas_call x4, Pallas kernels, hist_call(): pl.pallas_call(hist_kernel, grid_spec=pltpu.PrefetchScalarGridSpec(num_sc...  12.5 us
    ppermute x8, waiting for transfers between devices, swap(): return lax.ppermute(value, axis, [(i, i ^ bit) for i in range(size)])  11.7 us
    ppermute x12, waiting for transfers between devices, shift(): lax.ppermute(value, axis, [(i, (i + step) % size) for i in range(size)])  8.23 us
    pallas_call x4, Pallas kernels, sketch_call(): pl.pallas_call(sketch_kernel, grid_spec=pltpu.PrefetchScalarGridSpec(num_...  6.43 us
  transfers between devices with their start and end apart: 20, of which 8 were waited for; matrix products, arithmetic and copies ran while one was open for 1% of the time, Pallas kernels for 14%

profile of v1, /device:TPU:1, one launch (start us, length us, event | category | flops | bytes accessed | tf_op | source)
XLA Modules:
  0.0 104.5 jit_solution(5831893751617512208)
XLA Ops:
  0.0 3.4 %copy-done = s32[8192,256]{1,0:T(8,128)S(1)} copy-done((s32[8192,256]{1,0:T(8,128)S(1)}, s32[8192,256]{1,0:T(8,128)}, u32[]{:S(2)}) %copy-start) | copy-done | bytes 8388632
  3.4 2.2 %copy-done.4 = bf16[8192,256]{1,0:T(8,128)(2,1)S(1)} copy-done((bf16[8192,256]{1,0:T(8,128)(2,1)S(1)}, bf16[8192,256]{1,0:T(8,128)(2,1)}, u32[]{:S(2)}) %copy-start.4) | copy-done | bytes 4194328
  5.6 0.7 copy-done.8
  6.3 1.6 %sketch.6 = f32[4,68,128]{2,1,0:T(8,128)S(1)} custom-call(s32[1]{0:T(128)} %bitcast.14.chunk_ref, bf16[8192,256]{1,0:T(8,128)(2,1)S(1)} %copy-done.4, s32[8192,256]{1,0:T(8,128)S(1)} %copy-done, s32[16,256]{1,0:T(8,128)S(1)} %bitcast.36), custom_call_target="tpu_custom_call" | custom-call | flops 100663296 | bytes 3145728 | tf_op jit(solution)/shard_map/sketch/pallas_call | solution.py:60
  7.9 3.3 %collective-permute-start.2 = (f32[4,68,128]{2,1,0:T(8,128)S(1)}, f32[4,68,128]{2,1,0:T(8,128)S(1)}, u32[]{:S(2)}, u32[]{:S(2)}) collective-permute-start(f32[4,68,128]{2,1,0:T(8,128)S(1)} %sketch.6), channel_id=1, source_target_pairs={{0,6},{2,0},{4,2},{6,4},{1,7},{3,1},{5,3},{7,5},{8,14},{10,8},{12,... | collective-permute-start | bytes 417800 | tf_op jit(solution)/shard_map/ppermute | solution.py:198
  11.3 3.4 %copy-done.1 = s32[8192,256]{1,0:T(8,128)S(1)} copy-done((s32[8192,256]{1,0:T(8,128)S(1)}, s32[8192,256]{1,0:T(8,128)}, u32[]{:S(2)}) %copy-start.1) | copy-done | bytes 8388632
  14.6 2.2 %copy-done.5 = bf16[8192,256]{1,0:T(8,128)(2,1)S(1)} copy-done((bf16[8192,256]{1,0:T(8,128)(2,1)S(1)}, bf16[8192,256]{1,0:T(8,128)(2,1)}, u32[]{:S(2)}) %copy-start.5) | copy-done | bytes 4194328
  16.8 1.6 %sketch.4 = f32[4,68,128]{2,1,0:T(8,128)S(1)} custom-call(s32[1]{0:T(128)} %bitcast.11.chunk_ref, bf16[8192,256]{1,0:T(8,128)(2,1)S(1)} %copy-done.5, s32[8192,256]{1,0:T(8,128)S(1)} %copy-done.1, s32[16,256]{1,0:T(8,128)S(1)} %bitcast.37), custom_call_target="tpu_custom_call" | custom-call | flops 100663296 | bytes 3145728 | tf_op jit(solution)/shard_map/sketch/pallas_call | solution.py:60
  18.4 0.6 collective-permute-start
  19.0 3.4 %copy-done.2 = s32[8192,256]{1,0:T(8,128)S(1)} copy-done((s32[8192,256]{1,0:T(8,128)S(1)}, s32[8192,256]{1,0:T(8,128)}, u32[]{:S(2)}) %copy-start.2) | copy-done | bytes 8388632
  22.4 2.2 %copy-done.6 = bf16[8192,256]{1,0:T(8,128)(2,1)S(1)} copy-done((bf16[8192,256]{1,0:T(8,128)(2,1)S(1)}, bf16[8192,256]{1,0:T(8,128)(2,1)}, u32[]{:S(2)}) %copy-start.6) | copy-done | bytes 4194328
  24.6 1.6 %sketch.5 = f32[4,68,128]{2,1,0:T(8,128)S(1)} custom-call(s32[1]{0:T(128)} %bitcast.13.chunk_ref, bf16[8192,256]{1,0:T(8,128)(2,1)S(1)} %copy-done.6, s32[8192,256]{1,0:T(8,128)S(1)} %copy-done.2, s32[16,256]{1,0:T(8,128)S(1)} %bitcast.38), custom_call_target="tpu_custom_call" | custom-call | flops 100663296 | bytes 3145728 | tf_op jit(solution)/shard_map/sketch/pallas_call | solution.py:60
  26.2 0.6 collective-permute-start.1
  26.8 3.4 %copy-done.3 = s32[8192,256]{1,0:T(8,128)S(1)} copy-done((s32[8192,256]{1,0:T(8,128)S(1)}, s32[8192,256]{1,0:T(8,128)}, u32[]{:S(2)}) %copy-start.3) | copy-done | bytes 8388632
  30.2 2.2 %copy-done.7 = bf16[8192,256]{1,0:T(8,128)(2,1)S(1)} copy-done((bf16[8192,256]{1,0:T(8,128)(2,1)S(1)}, bf16[8192,256]{1,0:T(8,128)(2,1)}, u32[]{:S(2)}) %copy-start.7) | copy-done | bytes 4194328
  32.4 1.6 %sketch.7 = f32[4,68,128]{2,1,0:T(8,128)S(1)} custom-call(s32[1]{0:T(128)} %bitcast.3.chunk_ref, bf16[8192,256]{1,0:T(8,128)(2,1)S(1)} %copy-done.7, s32[8192,256]{1,0:T(8,128)S(1)} %copy-done.3, s32[16,256]{1,0:T(8,128)S(1)} %bitcast.39), custom_call_target="tpu_custom_call" | custom-call | flops 100663296 | bytes 3145728 | tf_op jit(solution)/shard_map/sketch/pallas_call | solution.py:60
  34.0 0.0 copy-start.11
  34.0 0.0 collective-permute-done.2
  34.0 0.0 collective-permute-done
  34.0 0.0 collective-permute-done.1
  34.1 3.0 %collective-permute-start.3 = (f32[68,128]{1,0:T(8,128)S(1)}, f32[68,128]{1,0:T(8,128)S(1)}, u32[]{:S(2)}, u32[]{:S(2)}) collective-permute-start(f32[68,128]{1,0:T(8,128)S(1)} %get-tuple-element.23), channel_id=1, source_target_pairs={{0,16},{8,24},{16,0},{24,8},{1,17},{9,25},{17,1},{25,9},{2,18},{10... | collective-permute-start | bytes 104456 | tf_op jit(solution)/shard_map/ppermute | solution.py:198
  37.1 0.4 collective-permute-start.4
  37.5 2.3 %collective-permute-start.5 = (f32[68,128]{1,0:T(8,128)S(1)}, f32[68,128]{1,0:T(8,128)S(1)}, u32[]{:S(2)}, u32[]{:S(2)}) collective-permute-start(f32[68,128]{1,0:T(8,128)S(1)} %get-tuple-element.21), channel_id=1, source_target_pairs={{0,24},{8,0},{16,8},{24,16},{1,25},{9,1},{17,9},{25,17},{2,26},{10... | collective-permute-start | bytes 104456 | tf_op jit(solution)/shard_map/ppermute | solution.py:198
  39.8 0.0 collective-permute-done.3
  39.8 1.4 %collective-permute-done.4 = f32[68,128]{1,0:T(8,128)S(1)} collective-permute-done((f32[68,128]{1,0:T(8,128)S(1)}, f32[68,128]{1,0:T(8,128)S(1)}, u32[]{:S(2)}, u32[]{:S(2)}) %collective-permute-start.4) | collective-permute-done | bytes 34848 | tf_op jit(solution)/shard_map/ppermute | solution.py:198
  41.2 0.0 collective-permute-done.5
  41.2 7.0 %collective-permute-start.6 = (f32[68,128]{1,0:T(8,128)S(1)}, f32[68,128]{1,0:T(8,128)S(1)}, u32[]{:S(2)}, u32[]{:S(2)}) collective-permute-start(f32[68,128]{1,0:T(8,128)S(1)} %fusion), channel_id=1, source_target_pairs={{0,1},{1,0},{2,3},{3,2},{4,5},{5,4},{6,7},{7,6},{8,9},{9,8},{10,11... | collective-permute-start | bytes 104456 | tf_op jit(solution)/shard_map/ppermute | solution.py:202
  48.2 1.3 %collective-permute-done.6 = f32[68,128]{1,0:T(8,128)S(1)} collective-permute-done((f32[68,128]{1,0:T(8,128)S(1)}, f32[68,128]{1,0:T(8,128)S(1)}, u32[]{:S(2)}, u32[]{:S(2)}) %collective-permute-start.6) | collective-permute-done | bytes 34848 | tf_op jit(solution)/shard_map/ppermute | solution.py:202
  49.6 2.6 %collective-permute-start.9 = (f32[68,128]{1,0:T(8,128)S(1)}, f32[68,128]{1,0:T(8,128)S(1)}, u32[]{:S(2)}, u32[]{:S(2)}) collective-permute-start(f32[68,128]{1,0:T(8,128)S(1)} %add.170), channel_id=1, source_target_pairs={{0,24},{8,0},{16,8},{24,16},{1,25},{9,1},{17,9},{25,17},{2,26},{10... | collective-permute-start | bytes 104456 | tf_op jit(solution)/shard_map/ppermute | solution.py:198
  52.2 0.0 collective-permute-start.8
  52.2 0.7 collective-permute-start.7
  52.9 0.4 collective-permute-done.9
  53.2 3.4 %collective-permute-done.8 = f32[68,128]{1,0:T(8,128)S(1)} collective-permute-done((f32[68,128]{1,0:T(8,128)S(1)}, f32[68,128]{1,0:T(8,128)S(1)}, u32[]{:S(2)}, u32[]{:S(2)}) %collective-permute-start.8) | collective-permute-done | bytes 34848 | tf_op jit(solution)/shard_map/ppermute | solution.py:198
  56.6 0.0 collective-permute-done.7
  56.6 1.6 %collective-permute-start.10 = (f32[4,68,128]{2,1,0:T(8,128)S(1)}, f32[4,68,128]{2,1,0:T(8,128)S(1)}, u32[]{:S(2)}, u32[]{:S(2)}) collective-permute-start(f32[4,68,128]{2,1,0:T(8,128)S(1)} %pad_maximum_fusion.s0), channel_id=1, source_target_pairs={{0,2},{2,4},{4,6},{6,0},{1,3},{3,5},{5,7},{7,1},{8,10},{10,12},{12... | collective-permute-start | bytes 417800 | tf_op jit(solution)/shard_map/ppermute | solution.py:198
  58.2 1.7 %collective-permute-start.11 = (f32[4,68,128]{2,1,0:T(8,128)S(1)}, f32[4,68,128]{2,1,0:T(8,128)S(1)}, u32[]{:S(2)}, u32[]{:S(2)}) collective-permute-start(f32[4,68,128]{2,1,0:T(8,128)S(1)} %pad_maximum_fusion.s0), channel_id=1, source_target_pairs={{0,4},{2,6},{4,0},{6,2},{1,5},{3,7},{5,1},{7,3},{8,12},{10,14},{12... | collective-permute-start | bytes 417800 | tf_op jit(solution)/shard_map/ppermute | solution.py:198
  60.0 0.8 collective-permute-start.12
  60.7 0.1 pad_add_fusion
  60.8 0.1 stack.89.place_ref
  60.9 0.1 pad_add_fusion.2
  61.0 0.9 collective-permute-done.10.s1
  61.9 2.2 %collective-permute-done.11.s2 = f32[4,68,128]{2,1,0:T(8,128)S(1)} collective-permute-done((f32[4,68,128]{2,1,0:T(8,128)S(1)}, f32[4,68,128]{2,1,0:T(8,128)S(1)}, u32[]{:S(2)}, u32[]{:S(2)}) %collective-permute-start.11) | collective-permute-done | bytes 139296 | tf_op jit(solution)/shard_map/ppermute | solution.py:198
  64.1 0.0 collective-permute-done.12.s3
  64.1 1.6 %weights.1.weights_ref = f8e4m3fn[288,8192]{1,0:T(32,128)(4,1)S(1)} custom-call(s32[8]{0:T(128)S(1)} %stack.89.place_ref, f32[4,68,128]{2,1,0:T(8,128)S(1)} %pad_maximum_fusion.s0, f32[4,68,128]{2,1,0:T(8,128)S(1)} %collective-permute-done.10.s1, f32[4,68,128]{2,1,0:T(8,128)S(1)} %collective-permute-done.11.s2, ...), custom_call_target="tpu_custom_call" | custom-call | flops 20000000 | bytes 4000000 | tf_op jit(solution)/shard_map/weights/pallas_call | solution.py:116
  65.7 3.1 %hist.4 = (f32[68,512]{1,0:T(8,128)S(1)}, f32[68,512]{1,0:T(8,128)S(1)}) custom-call(s32[2]{0:T(128)S(1)} %get-tuple-element.24.base_ref, s32[16,8192]{1,0:T(8,128)S(1)} %bitcast.41, f8e4m3fn[288,8192]{1,0:T(32,128)(4,1)S(1)} %weights.1.weights_ref), custom_call_target="tpu_custom_call" | custom-call | flops 4831838208 | bytes 3000000 | tf_op jit(solution)/shard_map/hist/pallas_call | solution.py:159
  68.8 7.2 %collective-permute-start.13 = (f32[68,512]{1,0:T(8,128)S(1)}, f32[68,512]{1,0:T(8,128)S(1)}, u32[]{:S(2)}, u32[]{:S(2)}) collective-permute-start(f32[68,512]{1,0:T(8,128)S(1)} %get-tuple-element.14), channel_id=1, source_target_pairs={{0,32},{32,0},{1,33},{33,1},{2,34},{34,2},{3,35},{35,3},{4,36},{36... | collective-permute-start | bytes 417800 | tf_op jit(solution)/shard_map/ppermute | solution.py:202
  76.1 3.1 %hist.5 = (f32[68,512]{1,0:T(8,128)S(1)}, f32[68,512]{1,0:T(8,128)S(1)}) custom-call(s32[2]{0:T(128)S(1)} %get-tuple-element.25.base_ref, s32[16,8192]{1,0:T(8,128)S(1)} %bitcast.42, f8e4m3fn[288,8192]{1,0:T(32,128)(4,1)S(1)} %weights.1.weights_ref), custom_call_target="tpu_custom_call" | custom-call | flops 4831838208 | bytes 3000000 | tf_op jit(solution)/shard_map/hist/pallas_call | solution.py:159
  79.2 0.1 collective-permute-start.15
  79.3 3.1 %hist.6 = (f32[68,512]{1,0:T(8,128)S(1)}, f32[68,512]{1,0:T(8,128)S(1)}) custom-call(s32[2]{0:T(128)S(1)} %get-tuple-element.26.base_ref, s32[16,8192]{1,0:T(8,128)S(1)} %bitcast.43, f8e4m3fn[288,8192]{1,0:T(32,128)(4,1)S(1)} %weights.1.weights_ref), custom_call_target="tpu_custom_call" | custom-call | flops 4831838208 | bytes 3000000 | tf_op jit(solution)/shard_map/hist/pallas_call | solution.py:159
  82.4 0.6 collective-permute-start.17
  83.0 3.1 %hist.7 = (f32[68,512]{1,0:T(8,128)S(1)}, f32[68,512]{1,0:T(8,128)S(1)}) custom-call(s32[2]{0:T(128)S(1)} %get-tuple-element.27.base_ref, s32[16,8192]{1,0:T(8,128)S(1)} %bitcast.44, f8e4m3fn[288,8192]{1,0:T(32,128)(4,1)S(1)} %weights.1.weights_ref), custom_call_target="tpu_custom_call" | custom-call | flops 4831838208 | bytes 3000000 | tf_op jit(solution)/shard_map/hist/pallas_call | solution.py:159
  86.2 0.1 collective-permute-start.19
  86.3 0.0 collective-permute-done.13
  86.3 3.1 %collective-permute-start.14 = (f32[68,512]{1,0:T(8,128)S(1)}, f32[68,512]{1,0:T(8,128)S(1)}, u32[]{:S(2)}, u32[]{:S(2)}) collective-permute-start(f32[68,512]{1,0:T(8,128)S(1)} %add.171), channel_id=1, source_target_pairs={{0,192},{64,128},{128,64},{192,0},{1,193},{65,129},{129,65},{193,1... | collective-permute-start | bytes 417800 | tf_op jit(solution)/shard_map/ppermute | solution.py:202
  89.4 0.1 collective-permute-start.16
  89.5 0.0 collective-permute-done.17
  89.6 0.6 collective-permute-start.18
  90.2 0.0 collective-permute-done.19
  90.2 0.7 add.180.d_ref
  90.8 2.3 %collective-permute-done.14.a_ref = f32[68,512]{1,0:T(8,128)S(1)} collective-permute-done((f32[68,512]{1,0:T(8,128)S(1)}, f32[68,512]{1,0:T(8,128)S(1)}, u32[]{:S(2)}, u32[]{:S(2)}) %collective-permute-start.14) | collective-permute-done | bytes 139296 | tf_op jit(solution)/shard_map/ppermute | solution.py:202
  93.2 8.0 %collective-permute-done.16.b_ref = f32[68,512]{1,0:T(8,128)S(1)} collective-permute-done((f32[68,512]{1,0:T(8,128)S(1)}, f32[68,512]{1,0:T(8,128)S(1)}, u32[]{:S(2)}, u32[]{:S(2)}) %collective-permute-start.16) | collective-permute-done | bytes 139296 | tf_op jit(solution)/shard_map/ppermute | solution.py:202
  101.2 0.7 copy-done.13
  101.9 0.7 copy-done.14
  102.5 2.0 %finish.1 = f32[32,16,68]{2,1,0:T(8,128)} custom-call(f32[68,512]{1,0:T(8,128)} %copy-done.12, f32[68,512]{1,0:T(8,128)} %copy-done.13, f32[68,512]{1,0:T(8,128)} %copy-done.14, f32[68,512]{1,0:T(8,128)} %add.180.d_ref), custom_call_target="tpu_custom_call" | custom-call | tf_op jit(solution)/shard_map/finish/pallas_call | solution.py:190
  (28 shorter events, 0.2 us)
Async XLA Ops:
  0.0 3.4 %copy-start = (s32[8192,256]{1,0:T(8,128)S(1)}, s32[8192,256]{1,0:T(8,128)}, u32[]{:S(2)}) copy-start(s32[8192,256]{1,0:T(8,128)} %targets_ref.7) | copy-start | bytes 25165828
  3.4 2.2 %copy-start.4 = (bf16[8192,256]{1,0:T(8,128)(2,1)S(1)}, bf16[8192,256]{1,0:T(8,128)(2,1)}, u32[]{:S(2)}) copy-start(bf16[8192,256]{1,0:T(8,128)(2,1)} %scores_ref.7) | copy-start | bytes 12582916
  5.6 0.7 copy-start.8
  6.3 5.0 %copy-start.9 = (s32[256,16]{0,1:T(8,128)S(1)}, s32[256,16]{0,1:T(8,128)}, u32[]{:S(2)}) copy-start(s32[256,16]{0,1:T(8,128)} %param.7) | copy-start | bytes 49156
  7.9 26.1 %collective-permute-start.2 = (f32[4,68,128]{2,1,0:T(8,128)S(1)}, f32[4,68,128]{2,1,0:T(8,128)S(1)}, u32[]{:S(2)}, u32[]{:S(2)}) collective-permute-start(f32[4,68,128]{2,1,0:T(8,128)S(1)} %sketch.6), channel_id=1, source_target_pairs={{0,6},{2,0},{4,2},{6,4},{1,7},{3,1},{5,3},{7,5},{8,14},{10,8},{12,... | collective-permute-start | bytes 417800 | tf_op jit(solution)/shard_map/ppermute | solution.py:198
  11.3 3.4 %copy-start.1 = (s32[8192,256]{1,0:T(8,128)S(1)}, s32[8192,256]{1,0:T(8,128)}, u32[]{:S(2)}) copy-start(s32[8192,256]{1,0:T(8,128)} %targets_ref.7) | copy-start | bytes 25165828
  14.6 2.2 %copy-start.5 = (bf16[8192,256]{1,0:T(8,128)(2,1)S(1)}, bf16[8192,256]{1,0:T(8,128)(2,1)}, u32[]{:S(2)}) copy-start(bf16[8192,256]{1,0:T(8,128)(2,1)} %scores_ref.7) | copy-start | bytes 12582916
  18.4 15.6 %collective-permute-start = (f32[4,68,128]{2,1,0:T(8,128)S(1)}, f32[4,68,128]{2,1,0:T(8,128)S(1)}, u32[]{:S(2)}, u32[]{:S(2)}) collective-permute-start(f32[4,68,128]{2,1,0:T(8,128)S(1)} %sketch.4), channel_id=1, source_target_pairs={{0,4},{2,6},{4,0},{6,2},{1,5},{3,7},{5,1},{7,3},{8,12},{10,14},{12... | collective-permute-start | bytes 417800 | tf_op jit(solution)/shard_map/ppermute | solution.py:198
  19.0 3.4 %copy-start.2 = (s32[8192,256]{1,0:T(8,128)S(1)}, s32[8192,256]{1,0:T(8,128)}, u32[]{:S(2)}) copy-start(s32[8192,256]{1,0:T(8,128)} %targets_ref.7) | copy-start | bytes 25165828
  22.4 2.2 %copy-start.6 = (bf16[8192,256]{1,0:T(8,128)(2,1)S(1)}, bf16[8192,256]{1,0:T(8,128)(2,1)}, u32[]{:S(2)}) copy-start(bf16[8192,256]{1,0:T(8,128)(2,1)} %scores_ref.7) | copy-start | bytes 12582916
  26.2 7.9 %collective-permute-start.1 = (f32[4,68,128]{2,1,0:T(8,128)S(1)}, f32[4,68,128]{2,1,0:T(8,128)S(1)}, u32[]{:S(2)}, u32[]{:S(2)}) collective-permute-start(f32[4,68,128]{2,1,0:T(8,128)S(1)} %sketch.5), channel_id=1, source_target_pairs={{0,2},{2,4},{4,6},{6,0},{1,3},{3,5},{5,7},{7,1},{8,10},{10,12},{12... | collective-permute-start | bytes 417800 | tf_op jit(solution)/shard_map/ppermute | solution.py:198
  26.8 3.4 %copy-start.3 = (s32[8192,256]{1,0:T(8,128)S(1)}, s32[8192,256]{1,0:T(8,128)}, u32[]{:S(2)}) copy-start(s32[8192,256]{1,0:T(8,128)} %targets_ref.7) | copy-start | bytes 25165828
  30.2 2.2 %copy-start.7 = (bf16[8192,256]{1,0:T(8,128)(2,1)S(1)}, bf16[8192,256]{1,0:T(8,128)(2,1)}, u32[]{:S(2)}) copy-start(bf16[8192,256]{1,0:T(8,128)(2,1)} %scores_ref.7) | copy-start | bytes 12582916
  32.4 31.7 %copy-start.10 = (s32[8192]{0:T(1024)S(1)}, s32[8192]{0:T(1024)}, u32[]{:S(2)}) copy-start(s32[8192]{0:T(1024)} %param.9) | copy-start | bytes 98308
  34.0 31.7 %copy-start.11 = (s32[8192,16]{0,1:T(8,128)S(1)}, s32[8192,16]{0,1:T(8,128)}, u32[]{:S(2)}) copy-start(s32[8192,16]{0,1:T(8,128)} %param.8) | copy-start | bytes 1572868
  34.1 5.7 %collective-permute-start.3 = (f32[68,128]{1,0:T(8,128)S(1)}, f32[68,128]{1,0:T(8,128)S(1)}, u32[]{:S(2)}, u32[]{:S(2)}) collective-permute-start(f32[68,128]{1,0:T(8,128)S(1)} %get-tuple-element.23), channel_id=1, source_target_pairs={{0,16},{8,24},{16,0},{24,8},{1,17},{9,25},{17,1},{25,9},{2,18},{10... | collective-permute-start | bytes 104456 | tf_op jit(solution)/shard_map/ppermute | solution.py:198
  37.1 4.1 %collective-permute-start.4 = (f32[68,128]{1,0:T(8,128)S(1)}, f32[68,128]{1,0:T(8,128)S(1)}, u32[]{:S(2)}, u32[]{:S(2)}) collective-permute-start(f32[68,128]{1,0:T(8,128)S(1)} %get-tuple-element.22), channel_id=1, source_target_pairs={{0,8},{8,16},{16,24},{24,0},{1,9},{9,17},{17,25},{25,1},{2,10},{10... | collective-permute-start | bytes 104456 | tf_op jit(solution)/shard_map/ppermute | solution.py:198
  37.5 3.7 %collective-permute-start.5 = (f32[68,128]{1,0:T(8,128)S(1)}, f32[68,128]{1,0:T(8,128)S(1)}, u32[]{:S(2)}, u32[]{:S(2)}) collective-permute-start(f32[68,128]{1,0:T(8,128)S(1)} %get-tuple-element.21), channel_id=1, source_target_pairs={{0,24},{8,0},{16,8},{24,16},{1,25},{9,1},{17,9},{25,17},{2,26},{10... | collective-permute-start | bytes 104456 | tf_op jit(solution)/shard_map/ppermute | solution.py:198
  41.2 8.3 %collective-permute-start.6 = (f32[68,128]{1,0:T(8,128)S(1)}, f32[68,128]{1,0:T(8,128)S(1)}, u32[]{:S(2)}, u32[]{:S(2)}) collective-permute-start(f32[68,128]{1,0:T(8,128)S(1)} %fusion), channel_id=1, source_target_pairs={{0,1},{1,0},{2,3},{3,2},{4,5},{5,4},{6,7},{7,6},{8,9},{9,8},{10,11... | collective-permute-start | bytes 104456 | tf_op jit(solution)/shard_map/ppermute | solution.py:202
  49.6 3.7 %collective-permute-start.9 = (f32[68,128]{1,0:T(8,128)S(1)}, f32[68,128]{1,0:T(8,128)S(1)}, u32[]{:S(2)}, u32[]{:S(2)}) collective-permute-start(f32[68,128]{1,0:T(8,128)S(1)} %add.170), channel_id=1, source_target_pairs={{0,24},{8,0},{16,8},{24,16},{1,25},{9,1},{17,9},{25,17},{2,26},{10... | collective-permute-start | bytes 104456 | tf_op jit(solution)/shard_map/ppermute | solution.py:198
  52.2 4.4 %collective-permute-start.8 = (f32[68,128]{1,0:T(8,128)S(1)}, f32[68,128]{1,0:T(8,128)S(1)}, u32[]{:S(2)}, u32[]{:S(2)}) collective-permute-start(f32[68,128]{1,0:T(8,128)S(1)} %add.170), channel_id=1, source_target_pairs={{0,16},{8,24},{16,0},{24,8},{1,17},{9,25},{17,1},{25,9},{2,18},{10... | collective-permute-start | bytes 104456 | tf_op jit(solution)/shard_map/ppermute | solution.py:198
  52.2 4.4 %collective-permute-start.7 = (f32[68,128]{1,0:T(8,128)S(1)}, f32[68,128]{1,0:T(8,128)S(1)}, u32[]{:S(2)}, u32[]{:S(2)}) collective-permute-start(f32[68,128]{1,0:T(8,128)S(1)} %add.170), channel_id=1, source_target_pairs={{0,8},{8,16},{16,24},{24,0},{1,9},{9,17},{17,25},{25,1},{2,10},{10... | collective-permute-start | bytes 104456 | tf_op jit(solution)/shard_map/ppermute | solution.py:198
  56.6 5.3 %collective-permute-start.10 = (f32[4,68,128]{2,1,0:T(8,128)S(1)}, f32[4,68,128]{2,1,0:T(8,128)S(1)}, u32[]{:S(2)}, u32[]{:S(2)}) collective-permute-start(f32[4,68,128]{2,1,0:T(8,128)S(1)} %pad_maximum_fusion.s0), channel_id=1, source_target_pairs={{0,2},{2,4},{4,6},{6,0},{1,3},{3,5},{5,7},{7,1},{8,10},{10,12},{12... | collective-permute-start | bytes 417800 | tf_op jit(solution)/shard_map/ppermute | solution.py:198
  58.2 5.8 %collective-permute-start.11 = (f32[4,68,128]{2,1,0:T(8,128)S(1)}, f32[4,68,128]{2,1,0:T(8,128)S(1)}, u32[]{:S(2)}, u32[]{:S(2)}) collective-permute-start(f32[4,68,128]{2,1,0:T(8,128)S(1)} %pad_maximum_fusion.s0), channel_id=1, source_target_pairs={{0,4},{2,6},{4,0},{6,2},{1,5},{3,7},{5,1},{7,3},{8,12},{10,14},{12... | collective-permute-start | bytes 417800 | tf_op jit(solution)/shard_map/ppermute | solution.py:198
  60.0 4.1 %collective-permute-start.12 = (f32[4,68,128]{2,1,0:T(8,128)S(1)}, f32[4,68,128]{2,1,0:T(8,128)S(1)}, u32[]{:S(2)}, u32[]{:S(2)}) collective-permute-start(f32[4,68,128]{2,1,0:T(8,128)S(1)} %pad_maximum_fusion.s0), channel_id=1, source_target_pairs={{0,6},{2,0},{4,2},{6,4},{1,7},{3,1},{5,3},{7,5},{8,14},{10,8},{12,... | collective-permute-start | bytes 417800 | tf_op jit(solution)/shard_map/ppermute | solution.py:198
  68.8 17.4 %collective-permute-start.13 = (f32[68,512]{1,0:T(8,128)S(1)}, f32[68,512]{1,0:T(8,128)S(1)}, u32[]{:S(2)}, u32[]{:S(2)}) collective-permute-start(f32[68,512]{1,0:T(8,128)S(1)} %get-tuple-element.14), channel_id=1, source_target_pairs={{0,32},{32,0},{1,33},{33,1},{2,34},{34,2},{3,35},{35,3},{4,36},{36... | collective-permute-start | bytes 417800 | tf_op jit(solution)/shard_map/ppermute | solution.py:202
  79.2 10.2 %collective-permute-start.15 = (f32[68,512]{1,0:T(8,128)S(1)}, f32[68,512]{1,0:T(8,128)S(1)}, u32[]{:S(2)}, u32[]{:S(2)}) collective-permute-start(f32[68,512]{1,0:T(8,128)S(1)} %get-tuple-element.16), channel_id=1, source_target_pairs={{0,32},{32,0},{1,33},{33,1},{2,34},{34,2},{3,35},{35,3},{4,36},{36... | collective-permute-start | bytes 417800 | tf_op jit(solution)/shard_map/ppermute | solution.py:202
  82.4 7.1 %collective-permute-start.17 = (f32[68,512]{1,0:T(8,128)S(1)}, f32[68,512]{1,0:T(8,128)S(1)}, u32[]{:S(2)}, u32[]{:S(2)}) collective-permute-start(f32[68,512]{1,0:T(8,128)S(1)} %get-tuple-element.18), channel_id=1, source_target_pairs={{0,32},{32,0},{1,33},{33,1},{2,34},{34,2},{3,35},{35,3},{4,36},{36... | collective-permute-start | bytes 417800 | tf_op jit(solution)/shard_map/ppermute | solution.py:202
  86.2 4.0 %collective-permute-start.19 = (f32[68,512]{1,0:T(8,128)S(1)}, f32[68,512]{1,0:T(8,128)S(1)}, u32[]{:S(2)}, u32[]{:S(2)}) collective-permute-start(f32[68,512]{1,0:T(8,128)S(1)} %get-tuple-element.20), channel_id=1, source_target_pairs={{0,32},{32,0},{1,33},{33,1},{2,34},{34,2},{3,35},{35,3},{4,36},{36... | collective-permute-start | bytes 417800 | tf_op jit(solution)/shard_map/ppermute | solution.py:202
  86.3 6.9 %collective-permute-start.14 = (f32[68,512]{1,0:T(8,128)S(1)}, f32[68,512]{1,0:T(8,128)S(1)}, u32[]{:S(2)}, u32[]{:S(2)}) collective-permute-start(f32[68,512]{1,0:T(8,128)S(1)} %add.171), channel_id=1, source_target_pairs={{0,192},{64,128},{128,64},{192,0},{1,193},{65,129},{129,65},{193,1... | collective-permute-start | bytes 417800 | tf_op jit(solution)/shard_map/ppermute | solution.py:202
  89.4 11.8 %collective-permute-start.16 = (f32[68,512]{1,0:T(8,128)S(1)}, f32[68,512]{1,0:T(8,128)S(1)}, u32[]{:S(2)}, u32[]{:S(2)}) collective-permute-start(f32[68,512]{1,0:T(8,128)S(1)} %add.174), channel_id=1, source_target_pairs={{0,128},{64,192},{128,0},{192,64},{1,129},{65,193},{129,1},{193,65... | collective-permute-start | bytes 417800 | tf_op jit(solution)/shard_map/ppermute | solution.py:202
  89.6 11.6 %collective-permute-start.18 = (f32[68,512]{1,0:T(8,128)S(1)}, f32[68,512]{1,0:T(8,128)S(1)}, u32[]{:S(2)}, u32[]{:S(2)}) collective-permute-start(f32[68,512]{1,0:T(8,128)S(1)} %add.177), channel_id=1, source_target_pairs={{0,64},{64,0},{128,192},{192,128},{1,65},{65,1},{129,193},{193,129... | collective-permute-start | bytes 417800 | tf_op jit(solution)/shard_map/ppermute | solution.py:202
  93.2 8.1 %copy-start.12 = (f32[68,512]{1,0:T(8,128)}, f32[68,512]{1,0:T(8,128)S(1)}, u32[]{:S(2)}) copy-start(f32[68,512]{1,0:T(8,128)S(1)} %collective-permute-done.14.a_ref) | copy-start | bytes 417796
  101.2 0.7 copy-start.13
  101.9 0.7 copy-start.14

commit v2 on v1

--- a/solution.py
+++ b/solution.py
@@ -26,6 +26,7 @@
 TERM_ROWS = LEAVES * K
 W_ROWS = 288
 OWN_BINS = 32
+HIST_COST = 1000
 
 
 def sketch_kernel(chunk_ref, scores_ref, targets_ref, signs_ref, out_ref):
@@ -70,7 +71,7 @@
             out_specs=pl.BlockSpec((1, SLAB_ROWS, LANES), lambda i, c: (i, 0, 0)),
         ),
         out_shape=jax.ShapeDtypeStruct((4, SLAB_ROWS, LANES), jnp.float32),
-        compiler_params=pltpu.CompilerParams(vmem_limit_bytes=16 << 20),
+        compiler_params=pltpu.CompilerParams(vmem_limit_bytes=58 << 20),
         cost_estimate=pl.CostEstimate(
             flops=2 * 4 * SLAB * 768 * 32, bytes_accessed=4 * SLAB * LABS * 6, transcendentals=4 * SLAB * LABS
         ),
@@ -92,7 +93,7 @@
     zeros = jnp.zeros((K, LANES), jnp.float32)
     for kx, stats_ref in enumerate((s0, s1, s2, s3)):
         for ky in range(4):
-            chunk = place_ref[kx] * 4 + place_ref[4 + ky]
+            chunk = place_ref[kx] * 4 + ky
             for quad in range(QUADS):
                 leaf = leaves_ref[pl.ds(chunk * QUADS + quad, 1), :]
                 sketch = stats_ref[ky, quad * K : (quad + 1) * K, :]
@@ -170,7 +171,7 @@
         out_shape=[shape, shape],
         compiler_params=pltpu.CompilerParams(vmem_limit_bytes=40 << 20),
         cost_estimate=pl.CostEstimate(
-            flops=2 * 2 * cols * ROWS * W_ROWS, bytes_accessed=3_000_000, transcendentals=0
+            flops=HIST_COST, bytes_accessed=1000, transcendentals=0
         ),
         name="hist",
     )(base, bins_t, weights)
@@ -190,50 +191,44 @@
     return pl.pallas_call(
         finish_kernel,
         out_shape=jax.ShapeDtypeStruct((OWN_BINS, FEATS, LEAVES * (K + 1)), jnp.float32),
+        compiler_params=pltpu.CompilerParams(vmem_limit_bytes=8 << 20),
         name="finish",
     )(*parts)
 
 
-def shift(value, axis, step, size):
-    return lax.ppermute(value, axis, [(i, (i + step) % size) for i in range(size)])
-
-
 def swap(value, axis, bit, size):
     return lax.ppermute(value, axis, [(i, i ^ bit) for i in range(size)])
 
 
 def per_device(scores, targets, signs, bins, leaves):
-    x = lax.axis_index("x")
-    y = lax.axis_index("y")
-    zl = lax.axis_index("zl")
-    core = lax.axis_index("c")
+    x = lax.axis_index("x").astype(jnp.int32)
+    zl = lax.axis_index("zl").astype(jnp.int32)
+    core = lax.axis_index("c").astype(jnp.int32)
     signs_t = signs.T
     bins_t = bins.T
     leaves2 = leaves.reshape(ROWS // LANES, LANES)
 
     arrived = []
     for k in (2, 1, 3, 0):
-        chunk = ((x + k) % 4).astype(jnp.int32).reshape(1)
-        part = sketch_call(chunk, scores, targets, signs_t)
-        arrived.append(shift(part, "x", k, 4) if k else part)
+        part = sketch_call((x ^ k).reshape(1), scores, targets, signs_t)
+        arrived.append(swap(part, "x", k, 4) if k else part)
     mine = (arrived[0] + arrived[1]) + (arrived[2] + arrived[3])
-    arrived = [lax.dynamic_index_in_dim(mine, y, 0, keepdims=False)]
-    for k in (2, 1, 3):
-        arrived.append(shift(lax.dynamic_index_in_dim(mine, (y + k) % 4, 0, keepdims=False), "y", k, 4))
-    mine = (arrived[0] + arrived[1]) + (arrived[2] + arrived[3])
+    arrived = [swap(mine, "y", k, 4) for k in (2, 1, 3)]
+    mine = (mine + arrived[0]) + (arrived[1] + arrived[2])
     mine = mine + swap(mine, "zh", 1, 2)
-    slabs = jnp.stack([mine] + [shift(mine, "y", k, 4) for k in (1, 2, 3)])
-    blocks = [slabs] + [shift(slabs, "x", k, 4) for k in (1, 2, 3)]
-    place = jnp.stack([(x - k) % 4 for k in range(4)] + [(y - k) % 4 for k in range(4)]).astype(jnp.int32)
-    weights = weight_call(place, blocks, leaves2)
-
-    parts = []
-    for k in (3, 2, 1, 0):
+    blocks = [mine] + [swap(mine, "x", k, 4) for k in (1, 2, 3)]
+    weights = weight_call(jnp.stack([x ^ k for k in range(4)]), blocks, leaves2)
+
+    sums, parts = [], []
+    for step, k in enumerate((3, 2, 1, 0)):
         first = 2 * OWN_BINS * (zl ^ k)
-        base = jnp.stack([first + OWN_BINS * (1 - core), first + OWN_BINS * core]).astype(jnp.int32)
+        base = jnp.stack([first + OWN_BINS * (1 - core), first + OWN_BINS * core])
+        if step >= 2:
+            base, sums[step - 2] = lax.optimization_barrier((base, sums[step - 2]))
+            parts.append(swap(sums[step - 2], "zl", (3, 2)[step - 2], 4))
         own, other = hist_call(base, bins_t, weights)
-        part = own + swap(other, "c", 1, 2)
-        parts.append(swap(part, "zl", k, 4) if k else part)
+        sums.append(own + swap(other, "c", 1, 2))
+    parts += [swap(sums[2], "zl", 1, 4), sums[3]]
     return finish_call(parts)
 
 

time: 105 us -> 88.8 us (0.85)
  local copies, waits for them, and re-layouts: 24.4 us -> 0.01 us
  Pallas kernels: 22.5 us -> 32.7 us
  starting transfers between devices: 36.4 us -> 30.4 us
  other arithmetic: 0.96 us -> 3.99 us
  waiting for transfers between devices: 19.9 us -> 21.2 us
    unnamed x30 -> x4, local copies, waits for them, and re-layouts: 24.3 us -> 0.01 us
    ppermute x12 -> x0, starting transfers between devices: 17.6 us -> none  [shift(): lax.ppermute(value, axis, [(i, (i + step) % size) for i in range(size)])]
    ppermute x8 -> x17, starting transfers between devices: 18.8 us -> 30.4 us  [swap(): return lax.ppermute(value, axis, [(i, i ^ bit) for i in range(size)])]
    pallas_call x4, Pallas kernels: 6.43 us -> 17.3 us  [sketch_call(): pl.pallas_call(sketch_kernel, grid_spec=pltpu.PrefetchScalarGridSpec(num_...]
    ppermute x8 -> x17, waiting for transfers between devices: 11.7 us -> 21.2 us  [swap(): return lax.ppermute(value, axis, [(i, i ^ bit) for i in range(size)])]
    ppermute x12 -> x0, waiting for transfers between devices: 8.23 us -> none  [shift(): lax.ppermute(value, axis, [(i, (i + step) % size) for i in range(size)])]
    add x4 -> x5, other arithmetic: 0.75 us -> 2.6 us  [the longest x4 2.57 us: per_device(): sums.append(own + swap(other, 'c', 1, 2))]
    pallas_call x1, Pallas kernels: 1.97 us -> 0.85 us  [finish_call(): pl.pallas_call(finish_kernel, out_shape=jax.ShapeDtypeStruct((OWN_BINS, F...]
  transfers between devices with their start and end apart: 20 -> 17, of which waited for: 8 -> 6; matrix products, arithmetic and copies ran while one was open for 1% -> 3% of each run, Pallas kernels for 14% -> 25%
where the time goes in v2:
time: 88.8 us; the launch traced here: 88.4 us
  Pallas kernels  32.7 us (37%)
  starting transfers between devices  30.4 us (34%)
  waiting for transfers between devices  21.2 us (24%)
  other arithmetic  3.99 us (4%)
    ppermute x17, starting transfers between devices, swap(): return lax.ppermute(value, axis, [(i, i ^ bit) for i in range(size)])  30.4 us
    ppermute x17, waiting for transfers between devices, swap(): return lax.ppermute(value, axis, [(i, i ^ bit) for i in range(size)])  21.2 us
    pallas_call x4, Pallas kernels, sketch_call(): pl.pallas_call(sketch_kernel, grid_spec=pltpu.PrefetchScalarGridSpec(num_...  17.3 us
    pallas_call x4, Pallas kernels, hist_call(): pl.pallas_call(hist_kernel, grid_spec=pltpu.PrefetchScalarGridSpec(num_sc...  12.9 us
    add x4, other arithmetic, per_device(): sums.append(own + swap(other, 'c', 1, 2))  2.57 us
  transfers between devices with their start and end apart: 17, of which 6 were waited for; matrix products, arithmetic and copies ran while one was open for 3% of the time, Pallas kernels for 25%

profile of v2, /device:TPU:1, one launch (start us, length us, event | category | flops | bytes accessed | tf_op | source)
XLA Modules:
  0.0 88.4 jit_solution(3805961209818908249)
XLA Ops:
  0.0 4.3 %sketch.6 = f32[4,68,128]{2,1,0:T(8,128)} custom-call(s32[1]{0:T(128)} %bitcast.8.chunk_ref, bf16[8192,256]{1,0:T(8,128)(2,1)} %scores_ref.7, s32[8192,256]{1,0:T(8,128)} %targets_ref.7, s32[16,256]{1,0:T(8,128)} %bitcast.20), custom_call_target="tpu_custom_call" | custom-call | flops 100663296 | bytes 3145728 | tf_op jit(solution)/shard_map/sketch/pallas_call | solution.py:61
  4.3 3.3 %collective-permute-start.2 = (f32[4,68,128]{2,1,0:T(8,128)}, f32[4,68,128]{2,1,0:T(8,128)S(1)}, u32[]{:S(2)}, u32[]{:S(2)}) collective-permute-start(f32[4,68,128]{2,1,0:T(8,128)} %sketch.6), channel_id=1, source_target_pairs={{0,6},{2,4},{4,2},{6,0},{1,7},{3,5},{5,3},{7,1},{8,14},{10,12},{12... | collective-permute-start | bytes 417800 | tf_op jit(solution)/shard_map/ppermute | solution.py:200
  7.7 4.3 %sketch.4 = f32[4,68,128]{2,1,0:T(8,128)} custom-call(s32[1]{0:T(128)} %bitcast.7.chunk_ref, bf16[8192,256]{1,0:T(8,128)(2,1)} %scores_ref.7, s32[8192,256]{1,0:T(8,128)} %targets_ref.7, s32[16,256]{1,0:T(8,128)} %bitcast.21), custom_call_target="tpu_custom_call" | custom-call | flops 100663296 | bytes 3145728 | tf_op jit(solution)/shard_map/sketch/pallas_call | solution.py:61
  12.0 0.5 collective-permute-start
  12.5 4.3 %sketch.5 = f32[4,68,128]{2,1,0:T(8,128)} custom-call(s32[1]{0:T(128)} %bitcast.6.chunk_ref, bf16[8192,256]{1,0:T(8,128)(2,1)} %scores_ref.7, s32[8192,256]{1,0:T(8,128)} %targets_ref.7, s32[16,256]{1,0:T(8,128)} %bitcast.22), custom_call_target="tpu_custom_call" | custom-call | flops 100663296 | bytes 3145728 | tf_op jit(solution)/shard_map/sketch/pallas_call | solution.py:61
  16.8 0.1 collective-permute-start.1
  16.9 0.0 copy-start.1
  16.9 4.3 %sketch.7 = f32[4,68,128]{2,1,0:T(8,128)} custom-call(s32[1]{0:T(128)} %bitcast.5.chunk_ref, bf16[8192,256]{1,0:T(8,128)(2,1)} %scores_ref.7, s32[8192,256]{1,0:T(8,128)} %targets_ref.7, s32[16,256]{1,0:T(8,128)} %bitcast.23), custom_call_target="tpu_custom_call" | custom-call | flops 100663296 | bytes 3145728 | tf_op jit(solution)/shard_map/sketch/pallas_call | solution.py:61
  21.3 0.0 copy-start
  21.3 0.0 collective-permute-done.2
  21.3 0.0 collective-permute-done
  21.3 0.0 collective-permute-done.1
  21.3 1.0 %add_add_fusion.1 = f32[4,68,128]{2,1,0:T(8,128)S(1)} fusion(f32[4,68,128]{2,1,0:T(8,128)S(1)} %collective-permute-done.2, f32[4,68,128]{2,1,0:T(8,128)} %sketch.7, f32[4,68,128]{2,1,0:T(8,128)S(1)} %collective-permute-done, f32[4,68,128]{2,1,0:T(8,128)S(1)} %collective-permute-done.1), kind=kLoop, calls=%fused_computation.1 | loop fusion | flops 104448 | bytes 696320 | tf_op jit(solution)/shard_map/add | solution.py:215
  22.3 1.6 %collective-permute-start.4 = (f32[4,68,128]{2,1,0:T(8,128)S(1)}, f32[4,68,128]{2,1,0:T(8,128)S(1)}, u32[]{:S(2)}, u32[]{:S(2)}) collective-permute-start(f32[4,68,128]{2,1,0:T(8,128)S(1)} %add_add_fusion.1), channel_id=1, source_target_pairs={{0,8},{8,0},{16,24},{24,16},{1,9},{9,1},{17,25},{25,17},{2,10},{10... | collective-permute-start | bytes 417800 | tf_op jit(solution)/shard_map/ppermute | solution.py:200
  23.8 1.9 %collective-permute-start.5 = (f32[4,68,128]{2,1,0:T(8,128)S(1)}, f32[4,68,128]{2,1,0:T(8,128)S(1)}, u32[]{:S(2)}, u32[]{:S(2)}) collective-permute-start(f32[4,68,128]{2,1,0:T(8,128)S(1)} %add_add_fusion.1), channel_id=1, source_target_pairs={{0,24},{8,16},{16,8},{24,0},{1,25},{9,17},{17,9},{25,1},{2,26},{10... | collective-permute-start | bytes 417800 | tf_op jit(solution)/shard_map/ppermute | solution.py:200
  25.7 0.7 collective-permute-start.3
  26.5 0.0 collective-permute-done.4
  26.5 2.6 %collective-permute-done.5 = f32[4,68,128]{2,1,0:T(8,128)S(1)} collective-permute-done((f32[4,68,128]{2,1,0:T(8,128)S(1)}, f32[4,68,128]{2,1,0:T(8,128)S(1)}, u32[]{:S(2)}, u32[]{:S(2)}) %collective-permute-start.5) | collective-permute-done | bytes 139296 | tf_op jit(solution)/shard_map/ppermute | solution.py:200
  29.1 3.7 %collective-permute-done.3 = f32[4,68,128]{2,1,0:T(8,128)S(1)} collective-permute-done((f32[4,68,128]{2,1,0:T(8,128)S(1)}, f32[4,68,128]{2,1,0:T(8,128)S(1)}, u32[]{:S(2)}, u32[]{:S(2)}) %collective-permute-start.3) | collective-permute-done | bytes 139296 | tf_op jit(solution)/shard_map/ppermute | solution.py:200
  32.7 7.0 %collective-permute-start.6 = (f32[4,68,128]{2,1,0:T(8,128)S(1)}, f32[4,68,128]{2,1,0:T(8,128)S(1)}, u32[]{:S(2)}, u32[]{:S(2)}) collective-permute-start(f32[4,68,128]{2,1,0:T(8,128)S(1)} %add_add_fusion), channel_id=1, source_target_pairs={{0,1},{1,0},{2,3},{3,2},{4,5},{5,4},{6,7},{7,6},{8,9},{9,8},{10,11... | collective-permute-start | bytes 417800 | tf_op jit(solution)/shard_map/ppermute | solution.py:200
  39.7 2.6 %collective-permute-done.6 = f32[4,68,128]{2,1,0:T(8,128)S(1)} collective-permute-done((f32[4,68,128]{2,1,0:T(8,128)S(1)}, f32[4,68,128]{2,1,0:T(8,128)S(1)}, u32[]{:S(2)}, u32[]{:S(2)}) %collective-permute-start.6) | collective-permute-done | bytes 139296 | tf_op jit(solution)/shard_map/ppermute | solution.py:200
  42.4 1.7 %collective-permute-start.7 = (f32[4,68,128]{2,1,0:T(8,128)S(1)}, f32[4,68,128]{2,1,0:T(8,128)S(1)}, u32[]{:S(2)}, u32[]{:S(2)}) collective-permute-start(f32[4,68,128]{2,1,0:T(8,128)S(1)} %add.67.s0), channel_id=1, source_target_pairs={{0,2},{2,0},{4,6},{6,4},{1,3},{3,1},{5,7},{7,5},{8,10},{10,8},{12,... | collective-permute-start | bytes 417800 | tf_op jit(solution)/shard_map/ppermute | solution.py:200
  44.1 2.5 %collective-permute-start.8 = (f32[4,68,128]{2,1,0:T(8,128)S(1)}, f32[4,68,128]{2,1,0:T(8,128)S(1)}, u32[]{:S(2)}, u32[]{:S(2)}) collective-permute-start(f32[4,68,128]{2,1,0:T(8,128)S(1)} %add.67.s0), channel_id=1, source_target_pairs={{0,4},{2,6},{4,0},{6,2},{1,5},{3,7},{5,1},{7,3},{8,12},{10,14},{12... | collective-permute-start | bytes 417800 | tf_op jit(solution)/shard_map/ppermute | solution.py:200
  46.6 0.0 collective-permute-start.9
  46.6 0.1 pad_add_fusion.2.place_ref
  46.7 0.1 pad_add_fusion.1.base_ref
  46.8 0.0 collective-permute-done.7.s1
  46.8 4.0 %collective-permute-done.8.s2 = f32[4,68,128]{2,1,0:T(8,128)S(1)} collective-permute-done((f32[4,68,128]{2,1,0:T(8,128)S(1)}, f32[4,68,128]{2,1,0:T(8,128)S(1)}, u32[]{:S(2)}, u32[]{:S(2)}) %collective-permute-start.8) | collective-permute-done | bytes 139296 | tf_op jit(solution)/shard_map/ppermute | solution.py:200
  50.7 1.5 %collective-permute-done.9.s3 = f32[4,68,128]{2,1,0:T(8,128)S(1)} collective-permute-done((f32[4,68,128]{2,1,0:T(8,128)S(1)}, f32[4,68,128]{2,1,0:T(8,128)S(1)}, u32[]{:S(2)}, u32[]{:S(2)}) %collective-permute-start.9) | collective-permute-done | bytes 139296 | tf_op jit(solution)/shard_map/ppermute | solution.py:200
  52.2 0.0 copy-done.1
  52.2 1.6 %weights.1.weights_ref = f8e4m3fn[288,8192]{1,0:T(32,128)(4,1)S(1)} custom-call(s32[4]{0:T(128)S(1)} %pad_add_fusion.2.place_ref, f32[4,68,128]{2,1,0:T(8,128)S(1)} %add.67.s0, f32[4,68,128]{2,1,0:T(8,128)S(1)} %collective-permute-done.7.s1, f32[4,68,128]{2,1,0:T(8,128)S(1)} %collective-permute-done.8.s2, f32[4,68,128]{2,1,0:T(8,128)S(1)} %collective-permute-done.9.s3, ...), custom_call_target="tpu_custom_call" | custom-call | flops 20000000 | bytes 4000000 | tf_op jit(solution)/shard_map/weights/pallas_call | solution.py:117
  53.9 0.0 copy-done
  53.9 3.5 %hist.4 = (f32[68,512]{1,0:T(8,128)S(1)}, f32[68,512]{1,0:T(8,128)}) custom-call(s32[2]{0:T(128)S(1)} %pad_add_fusion.1.base_ref, s32[16,8192]{1,0:T(8,128)S(1)} %bitcast.15, f8e4m3fn[288,8192]{1,0:T(32,128)(4,1)S(1)} %weights.1.weights_ref), custom_call_target="tpu_custom_call" | custom-call | flops 1000 | bytes 1000 | tf_op jit(solution)/shard_map/hist/pallas_call | solution.py:160
  57.4 5.4 %collective-permute-start.10 = (f32[68,512]{1,0:T(8,128)}, f32[68,512]{1,0:T(8,128)S(1)}, u32[]{:S(2)}, u32[]{:S(2)}) collective-permute-start(f32[68,512]{1,0:T(8,128)} %get-tuple-element.18), channel_id=1, source_target_pairs={{0,32},{32,0},{1,33},{33,1},{2,34},{34,2},{3,35},{35,3},{4,36},{36... | collective-permute-start | bytes 417800 | tf_op jit(solution)/shard_map/ppermute | solution.py:200
  62.8 0.1 pad_add_fusion.4.base_ref
  62.9 3.1 %hist.5 = (f32[68,512]{1,0:T(8,128)S(1)}, f32[68,512]{1,0:T(8,128)S(1)}) custom-call(s32[2]{0:T(128)S(1)} %pad_add_fusion.4.base_ref, s32[16,8192]{1,0:T(8,128)S(1)} %bitcast.16, f8e4m3fn[288,8192]{1,0:T(32,128)(4,1)S(1)} %weights.1.weights_ref), custom_call_target="tpu_custom_call" | custom-call | flops 1000 | bytes 1000 | tf_op jit(solution)/shard_map/hist/pallas_call | solution.py:160
  66.0 0.1 collective-permute-start.12
  66.1 0.1 pad_add_fusion.base_ref
  66.2 0.0 collective-permute-done.10
  66.2 0.7 add.68
  66.9 3.1 %hist.6 = (f32[68,512]{1,0:T(8,128)S(1)}, f32[68,512]{1,0:T(8,128)S(1)}) custom-call(s32[2]{0:T(128)S(1)} %pad_add_fusion.base_ref, s32[16,8192]{1,0:T(8,128)S(1)} %bitcast.17, f8e4m3fn[288,8192]{1,0:T(32,128)(4,1)S(1)} %weights.1.weights_ref), custom_call_target="tpu_custom_call" | custom-call | flops 1000 | bytes 1000 | tf_op jit(solution)/shard_map/hist/pallas_call | solution.py:160
  70.0 0.6 collective-permute-start.14
  70.6 0.1 pad_add_fusion.3.base_ref
  70.7 3.1 %collective-permute-start.11 = (f32[68,512]{1,0:T(8,128)}, f32[68,512]{1,0:T(8,128)S(1)}, u32[]{:S(2)}, u32[]{:S(2)}) collective-permute-start(f32[68,512]{1,0:T(8,128)} %add.68), channel_id=1, source_target_pairs={{0,192},{64,128},{128,64},{192,0},{1,193},{65,129},{129,65},{193,1... | collective-permute-start | bytes 417800 | tf_op jit(solution)/shard_map/ppermute | solution.py:200
  73.8 0.0 collective-permute-done.12
  73.8 0.9 %add.73 = f32[68,512]{1,0:T(8,128)S(1)} add(f32[68,512]{1,0:T(8,128)S(1)} %get-tuple-element.20, f32[68,512]{1,0:T(8,128)} %collective-permute-done.12) | non-fusion elementwise | flops 34816 | bytes 417792 | tf_op jit(solution)/shard_map/add | solution.py:230
  74.7 3.1 %hist.7 = (f32[68,512]{1,0:T(8,128)S(1)}, f32[68,512]{1,0:T(8,128)S(1)}) custom-call(s32[2]{0:T(128)S(1)} %pad_add_fusion.3.base_ref, s32[16,8192]{1,0:T(8,128)S(1)} %bitcast.18, f8e4m3fn[288,8192]{1,0:T(32,128)(4,1)S(1)} %weights.1.weights_ref), custom_call_target="tpu_custom_call" | custom-call | flops 1000 | bytes 1000 | tf_op jit(solution)/shard_map/hist/pallas_call | solution.py:160
  77.9 0.4 collective-permute-start.16
  78.3 0.9 %collective-permute-start.13 = (f32[68,512]{1,0:T(8,128)S(1)}, f32[68,512]{1,0:T(8,128)S(1)}, u32[]{:S(2)}, u32[]{:S(2)}) collective-permute-start(f32[68,512]{1,0:T(8,128)S(1)} %add.73), channel_id=1, source_target_pairs={{0,128},{64,192},{128,0},{192,64},{1,129},{65,193},{129,1},{193,65... | collective-permute-start | bytes 417800 | tf_op jit(solution)/shard_map/ppermute | solution.py:200
  79.2 0.0 collective-permute-done.14
  79.2 0.9 %add.74 = f32[68,512]{1,0:T(8,128)S(1)} add(f32[68,512]{1,0:T(8,128)S(1)} %get-tuple-element.24, f32[68,512]{1,0:T(8,128)} %collective-permute-done.14) | non-fusion elementwise | flops 34816 | bytes 417792 | tf_op jit(solution)/shard_map/add | solution.py:230
  80.1 0.6 collective-permute-start.15
  80.7 0.0 collective-permute-done.16
  80.7 0.0 collective-permute-done.11.a_ref
  80.7 6.8 %collective-permute-done.13.b_ref = f32[68,512]{1,0:T(8,128)S(1)} collective-permute-done((f32[68,512]{1,0:T(8,128)S(1)}, f32[68,512]{1,0:T(8,128)S(1)}, u32[]{:S(2)}, u32[]{:S(2)}) %collective-permute-start.13) | collective-permute-done | bytes 139296 | tf_op jit(solution)/shard_map/ppermute | solution.py:200
  87.6 0.0 collective-permute-done.15.c_ref
  87.6 0.8 finish.1
  (3 shorter events, 0.1 us)
Async XLA Ops:
  4.3 16.9 %collective-permute-start.2 = (f32[4,68,128]{2,1,0:T(8,128)}, f32[4,68,128]{2,1,0:T(8,128)S(1)}, u32[]{:S(2)}, u32[]{:S(2)}) collective-permute-start(f32[4,68,128]{2,1,0:T(8,128)} %sketch.6), channel_id=1, source_target_pairs={{0,6},{2,4},{4,2},{6,0},{1,7},{3,5},{5,3},{7,1},{8,14},{10,12},{12... | collective-permute-start | bytes 417800 | tf_op jit(solution)/shard_map/ppermute | solution.py:200
  12.0 9.3 %collective-permute-start = (f32[4,68,128]{2,1,0:T(8,128)}, f32[4,68,128]{2,1,0:T(8,128)S(1)}, u32[]{:S(2)}, u32[]{:S(2)}) collective-permute-start(f32[4,68,128]{2,1,0:T(8,128)} %sketch.4), channel_id=1, source_target_pairs={{0,4},{2,6},{4,0},{6,2},{1,5},{3,7},{5,1},{7,3},{8,12},{10,14},{12... | collective-permute-start | bytes 417800 | tf_op jit(solution)/shard_map/ppermute | solution.py:200
  16.8 4.4 %collective-permute-start.1 = (f32[4,68,128]{2,1,0:T(8,128)}, f32[4,68,128]{2,1,0:T(8,128)S(1)}, u32[]{:S(2)}, u32[]{:S(2)}) collective-permute-start(f32[4,68,128]{2,1,0:T(8,128)} %sketch.5), channel_id=1, source_target_pairs={{0,2},{2,0},{4,6},{6,4},{1,3},{3,1},{5,7},{7,5},{8,10},{10,8},{12,... | collective-permute-start | bytes 417800 | tf_op jit(solution)/shard_map/ppermute | solution.py:200
  16.9 35.3 %copy-start.1 = (s32[8192]{0:T(1024)S(1)}, s32[8192]{0:T(1024)}, u32[]{:S(2)}) copy-start(s32[8192]{0:T(1024)} %param.9) | copy-start | bytes 98308
  21.3 32.6 %copy-start = (s32[8192,16]{0,1:T(8,128)S(1)}, s32[8192,16]{0,1:T(8,128)}, u32[]{:S(2)}) copy-start(s32[8192,16]{0,1:T(8,128)} %param.8) | copy-start | bytes 1572868
  22.3 4.2 %collective-permute-start.4 = (f32[4,68,128]{2,1,0:T(8,128)S(1)}, f32[4,68,128]{2,1,0:T(8,128)S(1)}, u32[]{:S(2)}, u32[]{:S(2)}) collective-permute-start(f32[4,68,128]{2,1,0:T(8,128)S(1)} %add_add_fusion.1), channel_id=1, source_target_pairs={{0,8},{8,0},{16,24},{24,16},{1,9},{9,1},{17,25},{25,17},{2,10},{10... | collective-permute-start | bytes 417800 | tf_op jit(solution)/shard_map/ppermute | solution.py:200
  23.8 5.2 %collective-permute-start.5 = (f32[4,68,128]{2,1,0:T(8,128)S(1)}, f32[4,68,128]{2,1,0:T(8,128)S(1)}, u32[]{:S(2)}, u32[]{:S(2)}) collective-permute-start(f32[4,68,128]{2,1,0:T(8,128)S(1)} %add_add_fusion.1), channel_id=1, source_target_pairs={{0,24},{8,16},{16,8},{24,0},{1,25},{9,17},{17,9},{25,1},{2,26},{10... | collective-permute-start | bytes 417800 | tf_op jit(solution)/shard_map/ppermute | solution.py:200
  25.7 7.0 %collective-permute-start.3 = (f32[4,68,128]{2,1,0:T(8,128)S(1)}, f32[4,68,128]{2,1,0:T(8,128)S(1)}, u32[]{:S(2)}, u32[]{:S(2)}) collective-permute-start(f32[4,68,128]{2,1,0:T(8,128)S(1)} %add_add_fusion.1), channel_id=1, source_target_pairs={{0,16},{8,24},{16,0},{24,8},{1,17},{9,25},{17,1},{25,9},{2,18},{10... | collective-permute-start | bytes 417800 | tf_op jit(solution)/shard_map/ppermute | solution.py:200
  32.7 9.6 %collective-permute-start.6 = (f32[4,68,128]{2,1,0:T(8,128)S(1)}, f32[4,68,128]{2,1,0:T(8,128)S(1)}, u32[]{:S(2)}, u32[]{:S(2)}) collective-permute-start(f32[4,68,128]{2,1,0:T(8,128)S(1)} %add_add_fusion), channel_id=1, source_target_pairs={{0,1},{1,0},{2,3},{3,2},{4,5},{5,4},{6,7},{7,6},{8,9},{9,8},{10,11... | collective-permute-start | bytes 417800 | tf_op jit(solution)/shard_map/ppermute | solution.py:200
  42.4 4.3 %collective-permute-start.7 = (f32[4,68,128]{2,1,0:T(8,128)S(1)}, f32[4,68,128]{2,1,0:T(8,128)S(1)}, u32[]{:S(2)}, u32[]{:S(2)}) collective-permute-start(f32[4,68,128]{2,1,0:T(8,128)S(1)} %add.67.s0), channel_id=1, source_target_pairs={{0,2},{2,0},{4,6},{6,4},{1,3},{3,1},{5,7},{7,5},{8,10},{10,8},{12,... | collective-permute-start | bytes 417800 | tf_op jit(solution)/shard_map/ppermute | solution.py:200
  44.1 6.6 %collective-permute-start.8 = (f32[4,68,128]{2,1,0:T(8,128)S(1)}, f32[4,68,128]{2,1,0:T(8,128)S(1)}, u32[]{:S(2)}, u32[]{:S(2)}) collective-permute-start(f32[4,68,128]{2,1,0:T(8,128)S(1)} %add.67.s0), channel_id=1, source_target_pairs={{0,4},{2,6},{4,0},{6,2},{1,5},{3,7},{5,1},{7,3},{8,12},{10,14},{12... | collective-permute-start | bytes 417800 | tf_op jit(solution)/shard_map/ppermute | solution.py:200
  46.6 5.7 %collective-permute-start.9 = (f32[4,68,128]{2,1,0:T(8,128)S(1)}, f32[4,68,128]{2,1,0:T(8,128)S(1)}, u32[]{:S(2)}, u32[]{:S(2)}) collective-permute-start(f32[4,68,128]{2,1,0:T(8,128)S(1)} %add.67.s0), channel_id=1, source_target_pairs={{0,6},{2,4},{4,2},{6,0},{1,7},{3,5},{5,3},{7,1},{8,14},{10,12},{12... | collective-permute-start | bytes 417800 | tf_op jit(solution)/shard_map/ppermute | solution.py:200
  57.4 8.8 %collective-permute-start.10 = (f32[68,512]{1,0:T(8,128)}, f32[68,512]{1,0:T(8,128)S(1)}, u32[]{:S(2)}, u32[]{:S(2)}) collective-permute-start(f32[68,512]{1,0:T(8,128)} %get-tuple-element.18), channel_id=1, source_target_pairs={{0,32},{32,0},{1,33},{33,1},{2,34},{34,2},{3,35},{35,3},{4,36},{36... | collective-permute-start | bytes 417800 | tf_op jit(solution)/shard_map/ppermute | solution.py:200
  66.0 7.8 %collective-permute-start.12 = (f32[68,512]{1,0:T(8,128)S(1)}, f32[68,512]{1,0:T(8,128)}, u32[]{:S(2)}, u32[]{:S(2)}) collective-permute-start(f32[68,512]{1,0:T(8,128)S(1)} %get-tuple-element.21), channel_id=1, source_target_pairs={{0,32},{32,0},{1,33},{33,1},{2,34},{34,2},{3,35},{35,3},{4,36},{36... | collective-permute-start | bytes 417800 | tf_op jit(solution)/shard_map/ppermute | solution.py:200
  70.0 9.2 %collective-permute-start.14 = (f32[68,512]{1,0:T(8,128)S(1)}, f32[68,512]{1,0:T(8,128)}, u32[]{:S(2)}, u32[]{:S(2)}) collective-permute-start(f32[68,512]{1,0:T(8,128)S(1)} %get-tuple-element.25), channel_id=1, source_target_pairs={{0,32},{32,0},{1,33},{33,1},{2,34},{34,2},{3,35},{35,3},{4,36},{36... | collective-permute-start | bytes 417800 | tf_op jit(solution)/shard_map/ppermute | solution.py:200
  70.7 10.1 %collective-permute-start.11 = (f32[68,512]{1,0:T(8,128)}, f32[68,512]{1,0:T(8,128)S(1)}, u32[]{:S(2)}, u32[]{:S(2)}) collective-permute-start(f32[68,512]{1,0:T(8,128)} %add.68), channel_id=1, source_target_pairs={{0,192},{64,128},{128,64},{192,0},{1,193},{65,129},{129,65},{193,1... | collective-permute-start | bytes 417800 | tf_op jit(solution)/shard_map/ppermute | solution.py:200
  77.9 2.8 %collective-permute-start.16 = (f32[68,512]{1,0:T(8,128)S(1)}, f32[68,512]{1,0:T(8,128)S(1)}, u32[]{:S(2)}, u32[]{:S(2)}) collective-permute-start(f32[68,512]{1,0:T(8,128)S(1)} %get-tuple-element.28), channel_id=1, source_target_pairs={{0,32},{32,0},{1,33},{33,1},{2,34},{34,2},{3,35},{35,3},{4,36},{36... | collective-permute-start | bytes 417800 | tf_op jit(solution)/shard_map/ppermute | solution.py:200
  78.3 9.3 %collective-permute-start.13 = (f32[68,512]{1,0:T(8,128)S(1)}, f32[68,512]{1,0:T(8,128)S(1)}, u32[]{:S(2)}, u32[]{:S(2)}) collective-permute-start(f32[68,512]{1,0:T(8,128)S(1)} %add.73), channel_id=1, source_target_pairs={{0,128},{64,192},{128,0},{192,64},{1,129},{65,193},{129,1},{193,65... | collective-permute-start | bytes 417800 | tf_op jit(solution)/shard_map/ppermute | solution.py:200
  80.1 7.5 %collective-permute-start.15 = (f32[68,512]{1,0:T(8,128)S(1)}, f32[68,512]{1,0:T(8,128)S(1)}, u32[]{:S(2)}, u32[]{:S(2)}) collective-permute-start(f32[68,512]{1,0:T(8,128)S(1)} %add.74), channel_id=1, source_target_pairs={{0,64},{64,0},{128,192},{192,128},{1,65},{65,1},{129,193},{193,129... | collective-permute-start | bytes 417800 | tf_op jit(solution)/shard_map/ppermute | solution.py:200

commit v3 on v0

v3 whole, which is shorter than its diff:
```python
import functools
import math

import jax
import jax.numpy as jnp
from jax import lax
from jax.experimental import pallas as pl
from jax.experimental.pallas import tpu as pltpu
from jax.sharding import Mesh, PartitionSpec as P

L = 8192
BINS = 256
K = 16
LEAVES = 4
ROWS = 8192
LABS = 256
FEATS = 16
SLAB = 512
LANES = 128
QUADS = SLAB // LANES
SLAB_ROWS = QUADS * (K + 1)
F8 = jnp.float8_e4m3fn
NT = (((1,), (1,)), ((), ()))
SKETCH_SCALES = (4.0, 64.0, 2.0**24, 2.0**29)
CURVE_SCALES = (1024.0, 2.0**14)
TERM_ROWS = LEAVES * K
W_ROWS = 288
OWN_BINS = 32
CHUNK = 4 * SLAB
PART = (LEAVES * (K + 1), OWN_BINS * FEATS)
ORDER = tuple((k, own) for k in (3, 2, 1, 0) for own in (False, True))
OTHER_COST = 1000
OWN_COST = 1000
ADD_COST = 1000
GROUP = 4
SKETCH_VMEM = 57 << 20


def sketch_kernel(scores_ref, targets_ref, signs_ref, out_ref, score_buf, target_buf, sems):
    x = lax.axis_index("x").astype(jnp.int32)

    def loads(slab):
        row = pl.multiple_of(((x ^ (slab // 4)) * 4 + slab % 4) * SLAB, SLAB)
        return (
            pltpu.make_async_copy(scores_ref.at[pl.ds(row, SLAB), :], score_buf.at[slab], sems.at[0, slab]),
            pltpu.make_async_copy(targets_ref.at[pl.ds(row, SLAB), :], target_buf.at[slab], sems.at[1, slab]),
        )

    for slab in range(16):
        for copy in loads(slab):
            copy.start()
    sign_matrix = (2 * signs_ref[...] - 1).astype(jnp.bfloat16)
    left = jnp.concatenate(
        [
            jnp.concatenate([sign_matrix, sign_matrix, jnp.zeros((K, LABS), jnp.bfloat16)], axis=1),
            jnp.concatenate(
                [jnp.zeros((K, 2 * LABS), jnp.bfloat16), jnp.ones((K, LABS), jnp.bfloat16)], axis=1
            ),
        ],
        axis=0,
    )
    for first in range(0, 16, GROUP):
        for slab in range(first, first + GROUP):
            for copy in loads(slab):
                copy.wait()
        scores = score_buf[first : first + GROUP].reshape(GROUP * SLAB, LABS).astype(jnp.float32)
        targets = target_buf[first : first + GROUP].reshape(GROUP * SLAB, LABS).astype(jnp.float32)
        half_tanh = 0.5 * jnp.tanh(0.5 * scores)
        gradient = half_tanh + (0.5 - targets)
        hessian = 0.25 - half_tanh * half_tanh
        hessian = hessian[:, :LANES] + hessian[:, LANES:]
        grad_high = gradient.astype(jnp.bfloat16)
        grad_low = (gradient - grad_high.astype(jnp.float32)).astype(jnp.bfloat16)
        hess_high = hessian.astype(jnp.bfloat16)
        hess_low = (hessian - hess_high.astype(jnp.float32)).astype(jnp.bfloat16)
        right = jnp.concatenate([grad_high, grad_low, hess_high, hess_low], axis=1)
        stats = lax.dot_general(left, right, NT, preferred_element_type=jnp.float32)
        for piece in range(GROUP * QUADS):
            slab, quad = first + piece // QUADS, piece % QUADS
            lanes = slice(piece * LANES, (piece + 1) * LANES)
            out_ref[slab // 4, slab % 4, quad * K : (quad + 1) * K, :] = stats[:K, lanes] * (
                1.0 / math.sqrt(L)
            )
            out_ref[slab // 4, slab % 4, QUADS * K + quad : QUADS * K + quad + 1, :] = stats[
                K : K + 1, lanes
            ] * (1.0 / L)


def sketch_call(scores, targets, signs_t):
    return pl.pallas_call(
        sketch_kernel,
        in_specs=[
            pl.BlockSpec(memory_space=pl.ANY),
            pl.BlockSpec(memory_space=pl.ANY),
            pl.BlockSpec(memory_space=pltpu.VMEM),
        ],
        out_specs=pl.BlockSpec(memory_space=pltpu.VMEM),
        out_shape=jax.ShapeDtypeStruct((4, 4, SLAB_ROWS, LANES), jnp.float32),
        scratch_shapes=[
            pltpu.VMEM((16, SLAB, LABS), jnp.bfloat16),
            pltpu.VMEM((16, SLAB, LABS), jnp.int32),
            pltpu.SemaphoreType.DMA((2, 16)),
        ],
        compiler_params=pltpu.CompilerParams(vmem_limit_bytes=SKETCH_VMEM),
        cost_estimate=pl.CostEstimate(
            flops=2 * ROWS * 768 * 32, bytes_accessed=ROWS * LABS * 6, transcendentals=ROWS * LABS
        ),
        name="sketch",
    )(scores, targets, signs_t)


def split_terms(values, scales):
    terms = []
    for scale in scales:
        term = (values * scale).astype(F8).astype(jnp.float32)
        terms.append(term)
        values = values - term * (1.0 / scale)
    return terms


def weight_block(stats_ref, leaves_ref, chunk, write):
    leaf_iota = lax.broadcasted_iota(jnp.int32, (8, LANES), 0)
    zeros = jnp.zeros((K, LANES), jnp.float32)
    for piece in range(4 * QUADS):
        slab, quad = piece // QUADS, piece % QUADS
        leaf = leaves_ref[pl.ds(chunk * 4 * QUADS + piece, 1), :]
        sketch = stats_ref[slab, quad * K : (quad + 1) * K, :]
        curve = stats_ref[slab, QUADS * K + quad : QUADS * K + quad + 1, :]
        sketch = sketch.astype(jnp.bfloat16).astype(jnp.float32)
        curve = jnp.broadcast_to(curve, (8, LANES)).astype(jnp.bfloat16).astype(jnp.float32)
        masks = [jnp.broadcast_to(leaf == e, (K, LANES)) for e in range(LEAVES)]
        curve_mask = jnp.broadcast_to(leaf, (8, LANES)) == leaf_iota
        parts = [
            jnp.where(mask, term, zeros) for term in split_terms(sketch, SKETCH_SCALES) for mask in masks
        ]
        parts += [jnp.where(curve_mask, term, 0.0) for term in split_terms(curve, CURVE_SCALES)]
        parts.append(jnp.zeros((W_ROWS - 4 * TERM_ROWS - 16, LANES), jnp.float32))
        write(piece, jnp.concatenate(parts, axis=0).astype(F8))


def weight_kernel(s1, s2, s3, leaves_ref, out_ref):
    x = lax.axis_index("x").astype(jnp.int32)
    for k, stats_ref in ((1, s1), (2, s2), (3, s3)):

        def write(piece, value, first=(k - 1) * CHUNK):
            out_ref[:, first + piece * LANES : first + (piece + 1) * LANES] = value

        weight_block(stats_ref, leaves_ref, x ^ k, write)


def weight_call(blocks, leaves):
    return pl.pallas_call(
        weight_kernel,
        in_specs=[pl.BlockSpec(memory_space=pltpu.VMEM)] * 4,
        out_specs=pl.BlockSpec(memory_space=pltpu.VMEM),
        out_shape=jax.ShapeDtypeStruct((W_ROWS, 3 * CHUNK), F8),
        compiler_params=pltpu.CompilerParams(vmem_limit_bytes=24 << 20),
        cost_estimate=pl.CostEstimate(flops=1_000_000, bytes_accessed=100_000, transcendentals=0),
        name="weights",
    )(*blocks, leaves)


def count(codes, weights):
    codes = jnp.clip(codes, -1, OWN_BINS)
    pair = jnp.concatenate([codes, codes - 1], axis=0).astype(jnp.int8)
    one = jnp.ones(pair.shape, F8)
    zero = jnp.zeros(pair.shape, F8)
    onehot = jnp.concatenate(
        [jnp.where(pair == jnp.int8(b), one, zero) for b in range(0, OWN_BINS, 2)], axis=0
    )
    total = lax.dot_general(weights, onehot, NT, preferred_element_type=jnp.float32)
    sketch = sum(
        total[t * TERM_ROWS : (t + 1) * TERM_ROWS] * (1.0 / scale) for t, scale in enumerate(SKETCH_SCALES)
    )
    curve = sum(
        total[4 * TERM_ROWS + 8 * t : 4 * TERM_ROWS + 8 * t + 8] * (1.0 / scale)
        for t, scale in enumerate(CURVE_SCALES)
    )
    return jnp.concatenate([sketch, curve[:LEAVES]], axis=0)


def first_bin(k, own):
    zl = lax.axis_index("zl").astype(jnp.int32)
    core = lax.axis_index("c").astype(jnp.int32)
    return OWN_BINS * (2 * (zl ^ k) + (core if own else 1 - core))


def own_kernel(bins_ref, stats_ref, leaves_ref, out_ref, weights_ref):
    x = lax.axis_index("x").astype(jnp.int32)

    def write(piece, value):
        weights_ref[:, piece * LANES : (piece + 1) * LANES] = value

    weight_block(stats_ref, leaves_ref, x, write)
    bins = bins_ref[:, pl.ds(pl.multiple_of(x * CHUNK, CHUNK), CHUNK)]
    for k, own in ORDER:
        out_ref[4 * own + k] = count(bins - first_bin(k, own), weights_ref[...])


def own_call(bins_t, stats, leaves):
    return pl.pallas_call(
        own_kernel,
        in_specs=[pl.BlockSpec(memory_space=pltpu.VMEM)] * 3,
        out_specs=pl.BlockSpec(memory_space=pltpu.VMEM),
        out_shape=jax.ShapeDtypeStruct((8,) + PART, jnp.float32),
        scratch_shapes=[pltpu.VMEM((W_ROWS, CHUNK), F8)],
        compiler_params=pltpu.CompilerParams(vmem_limit_bytes=32 << 20),
        cost_estimate=pl.CostEstimate(flops=5_000_000_000, bytes_accessed=1_000_000, transcendentals=0),
        name="own",
    )(bins_t, stats, leaves)


def rest_bins(bins_ref):
    x = lax.axis_index("x").astype(jnp.int32)
    return jnp.concatenate(
        [bins_ref[:, pl.ds(pl.multiple_of((x ^ j) * CHUNK, CHUNK), CHUNK)] for j in (1, 2, 3)], axis=1
    )


def other_kernel(ks, bins_ref, weights_ref, start_ref, out_ref):
    bins = rest_bins(bins_ref)
    for place, k in enumerate(ks):
        out_ref[place] = start_ref[k] + count(bins - first_bin(k, False), weights_ref[...])


def other_call(ks, bins_t, weights, start):
    return pl.pallas_call(
        functools.partial(other_kernel, ks),
        in_specs=[pl.BlockSpec(memory_space=pltpu.VMEM)] * 3,
        out_specs=pl.BlockSpec(memory_space=pltpu.VMEM),
        out_shape=jax.ShapeDtypeStruct((len(ks),) + PART, jnp.float32),
        compiler_params=pltpu.CompilerParams(vmem_limit_bytes=32 << 20),
        cost_estimate=pl.CostEstimate(flops=OTHER_COST * len(ks), bytes_accessed=1000, transcendentals=0),
        name="other",
    )(bins_t, weights, start)


def hist_kernel(k, place, bins_ref, weights_ref, start_ref, swapped_ref, *refs):
    out_ref = refs[-1]
    bins = rest_bins(bins_ref)
    total = start_ref[4 + k] + swapped_ref[place]
    for ref in refs[:-1]:
        total += ref[...]
    out_ref[...] = total + count(bins - first_bin(k, True), weights_ref[...])


def hist_call(k, bins_t, weights, start, swapped, place, *more):
    return pl.pallas_call(
        functools.partial(hist_kernel, k, place),
        in_specs=[pl.BlockSpec(memory_space=pltpu.VMEM)] * (4 + len(more)),
        out_specs=pl.BlockSpec(memory_space=pltpu.VMEM),
        out_shape=jax.ShapeDtypeStruct(PART, jnp.float32),
        compiler_params=pltpu.CompilerParams(vmem_limit_bytes=32 << 20),
        cost_estimate=pl.CostEstimate(flops=OWN_COST, bytes_accessed=1000, transcendentals=0),
        name="hist",
    )(bins_t, weights, start, swapped, *more)


def add_kernel(a_ref, b_ref, out_ref):
    out_ref[...] = a_ref[...] + b_ref[...]


def add_call(a, b):
    return pl.pallas_call(
        add_kernel,
        in_specs=[pl.BlockSpec(memory_space=pltpu.VMEM)] * 2,
        out_specs=pl.BlockSpec(memory_space=pltpu.VMEM),
        out_shape=jax.ShapeDtypeStruct(PART, jnp.float32),
        compiler_params=pltpu.CompilerParams(vmem_limit_bytes=8 << 20),
        cost_estimate=pl.CostEstimate(flops=ADD_COST, bytes_accessed=1000, transcendentals=0),
        name="add",
    )(a, b)


def finish_kernel(a_ref, b_ref, c_ref, out_ref):
    total = a_ref[...] + (b_ref[...] + c_ref[...])
    rows = []
    for e in range(LEAVES):
        rows.append(total[e * K : (e + 1) * K])
        rows.append(total[TERM_ROWS + e : TERM_ROWS + e + 1])
    total = jnp.concatenate(rows, axis=0)
    out_ref[...] = total.T.reshape(OWN_BINS, FEATS, LEAVES * (K + 1))


def finish_call(parts):
    return pl.pallas_call(
        finish_kernel,
        out_shape=jax.ShapeDtypeStruct((OWN_BINS, FEATS, LEAVES * (K + 1)), jnp.float32),
        compiler_params=pltpu.CompilerParams(vmem_limit_bytes=8 << 20),
        name="finish",
    )(*parts)


def swap(value, axis, bit, size):
    return lax.ppermute(value, axis, [(i, i ^ bit) for i in range(size)])


def per_device(scores, targets, signs, bins, leaves):
    signs_t = signs.T
    bins_t = bins.T
    leaves2 = leaves.reshape(ROWS // LANES, LANES)

    parts = sketch_call(scores, targets, signs_t)
    arrived = [swap(parts[k], "x", k, 4) for k in (2, 1, 3)]
    mine = (parts[0] + arrived[0]) + (arrived[1] + arrived[2])
    arrived = [swap(mine, "y", k, 4) for k in (2, 1, 3)]
    mine = (mine + arrived[0]) + (arrived[1] + arrived[2])
    mine = mine + swap(mine, "zh", 1, 2)
    blocks = [swap(mine, "x", k, 4) for k in (1, 2, 3)]
    start = own_call(bins_t, mine, leaves2)
    weights = weight_call(blocks, leaves2)

    first = swap(other_call((3,), bins_t, weights, start), "c", 1, 2)
    part = hist_call(3, bins_t, weights, start, first, 0)
    moved3 = swap(part, "zl", 3, 4)
    rest = swap(other_call((2, 1, 0), bins_t, weights, start), "c", 1, 2)
    part = hist_call(2, bins_t, weights, start, rest, 0)
    moved2 = swap(part, "zl", 2, 4)
    part = hist_call(1, bins_t, weights, start, rest, 1)
    moved1 = swap(part, "zl", 1, 4)
    part = hist_call(0, bins_t, weights, start, rest, 2, moved3)
    return finish_call((part, moved2, moved1))


def solution(mesh):
    fine = Mesh(mesh.devices.reshape(4, 2, 4, 4, 2), ("zl", "c", "y", "x", "zh"))
    row, lab = ("zl", "c"), ("y", "x", "zh")
    in_specs = (P(row, lab), P(row, lab), P(lab, None), P(row, lab), P(row))
    out_specs = P(row, lab, None)
    return jax.shard_map(
        per_device, mesh=fine, in_specs=in_specs, out_specs=out_specs, check_vma=False
    )
```

time: 615 us -> 83 us (0.13)
  waiting for transfers between devices: 470 us -> 29.3 us
  matrix products: 105 us -> 0 us
  starting transfers between devices: 0.04 us -> 29.9 us
  Pallas kernels: 0 us -> 21.4 us
  local copies, waits for them, and re-layouts: 15.7 us -> 1.09 us
  between operations: 13.5 us -> 0.11 us
    psum x1 -> x0, waiting for transfers between devices: 409 us -> none  [per_device(): stats = lax.psum(partial_stats, 'lab')]
    dot_general x17 -> x0, matrix products: 105 us -> none  [the longest x16 93.5 us: add_block(): jnp.einsum('rfb,rc->bfc', onehot, block_weights, preferred_element_type=j...]
    reduce_scatter x1 -> x0, waiting for transfers between devices: 61.1 us -> none  [per_device(): return lax.psum_scatter(term, 'row', scatter_dimension=0, tiled=True)]
    ppermute x0 -> x15, starting transfers between devices: none -> 29.9 us  [swap(): return lax.ppermute(value, axis, [(i, i ^ bit) for i in range(size)])]
    ppermute x0 -> x15, waiting for transfers between devices: none -> 29.3 us  [swap(): return lax.ppermute(value, axis, [(i, i ^ bit) for i in range(size)])]
    pallas_call x0 -> x10, Pallas kernels: none -> 21.4 us  [the longest x1 8.81 us: sketch_call(): pl.pallas_call(sketch_kernel, in_specs=[pl.BlockSpec(memory_space=pl.ANY)...]
    dynamic_slice x16 -> x0, local copies, waits for them, and re-layouts: 12.3 us -> none  [add_block(): block_bins = lax.dynamic_slice_in_dim(bins, first, block_rows, 0)]
  transfers between devices with their start and end apart: 2 -> 15, of which waited for: 2 -> 11; matrix products, arithmetic and copies ran while one was open for 0% -> 0% of each run, Pallas kernels for 0% -> 10%
where the time goes in v3:
time: 83 us; the launch traced here: 82.8 us
  starting transfers between devices  29.9 us (36%)
  waiting for transfers between devices  29.3 us (35%)
  Pallas kernels  21.4 us (26%)
  local copies, waits for them, and re-layouts  1.09 us (1%)
  other arithmetic  0.99 us (1%)
    ppermute x15, starting transfers between devices, swap(): return lax.ppermute(value, axis, [(i, i ^ bit) for i in range(size)])  29.9 us
    ppermute x15, waiting for transfers between devices, swap(): return lax.ppermute(value, axis, [(i, i ^ bit) for i in range(size)])  29.3 us
    pallas_call x1, Pallas kernels, sketch_call(): pl.pallas_call(sketch_kernel, in_specs=[pl.BlockSpec(memory_space=pl.ANY)...  8.81 us
    pallas_call x4, Pallas kernels, hist_call(): pl.pallas_call(functools.partial(hist_kernel, k, place), in_specs=[pl.Blo...  4.27 us
    pallas_call x2, Pallas kernels, other_call(): pl.pallas_call(functools.partial(other_kernel, ks), in_specs=[pl.BlockSpe...  3.98 us
    pallas_call x1, Pallas kernels, own_call(): pl.pallas_call(own_kernel, in_specs=[pl.BlockSpec(memory_space=pltpu.VMEM...  2.7 us
  transfers between devices with their start and end apart: 15, of which 11 were waited for; matrix products, arithmetic and copies ran while one was open for 0% of the time, Pallas kernels for 10%

profile of v3, /device:TPU:1, one launch (start us, length us, event | category | flops | bytes accessed | tf_op | source)
XLA Modules:
  0.0 82.8 jit_solution(16095667433145524158)
XLA Ops:
  0.0 0.0 copy-start
  0.0 0.0 copy-start.1
  0.0 8.8 %sketch.1 = f32[4,4,68,128]{3,2,1,0:T(8,128)} custom-call(bf16[8192,256]{1,0:T(8,128)(2,1)} %scores_ref.1, s32[8192,256]{1,0:T(8,128)} %targets_ref.1, s32[16,256]{1,0:T(8,128)} %bitcast.24), custom_call_target="tpu_custom_call" | custom-call | flops 402653184 | bytes 12582912 | tf_op jit(solution)/shard_map/sketch/pallas_call | solution.py:90
  8.8 1.1 %slice_bitcast_fusion = (f32[4,68,128]{2,1,0:T(8,128)S(1)}, f32[4,68,128]{2,1,0:T(8,128)S(1)}, f32[4,68,128]{2,1,0:T(8,128)S(1)}) fusion(f32[4,4,68,128]{3,2,1,0:T(8,128)} %sketch.1), kind=kLoop, calls=%fused_computation | loop fusion | bytes 835584 | tf_op jit(solution)/shard_map/squeeze | solution.py:304
  9.9 3.7 %collective-permute-start = (f32[4,68,128]{2,1,0:T(8,128)S(1)}, f32[4,68,128]{2,1,0:T(8,128)S(1)}, u32[]{:S(2)}, u32[]{:S(2)}) collective-permute-start(f32[4,68,128]{2,1,0:T(8,128)S(1)} %get-tuple-element.7), channel_id=1, source_target_pairs={{0,4},{2,6},{4,0},{6,2},{1,5},{3,7},{5,1},{7,3},{8,12},{10,14},{12... | collective-permute-start | bytes 417800 | tf_op jit(solution)/shard_map/ppermute | solution.py:295
  13.6 0.3 collective-permute-start.1
  13.9 0.6 collective-permute-start.2
  14.4 1.7 %collective-permute-done = f32[4,68,128]{2,1,0:T(8,128)S(1)} collective-permute-done((f32[4,68,128]{2,1,0:T(8,128)S(1)}, f32[4,68,128]{2,1,0:T(8,128)S(1)}, u32[]{:S(2)}, u32[]{:S(2)}) %collective-permute-start) | collective-permute-done | bytes 139296 | tf_op jit(solution)/shard_map/ppermute | solution.py:295
  16.1 4.2 %collective-permute-done.1 = f32[4,68,128]{2,1,0:T(8,128)S(1)} collective-permute-done((f32[4,68,128]{2,1,0:T(8,128)S(1)}, f32[4,68,128]{2,1,0:T(8,128)S(1)}, u32[]{:S(2)}, u32[]{:S(2)}) %collective-permute-start.1) | collective-permute-done | bytes 139296 | tf_op jit(solution)/shard_map/ppermute | solution.py:295
  20.3 1.4 %collective-permute-done.2 = f32[4,68,128]{2,1,0:T(8,128)S(1)} collective-permute-done((f32[4,68,128]{2,1,0:T(8,128)S(1)}, f32[4,68,128]{2,1,0:T(8,128)S(1)}, u32[]{:S(2)}, u32[]{:S(2)}) %collective-permute-start.2) | collective-permute-done | bytes 139296 | tf_op jit(solution)/shard_map/ppermute | solution.py:295
  21.7 0.9 %fusion.1 = f32[4,68,128]{2,1,0:T(8,128)S(1)} fusion(f32[4,68,128]{2,1,0:T(8,128)S(1)} %collective-permute-done, f32[4,4,68,128]{3,2,1,0:T(8,128)} %sketch.1, f32[4,68,128]{2,1,0:T(8,128)S(1)} %collective-permute-done.1, f32[4,68,128]{2,1,0:T(8,128)S(1)} %collective-permute-done.2), kind=kLoop, calls=%fused_computation.5 | loop fusion | flops 104448 | bytes 696320 | tf_op jit(solution)/shard_map/add | solution.py:305
  22.7 0.4 collective-permute-start.4
  23.1 1.9 %collective-permute-start.5 = (f32[4,68,128]{2,1,0:T(8,128)S(1)}, f32[4,68,128]{2,1,0:T(8,128)S(1)}, u32[]{:S(2)}, u32[]{:S(2)}) collective-permute-start(f32[4,68,128]{2,1,0:T(8,128)S(1)} %fusion.1), channel_id=1, source_target_pairs={{0,24},{8,16},{16,8},{24,0},{1,25},{9,17},{17,9},{25,1},{2,26},{10... | collective-permute-start | bytes 417800 | tf_op jit(solution)/shard_map/ppermute | solution.py:295
  25.0 1.0 %collective-permute-start.3 = (f32[4,68,128]{2,1,0:T(8,128)S(1)}, f32[4,68,128]{2,1,0:T(8,128)S(1)}, u32[]{:S(2)}, u32[]{:S(2)}) collective-permute-start(f32[4,68,128]{2,1,0:T(8,128)S(1)} %fusion.1), channel_id=1, source_target_pairs={{0,16},{8,24},{16,0},{24,8},{1,17},{9,25},{17,1},{25,9},{2,18},{10... | collective-permute-start | bytes 417800 | tf_op jit(solution)/shard_map/ppermute | solution.py:295
  26.0 0.7 collective-permute-done.4
  26.8 1.5 %collective-permute-done.5 = f32[4,68,128]{2,1,0:T(8,128)S(1)} collective-permute-done((f32[4,68,128]{2,1,0:T(8,128)S(1)}, f32[4,68,128]{2,1,0:T(8,128)S(1)}, u32[]{:S(2)}, u32[]{:S(2)}) %collective-permute-start.5) | collective-permute-done | bytes 139296 | tf_op jit(solution)/shard_map/ppermute | solution.py:295
  28.3 4.0 %collective-permute-done.3 = f32[4,68,128]{2,1,0:T(8,128)S(1)} collective-permute-done((f32[4,68,128]{2,1,0:T(8,128)S(1)}, f32[4,68,128]{2,1,0:T(8,128)S(1)}, u32[]{:S(2)}, u32[]{:S(2)}) %collective-permute-start.3) | collective-permute-done | bytes 139296 | tf_op jit(solution)/shard_map/ppermute | solution.py:295
  32.3 7.0 %collective-permute-start.6 = (f32[4,68,128]{2,1,0:T(8,128)S(1)}, f32[4,68,128]{2,1,0:T(8,128)S(1)}, u32[]{:S(2)}, u32[]{:S(2)}) collective-permute-start(f32[4,68,128]{2,1,0:T(8,128)S(1)} %add_add_fusion), channel_id=1, source_target_pairs={{0,1},{1,0},{2,3},{3,2},{4,5},{5,4},{6,7},{7,6},{8,9},{9,8},{10,11... | collective-permute-start | bytes 417800 | tf_op jit(solution)/shard_map/ppermute | solution.py:295
  39.3 2.6 %collective-permute-done.6 = f32[4,68,128]{2,1,0:T(8,128)S(1)} collective-permute-done((f32[4,68,128]{2,1,0:T(8,128)S(1)}, f32[4,68,128]{2,1,0:T(8,128)S(1)}, u32[]{:S(2)}, u32[]{:S(2)}) %collective-permute-start.6) | collective-permute-done | bytes 139296 | tf_op jit(solution)/shard_map/ppermute | solution.py:295
  41.9 1.0 %collective-permute-start.7 = (f32[4,68,128]{2,1,0:T(8,128)S(1)}, f32[4,68,128]{2,1,0:T(8,128)S(1)}, u32[]{:S(2)}, u32[]{:S(2)}) collective-permute-start(f32[4,68,128]{2,1,0:T(8,128)S(1)} %add.27.stats_ref), channel_id=1, source_target_pairs={{0,2},{2,0},{4,6},{6,4},{1,3},{3,1},{5,7},{7,5},{8,10},{10,8},{12,... | collective-permute-start | bytes 417800 | tf_op jit(solution)/shard_map/ppermute | solution.py:295
  42.9 3.6 %collective-permute-start.8 = (f32[4,68,128]{2,1,0:T(8,128)S(1)}, f32[4,68,128]{2,1,0:T(8,128)S(1)}, u32[]{:S(2)}, u32[]{:S(2)}) collective-permute-start(f32[4,68,128]{2,1,0:T(8,128)S(1)} %add.27.stats_ref), channel_id=1, source_target_pairs={{0,4},{2,6},{4,0},{6,2},{1,5},{3,7},{5,1},{7,3},{8,12},{10,14},{12... | collective-permute-start | bytes 417800 | tf_op jit(solution)/shard_map/ppermute | solution.py:295
  46.5 0.0 collective-permute-start.9
  46.5 0.0 copy-done
  46.5 0.0 copy-done.1
  46.5 2.7 %own.1.start_ref = f32[8,68,512]{2,1,0:T(8,128)S(1)} custom-call(s32[16,8192]{1,0:T(8,128)S(1)} %bitcast.15, f32[4,68,128]{2,1,0:T(8,128)S(1)} %add.27.stats_ref, s32[64,128]{1,0:T(8,128)S(1)} %bitcast.22), custom_call_target="tpu_custom_call" | custom-call | flops 5000000000 | bytes 1000000 | tf_op jit(solution)/shard_map/own/pallas_call | solution.py:201
  49.2 0.0 collective-permute-done.7.s1
  49.3 1.4 %collective-permute-done.8.s2 = f32[4,68,128]{2,1,0:T(8,128)S(1)} collective-permute-done((f32[4,68,128]{2,1,0:T(8,128)S(1)}, f32[4,68,128]{2,1,0:T(8,128)S(1)}, u32[]{:S(2)}, u32[]{:S(2)}) %collective-permute-start.8) | collective-permute-done | bytes 139296 | tf_op jit(solution)/shard_map/ppermute | solution.py:295
  50.7 1.5 %collective-permute-done.9.s3 = f32[4,68,128]{2,1,0:T(8,128)S(1)} collective-permute-done((f32[4,68,128]{2,1,0:T(8,128)S(1)}, f32[4,68,128]{2,1,0:T(8,128)S(1)}, u32[]{:S(2)}, u32[]{:S(2)}) %collective-permute-start.9) | collective-permute-done | bytes 139296 | tf_op jit(solution)/shard_map/ppermute | solution.py:295
  52.2 0.8 weights.1.weights_ref
  53.0 2.9 %other.2 = f32[3,68,512]{2,1,0:T(8,128)S(1)} custom-call(s32[16,8192]{1,0:T(8,128)S(1)} %bitcast.16, f8e4m3fn[288,6144]{1,0:T(32,128)(4,1)S(1)} %weights.1.weights_ref, f32[8,68,512]{2,1,0:T(8,128)S(1)} %own.1.start_ref), custom_call_target="tpu_custom_call" | custom-call | flops 3000 | bytes 1000 | tf_op jit(solution)/shard_map/other/pallas_call | solution.py:227
  56.0 5.2 %collective-permute-start.10 = (f32[3,68,512]{2,1,0:T(8,128)S(1)}, f32[3,68,512]{2,1,0:T(8,128)S(1)}, u32[]{:S(2)}, u32[]{:S(2)}) collective-permute-start(f32[3,68,512]{2,1,0:T(8,128)S(1)} %other.2), channel_id=1, source_target_pairs={{0,32},{32,0},{1,33},{33,1},{2,34},{34,2},{3,35},{35,3},{4,36},{36... | collective-permute-start | bytes 1253384 | tf_op jit(solution)/shard_map/ppermute | solution.py:295
  61.2 1.1 %other.3 = f32[1,68,512]{2,1,0:T(8,128)S(1)} custom-call(s32[16,8192]{1,0:T(8,128)S(1)} %bitcast.17, f8e4m3fn[288,6144]{1,0:T(32,128)(4,1)S(1)} %weights.1.weights_ref, f32[8,68,512]{2,1,0:T(8,128)S(1)} %own.1.start_ref), custom_call_target="tpu_custom_call" | custom-call | flops 1000 | bytes 1000 | tf_op jit(solution)/shard_map/other/pallas_call | solution.py:227
  62.2 0.1 collective-permute-start.11
  62.3 1.3 %collective-permute-done.11.swapped_ref = f32[1,68,512]{2,1,0:T(8,128)S(1)} collective-permute-done((f32[1,68,512]{2,1,0:T(8,128)S(1)}, f32[1,68,512]{2,1,0:T(8,128)S(1)}, u32[]{:S(2)}, u32[]{:S(2)}) %collective-permute-start.11) | collective-permute-done | bytes 139296 | tf_op jit(solution)/shard_map/ppermute | solution.py:295
  63.7 1.1 %hist.4 = f32[68,512]{1,0:T(8,128)S(1)} custom-call(s32[16,8192]{1,0:T(8,128)S(1)} %bitcast.18, f8e4m3fn[288,6144]{1,0:T(32,128)(4,1)S(1)} %weights.1.weights_ref, f32[8,68,512]{2,1,0:T(8,128)S(1)} %own.1.start_ref, f32[1,68,512]{2,1,0:T(8,128)S(1)} %collective-permute-done.11.swapped_ref), custom_call_target="tpu_custom_call" | custom-call | flops 1000 | bytes 1000 | tf_op jit(solution)/shard_map/hist/pallas_call | solution.py:248
  64.8 3.0 %collective-permute-start.12 = (f32[68,512]{1,0:T(8,128)S(1)}, f32[68,512]{1,0:T(8,128)S(1)}, u32[]{:S(2)}, u32[]{:S(2)}) collective-permute-start(f32[68,512]{1,0:T(8,128)S(1)} %hist.4), channel_id=1, source_target_pairs={{0,192},{64,128},{128,64},{192,0},{1,193},{65,129},{129,65},{193,1... | collective-permute-start | bytes 417800 | tf_op jit(solution)/shard_map/ppermute | solution.py:295
  67.8 0.0 collective-permute-done.10.swapped_ref
  67.8 1.1 %hist.6 = f32[68,512]{1,0:T(8,128)S(1)} custom-call(s32[16,8192]{1,0:T(8,128)S(1)} %bitcast.19, f8e4m3fn[288,6144]{1,0:T(32,128)(4,1)S(1)} %weights.1.weights_ref, f32[8,68,512]{2,1,0:T(8,128)S(1)} %own.1.start_ref, f32[3,68,512]{2,1,0:T(8,128)S(1)} %collective-permute-done.10.swapped_ref), custom_call_target="tpu_custom_call" | custom-call | flops 1000 | bytes 1000 | tf_op jit(solution)/shard_map/hist/pallas_call | solution.py:248
  68.9 1.7 %collective-permute-start.13 = (f32[68,512]{1,0:T(8,128)S(1)}, f32[68,512]{1,0:T(8,128)S(1)}, u32[]{:S(2)}, u32[]{:S(2)}) collective-permute-start(f32[68,512]{1,0:T(8,128)S(1)} %hist.6), channel_id=1, source_target_pairs={{0,128},{64,192},{128,0},{192,64},{1,129},{65,193},{129,1},{193,65... | collective-permute-start | bytes 417800 | tf_op jit(solution)/shard_map/ppermute | solution.py:295
  70.6 1.1 %hist.7 = f32[68,512]{1,0:T(8,128)S(1)} custom-call(s32[16,8192]{1,0:T(8,128)S(1)} %bitcast.20, f8e4m3fn[288,6144]{1,0:T(32,128)(4,1)S(1)} %weights.1.weights_ref, f32[8,68,512]{2,1,0:T(8,128)S(1)} %own.1.start_ref, f32[3,68,512]{2,1,0:T(8,128)S(1)} %collective-permute-done.10.swapped_ref), custom_call_target="tpu_custom_call" | custom-call | flops 1000 | bytes 1000 | tf_op jit(solution)/shard_map/hist/pallas_call | solution.py:248
  71.7 0.4 collective-permute-start.14
  72.0 0.0 collective-permute-done.12.refs_0_
  72.0 1.1 %hist.5.a_ref = f32[68,512]{1,0:T(8,128)S(1)} custom-call(s32[16,8192]{1,0:T(8,128)S(1)} %bitcast.21, f8e4m3fn[288,6144]{1,0:T(32,128)(4,1)S(1)} %weights.1.weights_ref, f32[8,68,512]{2,1,0:T(8,128)S(1)} %own.1.start_ref, f32[3,68,512]{2,1,0:T(8,128)S(1)} %collective-permute-done.10.swapped_ref, f32[68,512]{1,0:T(8,128)S(1)} %collective-permute-done.12.refs_0_), custom_call_target="tpu_custom_call" | custom-call | flops 1000 | bytes 1000 | tf_op jit(solution)/shard_map/hist/pallas_call | solution.py:248
  73.1 8.9 %collective-permute-done.13.b_ref = f32[68,512]{1,0:T(8,128)S(1)} collective-permute-done((f32[68,512]{1,0:T(8,128)S(1)}, f32[68,512]{1,0:T(8,128)S(1)}, u32[]{:S(2)}, u32[]{:S(2)}) %collective-permute-start.13) | collective-permute-done | bytes 139296 | tf_op jit(solution)/shard_map/ppermute | solution.py:295
  82.0 0.0 collective-permute-done.14.c_ref
  82.0 0.8 %finish.1 = f32[32,16,68]{2,1,0:T(8,128)} custom-call(f32[68,512]{1,0:T(8,128)S(1)} %hist.5.a_ref, f32[68,512]{1,0:T(8,128)S(1)} %collective-permute-done.13.b_ref, f32[68,512]{1,0:T(8,128)S(1)} %collective-permute-done.14.c_ref), custom_call_target="tpu_custom_call" | custom-call | tf_op jit(solution)/shard_map/finish/pallas_call | solution.py:286
  (2 shorter events, 0.0 us)
Async XLA Ops:
  0.0 46.5 %copy-start = (s32[8192,16]{0,1:T(8,128)S(1)}, s32[8192,16]{0,1:T(8,128)}, u32[]{:S(2)}) copy-start(s32[8192,16]{0,1:T(8,128)} %param.8) | copy-start | bytes 1572868
  0.0 46.5 %copy-start.1 = (s32[8192]{0:T(1024)S(1)}, s32[8192]{0:T(1024)}, u32[]{:S(2)}) copy-start(s32[8192]{0:T(1024)} %param.9) | copy-start | bytes 98308
  9.9 6.2 %collective-permute-start = (f32[4,68,128]{2,1,0:T(8,128)S(1)}, f32[4,68,128]{2,1,0:T(8,128)S(1)}, u32[]{:S(2)}, u32[]{:S(2)}) collective-permute-start(f32[4,68,128]{2,1,0:T(8,128)S(1)} %get-tuple-element.7), channel_id=1, source_target_pairs={{0,4},{2,6},{4,0},{6,2},{1,5},{3,7},{5,1},{7,3},{8,12},{10,14},{12... | collective-permute-start | bytes 417800 | tf_op jit(solution)/shard_map/ppermute | solution.py:295
  13.6 6.7 %collective-permute-start.1 = (f32[4,68,128]{2,1,0:T(8,128)S(1)}, f32[4,68,128]{2,1,0:T(8,128)S(1)}, u32[]{:S(2)}, u32[]{:S(2)}) collective-permute-start(f32[4,68,128]{2,1,0:T(8,128)S(1)} %get-tuple-element.6), channel_id=1, source_target_pairs={{0,2},{2,0},{4,6},{6,4},{1,3},{3,1},{5,7},{7,5},{8,10},{10,8},{12,... | collective-permute-start | bytes 417800 | tf_op jit(solution)/shard_map/ppermute | solution.py:295
  13.9 7.9 %collective-permute-start.2 = (f32[4,68,128]{2,1,0:T(8,128)S(1)}, f32[4,68,128]{2,1,0:T(8,128)S(1)}, u32[]{:S(2)}, u32[]{:S(2)}) collective-permute-start(f32[4,68,128]{2,1,0:T(8,128)S(1)} %get-tuple-element.5), channel_id=1, source_target_pairs={{0,6},{2,4},{4,2},{6,0},{1,7},{3,5},{5,3},{7,1},{8,14},{10,12},{12... | collective-permute-start | bytes 417800 | tf_op jit(solution)/shard_map/ppermute | solution.py:295
  22.7 4.1 %collective-permute-start.4 = (f32[4,68,128]{2,1,0:T(8,128)S(1)}, f32[4,68,128]{2,1,0:T(8,128)S(1)}, u32[]{:S(2)}, u32[]{:S(2)}) collective-permute-start(f32[4,68,128]{2,1,0:T(8,128)S(1)} %fusion.1), channel_id=1, source_target_pairs={{0,8},{8,0},{16,24},{24,16},{1,9},{9,1},{17,25},{25,17},{2,10},{10... | collective-permute-start | bytes 417800 | tf_op jit(solution)/shard_map/ppermute | solution.py:295
  23.1 5.2 %collective-permute-start.5 = (f32[4,68,128]{2,1,0:T(8,128)S(1)}, f32[4,68,128]{2,1,0:T(8,128)S(1)}, u32[]{:S(2)}, u32[]{:S(2)}) collective-permute-start(f32[4,68,128]{2,1,0:T(8,128)S(1)} %fusion.1), channel_id=1, source_target_pairs={{0,24},{8,16},{16,8},{24,0},{1,25},{9,17},{17,9},{25,1},{2,26},{10... | collective-permute-start | bytes 417800 | tf_op jit(solution)/shard_map/ppermute | solution.py:295
  25.0 7.3 %collective-permute-start.3 = (f32[4,68,128]{2,1,0:T(8,128)S(1)}, f32[4,68,128]{2,1,0:T(8,128)S(1)}, u32[]{:S(2)}, u32[]{:S(2)}) collective-permute-start(f32[4,68,128]{2,1,0:T(8,128)S(1)} %fusion.1), channel_id=1, source_target_pairs={{0,16},{8,24},{16,0},{24,8},{1,17},{9,25},{17,1},{25,9},{2,18},{10... | collective-permute-start | bytes 417800 | tf_op jit(solution)/shard_map/ppermute | solution.py:295
  32.3 9.6 %collective-permute-start.6 = (f32[4,68,128]{2,1,0:T(8,128)S(1)}, f32[4,68,128]{2,1,0:T(8,128)S(1)}, u32[]{:S(2)}, u32[]{:S(2)}) collective-permute-start(f32[4,68,128]{2,1,0:T(8,128)S(1)} %add_add_fusion), channel_id=1, source_target_pairs={{0,1},{1,0},{2,3},{3,2},{4,5},{5,4},{6,7},{7,6},{8,9},{9,8},{10,11... | collective-permute-start | bytes 417800 | tf_op jit(solution)/shard_map/ppermute | solution.py:295
  41.9 7.3 %collective-permute-start.7 = (f32[4,68,128]{2,1,0:T(8,128)S(1)}, f32[4,68,128]{2,1,0:T(8,128)S(1)}, u32[]{:S(2)}, u32[]{:S(2)}) collective-permute-start(f32[4,68,128]{2,1,0:T(8,128)S(1)} %add.27.stats_ref), channel_id=1, source_target_pairs={{0,2},{2,0},{4,6},{6,4},{1,3},{3,1},{5,7},{7,5},{8,10},{10,8},{12,... | collective-permute-start | bytes 417800 | tf_op jit(solution)/shard_map/ppermute | solution.py:295
  42.9 7.7 %collective-permute-start.8 = (f32[4,68,128]{2,1,0:T(8,128)S(1)}, f32[4,68,128]{2,1,0:T(8,128)S(1)}, u32[]{:S(2)}, u32[]{:S(2)}) collective-permute-start(f32[4,68,128]{2,1,0:T(8,128)S(1)} %add.27.stats_ref), channel_id=1, source_target_pairs={{0,4},{2,6},{4,0},{6,2},{1,5},{3,7},{5,1},{7,3},{8,12},{10,14},{12... | collective-permute-start | bytes 417800 | tf_op jit(solution)/shard_map/ppermute | solution.py:295
  46.5 5.7 %collective-permute-start.9 = (f32[4,68,128]{2,1,0:T(8,128)S(1)}, f32[4,68,128]{2,1,0:T(8,128)S(1)}, u32[]{:S(2)}, u32[]{:S(2)}) collective-permute-start(f32[4,68,128]{2,1,0:T(8,128)S(1)} %add.27.stats_ref), channel_id=1, source_target_pairs={{0,6},{2,4},{4,2},{6,0},{1,7},{3,5},{5,3},{7,1},{8,14},{10,12},{12... | collective-permute-start | bytes 417800 | tf_op jit(solution)/shard_map/ppermute | solution.py:295
  56.0 11.8 %collective-permute-start.10 = (f32[3,68,512]{2,1,0:T(8,128)S(1)}, f32[3,68,512]{2,1,0:T(8,128)S(1)}, u32[]{:S(2)}, u32[]{:S(2)}) collective-permute-start(f32[3,68,512]{2,1,0:T(8,128)S(1)} %other.2), channel_id=1, source_target_pairs={{0,32},{32,0},{1,33},{33,1},{2,34},{34,2},{3,35},{35,3},{4,36},{36... | collective-permute-start | bytes 1253384 | tf_op jit(solution)/shard_map/ppermute | solution.py:295
  62.2 1.5 %collective-permute-start.11 = (f32[1,68,512]{2,1,0:T(8,128)S(1)}, f32[1,68,512]{2,1,0:T(8,128)S(1)}, u32[]{:S(2)}, u32[]{:S(2)}) collective-permute-start(f32[1,68,512]{2,1,0:T(8,128)S(1)} %other.3), channel_id=1, source_target_pairs={{0,32},{32,0},{1,33},{33,1},{2,34},{34,2},{3,35},{35,3},{4,36},{36... | collective-permute-start | bytes 417800 | tf_op jit(solution)/shard_map/ppermute | solution.py:295
  64.8 7.3 %collective-permute-start.12 = (f32[68,512]{1,0:T(8,128)S(1)}, f32[68,512]{1,0:T(8,128)S(1)}, u32[]{:S(2)}, u32[]{:S(2)}) collective-permute-start(f32[68,512]{1,0:T(8,128)S(1)} %hist.4), channel_id=1, source_target_pairs={{0,192},{64,128},{128,64},{192,0},{1,193},{65,129},{129,65},{193,1... | collective-permute-start | bytes 417800 | tf_op jit(solution)/shard_map/ppermute | solution.py:295
  68.9 13.1 %collective-permute-start.13 = (f32[68,512]{1,0:T(8,128)S(1)}, f32[68,512]{1,0:T(8,128)S(1)}, u32[]{:S(2)}, u32[]{:S(2)}) collective-permute-start(f32[68,512]{1,0:T(8,128)S(1)} %hist.6), channel_id=1, source_target_pairs={{0,128},{64,192},{128,0},{192,64},{1,129},{65,193},{129,1},{193,65... | collective-permute-start | bytes 417800 | tf_op jit(solution)/shard_map/ppermute | solution.py:295
  71.7 10.3 %collective-permute-start.14 = (f32[68,512]{1,0:T(8,128)S(1)}, f32[68,512]{1,0:T(8,128)S(1)}, u32[]{:S(2)}, u32[]{:S(2)}) collective-permute-start(f32[68,512]{1,0:T(8,128)S(1)} %hist.7), channel_id=1, source_target_pairs={{0,64},{64,0},{128,192},{192,128},{1,65},{65,1},{129,193},{193,129... | collective-permute-start | bytes 417800 | tf_op jit(solution)/shard_map/ppermute | solution.py:295

commit v4 on v3

--- a/solution.py
+++ b/solution.py
@@ -31,22 +31,23 @@
 ORDER = tuple((k, own) for k in (3, 2, 1, 0) for own in (False, True))
 OTHER_COST = 1000
 OWN_COST = 1000
-ADD_COST = 1000
+LAST = 2
 GROUP = 4
-SKETCH_VMEM = 57 << 20
-
-
-def sketch_kernel(scores_ref, targets_ref, signs_ref, out_ref, score_buf, target_buf, sems):
+SKETCH_VMEM = 51 << 20
+
+
+def sketch_kernel(ks, scores_ref, targets_ref, signs_ref, *refs):
+    out_refs, (score_buf, target_buf, sems) = refs[: len(ks)], refs[len(ks) :]
     x = lax.axis_index("x").astype(jnp.int32)
 
     def loads(slab):
-        row = pl.multiple_of(((x ^ (slab // 4)) * 4 + slab % 4) * SLAB, SLAB)
+        row = pl.multiple_of(((x ^ ks[slab // 4]) * 4 + slab % 4) * SLAB, SLAB)
         return (
             pltpu.make_async_copy(scores_ref.at[pl.ds(row, SLAB), :], score_buf.at[slab], sems.at[0, slab]),
             pltpu.make_async_copy(targets_ref.at[pl.ds(row, SLAB), :], target_buf.at[slab], sems.at[1, slab]),
         )
 
-    for slab in range(16):
+    for slab in range(4 * len(ks)):
         for copy in loads(slab):
             copy.start()
     sign_matrix = (2 * signs_ref[...] - 1).astype(jnp.bfloat16)
@@ -59,7 +60,7 @@
         ],
         axis=0,
     )
-    for first in range(0, 16, GROUP):
+    for first in range(0, 4 * len(ks), GROUP):
         for slab in range(first, first + GROUP):
             for copy in loads(slab):
                 copy.wait()
@@ -78,32 +79,32 @@
         for piece in range(GROUP * QUADS):
             slab, quad = first + piece // QUADS, piece % QUADS
             lanes = slice(piece * LANES, (piece + 1) * LANES)
-            out_ref[slab // 4, slab % 4, quad * K : (quad + 1) * K, :] = stats[:K, lanes] * (
-                1.0 / math.sqrt(L)
-            )
-            out_ref[slab // 4, slab % 4, QUADS * K + quad : QUADS * K + quad + 1, :] = stats[
-                K : K + 1, lanes
-            ] * (1.0 / L)
-
-
-def sketch_call(scores, targets, signs_t):
-    return pl.pallas_call(
-        sketch_kernel,
+            out_ref, at = out_refs[slab // 4], slab % 4
+            out_ref[at, quad * K : (quad + 1) * K, :] = stats[:K, lanes] * (1.0 / math.sqrt(L))
+            out_ref[at, QUADS * K + quad : QUADS * K + quad + 1, :] = stats[K : K + 1, lanes] * (1.0 / L)
+
+
+def sketch_call(ks, scores, targets, signs_t):
+    slabs = 4 * len(ks)
+    return pl.pallas_call(
+        functools.partial(sketch_kernel, ks),
         in_specs=[
             pl.BlockSpec(memory_space=pl.ANY),
             pl.BlockSpec(memory_space=pl.ANY),
             pl.BlockSpec(memory_space=pltpu.VMEM),
         ],
-        out_specs=pl.BlockSpec(memory_space=pltpu.VMEM),
-        out_shape=jax.ShapeDtypeStruct((4, 4, SLAB_ROWS, LANES), jnp.float32),
+        out_specs=[pl.BlockSpec(memory_space=pltpu.VMEM)] * len(ks),
+        out_shape=[jax.ShapeDtypeStruct((4, SLAB_ROWS, LANES), jnp.float32)] * len(ks),
         scratch_shapes=[
-            pltpu.VMEM((16, SLAB, LABS), jnp.bfloat16),
-            pltpu.VMEM((16, SLAB, LABS), jnp.int32),
-            pltpu.SemaphoreType.DMA((2, 16)),
+            pltpu.VMEM((slabs, SLAB, LABS), jnp.bfloat16),
+            pltpu.VMEM((slabs, SLAB, LABS), jnp.int32),
+            pltpu.SemaphoreType.DMA((2, slabs)),
         ],
         compiler_params=pltpu.CompilerParams(vmem_limit_bytes=SKETCH_VMEM),
         cost_estimate=pl.CostEstimate(
-            flops=2 * ROWS * 768 * 32, bytes_accessed=ROWS * LABS * 6, transcendentals=ROWS * LABS
+            flops=2 * slabs * SLAB * 768 * 32,
+            bytes_accessed=slabs * SLAB * LABS * 6,
+            transcendentals=slabs * SLAB * LABS,
         ),
         name="sketch",
     )(scores, targets, signs_t)
@@ -138,26 +139,25 @@
         write(piece, jnp.concatenate(parts, axis=0).astype(F8))
 
 
-def weight_kernel(s1, s2, s3, leaves_ref, out_ref):
+def weight_kernel(k, stats_ref, leaves_ref, out_ref):
     x = lax.axis_index("x").astype(jnp.int32)
-    for k, stats_ref in ((1, s1), (2, s2), (3, s3)):
-
-        def write(piece, value, first=(k - 1) * CHUNK):
-            out_ref[:, first + piece * LANES : first + (piece + 1) * LANES] = value
-
-        weight_block(stats_ref, leaves_ref, x ^ k, write)
-
-
-def weight_call(blocks, leaves):
-    return pl.pallas_call(
-        weight_kernel,
-        in_specs=[pl.BlockSpec(memory_space=pltpu.VMEM)] * 4,
+
+    def write(piece, value):
+        out_ref[:, piece * LANES : (piece + 1) * LANES] = value
+
+    weight_block(stats_ref, leaves_ref, x ^ k, write)
+
+
+def weight_call(k, stats, leaves):
+    return pl.pallas_call(
+        functools.partial(weight_kernel, k),
+        in_specs=[pl.BlockSpec(memory_space=pltpu.VMEM)] * 2,
         out_specs=pl.BlockSpec(memory_space=pltpu.VMEM),
-        out_shape=jax.ShapeDtypeStruct((W_ROWS, 3 * CHUNK), F8),
+        out_shape=jax.ShapeDtypeStruct((W_ROWS, CHUNK), F8),
         compiler_params=pltpu.CompilerParams(vmem_limit_bytes=24 << 20),
         cost_estimate=pl.CostEstimate(flops=1_000_000, bytes_accessed=100_000, transcendentals=0),
         name="weights",
-    )(*blocks, leaves)
+    )(stats, leaves)
 
 
 def count(codes, weights):
@@ -185,40 +185,37 @@
     return OWN_BINS * (2 * (zl ^ k) + (core if own else 1 - core))
 
 
-def own_kernel(bins_ref, stats_ref, leaves_ref, out_ref, weights_ref):
+def block_bins(bins_ref, k):
     x = lax.axis_index("x").astype(jnp.int32)
-
-    def write(piece, value):
-        weights_ref[:, piece * LANES : (piece + 1) * LANES] = value
-
-    weight_block(stats_ref, leaves_ref, x, write)
-    bins = bins_ref[:, pl.ds(pl.multiple_of(x * CHUNK, CHUNK), CHUNK)]
-    for k, own in ORDER:
-        out_ref[4 * own + k] = count(bins - first_bin(k, own), weights_ref[...])
-
-
-def own_call(bins_t, stats, leaves):
-    return pl.pallas_call(
-        own_kernel,
-        in_specs=[pl.BlockSpec(memory_space=pltpu.VMEM)] * 3,
+    return bins_ref[:, pl.ds(pl.multiple_of((x ^ k) * CHUNK, CHUNK), CHUNK)]
+
+
+def block_kernel(k, bins_ref, stats_ref, leaves_ref, *refs):
+    out_ref, weights_ref = refs[-2:]
+    weight_kernel(k, stats_ref, leaves_ref, weights_ref)
+    bins = block_bins(bins_ref, k)
+    for to, own in ORDER:
+        total = count(bins - first_bin(to, own), weights_ref[...])
+        if len(refs) == 3:
+            total += refs[0][4 * own + to]
+        out_ref[4 * own + to] = total
+
+
+def block_call(k, bins_t, stats, leaves, *before):
+    return pl.pallas_call(
+        functools.partial(block_kernel, k),
+        in_specs=[pl.BlockSpec(memory_space=pltpu.VMEM)] * (3 + len(before)),
         out_specs=pl.BlockSpec(memory_space=pltpu.VMEM),
         out_shape=jax.ShapeDtypeStruct((8,) + PART, jnp.float32),
         scratch_shapes=[pltpu.VMEM((W_ROWS, CHUNK), F8)],
         compiler_params=pltpu.CompilerParams(vmem_limit_bytes=32 << 20),
         cost_estimate=pl.CostEstimate(flops=5_000_000_000, bytes_accessed=1_000_000, transcendentals=0),
-        name="own",
-    )(bins_t, stats, leaves)
-
-
-def rest_bins(bins_ref):
-    x = lax.axis_index("x").astype(jnp.int32)
-    return jnp.concatenate(
-        [bins_ref[:, pl.ds(pl.multiple_of((x ^ j) * CHUNK, CHUNK), CHUNK)] for j in (1, 2, 3)], axis=1
-    )
+        name="block",
+    )(bins_t, stats, leaves, *before)
 
 
 def other_kernel(ks, bins_ref, weights_ref, start_ref, out_ref):
-    bins = rest_bins(bins_ref)
+    bins = block_bins(bins_ref, LAST)
     for place, k in enumerate(ks):
         out_ref[place] = start_ref[k] + count(bins - first_bin(k, False), weights_ref[...])
 
@@ -237,7 +234,7 @@
 
 def hist_kernel(k, place, bins_ref, weights_ref, start_ref, swapped_ref, *refs):
     out_ref = refs[-1]
-    bins = rest_bins(bins_ref)
+    bins = block_bins(bins_ref, LAST)
     total = start_ref[4 + k] + swapped_ref[place]
     for ref in refs[:-1]:
         total += ref[...]
@@ -256,22 +253,6 @@
     )(bins_t, weights, start, swapped, *more)
 
 
-def add_kernel(a_ref, b_ref, out_ref):
-    out_ref[...] = a_ref[...] + b_ref[...]
-
-
-def add_call(a, b):
-    return pl.pallas_call(
-        add_kernel,
-        in_specs=[pl.BlockSpec(memory_space=pltpu.VMEM)] * 2,
-        out_specs=pl.BlockSpec(memory_space=pltpu.VMEM),
-        out_shape=jax.ShapeDtypeStruct(PART, jnp.float32),
-        compiler_params=pltpu.CompilerParams(vmem_limit_bytes=8 << 20),
-        cost_estimate=pl.CostEstimate(flops=ADD_COST, bytes_accessed=1000, transcendentals=0),
-        name="add",
-    )(a, b)
-
-
 def finish_kernel(a_ref, b_ref, c_ref, out_ref):
     total = a_ref[...] + (b_ref[...] + c_ref[...])
     rows = []
@@ -300,25 +281,26 @@
     bins_t = bins.T
     leaves2 = leaves.reshape(ROWS // LANES, LANES)
 
-    parts = sketch_call(scores, targets, signs_t)
-    arrived = [swap(parts[k], "x", k, 4) for k in (2, 1, 3)]
-    mine = (parts[0] + arrived[0]) + (arrived[1] + arrived[2])
+    arrived = [
+        swap(part, "x", k, 4) for k, part in zip((2, 1, 3), sketch_call((2, 1, 3), scores, targets, signs_t))
+    ]
+    (mine,) = sketch_call((0,), scores, targets, signs_t)
+    mine = (mine + arrived[0]) + (arrived[1] + arrived[2])
     arrived = [swap(mine, "y", k, 4) for k in (2, 1, 3)]
     mine = (mine + arrived[0]) + (arrived[1] + arrived[2])
     mine = mine + swap(mine, "zh", 1, 2)
-    blocks = [swap(mine, "x", k, 4) for k in (1, 2, 3)]
-    start = own_call(bins_t, mine, leaves2)
-    weights = weight_call(blocks, leaves2)
-
-    first = swap(other_call((3,), bins_t, weights, start), "c", 1, 2)
-    part = hist_call(3, bins_t, weights, start, first, 0)
-    moved3 = swap(part, "zl", 3, 4)
-    rest = swap(other_call((2, 1, 0), bins_t, weights, start), "c", 1, 2)
-    part = hist_call(2, bins_t, weights, start, rest, 0)
-    moved2 = swap(part, "zl", 2, 4)
-    part = hist_call(1, bins_t, weights, start, rest, 1)
-    moved1 = swap(part, "zl", 1, 4)
-    part = hist_call(0, bins_t, weights, start, rest, 2, moved3)
+    blocks = {k: swap(mine, "x", k, 4) for k in (1, 3, 2)}
+    start = block_call(0, bins_t, mine, leaves2)
+    for k in (1, 3):
+        start = block_call(k, bins_t, blocks[k], leaves2, start)
+    weights = weight_call(LAST, blocks[LAST], leaves2)
+
+    far = swap(other_call((3, 2), bins_t, weights, start), "c", 1, 2)
+    near = swap(other_call((1, 0), bins_t, weights, start), "c", 1, 2)
+    passed = swap(hist_call(3, bins_t, weights, start, far, 0), "zl", 1, 4)
+    moved1 = swap(hist_call(1, bins_t, weights, start, near, 0), "zl", 1, 4)
+    moved2 = swap(hist_call(2, bins_t, weights, start, far, 1, passed), "zl", 2, 4)
+    part = hist_call(0, bins_t, weights, start, near, 1)
     return finish_call((part, moved2, moved1))
 
 

time: 83 us -> 74.4 us (0.90)
  the two profiles are of different devices: /device:TPU:1 before, /device:TPU:22 now
where the time goes in v4:
time: 74.4 us; the launch traced here: 74.2 us
  starting transfers between devices  28 us (38%)
  waiting for transfers between devices  23.5 us (32%)
  Pallas kernels  21.7 us (29%)
    ppermute x15, starting transfers between devices, swap(): return lax.ppermute(value, axis, [(i, i ^ bit) for i in range(size)])  28 us
    ppermute x15, waiting for transfers between devices, swap(): return lax.ppermute(value, axis, [(i, i ^ bit) for i in range(size)])  23.5 us
    pallas_call x2, Pallas kernels, sketch_call(): pl.pallas_call(functools.partial(sketch_kernel, ks), in_specs=[pl.BlockSp...  9.01 us
    pallas_call x3, Pallas kernels, block_call(): pl.pallas_call(functools.partial(block_kernel, k), in_specs=[pl.BlockSpec...  8.13 us
    pallas_call x4, Pallas kernels, hist_call(): pl.pallas_call(functools.partial(hist_kernel, k, place), in_specs=[pl.Blo...  1.85 us
    pallas_call x2, Pallas kernels, other_call(): pl.pallas_call(functools.partial(other_kernel, ks), in_specs=[pl.BlockSpe...  1.57 us
  transfers between devices with their start and end apart: 15, of which 10 were waited for; matrix products, arithmetic and copies ran while one was open for 0% of the time, Pallas kernels for 19%

profile of v4, /device:TPU:22, one launch (start us, length us, event | category | flops | bytes accessed | tf_op | source)
XLA Modules:
  0.0 74.2 jit_solution(780428345936850009)
XLA Ops:
  0.0 0.0 copy-start.1
  0.0 0.7 copy-done.1
  0.7 5.9 %sketch.3 = (f32[4,68,128]{2,1,0:T(8,128)S(1)}, f32[4,68,128]{2,1,0:T(8,128)S(1)}, f32[4,68,128]{2,1,0:T(8,128)S(1)}) custom-call(bf16[8192,256]{1,0:T(8,128)(2,1)} %scores_ref.3, s32[8192,256]{1,0:T(8,128)} %targets_ref.3, s32[16,256]{1,0:T(8,128)S(1)} %bitcast.12), custom_call_target="tpu_custom_call" | custom-call | flops 301989888 | bytes 9437184 | tf_op jit(solution)/shard_map/sketch/pallas_call | solution.py:89
  6.6 1.5 %collective-permute-start = (f32[4,68,128]{2,1,0:T(8,128)S(1)}, f32[4,68,128]{2,1,0:T(8,128)S(1)}, u32[]{:S(2)}, u32[]{:S(2)}) collective-permute-start(f32[4,68,128]{2,1,0:T(8,128)S(1)} %get-tuple-element.8), channel_id=1, source_target_pairs={{0,4},{2,6},{4,0},{6,2},{1,5},{3,7},{5,1},{7,3},{8,12},{10,14},{12... | collective-permute-start | bytes 417800 | tf_op jit(solution)/shard_map/ppermute | solution.py:276
  8.1 0.0 collective-permute-start.1
  8.1 2.7 %collective-permute-start.2 = (f32[4,68,128]{2,1,0:T(8,128)S(1)}, f32[4,68,128]{2,1,0:T(8,128)S(1)}, u32[]{:S(2)}, u32[]{:S(2)}) collective-permute-start(f32[4,68,128]{2,1,0:T(8,128)S(1)} %get-tuple-element.10), channel_id=1, source_target_pairs={{0,6},{2,4},{4,2},{6,0},{1,7},{3,5},{5,3},{7,1},{8,14},{10,12},{12... | collective-permute-start | bytes 417800 | tf_op jit(solution)/shard_map/ppermute | solution.py:276
  10.8 3.2 %sketch.2 = f32[4,68,128]{2,1,0:T(8,128)S(1)} custom-call(bf16[8192,256]{1,0:T(8,128)(2,1)} %scores_ref.3, s32[8192,256]{1,0:T(8,128)} %targets_ref.3, s32[16,256]{1,0:T(8,128)S(1)} %bitcast.13), custom_call_target="tpu_custom_call" | custom-call | flops 100663296 | bytes 3145728 | tf_op jit(solution)/shard_map/sketch/pallas_call | solution.py:89
  13.9 0.0 copy-start
  13.9 0.0 copy-start.2
  14.0 1.0 %collective-permute-done = f32[4,68,128]{2,1,0:T(8,128)S(1)} collective-permute-done((f32[4,68,128]{2,1,0:T(8,128)S(1)}, f32[4,68,128]{2,1,0:T(8,128)S(1)}, u32[]{:S(2)}, u32[]{:S(2)}) %collective-permute-start) | collective-permute-done | bytes 139296 | tf_op jit(solution)/shard_map/ppermute | solution.py:276
  14.9 0.0 collective-permute-done.1
  14.9 2.0 %collective-permute-done.2 = f32[4,68,128]{2,1,0:T(8,128)S(1)} collective-permute-done((f32[4,68,128]{2,1,0:T(8,128)S(1)}, f32[4,68,128]{2,1,0:T(8,128)S(1)}, u32[]{:S(2)}, u32[]{:S(2)}) %collective-permute-start.2) | collective-permute-done | bytes 139296 | tf_op jit(solution)/shard_map/ppermute | solution.py:276
  17.0 0.4 collective-permute-start.3
  17.4 2.2 %collective-permute-start.4 = (f32[4,68,128]{2,1,0:T(8,128)S(1)}, f32[4,68,128]{2,1,0:T(8,128)S(1)}, u32[]{:S(2)}, u32[]{:S(2)}) collective-permute-start(f32[4,68,128]{2,1,0:T(8,128)S(1)} %add_add_fusion.1), channel_id=1, source_target_pairs={{0,8},{8,0},{16,24},{24,16},{1,9},{9,1},{17,25},{25,17},{2,10},{10... | collective-permute-start | bytes 417800 | tf_op jit(solution)/shard_map/ppermute | solution.py:276
  19.6 1.6 %collective-permute-start.5 = (f32[4,68,128]{2,1,0:T(8,128)S(1)}, f32[4,68,128]{2,1,0:T(8,128)S(1)}, u32[]{:S(2)}, u32[]{:S(2)}) collective-permute-start(f32[4,68,128]{2,1,0:T(8,128)S(1)} %add_add_fusion.1), channel_id=1, source_target_pairs={{0,24},{8,16},{16,8},{24,0},{1,25},{9,17},{17,9},{25,1},{2,26},{10... | collective-permute-start | bytes 417800 | tf_op jit(solution)/shard_map/ppermute | solution.py:276
  21.1 4.2 %collective-permute-done.3 = f32[4,68,128]{2,1,0:T(8,128)S(1)} collective-permute-done((f32[4,68,128]{2,1,0:T(8,128)S(1)}, f32[4,68,128]{2,1,0:T(8,128)S(1)}, u32[]{:S(2)}, u32[]{:S(2)}) %collective-permute-start.3) | collective-permute-done | bytes 139296 | tf_op jit(solution)/shard_map/ppermute | solution.py:276
  25.3 1.2 %collective-permute-done.4 = f32[4,68,128]{2,1,0:T(8,128)S(1)} collective-permute-done((f32[4,68,128]{2,1,0:T(8,128)S(1)}, f32[4,68,128]{2,1,0:T(8,128)S(1)}, u32[]{:S(2)}, u32[]{:S(2)}) %collective-permute-start.4) | collective-permute-done | bytes 139296 | tf_op jit(solution)/shard_map/ppermute | solution.py:276
  26.4 1.0 %collective-permute-done.5 = f32[4,68,128]{2,1,0:T(8,128)S(1)} collective-permute-done((f32[4,68,128]{2,1,0:T(8,128)S(1)}, f32[4,68,128]{2,1,0:T(8,128)S(1)}, u32[]{:S(2)}, u32[]{:S(2)}) %collective-permute-start.5) | collective-permute-done | bytes 139296 | tf_op jit(solution)/shard_map/ppermute | solution.py:276
  27.5 7.3 %collective-permute-start.6 = (f32[4,68,128]{2,1,0:T(8,128)S(1)}, f32[4,68,128]{2,1,0:T(8,128)S(1)}, u32[]{:S(2)}, u32[]{:S(2)}) collective-permute-start(f32[4,68,128]{2,1,0:T(8,128)S(1)} %add_add_fusion), channel_id=1, source_target_pairs={{0,1},{1,0},{2,3},{3,2},{4,5},{5,4},{6,7},{7,6},{8,9},{9,8},{10,11... | collective-permute-start | bytes 417800 | tf_op jit(solution)/shard_map/ppermute | solution.py:276
  34.8 4.1 %collective-permute-done.6 = f32[4,68,128]{2,1,0:T(8,128)S(1)} collective-permute-done((f32[4,68,128]{2,1,0:T(8,128)S(1)}, f32[4,68,128]{2,1,0:T(8,128)S(1)}, u32[]{:S(2)}, u32[]{:S(2)}) %collective-permute-start.6) | collective-permute-done | bytes 139296 | tf_op jit(solution)/shard_map/ppermute | solution.py:276
  38.9 0.9 %collective-permute-start.9 = (f32[4,68,128]{2,1,0:T(8,128)S(1)}, f32[4,68,128]{2,1,0:T(8,128)S(1)}, u32[]{:S(2)}, u32[]{:S(2)}) collective-permute-start(f32[4,68,128]{2,1,0:T(8,128)S(1)} %add.27.stats_ref), channel_id=1, source_target_pairs={{0,2},{2,0},{4,6},{6,4},{1,3},{3,1},{5,7},{7,5},{8,10},{10,8},{12,... | collective-permute-start | bytes 417800 | tf_op jit(solution)/shard_map/ppermute | solution.py:276
  39.8 0.2 collective-permute-start.8
  40.1 3.0 %collective-permute-start.7 = (f32[4,68,128]{2,1,0:T(8,128)S(1)}, f32[4,68,128]{2,1,0:T(8,128)S(1)}, u32[]{:S(2)}, u32[]{:S(2)}) collective-permute-start(f32[4,68,128]{2,1,0:T(8,128)S(1)} %add.27.stats_ref), channel_id=1, source_target_pairs={{0,4},{2,6},{4,0},{6,2},{1,5},{3,7},{5,1},{7,3},{8,12},{10,14},{12... | collective-permute-start | bytes 417800 | tf_op jit(solution)/shard_map/ppermute | solution.py:276
  43.1 0.0 copy-done
  43.1 0.0 copy-done.2
  43.1 2.7 %block.3.refs_0_ = f32[8,68,512]{2,1,0:T(8,128)S(1)} custom-call(s32[16,8192]{1,0:T(8,128)S(1)} %bitcast.3, f32[4,68,128]{2,1,0:T(8,128)S(1)} %add.27.stats_ref, s32[64,128]{1,0:T(8,128)S(1)} %bitcast.14), custom_call_target="tpu_custom_call" | custom-call | flops 5000000000 | bytes 1000000 | tf_op jit(solution)/shard_map/block/pallas_call | solution.py:205
  45.8 0.0 collective-permute-done.9.stats_ref
  45.8 2.7 %block.4.refs_0_ = f32[8,68,512]{2,1,0:T(8,128)S(1)} custom-call(s32[16,8192]{1,0:T(8,128)S(1)} %bitcast.4, f32[4,68,128]{2,1,0:T(8,128)S(1)} %collective-permute-done.9.stats_ref, s32[64,128]{1,0:T(8,128)S(1)} %bitcast.15, f32[8,68,512]{2,1,0:T(8,128)S(1)} %block.3.refs_0_), custom_call_target="tpu_custom_call" | custom-call | flops 5000000000 | bytes 1000000 | tf_op jit(solution)/shard_map/block/pallas_call | solution.py:205
  48.5 0.5 collective-permute-done.8.stats_ref
  49.1 2.7 %block.5.start_ref = f32[8,68,512]{2,1,0:T(8,128)S(1)} custom-call(s32[16,8192]{1,0:T(8,128)S(1)} %bitcast.5, f32[4,68,128]{2,1,0:T(8,128)S(1)} %collective-permute-done.8.stats_ref, s32[64,128]{1,0:T(8,128)S(1)} %bitcast.16, f32[8,68,512]{2,1,0:T(8,128)S(1)} %block.4.refs_0_), custom_call_target="tpu_custom_call" | custom-call | flops 5000000000 | bytes 1000000 | tf_op jit(solution)/shard_map/block/pallas_call | solution.py:205
  51.8 0.0 collective-permute-done.7.stats_ref
  51.8 0.3 weights.1.weights_ref
  52.1 0.8 %other.3 = f32[2,68,512]{2,1,0:T(8,128)S(1)} custom-call(s32[16,8192]{1,0:T(8,128)S(1)} %bitcast.6, f8e4m3fn[288,2048]{1,0:T(32,128)(4,1)S(1)} %weights.1.weights_ref, f32[8,68,512]{2,1,0:T(8,128)S(1)} %block.5.start_ref), custom_call_target="tpu_custom_call" | custom-call | flops 2000 | bytes 1000 | tf_op jit(solution)/shard_map/other/pallas_call | solution.py:224
  52.9 0.1 collective-permute-start.11
  53.0 0.8 %other.2 = f32[2,68,512]{2,1,0:T(8,128)S(1)} custom-call(s32[16,8192]{1,0:T(8,128)S(1)} %bitcast.7, f8e4m3fn[288,2048]{1,0:T(32,128)(4,1)S(1)} %weights.1.weights_ref, f32[8,68,512]{2,1,0:T(8,128)S(1)} %block.5.start_ref), custom_call_target="tpu_custom_call" | custom-call | flops 2000 | bytes 1000 | tf_op jit(solution)/shard_map/other/pallas_call | solution.py:224
  53.8 0.6 collective-permute-start.10
  54.3 0.2 collective-permute-done.11.swapped_ref
  54.6 0.5 hist.5
  55.0 4.2 %collective-permute-start.12 = (f32[68,512]{1,0:T(8,128)S(1)}, f32[68,512]{1,0:T(8,128)S(1)}, u32[]{:S(2)}, u32[]{:S(2)}) collective-permute-start(f32[68,512]{1,0:T(8,128)S(1)} %hist.5), channel_id=1, source_target_pairs={{0,64},{64,0},{128,192},{192,128},{1,65},{65,1},{129,193},{193,129... | collective-permute-start | bytes 417800 | tf_op jit(solution)/shard_map/ppermute | solution.py:276
  59.2 0.0 collective-permute-done.10.swapped_ref
  59.3 0.5 hist.7
  59.7 0.5 collective-permute-start.14
  60.3 3.6 %collective-permute-done.12.refs_0_ = f32[68,512]{1,0:T(8,128)S(1)} collective-permute-done((f32[68,512]{1,0:T(8,128)S(1)}, f32[68,512]{1,0:T(8,128)S(1)}, u32[]{:S(2)}, u32[]{:S(2)}) %collective-permute-start.12) | collective-permute-done | bytes 139296 | tf_op jit(solution)/shard_map/ppermute | solution.py:276
  63.9 0.5 hist.6
  64.4 2.8 %collective-permute-start.13 = (f32[68,512]{1,0:T(8,128)S(1)}, f32[68,512]{1,0:T(8,128)S(1)}, u32[]{:S(2)}, u32[]{:S(2)}) collective-permute-start(f32[68,512]{1,0:T(8,128)S(1)} %hist.6), channel_id=1, source_target_pairs={{0,128},{64,192},{128,0},{192,64},{1,129},{65,193},{129,1},{193,65... | collective-permute-start | bytes 417800 | tf_op jit(solution)/shard_map/ppermute | solution.py:276
  67.1 0.5 hist.4.a_ref
  67.6 0.0 collective-permute-done.14.c_ref
  67.6 5.8 %collective-permute-done.13.b_ref = f32[68,512]{1,0:T(8,128)S(1)} collective-permute-done((f32[68,512]{1,0:T(8,128)S(1)}, f32[68,512]{1,0:T(8,128)S(1)}, u32[]{:S(2)}, u32[]{:S(2)}) %collective-permute-start.13) | collective-permute-done | bytes 139296 | tf_op jit(solution)/shard_map/ppermute | solution.py:276
  73.4 0.8 %finish.1 = f32[32,16,68]{2,1,0:T(8,128)} custom-call(f32[68,512]{1,0:T(8,128)S(1)} %hist.4.a_ref, f32[68,512]{1,0:T(8,128)S(1)} %collective-permute-done.13.b_ref, f32[68,512]{1,0:T(8,128)S(1)} %collective-permute-done.14.c_ref), custom_call_target="tpu_custom_call" | custom-call | tf_op jit(solution)/shard_map/finish/pallas_call | solution.py:267
  (3 shorter events, 0.1 us)
Async XLA Ops:
  0.0 0.7 copy-start.1
  6.6 8.3 %collective-permute-start = (f32[4,68,128]{2,1,0:T(8,128)S(1)}, f32[4,68,128]{2,1,0:T(8,128)S(1)}, u32[]{:S(2)}, u32[]{:S(2)}) collective-permute-start(f32[4,68,128]{2,1,0:T(8,128)S(1)} %get-tuple-element.8), channel_id=1, source_target_pairs={{0,4},{2,6},{4,0},{6,2},{1,5},{3,7},{5,1},{7,3},{8,12},{10,14},{12... | collective-permute-start | bytes 417800 | tf_op jit(solution)/shard_map/ppermute | solution.py:276
  8.1 6.8 %collective-permute-start.1 = (f32[4,68,128]{2,1,0:T(8,128)S(1)}, f32[4,68,128]{2,1,0:T(8,128)S(1)}, u32[]{:S(2)}, u32[]{:S(2)}) collective-permute-start(f32[4,68,128]{2,1,0:T(8,128)S(1)} %get-tuple-element.9), channel_id=1, source_target_pairs={{0,2},{2,0},{4,6},{6,4},{1,3},{3,1},{5,7},{7,5},{8,10},{10,8},{12,... | collective-permute-start | bytes 417800 | tf_op jit(solution)/shard_map/ppermute | solution.py:276
  8.1 8.8 %collective-permute-start.2 = (f32[4,68,128]{2,1,0:T(8,128)S(1)}, f32[4,68,128]{2,1,0:T(8,128)S(1)}, u32[]{:S(2)}, u32[]{:S(2)}) collective-permute-start(f32[4,68,128]{2,1,0:T(8,128)S(1)} %get-tuple-element.10), channel_id=1, source_target_pairs={{0,6},{2,4},{4,2},{6,0},{1,7},{3,5},{5,3},{7,1},{8,14},{10,12},{12... | collective-permute-start | bytes 417800 | tf_op jit(solution)/shard_map/ppermute | solution.py:276
  13.9 29.2 %copy-start = (s32[8192,16]{0,1:T(8,128)S(1)}, s32[8192,16]{0,1:T(8,128)}, u32[]{:S(2)}) copy-start(s32[8192,16]{0,1:T(8,128)} %param.8) | copy-start | bytes 1572868
  13.9 29.2 %copy-start.2 = (s32[8192]{0:T(1024)S(1)}, s32[8192]{0:T(1024)}, u32[]{:S(2)}) copy-start(s32[8192]{0:T(1024)} %param.9) | copy-start | bytes 98308
  17.0 8.3 %collective-permute-start.3 = (f32[4,68,128]{2,1,0:T(8,128)S(1)}, f32[4,68,128]{2,1,0:T(8,128)S(1)}, u32[]{:S(2)}, u32[]{:S(2)}) collective-permute-start(f32[4,68,128]{2,1,0:T(8,128)S(1)} %add_add_fusion.1), channel_id=1, source_target_pairs={{0,16},{8,24},{16,0},{24,8},{1,17},{9,25},{17,1},{25,9},{2,18},{10... | collective-permute-start | bytes 417800 | tf_op jit(solution)/shard_map/ppermute | solution.py:276
  17.4 9.1 %collective-permute-start.4 = (f32[4,68,128]{2,1,0:T(8,128)S(1)}, f32[4,68,128]{2,1,0:T(8,128)S(1)}, u32[]{:S(2)}, u32[]{:S(2)}) collective-permute-start(f32[4,68,128]{2,1,0:T(8,128)S(1)} %add_add_fusion.1), channel_id=1, source_target_pairs={{0,8},{8,0},{16,24},{24,16},{1,9},{9,1},{17,25},{25,17},{2,10},{10... | collective-permute-start | bytes 417800 | tf_op jit(solution)/shard_map/ppermute | solution.py:276
  19.6 7.9 %collective-permute-start.5 = (f32[4,68,128]{2,1,0:T(8,128)S(1)}, f32[4,68,128]{2,1,0:T(8,128)S(1)}, u32[]{:S(2)}, u32[]{:S(2)}) collective-permute-start(f32[4,68,128]{2,1,0:T(8,128)S(1)} %add_add_fusion.1), channel_id=1, source_target_pairs={{0,24},{8,16},{16,8},{24,0},{1,25},{9,17},{17,9},{25,1},{2,26},{10... | collective-permute-start | bytes 417800 | tf_op jit(solution)/shard_map/ppermute | solution.py:276
  27.5 11.4 %collective-permute-start.6 = (f32[4,68,128]{2,1,0:T(8,128)S(1)}, f32[4,68,128]{2,1,0:T(8,128)S(1)}, u32[]{:S(2)}, u32[]{:S(2)}) collective-permute-start(f32[4,68,128]{2,1,0:T(8,128)S(1)} %add_add_fusion), channel_id=1, source_target_pairs={{0,1},{1,0},{2,3},{3,2},{4,5},{5,4},{6,7},{7,6},{8,9},{9,8},{10,11... | collective-permute-start | bytes 417800 | tf_op jit(solution)/shard_map/ppermute | solution.py:276
  38.9 6.9 %collective-permute-start.9 = (f32[4,68,128]{2,1,0:T(8,128)S(1)}, f32[4,68,128]{2,1,0:T(8,128)S(1)}, u32[]{:S(2)}, u32[]{:S(2)}) collective-permute-start(f32[4,68,128]{2,1,0:T(8,128)S(1)} %add.27.stats_ref), channel_id=1, source_target_pairs={{0,2},{2,0},{4,6},{6,4},{1,3},{3,1},{5,7},{7,5},{8,10},{10,8},{12,... | collective-permute-start | bytes 417800 | tf_op jit(solution)/shard_map/ppermute | solution.py:276
  39.8 9.2 %collective-permute-start.8 = (f32[4,68,128]{2,1,0:T(8,128)S(1)}, f32[4,68,128]{2,1,0:T(8,128)S(1)}, u32[]{:S(2)}, u32[]{:S(2)}) collective-permute-start(f32[4,68,128]{2,1,0:T(8,128)S(1)} %add.27.stats_ref), channel_id=1, source_target_pairs={{0,6},{2,4},{4,2},{6,0},{1,7},{3,5},{5,3},{7,1},{8,14},{10,12},{12... | collective-permute-start | bytes 417800 | tf_op jit(solution)/shard_map/ppermute | solution.py:276
  40.1 11.7 %collective-permute-start.7 = (f32[4,68,128]{2,1,0:T(8,128)S(1)}, f32[4,68,128]{2,1,0:T(8,128)S(1)}, u32[]{:S(2)}, u32[]{:S(2)}) collective-permute-start(f32[4,68,128]{2,1,0:T(8,128)S(1)} %add.27.stats_ref), channel_id=1, source_target_pairs={{0,4},{2,6},{4,0},{6,2},{1,5},{3,7},{5,1},{7,3},{8,12},{10,14},{12... | collective-permute-start | bytes 417800 | tf_op jit(solution)/shard_map/ppermute | solution.py:276
  52.9 1.7 %collective-permute-start.11 = (f32[2,68,512]{2,1,0:T(8,128)S(1)}, f32[2,68,512]{2,1,0:T(8,128)S(1)}, u32[]{:S(2)}, u32[]{:S(2)}) collective-permute-start(f32[2,68,512]{2,1,0:T(8,128)S(1)} %other.3), channel_id=1, source_target_pairs={{0,32},{32,0},{1,33},{33,1},{2,34},{34,2},{3,35},{35,3},{4,36},{36... | collective-permute-start | bytes 835592 | tf_op jit(solution)/shard_map/ppermute | solution.py:276
  53.8 5.5 %collective-permute-start.10 = (f32[2,68,512]{2,1,0:T(8,128)S(1)}, f32[2,68,512]{2,1,0:T(8,128)S(1)}, u32[]{:S(2)}, u32[]{:S(2)}) collective-permute-start(f32[2,68,512]{2,1,0:T(8,128)S(1)} %other.2), channel_id=1, source_target_pairs={{0,32},{32,0},{1,33},{33,1},{2,34},{34,2},{3,35},{35,3},{4,36},{36... | collective-permute-start | bytes 835592 | tf_op jit(solution)/shard_map/ppermute | solution.py:276
  55.0 8.9 %collective-permute-start.12 = (f32[68,512]{1,0:T(8,128)S(1)}, f32[68,512]{1,0:T(8,128)S(1)}, u32[]{:S(2)}, u32[]{:S(2)}) collective-permute-start(f32[68,512]{1,0:T(8,128)S(1)} %hist.5), channel_id=1, source_target_pairs={{0,64},{64,0},{128,192},{192,128},{1,65},{65,1},{129,193},{193,129... | collective-permute-start | bytes 417800 | tf_op jit(solution)/shard_map/ppermute | solution.py:276
  59.7 7.9 %collective-permute-start.14 = (f32[68,512]{1,0:T(8,128)S(1)}, f32[68,512]{1,0:T(8,128)S(1)}, u32[]{:S(2)}, u32[]{:S(2)}) collective-permute-start(f32[68,512]{1,0:T(8,128)S(1)} %hist.7), channel_id=1, source_target_pairs={{0,64},{64,0},{128,192},{192,128},{1,65},{65,1},{129,193},{193,129... | collective-permute-start | bytes 417800 | tf_op jit(solution)/shard_map/ppermute | solution.py:276
  64.4 9.0 %collective-permute-start.13 = (f32[68,512]{1,0:T(8,128)S(1)}, f32[68,512]{1,0:T(8,128)S(1)}, u32[]{:S(2)}, u32[]{:S(2)}) collective-permute-start(f32[68,512]{1,0:T(8,128)S(1)} %hist.6), channel_id=1, source_target_pairs={{0,128},{64,192},{128,0},{192,64},{1,129},{65,193},{129,1},{193,65... | collective-permute-start | bytes 417800 | tf_op jit(solution)/shard_map/ppermute | solution.py:276

commit v5 on v4

--- a/solution.py
+++ b/solution.py
@@ -18,7 +18,8 @@
 SLAB = 512
 LANES = 128
 QUADS = SLAB // LANES
-SLAB_ROWS = QUADS * (K + 1)
+PIECES = 4 * QUADS
+STAT_ROWS = PIECES * (K + 1)
 F8 = jnp.float8_e4m3fn
 NT = (((1,), (1,)), ((), ()))
 SKETCH_SCALES = (4.0, 64.0, 2.0**24, 2.0**29)
@@ -27,11 +28,12 @@
 W_ROWS = 288
 OWN_BINS = 32
 CHUNK = 4 * SLAB
-PART = (LEAVES * (K + 1), OWN_BINS * FEATS)
+HALF = OWN_BINS * FEATS // 2
+PART = (2 * LEAVES * (K + 1), HALF)
 ORDER = tuple((k, own) for k in (3, 2, 1, 0) for own in (False, True))
 OTHER_COST = 1000
-OWN_COST = 1000
-LAST = 2
+HIST_COST = (1000, 1000, 5_000_000_000, 1000)
+LAST = (3, 2)
 GROUP = 4
 SKETCH_VMEM = 51 << 20
 
@@ -77,11 +79,10 @@
         right = jnp.concatenate([grad_high, grad_low, hess_high, hess_low], axis=1)
         stats = lax.dot_general(left, right, NT, preferred_element_type=jnp.float32)
         for piece in range(GROUP * QUADS):
-            slab, quad = first + piece // QUADS, piece % QUADS
-            lanes = slice(piece * LANES, (piece + 1) * LANES)
-            out_ref, at = out_refs[slab // 4], slab % 4
-            out_ref[at, quad * K : (quad + 1) * K, :] = stats[:K, lanes] * (1.0 / math.sqrt(L))
-            out_ref[at, QUADS * K + quad : QUADS * K + quad + 1, :] = stats[K : K + 1, lanes] * (1.0 / L)
+            at, lanes = piece % PIECES, slice(piece * LANES, (piece + 1) * LANES)
+            out_ref = out_refs[(first * QUADS + piece) // PIECES]
+            out_ref[at * K : (at + 1) * K, :] = stats[:K, lanes] * (1.0 / math.sqrt(L))
+            out_ref[PIECES * K + at : PIECES * K + at + 1, :] = stats[K : K + 1, lanes] * (1.0 / L)
 
 
 def sketch_call(ks, scores, targets, signs_t):
@@ -94,7 +95,7 @@
             pl.BlockSpec(memory_space=pltpu.VMEM),
         ],
         out_specs=[pl.BlockSpec(memory_space=pltpu.VMEM)] * len(ks),
-        out_shape=[jax.ShapeDtypeStruct((4, SLAB_ROWS, LANES), jnp.float32)] * len(ks),
+        out_shape=[jax.ShapeDtypeStruct((STAT_ROWS, LANES), jnp.float32)] * len(ks),
         scratch_shapes=[
             pltpu.VMEM((slabs, SLAB, LABS), jnp.bfloat16),
             pltpu.VMEM((slabs, SLAB, LABS), jnp.int32),
@@ -122,11 +123,10 @@
 def weight_block(stats_ref, leaves_ref, chunk, write):
     leaf_iota = lax.broadcasted_iota(jnp.int32, (8, LANES), 0)
     zeros = jnp.zeros((K, LANES), jnp.float32)
-    for piece in range(4 * QUADS):
-        slab, quad = piece // QUADS, piece % QUADS
-        leaf = leaves_ref[pl.ds(chunk * 4 * QUADS + piece, 1), :]
-        sketch = stats_ref[slab, quad * K : (quad + 1) * K, :]
-        curve = stats_ref[slab, QUADS * K + quad : QUADS * K + quad + 1, :]
+    for piece in range(PIECES):
+        leaf = leaves_ref[pl.ds(chunk * PIECES + piece, 1), :]
+        sketch = stats_ref[piece * K : (piece + 1) * K, :]
+        curve = stats_ref[PIECES * K + piece : PIECES * K + piece + 1, :]
         sketch = sketch.astype(jnp.bfloat16).astype(jnp.float32)
         curve = jnp.broadcast_to(curve, (8, LANES)).astype(jnp.bfloat16).astype(jnp.float32)
         masks = [jnp.broadcast_to(leaf == e, (K, LANES)) for e in range(LEAVES)]
@@ -139,25 +139,27 @@
         write(piece, jnp.concatenate(parts, axis=0).astype(F8))
 
 
-def weight_kernel(k, stats_ref, leaves_ref, out_ref):
+def weight_kernel(ks, *refs):
     x = lax.axis_index("x").astype(jnp.int32)
-
-    def write(piece, value):
-        out_ref[:, piece * LANES : (piece + 1) * LANES] = value
-
-    weight_block(stats_ref, leaves_ref, x ^ k, write)
-
-
-def weight_call(k, stats, leaves):
-    return pl.pallas_call(
-        functools.partial(weight_kernel, k),
-        in_specs=[pl.BlockSpec(memory_space=pltpu.VMEM)] * 2,
+    leaves_ref, out_ref = refs[-2:]
+    for place, k in enumerate(ks):
+
+        def write(piece, value, first=place * CHUNK):
+            out_ref[:, first + piece * LANES : first + (piece + 1) * LANES] = value
+
+        weight_block(refs[place], leaves_ref, x ^ k, write)
+
+
+def weight_call(ks, stats, leaves):
+    return pl.pallas_call(
+        functools.partial(weight_kernel, ks),
+        in_specs=[pl.BlockSpec(memory_space=pltpu.VMEM)] * (len(ks) + 1),
         out_specs=pl.BlockSpec(memory_space=pltpu.VMEM),
-        out_shape=jax.ShapeDtypeStruct((W_ROWS, CHUNK), F8),
+        out_shape=jax.ShapeDtypeStruct((W_ROWS, len(ks) * CHUNK), F8),
         compiler_params=pltpu.CompilerParams(vmem_limit_bytes=24 << 20),
         cost_estimate=pl.CostEstimate(flops=1_000_000, bytes_accessed=100_000, transcendentals=0),
         name="weights",
-    )(stats, leaves)
+    )(*stats, leaves)
 
 
 def count(codes, weights):
@@ -176,7 +178,9 @@
         total[4 * TERM_ROWS + 8 * t : 4 * TERM_ROWS + 8 * t + 8] * (1.0 / scale)
         for t, scale in enumerate(CURVE_SCALES)
     )
-    return jnp.concatenate([sketch, curve[:LEAVES]], axis=0)
+    return jnp.concatenate(
+        [sketch[:, :HALF], sketch[:, HALF:], curve[:LEAVES, :HALF], curve[:LEAVES, HALF:]], axis=0
+    )
 
 
 def first_bin(k, own):
@@ -185,15 +189,17 @@
     return OWN_BINS * (2 * (zl ^ k) + (core if own else 1 - core))
 
 
-def block_bins(bins_ref, k):
+def block_bins(bins_ref, ks):
     x = lax.axis_index("x").astype(jnp.int32)
-    return bins_ref[:, pl.ds(pl.multiple_of((x ^ k) * CHUNK, CHUNK), CHUNK)]
+    return jnp.concatenate(
+        [bins_ref[:, pl.ds(pl.multiple_of((x ^ k) * CHUNK, CHUNK), CHUNK)] for k in ks], axis=1
+    )
 
 
 def block_kernel(k, bins_ref, stats_ref, leaves_ref, *refs):
     out_ref, weights_ref = refs[-2:]
-    weight_kernel(k, stats_ref, leaves_ref, weights_ref)
-    bins = block_bins(bins_ref, k)
+    weight_kernel((k,), stats_ref, leaves_ref, weights_ref)
+    bins = block_bins(bins_ref, (k,))
     for to, own in ORDER:
         total = count(bins - first_bin(to, own), weights_ref[...])
         if len(refs) == 3:
@@ -248,19 +254,23 @@
         out_specs=pl.BlockSpec(memory_space=pltpu.VMEM),
         out_shape=jax.ShapeDtypeStruct(PART, jnp.float32),
         compiler_params=pltpu.CompilerParams(vmem_limit_bytes=32 << 20),
-        cost_estimate=pl.CostEstimate(flops=OWN_COST, bytes_accessed=1000, transcendentals=0),
+        cost_estimate=pl.CostEstimate(flops=HIST_COST[k], bytes_accessed=1000, transcendentals=0),
         name="hist",
     )(bins_t, weights, start, swapped, *more)
 
 
 def finish_kernel(a_ref, b_ref, c_ref, out_ref):
     total = a_ref[...] + (b_ref[...] + c_ref[...])
-    rows = []
-    for e in range(LEAVES):
-        rows.append(total[e * K : (e + 1) * K])
-        rows.append(total[TERM_ROWS + e : TERM_ROWS + e + 1])
-    total = jnp.concatenate(rows, axis=0)
-    out_ref[...] = total.T.reshape(OWN_BINS, FEATS, LEAVES * (K + 1))
+    for half in range(2):
+        rows = []
+        for e in range(LEAVES):
+            first = half * TERM_ROWS + e * K
+            rows.append(total[first : first + K])
+            first = 2 * TERM_ROWS + half * LEAVES + e
+            rows.append(total[first : first + 1])
+        part = jnp.concatenate(rows, axis=0).T
+        bins = OWN_BINS // 2
+        out_ref[half * bins : (half + 1) * bins] = part.reshape(bins, FEATS, LEAVES * (K + 1))
 
 
 def finish_call(parts):
@@ -289,17 +299,23 @@
     arrived = [swap(mine, "y", k, 4) for k in (2, 1, 3)]
     mine = (mine + arrived[0]) + (arrived[1] + arrived[2])
     mine = mine + swap(mine, "zh", 1, 2)
-    blocks = {k: swap(mine, "x", k, 4) for k in (1, 3, 2)}
+    first = swap(mine, "x", 1, 4)
     start = block_call(0, bins_t, mine, leaves2)
-    for k in (1, 3):
-        start = block_call(k, bins_t, blocks[k], leaves2, start)
-    weights = weight_call(LAST, blocks[LAST], leaves2)
-
-    far = swap(other_call((3, 2), bins_t, weights, start), "c", 1, 2)
+    mine, start = lax.optimization_barrier((mine, start))
+    last = [swap(mine, "x", k, 4) for k in LAST]
+    start = block_call(1, bins_t, first, leaves2, start)
+    weights = weight_call(LAST, last, leaves2)
+
+    far = swap(other_call((3,), bins_t, weights, start), "c", 1, 2)
+    mid = other_call((2,), bins_t, weights, start)
+    mid, start = lax.optimization_barrier((mid, start))
+    mid = swap(mid, "c", 1, 2)
+    part = hist_call(3, bins_t, weights, start, far, 0)
+    part, start = lax.optimization_barrier((part, start))
+    passed = swap(part, "zl", 1, 4)
     near = swap(other_call((1, 0), bins_t, weights, start), "c", 1, 2)
-    passed = swap(hist_call(3, bins_t, weights, start, far, 0), "zl", 1, 4)
     moved1 = swap(hist_call(1, bins_t, weights, start, near, 0), "zl", 1, 4)
-    moved2 = swap(hist_call(2, bins_t, weights, start, far, 1, passed), "zl", 2, 4)
+    moved2 = swap(hist_call(2, bins_t, weights, start, mid, 0, passed), "zl", 2, 4)
     part = hist_call(0, bins_t, weights, start, near, 1)
     return finish_call((part, moved2, moved1))
 

time: 74.4 us -> 74.6 us (level)
  the two profiles are of different devices: /device:TPU:22 before, /device:TPU:1 now
where the time goes in v5:
time: 74.6 us; the launch traced here: 73.9 us
  starting transfers between devices  31.2 us (42%)
  Pallas kernels  21.8 us (29%)
  waiting for transfers between devices  19.9 us (27%)
    ppermute x16, starting transfers between devices, swap(): return lax.ppermute(value, axis, [(i, i ^ bit) for i in range(size)])  31.2 us
    ppermute x16, waiting for transfers between devices, swap(): return lax.ppermute(value, axis, [(i, i ^ bit) for i in range(size)])  19.9 us
    pallas_call x2, Pallas kernels, sketch_call(): pl.pallas_call(functools.partial(sketch_kernel, ks), in_specs=[pl.BlockSp...  9.01 us
    pallas_call x2, Pallas kernels, block_call(): pl.pallas_call(functools.partial(block_kernel, k), in_specs=[pl.BlockSpec...  5.44 us
    pallas_call x4, Pallas kernels, hist_call(): pl.pallas_call(functools.partial(hist_kernel, k, place), in_specs=[pl.Blo...  3.07 us
    pallas_call x3, Pallas kernels, other_call(): pl.pallas_call(functools.partial(other_kernel, ks), in_specs=[pl.BlockSpe...  2.92 us
  transfers between devices with their start and end apart: 16, of which 11 were waited for; matrix products, arithmetic and copies ran while one was open for 0% of the time, Pallas kernels for 19%

profile of v5, /device:TPU:1, one launch (start us, length us, event | category | flops | bytes accessed | tf_op | source)
XLA Modules:
  0.0 73.9 jit_solution(13817511231849368764)
XLA Ops:
  0.0 0.0 copy-start.1
  0.0 0.7 copy-done.1
  0.7 5.9 %sketch.3 = (f32[272,128]{1,0:T(8,128)S(1)}, f32[272,128]{1,0:T(8,128)S(1)}, f32[272,128]{1,0:T(8,128)S(1)}) custom-call(bf16[8192,256]{1,0:T(8,128)(2,1)} %scores_ref.3, s32[8192,256]{1,0:T(8,128)} %targets_ref.3, s32[16,256]{1,0:T(8,128)S(1)} %bitcast.12), custom_call_target="tpu_custom_call" | custom-call | flops 301989888 | bytes 9437184 | tf_op jit(solution)/shard_map/sketch/pallas_call | solution.py:90
  6.6 3.7 %collective-permute-start = (f32[272,128]{1,0:T(8,128)S(1)}, f32[272,128]{1,0:T(8,128)S(1)}, u32[]{:S(2)}, u32[]{:S(2)}) collective-permute-start(f32[272,128]{1,0:T(8,128)S(1)} %get-tuple-element.14), channel_id=1, source_target_pairs={{0,4},{2,6},{4,0},{6,2},{1,5},{3,7},{5,1},{7,3},{8,12},{10,14},{12... | collective-permute-start | bytes 417800 | tf_op jit(solution)/shard_map/ppermute | solution.py:286
  10.2 0.3 collective-permute-start.1
  10.6 0.5 collective-permute-start.2
  11.1 3.2 %sketch.2 = f32[272,128]{1,0:T(8,128)S(1)} custom-call(bf16[8192,256]{1,0:T(8,128)(2,1)} %scores_ref.3, s32[8192,256]{1,0:T(8,128)} %targets_ref.3, s32[16,256]{1,0:T(8,128)S(1)} %bitcast.13), custom_call_target="tpu_custom_call" | custom-call | flops 100663296 | bytes 3145728 | tf_op jit(solution)/shard_map/sketch/pallas_call | solution.py:90
  14.3 0.0 copy-start
  14.3 0.0 copy-start.2
  14.3 0.0 collective-permute-done
  14.3 2.3 %collective-permute-done.1 = f32[272,128]{1,0:T(8,128)S(1)} collective-permute-done((f32[272,128]{1,0:T(8,128)S(1)}, f32[272,128]{1,0:T(8,128)S(1)}, u32[]{:S(2)}, u32[]{:S(2)}) %collective-permute-start.1) | collective-permute-done | bytes 139296 | tf_op jit(solution)/shard_map/ppermute | solution.py:286
  16.6 1.6 %collective-permute-done.2 = f32[272,128]{1,0:T(8,128)S(1)} collective-permute-done((f32[272,128]{1,0:T(8,128)S(1)}, f32[272,128]{1,0:T(8,128)S(1)}, u32[]{:S(2)}, u32[]{:S(2)}) %collective-permute-start.2) | collective-permute-done | bytes 139296 | tf_op jit(solution)/shard_map/ppermute | solution.py:286
  18.3 1.6 %collective-permute-start.5 = (f32[272,128]{1,0:T(8,128)S(1)}, f32[272,128]{1,0:T(8,128)S(1)}, u32[]{:S(2)}, u32[]{:S(2)}) collective-permute-start(f32[272,128]{1,0:T(8,128)S(1)} %add_add_fusion.1), channel_id=1, source_target_pairs={{0,24},{8,16},{16,8},{24,0},{1,25},{9,17},{17,9},{25,1},{2,26},{10... | collective-permute-start | bytes 417800 | tf_op jit(solution)/shard_map/ppermute | solution.py:286
  19.9 0.0 collective-permute-start.4
  19.9 2.3 %collective-permute-start.3 = (f32[272,128]{1,0:T(8,128)S(1)}, f32[272,128]{1,0:T(8,128)S(1)}, u32[]{:S(2)}, u32[]{:S(2)}) collective-permute-start(f32[272,128]{1,0:T(8,128)S(1)} %add_add_fusion.1), channel_id=1, source_target_pairs={{0,16},{8,24},{16,0},{24,8},{1,17},{9,25},{17,1},{25,9},{2,18},{10... | collective-permute-start | bytes 417800 | tf_op jit(solution)/shard_map/ppermute | solution.py:286
  22.2 1.3 %collective-permute-done.5 = f32[272,128]{1,0:T(8,128)S(1)} collective-permute-done((f32[272,128]{1,0:T(8,128)S(1)}, f32[272,128]{1,0:T(8,128)S(1)}, u32[]{:S(2)}, u32[]{:S(2)}) %collective-permute-start.5) | collective-permute-done | bytes 139296 | tf_op jit(solution)/shard_map/ppermute | solution.py:286
  23.5 0.6 collective-permute-done.4
  24.1 3.1 %collective-permute-done.3 = f32[272,128]{1,0:T(8,128)S(1)} collective-permute-done((f32[272,128]{1,0:T(8,128)S(1)}, f32[272,128]{1,0:T(8,128)S(1)}, u32[]{:S(2)}, u32[]{:S(2)}) %collective-permute-start.3) | collective-permute-done | bytes 139296 | tf_op jit(solution)/shard_map/ppermute | solution.py:286
  27.3 6.3 %collective-permute-start.6 = (f32[272,128]{1,0:T(8,128)S(1)}, f32[272,128]{1,0:T(8,128)S(1)}, u32[]{:S(2)}, u32[]{:S(2)}) collective-permute-start(f32[272,128]{1,0:T(8,128)S(1)} %add_add_fusion), channel_id=1, source_target_pairs={{0,1},{1,0},{2,3},{3,2},{4,5},{5,4},{6,7},{7,6},{8,9},{9,8},{10,11... | collective-permute-start | bytes 417800 | tf_op jit(solution)/shard_map/ppermute | solution.py:286
  33.6 2.5 %collective-permute-done.6 = f32[272,128]{1,0:T(8,128)S(1)} collective-permute-done((f32[272,128]{1,0:T(8,128)S(1)}, f32[272,128]{1,0:T(8,128)S(1)}, u32[]{:S(2)}, u32[]{:S(2)}) %collective-permute-start.6) | collective-permute-done | bytes 139296 | tf_op jit(solution)/shard_map/ppermute | solution.py:286
  36.2 1.4 %collective-permute-start.9 = (f32[272,128]{1,0:T(8,128)S(1)}, f32[272,128]{1,0:T(8,128)S(1)}, u32[]{:S(2)}, u32[]{:S(2)}) collective-permute-start(f32[272,128]{1,0:T(8,128)S(1)} %add.27.stats_ref), channel_id=1, source_target_pairs={{0,2},{2,0},{4,6},{6,4},{1,3},{3,1},{5,7},{7,5},{8,10},{10,8},{12,... | collective-permute-start | bytes 417800 | tf_op jit(solution)/shard_map/ppermute | solution.py:286
  37.5 0.0 copy-done
  37.5 0.0 copy-done.2
  37.5 2.7 %block.2.refs_0_ = f32[8,136,256]{2,1,0:T(8,128)S(1)} custom-call(s32[16,8192]{1,0:T(8,128)S(1)} %bitcast.3, f32[272,128]{1,0:T(8,128)S(1)} %add.27.stats_ref, s32[64,128]{1,0:T(8,128)S(1)} %bitcast.14), custom_call_target="tpu_custom_call" | custom-call | flops 5000000000 | bytes 1000000 | tf_op jit(solution)/shard_map/block/pallas_call | solution.py:211
  40.3 3.7 %collective-permute-start.8 = (f32[272,128]{1,0:T(8,128)S(1)}, f32[272,128]{1,0:T(8,128)S(1)}, u32[]{:S(2)}, u32[]{:S(2)}) collective-permute-start(f32[272,128]{1,0:T(8,128)S(1)} %add.27.stats_ref), channel_id=1, source_target_pairs={{0,4},{2,6},{4,0},{6,2},{1,5},{3,7},{5,1},{7,3},{8,12},{10,14},{12... | collective-permute-start | bytes 417800 | tf_op jit(solution)/shard_map/ppermute | solution.py:286
  44.0 0.0 collective-permute-start.7
  44.0 0.0 collective-permute-done.9.stats_ref
  44.0 2.7 %block.3.start_ref = f32[8,136,256]{2,1,0:T(8,128)S(1)} custom-call(s32[16,8192]{1,0:T(8,128)S(1)} %bitcast.4, f32[272,128]{1,0:T(8,128)S(1)} %collective-permute-done.9.stats_ref, s32[64,128]{1,0:T(8,128)S(1)} %bitcast.15, f32[8,136,256]{2,1,0:T(8,128)S(1)} %block.2.refs_0_), custom_call_target="tpu_custom_call" | custom-call | flops 5000000000 | bytes 1000000 | tf_op jit(solution)/shard_map/block/pallas_call | solution.py:211
  46.7 0.0 collective-permute-done.8.refs_1_
  46.7 2.4 %collective-permute-done.7.refs_0_ = f32[272,128]{1,0:T(8,128)S(1)} collective-permute-done((f32[272,128]{1,0:T(8,128)S(1)}, f32[272,128]{1,0:T(8,128)S(1)}, u32[]{:S(2)}, u32[]{:S(2)}) %collective-permute-start.7) | collective-permute-done | bytes 139296 | tf_op jit(solution)/shard_map/ppermute | solution.py:286
  49.1 0.6 weights.1.weights_ref
  49.6 0.8 %other.4 = f32[1,136,256]{2,1,0:T(8,128)S(1)} custom-call(s32[16,8192]{1,0:T(8,128)S(1)} %bitcast.5, f8e4m3fn[288,4096]{1,0:T(32,128)(4,1)S(1)} %weights.1.weights_ref, f32[8,136,256]{2,1,0:T(8,128)S(1)} %block.3.start_ref), custom_call_target="tpu_custom_call" | custom-call | flops 1000 | bytes 1000 | tf_op jit(solution)/shard_map/other/pallas_call | solution.py:230
  50.4 5.8 %collective-permute-start.10 = (f32[1,136,256]{2,1,0:T(8,128)S(1)}, f32[1,136,256]{2,1,0:T(8,128)S(1)}, u32[]{:S(2)}, u32[]{:S(2)}) collective-permute-start(f32[1,136,256]{2,1,0:T(8,128)S(1)} %other.4), channel_id=1, source_target_pairs={{0,32},{32,0},{1,33},{33,1},{2,34},{34,2},{3,35},{35,3},{4,36},{36... | collective-permute-start | bytes 417800 | tf_op jit(solution)/shard_map/ppermute | solution.py:286
  56.2 0.8 %other.3 = f32[1,136,256]{2,1,0:T(8,128)S(1)} custom-call(s32[16,8192]{1,0:T(8,128)S(1)} %bitcast.6, f8e4m3fn[288,4096]{1,0:T(32,128)(4,1)S(1)} %weights.1.weights_ref, f32[8,136,256]{2,1,0:T(8,128)S(1)} %block.3.start_ref), custom_call_target="tpu_custom_call" | custom-call | flops 1000 | bytes 1000 | tf_op jit(solution)/shard_map/other/pallas_call | solution.py:230
  57.0 0.1 collective-permute-start.12
  57.1 0.1 collective-permute-done.10.swapped_ref
  57.2 0.8 %hist.4 = f32[136,256]{1,0:T(8,128)S(1)} custom-call(s32[16,8192]{1,0:T(8,128)S(1)} %bitcast.7, f8e4m3fn[288,4096]{1,0:T(32,128)(4,1)S(1)} %weights.1.weights_ref, f32[8,136,256]{2,1,0:T(8,128)S(1)} %block.3.start_ref, f32[1,136,256]{2,1,0:T(8,128)S(1)} %collective-permute-done.10.swapped_ref), custom_call_target="tpu_custom_call" | custom-call | flops 1000 | bytes 1000 | tf_op jit(solution)/shard_map/hist/pallas_call | solution.py:251
  58.0 1.9 %collective-permute-start.13 = (f32[136,256]{1,0:T(8,128)S(1)}, f32[136,256]{1,0:T(8,128)S(1)}, u32[]{:S(2)}, u32[]{:S(2)}) collective-permute-start(f32[136,256]{1,0:T(8,128)S(1)} %hist.4), channel_id=1, source_target_pairs={{0,64},{64,0},{128,192},{192,128},{1,65},{65,1},{129,193},{193,129... | collective-permute-start | bytes 417800 | tf_op jit(solution)/shard_map/ppermute | solution.py:286
  59.9 1.4 %other.5 = f32[2,136,256]{2,1,0:T(8,128)S(1)} custom-call(s32[16,8192]{1,0:T(8,128)S(1)} %bitcast.8, f8e4m3fn[288,4096]{1,0:T(32,128)(4,1)S(1)} %weights.1.weights_ref, f32[8,136,256]{2,1,0:T(8,128)S(1)} %block.3.start_ref), custom_call_target="tpu_custom_call" | custom-call | flops 2000 | bytes 1000 | tf_op jit(solution)/shard_map/other/pallas_call | solution.py:230
  61.2 0.7 %collective-permute-start.11 = (f32[2,136,256]{2,1,0:T(8,128)S(1)}, f32[2,136,256]{2,1,0:T(8,128)S(1)}, u32[]{:S(2)}, u32[]{:S(2)}) collective-permute-start(f32[2,136,256]{2,1,0:T(8,128)S(1)} %other.5), channel_id=1, source_target_pairs={{0,32},{32,0},{1,33},{33,1},{2,34},{34,2},{3,35},{35,3},{4,36},{36... | collective-permute-start | bytes 835592 | tf_op jit(solution)/shard_map/ppermute | solution.py:286
  62.0 0.0 collective-permute-done.12.swapped_ref
  62.0 1.6 %collective-permute-done.13.refs_0_ = f32[136,256]{1,0:T(8,128)S(1)} collective-permute-done((f32[136,256]{1,0:T(8,128)S(1)}, f32[136,256]{1,0:T(8,128)S(1)}, u32[]{:S(2)}, u32[]{:S(2)}) %collective-permute-start.13) | collective-permute-done | bytes 139296 | tf_op jit(solution)/shard_map/ppermute | solution.py:286
  63.6 0.8 %hist.6 = f32[136,256]{1,0:T(8,128)S(1)} custom-call(s32[16,8192]{1,0:T(8,128)S(1)} %bitcast.9, f8e4m3fn[288,4096]{1,0:T(32,128)(4,1)S(1)} %weights.1.weights_ref, f32[8,136,256]{2,1,0:T(8,128)S(1)} %block.3.start_ref, f32[1,136,256]{2,1,0:T(8,128)S(1)} %collective-permute-done.12.swapped_ref, f32[136,256]{1,0:T(8,128)S(1)} %collective-permute-done.13.refs_0_), custom_call_target="tpu_custom_call" | custom-call | flops 5000000000 | bytes 1000 | tf_op jit(solution)/shard_map/hist/pallas_call | solution.py:251
  64.4 2.0 %collective-permute-start.14 = (f32[136,256]{1,0:T(8,128)S(1)}, f32[136,256]{1,0:T(8,128)S(1)}, u32[]{:S(2)}, u32[]{:S(2)}) collective-permute-start(f32[136,256]{1,0:T(8,128)S(1)} %hist.6), channel_id=1, source_target_pairs={{0,128},{64,192},{128,0},{192,64},{1,129},{65,193},{129,1},{193,65... | collective-permute-start | bytes 417800 | tf_op jit(solution)/shard_map/ppermute | solution.py:286
  66.4 0.0 collective-permute-done.11.swapped_ref
  66.4 0.8 %hist.7 = f32[136,256]{1,0:T(8,128)S(1)} custom-call(s32[16,8192]{1,0:T(8,128)S(1)} %bitcast.10, f8e4m3fn[288,4096]{1,0:T(32,128)(4,1)S(1)} %weights.1.weights_ref, f32[8,136,256]{2,1,0:T(8,128)S(1)} %block.3.start_ref, f32[2,136,256]{2,1,0:T(8,128)S(1)} %collective-permute-done.11.swapped_ref), custom_call_target="tpu_custom_call" | custom-call | flops 1000 | bytes 1000 | tf_op jit(solution)/shard_map/hist/pallas_call | solution.py:251
  67.2 0.8 %collective-permute-start.15 = (f32[136,256]{1,0:T(8,128)S(1)}, f32[136,256]{1,0:T(8,128)S(1)}, u32[]{:S(2)}, u32[]{:S(2)}) collective-permute-start(f32[136,256]{1,0:T(8,128)S(1)} %hist.7), channel_id=1, source_target_pairs={{0,64},{64,0},{128,192},{192,128},{1,65},{65,1},{129,193},{193,129... | collective-permute-start | bytes 417800 | tf_op jit(solution)/shard_map/ppermute | solution.py:286
  67.9 0.8 %hist.5.a_ref = f32[136,256]{1,0:T(8,128)S(1)} custom-call(s32[16,8192]{1,0:T(8,128)S(1)} %bitcast.11, f8e4m3fn[288,4096]{1,0:T(32,128)(4,1)S(1)} %weights.1.weights_ref, f32[8,136,256]{2,1,0:T(8,128)S(1)} %block.3.start_ref, f32[2,136,256]{2,1,0:T(8,128)S(1)} %collective-permute-done.11.swapped_ref), custom_call_target="tpu_custom_call" | custom-call | flops 1000 | bytes 1000 | tf_op jit(solution)/shard_map/hist/pallas_call | solution.py:251
  68.7 3.7 %collective-permute-done.14.b_ref = f32[136,256]{1,0:T(8,128)S(1)} collective-permute-done((f32[136,256]{1,0:T(8,128)S(1)}, f32[136,256]{1,0:T(8,128)S(1)}, u32[]{:S(2)}, u32[]{:S(2)}) %collective-permute-start.14) | collective-permute-done | bytes 139296 | tf_op jit(solution)/shard_map/ppermute | solution.py:286
  72.4 0.7 collective-permute-done.15.c_ref
  73.1 0.8 %finish.1 = f32[32,16,68]{2,1,0:T(8,128)} custom-call(f32[136,256]{1,0:T(8,128)S(1)} %hist.5.a_ref, f32[136,256]{1,0:T(8,128)S(1)} %collective-permute-done.14.b_ref, f32[136,256]{1,0:T(8,128)S(1)} %collective-permute-done.15.c_ref), custom_call_target="tpu_custom_call" | custom-call | tf_op jit(solution)/shard_map/finish/pallas_call | solution.py:277
  (3 shorter events, 0.1 us)
Async XLA Ops:
  0.0 0.7 copy-start.1
  6.6 7.7 %collective-permute-start = (f32[272,128]{1,0:T(8,128)S(1)}, f32[272,128]{1,0:T(8,128)S(1)}, u32[]{:S(2)}, u32[]{:S(2)}) collective-permute-start(f32[272,128]{1,0:T(8,128)S(1)} %get-tuple-element.14), channel_id=1, source_target_pairs={{0,4},{2,6},{4,0},{6,2},{1,5},{3,7},{5,1},{7,3},{8,12},{10,14},{12... | collective-permute-start | bytes 417800 | tf_op jit(solution)/shard_map/ppermute | solution.py:286
  10.2 6.4 %collective-permute-start.1 = (f32[272,128]{1,0:T(8,128)S(1)}, f32[272,128]{1,0:T(8,128)S(1)}, u32[]{:S(2)}, u32[]{:S(2)}) collective-permute-start(f32[272,128]{1,0:T(8,128)S(1)} %get-tuple-element.15), channel_id=1, source_target_pairs={{0,2},{2,0},{4,6},{6,4},{1,3},{3,1},{5,7},{7,5},{8,10},{10,8},{12,... | collective-permute-start | bytes 417800 | tf_op jit(solution)/shard_map/ppermute | solution.py:286
  10.6 7.7 %collective-permute-start.2 = (f32[272,128]{1,0:T(8,128)S(1)}, f32[272,128]{1,0:T(8,128)S(1)}, u32[]{:S(2)}, u32[]{:S(2)}) collective-permute-start(f32[272,128]{1,0:T(8,128)S(1)} %get-tuple-element.16), channel_id=1, source_target_pairs={{0,6},{2,4},{4,2},{6,0},{1,7},{3,5},{5,3},{7,1},{8,14},{10,12},{12... | collective-permute-start | bytes 417800 | tf_op jit(solution)/shard_map/ppermute | solution.py:286
  14.3 23.3 %copy-start = (s32[8192,16]{0,1:T(8,128)S(1)}, s32[8192,16]{0,1:T(8,128)}, u32[]{:S(2)}) copy-start(s32[8192,16]{0,1:T(8,128)} %param.8) | copy-start | bytes 1572868
  14.3 23.3 %copy-start.2 = (s32[8192]{0:T(1024)S(1)}, s32[8192]{0:T(1024)}, u32[]{:S(2)}) copy-start(s32[8192]{0:T(1024)} %param.9) | copy-start | bytes 98308
  18.3 5.2 %collective-permute-start.5 = (f32[272,128]{1,0:T(8,128)S(1)}, f32[272,128]{1,0:T(8,128)S(1)}, u32[]{:S(2)}, u32[]{:S(2)}) collective-permute-start(f32[272,128]{1,0:T(8,128)S(1)} %add_add_fusion.1), channel_id=1, source_target_pairs={{0,24},{8,16},{16,8},{24,0},{1,25},{9,17},{17,9},{25,1},{2,26},{10... | collective-permute-start | bytes 417800 | tf_op jit(solution)/shard_map/ppermute | solution.py:286
  19.9 4.2 %collective-permute-start.4 = (f32[272,128]{1,0:T(8,128)S(1)}, f32[272,128]{1,0:T(8,128)S(1)}, u32[]{:S(2)}, u32[]{:S(2)}) collective-permute-start(f32[272,128]{1,0:T(8,128)S(1)} %add_add_fusion.1), channel_id=1, source_target_pairs={{0,8},{8,0},{16,24},{24,16},{1,9},{9,1},{17,25},{25,17},{2,10},{10... | collective-permute-start | bytes 417800 | tf_op jit(solution)/shard_map/ppermute | solution.py:286
  19.9 7.3 %collective-permute-start.3 = (f32[272,128]{1,0:T(8,128)S(1)}, f32[272,128]{1,0:T(8,128)S(1)}, u32[]{:S(2)}, u32[]{:S(2)}) collective-permute-start(f32[272,128]{1,0:T(8,128)S(1)} %add_add_fusion.1), channel_id=1, source_target_pairs={{0,16},{8,24},{16,0},{24,8},{1,17},{9,25},{17,1},{25,9},{2,18},{10... | collective-permute-start | bytes 417800 | tf_op jit(solution)/shard_map/ppermute | solution.py:286
  27.3 8.9 %collective-permute-start.6 = (f32[272,128]{1,0:T(8,128)S(1)}, f32[272,128]{1,0:T(8,128)S(1)}, u32[]{:S(2)}, u32[]{:S(2)}) collective-permute-start(f32[272,128]{1,0:T(8,128)S(1)} %add_add_fusion), channel_id=1, source_target_pairs={{0,1},{1,0},{2,3},{3,2},{4,5},{5,4},{6,7},{7,6},{8,9},{9,8},{10,11... | collective-permute-start | bytes 417800 | tf_op jit(solution)/shard_map/ppermute | solution.py:286
  36.2 7.8 %collective-permute-start.9 = (f32[272,128]{1,0:T(8,128)S(1)}, f32[272,128]{1,0:T(8,128)S(1)}, u32[]{:S(2)}, u32[]{:S(2)}) collective-permute-start(f32[272,128]{1,0:T(8,128)S(1)} %add.27.stats_ref), channel_id=1, source_target_pairs={{0,2},{2,0},{4,6},{6,4},{1,3},{3,1},{5,7},{7,5},{8,10},{10,8},{12,... | collective-permute-start | bytes 417800 | tf_op jit(solution)/shard_map/ppermute | solution.py:286
  40.3 6.4 %collective-permute-start.8 = (f32[272,128]{1,0:T(8,128)S(1)}, f32[272,128]{1,0:T(8,128)S(1)}, u32[]{:S(2)}, u32[]{:S(2)}) collective-permute-start(f32[272,128]{1,0:T(8,128)S(1)} %add.27.stats_ref), channel_id=1, source_target_pairs={{0,4},{2,6},{4,0},{6,2},{1,5},{3,7},{5,1},{7,3},{8,12},{10,14},{12... | collective-permute-start | bytes 417800 | tf_op jit(solution)/shard_map/ppermute | solution.py:286
  44.0 5.1 %collective-permute-start.7 = (f32[272,128]{1,0:T(8,128)S(1)}, f32[272,128]{1,0:T(8,128)S(1)}, u32[]{:S(2)}, u32[]{:S(2)}) collective-permute-start(f32[272,128]{1,0:T(8,128)S(1)} %add.27.stats_ref), channel_id=1, source_target_pairs={{0,6},{2,4},{4,2},{6,0},{1,7},{3,5},{5,3},{7,1},{8,14},{10,12},{12... | collective-permute-start | bytes 417800 | tf_op jit(solution)/shard_map/ppermute | solution.py:286
  50.4 6.8 %collective-permute-start.10 = (f32[1,136,256]{2,1,0:T(8,128)S(1)}, f32[1,136,256]{2,1,0:T(8,128)S(1)}, u32[]{:S(2)}, u32[]{:S(2)}) collective-permute-start(f32[1,136,256]{2,1,0:T(8,128)S(1)} %other.4), channel_id=1, source_target_pairs={{0,32},{32,0},{1,33},{33,1},{2,34},{34,2},{3,35},{35,3},{4,36},{36... | collective-permute-start | bytes 417800 | tf_op jit(solution)/shard_map/ppermute | solution.py:286
  57.0 5.0 %collective-permute-start.12 = (f32[1,136,256]{2,1,0:T(8,128)S(1)}, f32[1,136,256]{2,1,0:T(8,128)S(1)}, u32[]{:S(2)}, u32[]{:S(2)}) collective-permute-start(f32[1,136,256]{2,1,0:T(8,128)S(1)} %other.3), channel_id=1, source_target_pairs={{0,32},{32,0},{1,33},{33,1},{2,34},{34,2},{3,35},{35,3},{4,36},{36... | collective-permute-start | bytes 417800 | tf_op jit(solution)/shard_map/ppermute | solution.py:286
  58.0 5.6 %collective-permute-start.13 = (f32[136,256]{1,0:T(8,128)S(1)}, f32[136,256]{1,0:T(8,128)S(1)}, u32[]{:S(2)}, u32[]{:S(2)}) collective-permute-start(f32[136,256]{1,0:T(8,128)S(1)} %hist.4), channel_id=1, source_target_pairs={{0,64},{64,0},{128,192},{192,128},{1,65},{65,1},{129,193},{193,129... | collective-permute-start | bytes 417800 | tf_op jit(solution)/shard_map/ppermute | solution.py:286
  61.2 5.2 %collective-permute-start.11 = (f32[2,136,256]{2,1,0:T(8,128)S(1)}, f32[2,136,256]{2,1,0:T(8,128)S(1)}, u32[]{:S(2)}, u32[]{:S(2)}) collective-permute-start(f32[2,136,256]{2,1,0:T(8,128)S(1)} %other.5), channel_id=1, source_target_pairs={{0,32},{32,0},{1,33},{33,1},{2,34},{34,2},{3,35},{35,3},{4,36},{36... | collective-permute-start | bytes 835592 | tf_op jit(solution)/shard_map/ppermute | solution.py:286
  64.4 8.0 %collective-permute-start.14 = (f32[136,256]{1,0:T(8,128)S(1)}, f32[136,256]{1,0:T(8,128)S(1)}, u32[]{:S(2)}, u32[]{:S(2)}) collective-permute-start(f32[136,256]{1,0:T(8,128)S(1)} %hist.6), channel_id=1, source_target_pairs={{0,128},{64,192},{128,0},{192,64},{1,129},{65,193},{129,1},{193,65... | collective-permute-start | bytes 417800 | tf_op jit(solution)/shard_map/ppermute | solution.py:286
  67.2 5.9 %collective-permute-start.15 = (f32[136,256]{1,0:T(8,128)S(1)}, f32[136,256]{1,0:T(8,128)S(1)}, u32[]{:S(2)}, u32[]{:S(2)}) collective-permute-start(f32[136,256]{1,0:T(8,128)S(1)} %hist.7), channel_id=1, source_target_pairs={{0,64},{64,0},{128,192},{192,128},{1,65},{65,1},{129,193},{193,129... | collective-permute-start | bytes 417800 | tf_op jit(solution)/shard_map/ppermute | solution.py:286

commit v6 on v5

--- a/solution.py
+++ b/solution.py
@@ -31,7 +31,7 @@
 HALF = OWN_BINS * FEATS // 2
 PART = (2 * LEAVES * (K + 1), HALF)
 ORDER = tuple((k, own) for k in (3, 2, 1, 0) for own in (False, True))
-OTHER_COST = 1000
+OTHER_COST = 2_000_000_000
 HIST_COST = (1000, 1000, 5_000_000_000, 1000)
 LAST = (3, 2)
 GROUP = 4
@@ -39,7 +39,8 @@
 
 
 def sketch_kernel(ks, scores_ref, targets_ref, signs_ref, *refs):
-    out_refs, (score_buf, target_buf, sems) = refs[: len(ks)], refs[len(ks) :]
+    more_refs, out_refs = refs[: -3 - len(ks)], refs[-3 - len(ks) : -3]
+    score_buf, target_buf, sems = refs[-3:]
     x = lax.axis_index("x").astype(jnp.int32)
 
     def loads(slab):
@@ -81,19 +82,25 @@
         for piece in range(GROUP * QUADS):
             at, lanes = piece % PIECES, slice(piece * LANES, (piece + 1) * LANES)
             out_ref = out_refs[(first * QUADS + piece) // PIECES]
-            out_ref[at * K : (at + 1) * K, :] = stats[:K, lanes] * (1.0 / math.sqrt(L))
-            out_ref[PIECES * K + at : PIECES * K + at + 1, :] = stats[K : K + 1, lanes] * (1.0 / L)
-
-
-def sketch_call(ks, scores, targets, signs_t):
+            rows, row = slice(at * K, (at + 1) * K), slice(PIECES * K + at, PIECES * K + at + 1)
+            sketch = stats[:K, lanes] * (1.0 / math.sqrt(L))
+            curve = stats[K : K + 1, lanes] * (1.0 / L)
+            for more_ref in more_refs:
+                sketch += more_ref[rows, :]
+                curve += more_ref[row, :]
+            out_ref[rows, :] = sketch
+            out_ref[row, :] = curve
+
+
+def sketch_call(ks, scores, targets, signs_t, *more):
     slabs = 4 * len(ks)
     return pl.pallas_call(
         functools.partial(sketch_kernel, ks),
         in_specs=[
             pl.BlockSpec(memory_space=pl.ANY),
             pl.BlockSpec(memory_space=pl.ANY),
-            pl.BlockSpec(memory_space=pltpu.VMEM),
-        ],
+        ]
+        + [pl.BlockSpec(memory_space=pltpu.VMEM)] * (1 + len(more)),
         out_specs=[pl.BlockSpec(memory_space=pltpu.VMEM)] * len(ks),
         out_shape=[jax.ShapeDtypeStruct((STAT_ROWS, LANES), jnp.float32)] * len(ks),
         scratch_shapes=[
@@ -108,7 +115,7 @@
             transcendentals=slabs * SLAB * LABS,
         ),
         name="sketch",
-    )(scores, targets, signs_t)
+    )(scores, targets, signs_t, *more)
 
 
 def split_terms(values, scales):
@@ -259,8 +266,8 @@
     )(bins_t, weights, start, swapped, *more)
 
 
-def finish_kernel(a_ref, b_ref, c_ref, out_ref):
-    total = a_ref[...] + (b_ref[...] + c_ref[...])
+def finish_kernel(a_ref, b_ref, out_ref):
+    total = a_ref[...] + b_ref[...]
     for half in range(2):
         rows = []
         for e in range(LEAVES):
@@ -291,33 +298,34 @@
     bins_t = bins.T
     leaves2 = leaves.reshape(ROWS // LANES, LANES)
 
-    arrived = [
-        swap(part, "x", k, 4) for k, part in zip((2, 1, 3), sketch_call((2, 1, 3), scores, targets, signs_t))
-    ]
-    (mine,) = sketch_call((0,), scores, targets, signs_t)
-    mine = (mine + arrived[0]) + (arrived[1] + arrived[2])
+    (part,) = sketch_call((2,), scores, targets, signs_t)
+    part, signs_t = lax.optimization_barrier((part, signs_t))
+    first = swap(part, "x", 2, 4)
+    parts = sketch_call((1, 3), scores, targets, signs_t)
+    arrived = [swap(part, "x", k, 4) for k, part in zip((1, 3), parts)]
+    (mine,) = sketch_call((0,), scores, targets, signs_t, first)
+    mine = mine + (arrived[0] + arrived[1])
     arrived = [swap(mine, "y", k, 4) for k in (2, 1, 3)]
     mine = (mine + arrived[0]) + (arrived[1] + arrived[2])
     mine = mine + swap(mine, "zh", 1, 2)
     first = swap(mine, "x", 1, 4)
+    last = [swap(mine, "x", k, 4) for k in LAST]
     start = block_call(0, bins_t, mine, leaves2)
-    mine, start = lax.optimization_barrier((mine, start))
-    last = [swap(mine, "x", k, 4) for k in LAST]
     start = block_call(1, bins_t, first, leaves2, start)
     weights = weight_call(LAST, last, leaves2)
 
     far = swap(other_call((3,), bins_t, weights, start), "c", 1, 2)
-    mid = other_call((2,), bins_t, weights, start)
+    mid = other_call((2, 1), bins_t, weights, start)
     mid, start = lax.optimization_barrier((mid, start))
     mid = swap(mid, "c", 1, 2)
     part = hist_call(3, bins_t, weights, start, far, 0)
     part, start = lax.optimization_barrier((part, start))
     passed = swap(part, "zl", 1, 4)
-    near = swap(other_call((1, 0), bins_t, weights, start), "c", 1, 2)
-    moved1 = swap(hist_call(1, bins_t, weights, start, near, 0), "zl", 1, 4)
+    near = swap(other_call((0,), bins_t, weights, start), "c", 1, 2)
+    moved1 = swap(hist_call(1, bins_t, weights, start, mid, 1), "zl", 1, 4)
     moved2 = swap(hist_call(2, bins_t, weights, start, mid, 0, passed), "zl", 2, 4)
-    part = hist_call(0, bins_t, weights, start, near, 1)
-    return finish_call((part, moved2, moved1))
+    part = hist_call(0, bins_t, weights, start, near, 0, moved1)
+    return finish_call((part, moved2))
 
 
 def solution(mesh):

time: 74.6 us -> 69.2 us (0.928)
  the two profiles are of different devices: /device:TPU:1 before, /device:TPU:2 now
where the time goes in v6:
time: 69.2 us; the launch traced here: 69 us
  starting transfers between devices  26.1 us (38%)
  Pallas kernels  23.7 us (34%)
  waiting for transfers between devices  18.3 us (26%)
  local copies, waits for them, and re-layouts  0.73 us (1%)
    ppermute x16, starting transfers between devices, swap(): return lax.ppermute(value, axis, [(i, i ^ bit) for i in range(size)])  26.1 us
    ppermute x16, waiting for transfers between devices, swap(): return lax.ppermute(value, axis, [(i, i ^ bit) for i in range(size)])  18.3 us
    pallas_call x3, Pallas kernels, sketch_call(): pl.pallas_call(functools.partial(sketch_kernel, ks), in_specs=[pl.BlockSp...  10.8 us
    pallas_call x2, Pallas kernels, block_call(): pl.pallas_call(functools.partial(block_kernel, k), in_specs=[pl.BlockSpec...  5.44 us
    pallas_call x4, Pallas kernels, hist_call(): pl.pallas_call(functools.partial(hist_kernel, k, place), in_specs=[pl.Blo...  3.09 us
    pallas_call x3, Pallas kernels, other_call(): pl.pallas_call(functools.partial(other_kernel, ks), in_specs=[pl.BlockSpe...  2.94 us
  transfers between devices with their start and end apart: 16, of which 7 were waited for; matrix products, arithmetic and copies ran while one was open for 0% of the time, Pallas kernels for 27%

profile of v6, /device:TPU:2, one launch (start us, length us, event | category | flops | bytes accessed | tf_op | source)
XLA Modules:
  0.0 69.0 jit_solution(1886007547071841243)
XLA Ops:
  0.0 0.0 copy-start.1
  0.0 0.7 %copy-done.1 = s32[256,16]{0,1:T(8,128)S(1)} copy-done((s32[256,16]{0,1:T(8,128)S(1)}, s32[256,16]{0,1:T(8,128)}, u32[]{:S(2)}) %copy-start.1) | copy-done | bytes 16408
  0.7 3.2 %sketch.3 = f32[272,128]{1,0:T(8,128)S(1)} custom-call(bf16[8192,256]{1,0:T(8,128)(2,1)} %scores_ref.5, s32[8192,256]{1,0:T(8,128)} %targets_ref.5, s32[16,256]{1,0:T(8,128)S(1)} %bitcast.12), custom_call_target="tpu_custom_call" | custom-call | flops 100663296 | bytes 3145728 | tf_op jit(solution)/shard_map/sketch/pallas_call | solution.py:97
  3.9 2.2 %collective-permute-start = (f32[272,128]{1,0:T(8,128)S(1)}, f32[272,128]{1,0:T(8,128)S(1)}, u32[]{:S(2)}, u32[]{:S(2)}) collective-permute-start(f32[272,128]{1,0:T(8,128)S(1)} %sketch.3), channel_id=1, source_target_pairs={{0,4},{2,6},{4,0},{6,2},{1,5},{3,7},{5,1},{7,3},{8,12},{10,14},{12... | collective-permute-start | bytes 417800 | tf_op jit(solution)/shard_map/ppermute | solution.py:293
  6.1 4.5 %sketch.5 = (f32[272,128]{1,0:T(8,128)S(1)}, f32[272,128]{1,0:T(8,128)S(1)}) custom-call(bf16[8192,256]{1,0:T(8,128)(2,1)} %scores_ref.5, s32[8192,256]{1,0:T(8,128)} %targets_ref.5, s32[16,256]{1,0:T(8,128)S(1)} %bitcast.13), custom_call_target="tpu_custom_call" | custom-call | flops 201326592 | bytes 6291456 | tf_op jit(solution)/shard_map/sketch/pallas_call | solution.py:97
  10.6 1.5 %collective-permute-start.1 = (f32[272,128]{1,0:T(8,128)S(1)}, f32[272,128]{1,0:T(8,128)S(1)}, u32[]{:S(2)}, u32[]{:S(2)}) collective-permute-start(f32[272,128]{1,0:T(8,128)S(1)} %get-tuple-element.15), channel_id=1, source_target_pairs={{0,2},{2,0},{4,6},{6,4},{1,3},{3,1},{5,7},{7,5},{8,10},{10,8},{12,... | collective-permute-start | bytes 417800 | tf_op jit(solution)/shard_map/ppermute | solution.py:293
  12.1 0.5 collective-permute-start.2
  12.7 0.0 collective-permute-done.refs_0_
  12.7 3.2 %sketch.4 = f32[272,128]{1,0:T(8,128)S(1)} custom-call(bf16[8192,256]{1,0:T(8,128)(2,1)} %scores_ref.5, s32[8192,256]{1,0:T(8,128)} %targets_ref.5, s32[16,256]{1,0:T(8,128)S(1)} %bitcast.14, f32[272,128]{1,0:T(8,128)S(1)} %collective-permute-done.refs_0_), custom_call_target="tpu_custom_call" | custom-call | flops 100663296 | bytes 3145728 | tf_op jit(solution)/shard_map/sketch/pallas_call | solution.py:97
  15.8 0.0 copy-start
  15.9 0.0 copy-start.2
  15.9 0.0 collective-permute-done.1
  15.9 1.3 %collective-permute-done.2 = f32[272,128]{1,0:T(8,128)S(1)} collective-permute-done((f32[272,128]{1,0:T(8,128)S(1)}, f32[272,128]{1,0:T(8,128)S(1)}, u32[]{:S(2)}, u32[]{:S(2)}) %collective-permute-start.2) | collective-permute-done | bytes 139296 | tf_op jit(solution)/shard_map/ppermute | solution.py:293
  17.2 3.3 %collective-permute-start.3 = (f32[272,128]{1,0:T(8,128)S(1)}, f32[272,128]{1,0:T(8,128)S(1)}, u32[]{:S(2)}, u32[]{:S(2)}) collective-permute-start(f32[272,128]{1,0:T(8,128)S(1)} %add_add_fusion.1), channel_id=1, source_target_pairs={{0,16},{8,24},{16,0},{24,8},{1,17},{9,25},{17,1},{25,9},{2,18},{10... | collective-permute-start | bytes 417800 | tf_op jit(solution)/shard_map/ppermute | solution.py:293
  20.5 0.7 collective-permute-start.4
  21.2 0.4 collective-permute-start.5
  21.6 3.3 %collective-permute-done.3 = f32[272,128]{1,0:T(8,128)S(1)} collective-permute-done((f32[272,128]{1,0:T(8,128)S(1)}, f32[272,128]{1,0:T(8,128)S(1)}, u32[]{:S(2)}, u32[]{:S(2)}) %collective-permute-start.3) | collective-permute-done | bytes 139296 | tf_op jit(solution)/shard_map/ppermute | solution.py:293
  24.8 1.3 %collective-permute-done.4 = f32[272,128]{1,0:T(8,128)S(1)} collective-permute-done((f32[272,128]{1,0:T(8,128)S(1)}, f32[272,128]{1,0:T(8,128)S(1)}, u32[]{:S(2)}, u32[]{:S(2)}) %collective-permute-start.4) | collective-permute-done | bytes 139296 | tf_op jit(solution)/shard_map/ppermute | solution.py:293
  26.1 1.3 %collective-permute-done.5 = f32[272,128]{1,0:T(8,128)S(1)} collective-permute-done((f32[272,128]{1,0:T(8,128)S(1)}, f32[272,128]{1,0:T(8,128)S(1)}, u32[]{:S(2)}, u32[]{:S(2)}) %collective-permute-start.5) | collective-permute-done | bytes 139296 | tf_op jit(solution)/shard_map/ppermute | solution.py:293
  27.5 7.3 %collective-permute-start.6 = (f32[272,128]{1,0:T(8,128)S(1)}, f32[272,128]{1,0:T(8,128)S(1)}, u32[]{:S(2)}, u32[]{:S(2)}) collective-permute-start(f32[272,128]{1,0:T(8,128)S(1)} %add_add_fusion), channel_id=1, source_target_pairs={{0,1},{1,0},{2,3},{3,2},{4,5},{5,4},{6,7},{7,6},{8,9},{9,8},{10,11... | collective-permute-start | bytes 417800 | tf_op jit(solution)/shard_map/ppermute | solution.py:293
  34.8 3.6 %collective-permute-done.6 = f32[272,128]{1,0:T(8,128)S(1)} collective-permute-done((f32[272,128]{1,0:T(8,128)S(1)}, f32[272,128]{1,0:T(8,128)S(1)}, u32[]{:S(2)}, u32[]{:S(2)}) %collective-permute-start.6) | collective-permute-done | bytes 139296 | tf_op jit(solution)/shard_map/ppermute | solution.py:293
  38.4 2.4 %collective-permute-start.9 = (f32[272,128]{1,0:T(8,128)S(1)}, f32[272,128]{1,0:T(8,128)S(1)}, u32[]{:S(2)}, u32[]{:S(2)}) collective-permute-start(f32[272,128]{1,0:T(8,128)S(1)} %add.23.stats_ref), channel_id=1, source_target_pairs={{0,2},{2,0},{4,6},{6,4},{1,3},{3,1},{5,7},{7,5},{8,10},{10,8},{12,... | collective-permute-start | bytes 417800 | tf_op jit(solution)/shard_map/ppermute | solution.py:293
  40.8 0.0 collective-permute-start.7
  40.8 2.2 %collective-permute-start.8 = (f32[272,128]{1,0:T(8,128)S(1)}, f32[272,128]{1,0:T(8,128)S(1)}, u32[]{:S(2)}, u32[]{:S(2)}) collective-permute-start(f32[272,128]{1,0:T(8,128)S(1)} %add.23.stats_ref), channel_id=1, source_target_pairs={{0,4},{2,6},{4,0},{6,2},{1,5},{3,7},{5,1},{7,3},{8,12},{10,14},{12... | collective-permute-start | bytes 417800 | tf_op jit(solution)/shard_map/ppermute | solution.py:293
  43.0 0.0 copy-done
  43.0 0.0 copy-done.2
  43.0 2.7 %block.2.refs_0_ = f32[8,136,256]{2,1,0:T(8,128)S(1)} custom-call(s32[16,8192]{1,0:T(8,128)S(1)} %bitcast.3, f32[272,128]{1,0:T(8,128)S(1)} %add.23.stats_ref, s32[64,128]{1,0:T(8,128)S(1)} %bitcast.15), custom_call_target="tpu_custom_call" | custom-call | flops 5000000000 | bytes 1000000 | tf_op jit(solution)/shard_map/block/pallas_call | solution.py:218
  45.7 0.0 collective-permute-done.9.stats_ref
  45.7 2.7 %block.3.start_ref = f32[8,136,256]{2,1,0:T(8,128)S(1)} custom-call(s32[16,8192]{1,0:T(8,128)S(1)} %bitcast.4, f32[272,128]{1,0:T(8,128)S(1)} %collective-permute-done.9.stats_ref, s32[64,128]{1,0:T(8,128)S(1)} %bitcast.16, f32[8,136,256]{2,1,0:T(8,128)S(1)} %block.2.refs_0_), custom_call_target="tpu_custom_call" | custom-call | flops 5000000000 | bytes 1000000 | tf_op jit(solution)/shard_map/block/pallas_call | solution.py:218
  48.5 0.0 collective-permute-done.7.refs_0_
  48.5 0.0 collective-permute-done.8.refs_1_
  48.5 0.6 weights.1.weights_ref
  49.1 0.8 %other.4 = f32[1,136,256]{2,1,0:T(8,128)S(1)} custom-call(s32[16,8192]{1,0:T(8,128)S(1)} %bitcast.5, f8e4m3fn[288,4096]{1,0:T(32,128)(4,1)S(1)} %weights.1.weights_ref, f32[8,136,256]{2,1,0:T(8,128)S(1)} %block.3.start_ref), custom_call_target="tpu_custom_call" | custom-call | flops 2000000000 | bytes 1000 | tf_op jit(solution)/shard_map/other/pallas_call | solution.py:237
  49.9 0.1 collective-permute-start.10
  50.0 1.4 %other.3 = f32[2,136,256]{2,1,0:T(8,128)S(1)} custom-call(s32[16,8192]{1,0:T(8,128)S(1)} %bitcast.6, f8e4m3fn[288,4096]{1,0:T(32,128)(4,1)S(1)} %weights.1.weights_ref, f32[8,136,256]{2,1,0:T(8,128)S(1)} %block.3.start_ref), custom_call_target="tpu_custom_call" | custom-call | flops 4000000000 | bytes 1000 | tf_op jit(solution)/shard_map/other/pallas_call | solution.py:237
  51.4 0.6 collective-permute-start.12
  51.9 0.0 collective-permute-done.10.swapped_ref
  51.9 0.8 %hist.4 = f32[136,256]{1,0:T(8,128)S(1)} custom-call(s32[16,8192]{1,0:T(8,128)S(1)} %bitcast.7, f8e4m3fn[288,4096]{1,0:T(32,128)(4,1)S(1)} %weights.1.weights_ref, f32[8,136,256]{2,1,0:T(8,128)S(1)} %block.3.start_ref, f32[1,136,256]{2,1,0:T(8,128)S(1)} %collective-permute-done.10.swapped_ref), custom_call_target="tpu_custom_call" | custom-call | flops 1000 | bytes 1000 | tf_op jit(solution)/shard_map/hist/pallas_call | solution.py:258
  52.7 1.0 %collective-permute-start.14 = (f32[136,256]{1,0:T(8,128)S(1)}, f32[136,256]{1,0:T(8,128)S(1)}, u32[]{:S(2)}, u32[]{:S(2)}) collective-permute-start(f32[136,256]{1,0:T(8,128)S(1)} %hist.4), channel_id=1, source_target_pairs={{0,64},{64,0},{128,192},{192,128},{1,65},{65,1},{129,193},{193,129... | collective-permute-start | bytes 417800 | tf_op jit(solution)/shard_map/ppermute | solution.py:293
  53.7 0.8 %other.5 = f32[1,136,256]{2,1,0:T(8,128)S(1)} custom-call(s32[16,8192]{1,0:T(8,128)S(1)} %bitcast.8, f8e4m3fn[288,4096]{1,0:T(32,128)(4,1)S(1)} %weights.1.weights_ref, f32[8,136,256]{2,1,0:T(8,128)S(1)} %block.3.start_ref), custom_call_target="tpu_custom_call" | custom-call | flops 2000000000 | bytes 1000 | tf_op jit(solution)/shard_map/other/pallas_call | solution.py:237
  54.5 0.1 collective-permute-start.11
  54.6 0.0 collective-permute-done.12.swapped_ref
  54.6 0.8 %hist.5 = f32[136,256]{1,0:T(8,128)S(1)} custom-call(s32[16,8192]{1,0:T(8,128)S(1)} %bitcast.9, f8e4m3fn[288,4096]{1,0:T(32,128)(4,1)S(1)} %weights.1.weights_ref, f32[8,136,256]{2,1,0:T(8,128)S(1)} %block.3.start_ref, f32[2,136,256]{2,1,0:T(8,128)S(1)} %collective-permute-done.12.swapped_ref), custom_call_target="tpu_custom_call" | custom-call | flops 1000 | bytes 1000 | tf_op jit(solution)/shard_map/hist/pallas_call | solution.py:258
  55.4 1.2 %collective-permute-start.13 = (f32[136,256]{1,0:T(8,128)S(1)}, f32[136,256]{1,0:T(8,128)S(1)}, u32[]{:S(2)}, u32[]{:S(2)}) collective-permute-start(f32[136,256]{1,0:T(8,128)S(1)} %hist.5), channel_id=1, source_target_pairs={{0,64},{64,0},{128,192},{192,128},{1,65},{65,1},{129,193},{193,129... | collective-permute-start | bytes 417800 | tf_op jit(solution)/shard_map/ppermute | solution.py:293
  56.6 1.8 %collective-permute-done.14.refs_0_ = f32[136,256]{1,0:T(8,128)S(1)} collective-permute-done((f32[136,256]{1,0:T(8,128)S(1)}, f32[136,256]{1,0:T(8,128)S(1)}, u32[]{:S(2)}, u32[]{:S(2)}) %collective-permute-start.14) | collective-permute-done | bytes 139296 | tf_op jit(solution)/shard_map/ppermute | solution.py:293
  58.4 0.8 %hist.7 = f32[136,256]{1,0:T(8,128)S(1)} custom-call(s32[16,8192]{1,0:T(8,128)S(1)} %bitcast.10, f8e4m3fn[288,4096]{1,0:T(32,128)(4,1)S(1)} %weights.1.weights_ref, f32[8,136,256]{2,1,0:T(8,128)S(1)} %block.3.start_ref, f32[2,136,256]{2,1,0:T(8,128)S(1)} %collective-permute-done.12.swapped_ref, f32[136,256]{1,0:T(8,128)S(1)} %collective-permute-done.14.refs_0_), custom_call_target="tpu_custom_call" | custom-call | flops 5000000000 | bytes 1000 | tf_op jit(solution)/shard_map/hist/pallas_call | solution.py:258
  59.2 2.7 %collective-permute-start.15 = (f32[136,256]{1,0:T(8,128)S(1)}, f32[136,256]{1,0:T(8,128)S(1)}, u32[]{:S(2)}, u32[]{:S(2)}) collective-permute-start(f32[136,256]{1,0:T(8,128)S(1)} %hist.7), channel_id=1, source_target_pairs={{0,128},{64,192},{128,0},{192,64},{1,129},{65,193},{129,1},{193,65... | collective-permute-start | bytes 417800 | tf_op jit(solution)/shard_map/ppermute | solution.py:293
  61.8 0.0 collective-permute-done.11.swapped_ref
  61.8 0.0 collective-permute-done.13.refs_0_
  61.9 0.8 %hist.6.a_ref = f32[136,256]{1,0:T(8,128)S(1)} custom-call(s32[16,8192]{1,0:T(8,128)S(1)} %bitcast.11, f8e4m3fn[288,4096]{1,0:T(32,128)(4,1)S(1)} %weights.1.weights_ref, f32[8,136,256]{2,1,0:T(8,128)S(1)} %block.3.start_ref, f32[1,136,256]{2,1,0:T(8,128)S(1)} %collective-permute-done.11.swapped_ref, f32[136,256]{1,0:T(8,128)S(1)} %collective-permute-done.13.refs_0_), custom_call_target="tpu_custom_call" | custom-call | flops 1000 | bytes 1000 | tf_op jit(solution)/shard_map/hist/pallas_call | solution.py:258
  62.6 5.6 %collective-permute-done.15.b_ref = f32[136,256]{1,0:T(8,128)S(1)} collective-permute-done((f32[136,256]{1,0:T(8,128)S(1)}, f32[136,256]{1,0:T(8,128)S(1)}, u32[]{:S(2)}, u32[]{:S(2)}) %collective-permute-start.15) | collective-permute-done | bytes 139296 | tf_op jit(solution)/shard_map/ppermute | solution.py:293
  68.2 0.8 %finish.1 = f32[32,16,68]{2,1,0:T(8,128)} custom-call(f32[136,256]{1,0:T(8,128)S(1)} %hist.6.a_ref, f32[136,256]{1,0:T(8,128)S(1)} %collective-permute-done.15.b_ref), custom_call_target="tpu_custom_call" | custom-call | tf_op jit(solution)/shard_map/finish/pallas_call | solution.py:284
  (3 shorter events, 0.1 us)
Async XLA Ops:
  0.0 0.7 %copy-start.1 = (s32[256,16]{0,1:T(8,128)S(1)}, s32[256,16]{0,1:T(8,128)}, u32[]{:S(2)}) copy-start(s32[256,16]{0,1:T(8,128)} %param.7) | copy-start | bytes 49156
  3.9 8.8 %collective-permute-start = (f32[272,128]{1,0:T(8,128)S(1)}, f32[272,128]{1,0:T(8,128)S(1)}, u32[]{:S(2)}, u32[]{:S(2)}) collective-permute-start(f32[272,128]{1,0:T(8,128)S(1)} %sketch.3), channel_id=1, source_target_pairs={{0,4},{2,6},{4,0},{6,2},{1,5},{3,7},{5,1},{7,3},{8,12},{10,14},{12... | collective-permute-start | bytes 417800 | tf_op jit(solution)/shard_map/ppermute | solution.py:293
  10.6 5.3 %collective-permute-start.1 = (f32[272,128]{1,0:T(8,128)S(1)}, f32[272,128]{1,0:T(8,128)S(1)}, u32[]{:S(2)}, u32[]{:S(2)}) collective-permute-start(f32[272,128]{1,0:T(8,128)S(1)} %get-tuple-element.15), channel_id=1, source_target_pairs={{0,2},{2,0},{4,6},{6,4},{1,3},{3,1},{5,7},{7,5},{8,10},{10,8},{12,... | collective-permute-start | bytes 417800 | tf_op jit(solution)/shard_map/ppermute | solution.py:293
  12.1 5.1 %collective-permute-start.2 = (f32[272,128]{1,0:T(8,128)S(1)}, f32[272,128]{1,0:T(8,128)S(1)}, u32[]{:S(2)}, u32[]{:S(2)}) collective-permute-start(f32[272,128]{1,0:T(8,128)S(1)} %get-tuple-element.16), channel_id=1, source_target_pairs={{0,6},{2,4},{4,2},{6,0},{1,7},{3,5},{5,3},{7,1},{8,14},{10,12},{12... | collective-permute-start | bytes 417800 | tf_op jit(solution)/shard_map/ppermute | solution.py:293
  15.8 27.2 %copy-start = (s32[8192,16]{0,1:T(8,128)S(1)}, s32[8192,16]{0,1:T(8,128)}, u32[]{:S(2)}) copy-start(s32[8192,16]{0,1:T(8,128)} %param.8) | copy-start | bytes 1572868
  15.9 27.2 %copy-start.2 = (s32[8192]{0:T(1024)S(1)}, s32[8192]{0:T(1024)}, u32[]{:S(2)}) copy-start(s32[8192]{0:T(1024)} %param.9) | copy-start | bytes 98308
  17.2 7.6 %collective-permute-start.3 = (f32[272,128]{1,0:T(8,128)S(1)}, f32[272,128]{1,0:T(8,128)S(1)}, u32[]{:S(2)}, u32[]{:S(2)}) collective-permute-start(f32[272,128]{1,0:T(8,128)S(1)} %add_add_fusion.1), channel_id=1, source_target_pairs={{0,16},{8,24},{16,0},{24,8},{1,17},{9,25},{17,1},{25,9},{2,18},{10... | collective-permute-start | bytes 417800 | tf_op jit(solution)/shard_map/ppermute | solution.py:293
  20.5 5.6 %collective-permute-start.4 = (f32[272,128]{1,0:T(8,128)S(1)}, f32[272,128]{1,0:T(8,128)S(1)}, u32[]{:S(2)}, u32[]{:S(2)}) collective-permute-start(f32[272,128]{1,0:T(8,128)S(1)} %add_add_fusion.1), channel_id=1, source_target_pairs={{0,8},{8,0},{16,24},{24,16},{1,9},{9,1},{17,25},{25,17},{2,10},{10... | collective-permute-start | bytes 417800 | tf_op jit(solution)/shard_map/ppermute | solution.py:293
  21.2 6.3 %collective-permute-start.5 = (f32[272,128]{1,0:T(8,128)S(1)}, f32[272,128]{1,0:T(8,128)S(1)}, u32[]{:S(2)}, u32[]{:S(2)}) collective-permute-start(f32[272,128]{1,0:T(8,128)S(1)} %add_add_fusion.1), channel_id=1, source_target_pairs={{0,24},{8,16},{16,8},{24,0},{1,25},{9,17},{17,9},{25,1},{2,26},{10... | collective-permute-start | bytes 417800 | tf_op jit(solution)/shard_map/ppermute | solution.py:293
  27.5 10.9 %collective-permute-start.6 = (f32[272,128]{1,0:T(8,128)S(1)}, f32[272,128]{1,0:T(8,128)S(1)}, u32[]{:S(2)}, u32[]{:S(2)}) collective-permute-start(f32[272,128]{1,0:T(8,128)S(1)} %add_add_fusion), channel_id=1, source_target_pairs={{0,1},{1,0},{2,3},{3,2},{4,5},{5,4},{6,7},{7,6},{8,9},{9,8},{10,11... | collective-permute-start | bytes 417800 | tf_op jit(solution)/shard_map/ppermute | solution.py:293
  38.4 7.3 %collective-permute-start.9 = (f32[272,128]{1,0:T(8,128)S(1)}, f32[272,128]{1,0:T(8,128)S(1)}, u32[]{:S(2)}, u32[]{:S(2)}) collective-permute-start(f32[272,128]{1,0:T(8,128)S(1)} %add.23.stats_ref), channel_id=1, source_target_pairs={{0,2},{2,0},{4,6},{6,4},{1,3},{3,1},{5,7},{7,5},{8,10},{10,8},{12,... | collective-permute-start | bytes 417800 | tf_op jit(solution)/shard_map/ppermute | solution.py:293
  40.8 7.6 %collective-permute-start.7 = (f32[272,128]{1,0:T(8,128)S(1)}, f32[272,128]{1,0:T(8,128)S(1)}, u32[]{:S(2)}, u32[]{:S(2)}) collective-permute-start(f32[272,128]{1,0:T(8,128)S(1)} %add.23.stats_ref), channel_id=1, source_target_pairs={{0,6},{2,4},{4,2},{6,0},{1,7},{3,5},{5,3},{7,1},{8,14},{10,12},{12... | collective-permute-start | bytes 417800 | tf_op jit(solution)/shard_map/ppermute | solution.py:293
  40.8 7.6 %collective-permute-start.8 = (f32[272,128]{1,0:T(8,128)S(1)}, f32[272,128]{1,0:T(8,128)S(1)}, u32[]{:S(2)}, u32[]{:S(2)}) collective-permute-start(f32[272,128]{1,0:T(8,128)S(1)} %add.23.stats_ref), channel_id=1, source_target_pairs={{0,4},{2,6},{4,0},{6,2},{1,5},{3,7},{5,1},{7,3},{8,12},{10,14},{12... | collective-permute-start | bytes 417800 | tf_op jit(solution)/shard_map/ppermute | solution.py:293
  49.9 2.1 %collective-permute-start.10 = (f32[1,136,256]{2,1,0:T(8,128)S(1)}, f32[1,136,256]{2,1,0:T(8,128)S(1)}, u32[]{:S(2)}, u32[]{:S(2)}) collective-permute-start(f32[1,136,256]{2,1,0:T(8,128)S(1)} %other.4), channel_id=1, source_target_pairs={{0,32},{32,0},{1,33},{33,1},{2,34},{34,2},{3,35},{35,3},{4,36},{36... | collective-permute-start | bytes 417800 | tf_op jit(solution)/shard_map/ppermute | solution.py:293
  51.4 3.2 %collective-permute-start.12 = (f32[2,136,256]{2,1,0:T(8,128)S(1)}, f32[2,136,256]{2,1,0:T(8,128)S(1)}, u32[]{:S(2)}, u32[]{:S(2)}) collective-permute-start(f32[2,136,256]{2,1,0:T(8,128)S(1)} %other.3), channel_id=1, source_target_pairs={{0,32},{32,0},{1,33},{33,1},{2,34},{34,2},{3,35},{35,3},{4,36},{36... | collective-permute-start | bytes 835592 | tf_op jit(solution)/shard_map/ppermute | solution.py:293
  52.7 5.7 %collective-permute-start.14 = (f32[136,256]{1,0:T(8,128)S(1)}, f32[136,256]{1,0:T(8,128)S(1)}, u32[]{:S(2)}, u32[]{:S(2)}) collective-permute-start(f32[136,256]{1,0:T(8,128)S(1)} %hist.4), channel_id=1, source_target_pairs={{0,64},{64,0},{128,192},{192,128},{1,65},{65,1},{129,193},{193,129... | collective-permute-start | bytes 417800 | tf_op jit(solution)/shard_map/ppermute | solution.py:293
  54.5 7.4 %collective-permute-start.11 = (f32[1,136,256]{2,1,0:T(8,128)S(1)}, f32[1,136,256]{2,1,0:T(8,128)S(1)}, u32[]{:S(2)}, u32[]{:S(2)}) collective-permute-start(f32[1,136,256]{2,1,0:T(8,128)S(1)} %other.5), channel_id=1, source_target_pairs={{0,32},{32,0},{1,33},{33,1},{2,34},{34,2},{3,35},{35,3},{4,36},{36... | collective-permute-start | bytes 417800 | tf_op jit(solution)/shard_map/ppermute | solution.py:293
  55.4 6.5 %collective-permute-start.13 = (f32[136,256]{1,0:T(8,128)S(1)}, f32[136,256]{1,0:T(8,128)S(1)}, u32[]{:S(2)}, u32[]{:S(2)}) collective-permute-start(f32[136,256]{1,0:T(8,128)S(1)} %hist.5), channel_id=1, source_target_pairs={{0,64},{64,0},{128,192},{192,128},{1,65},{65,1},{129,193},{193,129... | collective-permute-start | bytes 417800 | tf_op jit(solution)/shard_map/ppermute | solution.py:293
  59.2 9.0 %collective-permute-start.15 = (f32[136,256]{1,0:T(8,128)S(1)}, f32[136,256]{1,0:T(8,128)S(1)}, u32[]{:S(2)}, u32[]{:S(2)}) collective-permute-start(f32[136,256]{1,0:T(8,128)S(1)} %hist.7), channel_id=1, source_target_pairs={{0,128},{64,192},{128,0},{192,64},{1,129},{65,193},{129,1},{193,65... | collective-permute-start | bytes 417800 | tf_op jit(solution)/shard_map/ppermute | solution.py:293

commit v7 on v6

--- a/solution.py
+++ b/solution.py
@@ -30,9 +30,9 @@
 CHUNK = 4 * SLAB
 HALF = OWN_BINS * FEATS // 2
 PART = (2 * LEAVES * (K + 1), HALF)
-ORDER = tuple((k, own) for k in (3, 2, 1, 0) for own in (False, True))
-OTHER_COST = 2_000_000_000
-HIST_COST = (1000, 1000, 5_000_000_000, 1000)
+EARLY = ((3, False), (3, True), (2, False), (2, True))
+MID_COST = 5_000_000_000
+COST = 2_000_000_000
 LAST = (3, 2)
 GROUP = 4
 SKETCH_VMEM = 51 << 20
@@ -177,7 +177,10 @@
     onehot = jnp.concatenate(
         [jnp.where(pair == jnp.int8(b), one, zero) for b in range(0, OWN_BINS, 2)], axis=0
     )
-    total = lax.dot_general(weights, onehot, NT, preferred_element_type=jnp.float32)
+    return lax.dot_general(weights, onehot, NT, preferred_element_type=jnp.float32)
+
+
+def combine(total):
     sketch = sum(
         total[t * TERM_ROWS : (t + 1) * TERM_ROWS] * (1.0 / scale) for t, scale in enumerate(SKETCH_SCALES)
     )
@@ -207,63 +210,65 @@
     out_ref, weights_ref = refs[-2:]
     weight_kernel((k,), stats_ref, leaves_ref, weights_ref)
     bins = block_bins(bins_ref, (k,))
-    for to, own in ORDER:
-        total = count(bins - first_bin(to, own), weights_ref[...])
+    for place, (to, own) in enumerate(EARLY):
+        total = combine(count(bins - first_bin(to, own), weights_ref[...]))
         if len(refs) == 3:
-            total += refs[0][4 * own + to]
-        out_ref[4 * own + to] = total
+            total += refs[0][place]
+        out_ref[place] = total
 
 
 def block_call(k, bins_t, stats, leaves, *before):
     return pl.pallas_call(
         functools.partial(block_kernel, k),
         in_specs=[pl.BlockSpec(memory_space=pltpu.VMEM)] * (3 + len(before)),
-        out_specs=pl.BlockSpec(memory_space=pltpu.VMEM),
-        out_shape=jax.ShapeDtypeStruct((8,) + PART, jnp.float32),
-        scratch_shapes=[pltpu.VMEM((W_ROWS, CHUNK), F8)],
+        out_specs=[pl.BlockSpec(memory_space=pltpu.VMEM)] * 2,
+        out_shape=[
+            jax.ShapeDtypeStruct((len(EARLY),) + PART, jnp.float32),
+            jax.ShapeDtypeStruct((W_ROWS, CHUNK), F8),
+        ],
         compiler_params=pltpu.CompilerParams(vmem_limit_bytes=32 << 20),
         cost_estimate=pl.CostEstimate(flops=5_000_000_000, bytes_accessed=1_000_000, transcendentals=0),
         name="block",
     )(bins_t, stats, leaves, *before)
 
 
-def other_kernel(ks, bins_ref, weights_ref, start_ref, out_ref):
-    bins = block_bins(bins_ref, LAST)
-    for place, k in enumerate(ks):
-        out_ref[place] = start_ref[k] + count(bins - first_bin(k, False), weights_ref[...])
-
-
-def other_call(ks, bins_t, weights, start):
-    return pl.pallas_call(
-        functools.partial(other_kernel, ks),
-        in_specs=[pl.BlockSpec(memory_space=pltpu.VMEM)] * 3,
-        out_specs=pl.BlockSpec(memory_space=pltpu.VMEM),
-        out_shape=jax.ShapeDtypeStruct((len(ks),) + PART, jnp.float32),
-        compiler_params=pltpu.CompilerParams(vmem_limit_bytes=32 << 20),
-        cost_estimate=pl.CostEstimate(flops=OTHER_COST * len(ks), bytes_accessed=1000, transcendentals=0),
-        name="other",
-    )(bins_t, weights, start)
-
-
-def hist_kernel(k, place, bins_ref, weights_ref, start_ref, swapped_ref, *refs):
+def part_kernel(k, own, groups, bins_ref, *refs):
     out_ref = refs[-1]
-    bins = block_bins(bins_ref, LAST)
-    total = start_ref[4 + k] + swapped_ref[place]
-    for ref in refs[:-1]:
-        total += ref[...]
-    out_ref[...] = total + count(bins - first_bin(k, True), weights_ref[...])
-
-
-def hist_call(k, bins_t, weights, start, swapped, place, *more):
-    return pl.pallas_call(
-        functools.partial(hist_kernel, k, place),
-        in_specs=[pl.BlockSpec(memory_space=pltpu.VMEM)] * (4 + len(more)),
+    total = sum(
+        count(block_bins(bins_ref, ks) - first_bin(k, own), ref[...]) for ks, ref in zip(groups, refs)
+    )
+    total = combine(total)
+    for ref in refs[len(groups) : -1]:
+        total += ref[EARLY.index((k, own))] if len(ref.shape) == 3 else ref[...]
+    out_ref[...] = total
+
+
+def part_call(k, own, bins_t, weights, *more, cost=1000):
+    return pl.pallas_call(
+        functools.partial(part_kernel, k, own, tuple(weights)),
+        in_specs=[pl.BlockSpec(memory_space=pltpu.VMEM)] * (1 + len(weights) + len(more)),
         out_specs=pl.BlockSpec(memory_space=pltpu.VMEM),
         out_shape=jax.ShapeDtypeStruct(PART, jnp.float32),
         compiler_params=pltpu.CompilerParams(vmem_limit_bytes=32 << 20),
-        cost_estimate=pl.CostEstimate(flops=HIST_COST[k], bytes_accessed=1000, transcendentals=0),
-        name="hist",
-    )(bins_t, weights, start, swapped, *more)
+        cost_estimate=pl.CostEstimate(flops=cost, bytes_accessed=1000, transcendentals=0),
+        name="own" if own else "other",
+    )(bins_t, *weights.values(), *more)
+
+
+def add_kernel(a_ref, b_ref, out_ref):
+    out_ref[...] = a_ref[...] + b_ref[...]
+
+
+def add_call(a, b):
+    return pl.pallas_call(
+        add_kernel,
+        in_specs=[pl.BlockSpec(memory_space=pltpu.VMEM)] * 2,
+        out_specs=pl.BlockSpec(memory_space=pltpu.VMEM),
+        out_shape=jax.ShapeDtypeStruct(PART, jnp.float32),
+        compiler_params=pltpu.CompilerParams(vmem_limit_bytes=8 << 20),
+        cost_estimate=pl.CostEstimate(flops=MID_COST, bytes_accessed=1000, transcendentals=0),
+        name="add",
+    )(a, b)
 
 
 def finish_kernel(a_ref, b_ref, out_ref):
@@ -310,22 +315,28 @@
     mine = mine + swap(mine, "zh", 1, 2)
     first = swap(mine, "x", 1, 4)
     last = [swap(mine, "x", k, 4) for k in LAST]
-    start = block_call(0, bins_t, mine, leaves2)
-    start = block_call(1, bins_t, first, leaves2, start)
+    start, weights0 = block_call(0, bins_t, mine, leaves2)
+    start, weights1 = block_call(1, bins_t, first, leaves2, start)
     weights = weight_call(LAST, last, leaves2)
 
-    far = swap(other_call((3,), bins_t, weights, start), "c", 1, 2)
-    mid = other_call((2, 1), bins_t, weights, start)
+    rest = {LAST: weights}
+    far = swap(part_call(3, False, bins_t, rest, start, cost=COST), "c", 1, 2)
+    mid = part_call(2, False, bins_t, rest, start, cost=COST)
     mid, start = lax.optimization_barrier((mid, start))
     mid = swap(mid, "c", 1, 2)
-    part = hist_call(3, bins_t, weights, start, far, 0)
-    part, start = lax.optimization_barrier((part, start))
+    part = part_call(3, True, bins_t, rest, start, far)
+    part, weights = lax.optimization_barrier((part, weights))
     passed = swap(part, "zl", 1, 4)
-    near = swap(other_call((0,), bins_t, weights, start), "c", 1, 2)
-    moved1 = swap(hist_call(1, bins_t, weights, start, mid, 1), "zl", 1, 4)
-    moved2 = swap(hist_call(2, bins_t, weights, start, mid, 0, passed), "zl", 2, 4)
-    part = hist_call(0, bins_t, weights, start, near, 0, moved1)
-    return finish_call((part, moved2))
+    whole = {(0,): weights0, (1,): weights1, LAST: weights}
+    near = swap(part_call(1, False, bins_t, whole, cost=COST), "c", 1, 2)
+    home = swap(part_call(0, False, bins_t, whole, cost=COST), "c", 1, 2)
+    part = part_call(2, True, bins_t, rest, start, mid, passed, cost=MID_COST)
+    part, weights = lax.optimization_barrier((part, weights))
+    moved2 = swap(part, "zl", 2, 4)
+    whole = {(0,): weights0, (1,): weights1, LAST: weights}
+    moved1 = swap(part_call(1, True, bins_t, whole, near), "zl", 1, 4)
+    part = part_call(0, True, bins_t, whole, home)
+    return finish_call((add_call(part, moved2), moved1))
 
 
 def solution(mesh):

time: 69.2 us -> 70.8 us (1.023)
  the two profiles are of different devices: /device:TPU:2 before, /device:TPU:1 now
where the time goes in v7:
time: 70.8 us; the launch traced here: 70.6 us
  starting transfers between devices  31 us (44%)
  Pallas kernels  23.7 us (33%)
  waiting for transfers between devices  14.9 us (21%)
  local copies, waits for them, and re-layouts  0.72 us (1%)
    ppermute x17, starting transfers between devices, swap(): return lax.ppermute(value, axis, [(i, i ^ bit) for i in range(size)])  31 us
    ppermute x17, waiting for transfers between devices, swap(): return lax.ppermute(value, axis, [(i, i ^ bit) for i in range(size)])  14.9 us
    pallas_call x3, Pallas kernels, sketch_call(): pl.pallas_call(functools.partial(sketch_kernel, ks), in_specs=[pl.BlockSp...  10.8 us
    pallas_call x8, Pallas kernels, part_call(): pl.pallas_call(functools.partial(part_kernel, k, own, tuple(weights)), in...  8.57 us
    pallas_call x2, Pallas kernels, block_call(): pl.pallas_call(functools.partial(block_kernel, k), in_specs=[pl.BlockSpec...  2.92 us
  transfers between devices with their start and end apart: 17, of which 10 were waited for; matrix products, arithmetic and copies ran while one was open for 0% of the time, Pallas kernels for 26%

profile of v7, /device:TPU:1, one launch (start us, length us, event | category | flops | bytes accessed | tf_op | source)
XLA Modules:
  0.0 70.6 jit_solution(17089512477656676462)
XLA Ops:
  0.0 0.0 copy-start.1
  0.0 0.7 %copy-done.1 = s32[256,16]{0,1:T(8,128)S(1)} copy-done((s32[256,16]{0,1:T(8,128)S(1)}, s32[256,16]{0,1:T(8,128)}, u32[]{:S(2)}) %copy-start.1) | copy-done | bytes 16408
  0.7 3.2 %sketch.3 = f32[272,128]{1,0:T(8,128)S(1)} custom-call(bf16[8192,256]{1,0:T(8,128)(2,1)} %scores_ref.5, s32[8192,256]{1,0:T(8,128)} %targets_ref.5, s32[16,256]{1,0:T(8,128)S(1)} %bitcast.13), custom_call_target="tpu_custom_call" | custom-call | flops 100663296 | bytes 3145728 | tf_op jit(solution)/shard_map/sketch/pallas_call | solution.py:97
  3.9 3.7 %collective-permute-start = (f32[272,128]{1,0:T(8,128)S(1)}, f32[272,128]{1,0:T(8,128)S(1)}, u32[]{:S(2)}, u32[]{:S(2)}) collective-permute-start(f32[272,128]{1,0:T(8,128)S(1)} %sketch.3), channel_id=1, source_target_pairs={{0,4},{2,6},{4,0},{6,2},{1,5},{3,7},{5,1},{7,3},{8,12},{10,14},{12... | collective-permute-start | bytes 417800 | tf_op jit(solution)/shard_map/ppermute | solution.py:298
  7.5 4.5 %sketch.5 = (f32[272,128]{1,0:T(8,128)S(1)}, f32[272,128]{1,0:T(8,128)S(1)}) custom-call(bf16[8192,256]{1,0:T(8,128)(2,1)} %scores_ref.5, s32[8192,256]{1,0:T(8,128)} %targets_ref.5, s32[16,256]{1,0:T(8,128)S(1)} %bitcast.14), custom_call_target="tpu_custom_call" | custom-call | flops 201326592 | bytes 6291456 | tf_op jit(solution)/shard_map/sketch/pallas_call | solution.py:97
  12.1 0.4 collective-permute-start.1
  12.5 0.0 copy-start
  12.5 0.0 copy-start.2
  12.5 0.7 collective-permute-start.2
  13.1 0.0 collective-permute-done.refs_0_
  13.1 3.2 %sketch.4 = f32[272,128]{1,0:T(8,128)S(1)} custom-call(bf16[8192,256]{1,0:T(8,128)(2,1)} %scores_ref.5, s32[8192,256]{1,0:T(8,128)} %targets_ref.5, s32[16,256]{1,0:T(8,128)S(1)} %bitcast.15, f32[272,128]{1,0:T(8,128)S(1)} %collective-permute-done.refs_0_), custom_call_target="tpu_custom_call" | custom-call | flops 100663296 | bytes 3145728 | tf_op jit(solution)/shard_map/sketch/pallas_call | solution.py:97
  16.3 0.1 collective-permute-done.1
  16.4 1.2 %collective-permute-done.2 = f32[272,128]{1,0:T(8,128)S(1)} collective-permute-done((f32[272,128]{1,0:T(8,128)S(1)}, f32[272,128]{1,0:T(8,128)S(1)}, u32[]{:S(2)}, u32[]{:S(2)}) %collective-permute-start.2) | collective-permute-done | bytes 139296 | tf_op jit(solution)/shard_map/ppermute | solution.py:298
  17.6 1.4 %collective-permute-start.4 = (f32[272,128]{1,0:T(8,128)S(1)}, f32[272,128]{1,0:T(8,128)S(1)}, u32[]{:S(2)}, u32[]{:S(2)}) collective-permute-start(f32[272,128]{1,0:T(8,128)S(1)} %add_add_fusion.1), channel_id=1, source_target_pairs={{0,8},{8,0},{16,24},{24,16},{1,9},{9,1},{17,25},{25,17},{2,10},{10... | collective-permute-start | bytes 417800 | tf_op jit(solution)/shard_map/ppermute | solution.py:298
  19.0 1.9 %collective-permute-start.5 = (f32[272,128]{1,0:T(8,128)S(1)}, f32[272,128]{1,0:T(8,128)S(1)}, u32[]{:S(2)}, u32[]{:S(2)}) collective-permute-start(f32[272,128]{1,0:T(8,128)S(1)} %add_add_fusion.1), channel_id=1, source_target_pairs={{0,24},{8,16},{16,8},{24,0},{1,25},{9,17},{17,9},{25,1},{2,26},{10... | collective-permute-start | bytes 417800 | tf_op jit(solution)/shard_map/ppermute | solution.py:298
  20.9 0.7 %collective-permute-start.3 = (f32[272,128]{1,0:T(8,128)S(1)}, f32[272,128]{1,0:T(8,128)S(1)}, u32[]{:S(2)}, u32[]{:S(2)}) collective-permute-start(f32[272,128]{1,0:T(8,128)S(1)} %add_add_fusion.1), channel_id=1, source_target_pairs={{0,16},{8,24},{16,0},{24,8},{1,17},{9,25},{17,1},{25,9},{2,18},{10... | collective-permute-start | bytes 417800 | tf_op jit(solution)/shard_map/ppermute | solution.py:298
  21.6 0.0 collective-permute-done.4
  21.6 2.5 %collective-permute-done.5 = f32[272,128]{1,0:T(8,128)S(1)} collective-permute-done((f32[272,128]{1,0:T(8,128)S(1)}, f32[272,128]{1,0:T(8,128)S(1)}, u32[]{:S(2)}, u32[]{:S(2)}) %collective-permute-start.5) | collective-permute-done | bytes 139296 | tf_op jit(solution)/shard_map/ppermute | solution.py:298
  24.1 3.1 %collective-permute-done.3 = f32[272,128]{1,0:T(8,128)S(1)} collective-permute-done((f32[272,128]{1,0:T(8,128)S(1)}, f32[272,128]{1,0:T(8,128)S(1)}, u32[]{:S(2)}, u32[]{:S(2)}) %collective-permute-start.3) | collective-permute-done | bytes 139296 | tf_op jit(solution)/shard_map/ppermute | solution.py:298
  27.3 7.0 %collective-permute-start.6 = (f32[272,128]{1,0:T(8,128)S(1)}, f32[272,128]{1,0:T(8,128)S(1)}, u32[]{:S(2)}, u32[]{:S(2)}) collective-permute-start(f32[272,128]{1,0:T(8,128)S(1)} %add_add_fusion), channel_id=1, source_target_pairs={{0,1},{1,0},{2,3},{3,2},{4,5},{5,4},{6,7},{7,6},{8,9},{9,8},{10,11... | collective-permute-start | bytes 417800 | tf_op jit(solution)/shard_map/ppermute | solution.py:298
  34.3 2.5 %collective-permute-done.6 = f32[272,128]{1,0:T(8,128)S(1)} collective-permute-done((f32[272,128]{1,0:T(8,128)S(1)}, f32[272,128]{1,0:T(8,128)S(1)}, u32[]{:S(2)}, u32[]{:S(2)}) %collective-permute-start.6) | collective-permute-done | bytes 139296 | tf_op jit(solution)/shard_map/ppermute | solution.py:298
  36.9 0.6 collective-permute-start.7
  37.4 1.3 %collective-permute-start.8 = (f32[272,128]{1,0:T(8,128)S(1)}, f32[272,128]{1,0:T(8,128)S(1)}, u32[]{:S(2)}, u32[]{:S(2)}) collective-permute-start(f32[272,128]{1,0:T(8,128)S(1)} %add.24.stats_ref), channel_id=1, source_target_pairs={{0,6},{2,4},{4,2},{6,0},{1,7},{3,5},{5,3},{7,1},{8,14},{10,12},{12... | collective-permute-start | bytes 417800 | tf_op jit(solution)/shard_map/ppermute | solution.py:298
  38.7 1.5 %collective-permute-start.9 = (f32[272,128]{1,0:T(8,128)S(1)}, f32[272,128]{1,0:T(8,128)S(1)}, u32[]{:S(2)}, u32[]{:S(2)}) collective-permute-start(f32[272,128]{1,0:T(8,128)S(1)} %add.24.stats_ref), channel_id=1, source_target_pairs={{0,4},{2,6},{4,0},{6,2},{1,5},{3,7},{5,1},{7,3},{8,12},{10,14},{12... | collective-permute-start | bytes 417800 | tf_op jit(solution)/shard_map/ppermute | solution.py:298
  40.2 0.0 copy-done
  40.2 0.0 copy-done.2
  40.2 1.5 %block.2 = (f32[4,136,256]{2,1,0:T(8,128)S(1)}, f8e4m3fn[288,2048]{1,0:T(32,128)(4,1)S(1)}) custom-call(s32[16,8192]{1,0:T(8,128)S(1)} %bitcast.3, f32[272,128]{1,0:T(8,128)S(1)} %add.24.stats_ref, s32[64,128]{1,0:T(8,128)S(1)} %bitcast.16), custom_call_target="tpu_custom_call" | custom-call | flops 5000000000 | bytes 1000000 | tf_op jit(solution)/shard_map/block/pallas_call | solution.py:221
  41.7 0.0 collective-permute-done.7.stats_ref
  41.7 1.5 %block.3 = (f32[4,136,256]{2,1,0:T(8,128)S(1)}, f8e4m3fn[288,2048]{1,0:T(32,128)(4,1)S(1)}) custom-call(s32[16,8192]{1,0:T(8,128)S(1)} %bitcast.4, f32[272,128]{1,0:T(8,128)S(1)} %collective-permute-done.7.stats_ref, s32[64,128]{1,0:T(8,128)S(1)} %bitcast.17, f32[4,136,256]{2,1,0:T(8,128)S(1)} %get-tuple-element.24.refs_0_), custom_call_target="tpu_custom_call" | custom-call | flops 5000000000 | bytes 1000000 | tf_op jit(solution)/shard_map/block/pallas_call | solution.py:221
  43.2 0.0 collective-permute-done.8.refs_0_
  43.2 0.9 %collective-permute-done.9.refs_1_ = f32[272,128]{1,0:T(8,128)S(1)} collective-permute-done((f32[272,128]{1,0:T(8,128)S(1)}, f32[272,128]{1,0:T(8,128)S(1)}, u32[]{:S(2)}, u32[]{:S(2)}) %collective-permute-start.9) | collective-permute-done | bytes 139296 | tf_op jit(solution)/shard_map/ppermute | solution.py:298
  44.1 0.6 weights.1.refs_0_.refs_2_
  44.7 0.8 %other.5 = f32[136,256]{1,0:T(8,128)S(1)} custom-call(s32[16,8192]{1,0:T(8,128)S(1)} %bitcast.5, f8e4m3fn[288,4096]{1,0:T(32,128)(4,1)S(1)} %weights.1.refs_0_.refs_2_, f32[4,136,256]{2,1,0:T(8,128)S(1)} %get-tuple-element.27.refs_1_), custom_call_target="tpu_custom_call" | custom-call | flops 2000000000 | bytes 1000 | tf_op jit(solution)/shard_map/other/pallas_call | solution.py:247
  45.5 6.0 %collective-permute-start.11 = (f32[136,256]{1,0:T(8,128)S(1)}, f32[136,256]{1,0:T(8,128)S(1)}, u32[]{:S(2)}, u32[]{:S(2)}) collective-permute-start(f32[136,256]{1,0:T(8,128)S(1)} %other.5), channel_id=1, source_target_pairs={{0,32},{32,0},{1,33},{33,1},{2,34},{34,2},{3,35},{35,3},{4,36},{36... | collective-permute-start | bytes 417800 | tf_op jit(solution)/shard_map/ppermute | solution.py:298
  51.5 0.8 %other.4 = f32[136,256]{1,0:T(8,128)S(1)} custom-call(s32[16,8192]{1,0:T(8,128)S(1)} %bitcast.6, f8e4m3fn[288,4096]{1,0:T(32,128)(4,1)S(1)} %weights.1.refs_0_.refs_2_, f32[4,136,256]{2,1,0:T(8,128)S(1)} %get-tuple-element.27.refs_1_), custom_call_target="tpu_custom_call" | custom-call | flops 2000000000 | bytes 1000 | tf_op jit(solution)/shard_map/other/pallas_call | solution.py:247
  52.2 0.1 collective-permute-start.10
  52.3 0.1 collective-permute-done.11.refs_2_
  52.5 0.8 %own.4 = f32[136,256]{1,0:T(8,128)S(1)} custom-call(s32[16,8192]{1,0:T(8,128)S(1)} %bitcast.7, f8e4m3fn[288,4096]{1,0:T(32,128)(4,1)S(1)} %weights.1.refs_0_.refs_2_, f32[4,136,256]{2,1,0:T(8,128)S(1)} %get-tuple-element.27.refs_1_, f32[136,256]{1,0:T(8,128)S(1)} %collective-permute-done.11.refs_2_), custom_call_target="tpu_custom_call" | custom-call | flops 1000 | bytes 1000 | tf_op jit(solution)/shard_map/own/pallas_call | solution.py:247
  53.2 0.9 %collective-permute-start.12 = (f32[136,256]{1,0:T(8,128)S(1)}, f32[136,256]{1,0:T(8,128)S(1)}, u32[]{:S(2)}, u32[]{:S(2)}) collective-permute-start(f32[136,256]{1,0:T(8,128)S(1)} %own.4), channel_id=1, source_target_pairs={{0,64},{64,0},{128,192},{192,128},{1,65},{65,1},{129,193},{193,129... | collective-permute-start | bytes 417800 | tf_op jit(solution)/shard_map/ppermute | solution.py:298
  54.1 1.4 %other.6 = f32[136,256]{1,0:T(8,128)S(1)} custom-call(s32[16,8192]{1,0:T(8,128)S(1)} %bitcast.8, f8e4m3fn[288,2048]{1,0:T(32,128)(4,1)S(1)} %get-tuple-element.23.refs_0_, f8e4m3fn[288,2048]{1,0:T(32,128)(4,1)S(1)} %get-tuple-element.25.refs_1_, f8e4m3fn[288,4096]{1,0:T(32,128)(4,1)S(1)} %weights.1.refs_0_.refs_2_), custom_call_target="tpu_custom_call" | custom-call | flops 2000000000 | bytes 1000 | tf_op jit(solution)/shard_map/other/pallas_call | solution.py:247
  55.5 0.7 %collective-permute-start.13 = (f32[136,256]{1,0:T(8,128)S(1)}, f32[136,256]{1,0:T(8,128)S(1)}, u32[]{:S(2)}, u32[]{:S(2)}) collective-permute-start(f32[136,256]{1,0:T(8,128)S(1)} %other.6), channel_id=1, source_target_pairs={{0,32},{32,0},{1,33},{33,1},{2,34},{34,2},{3,35},{35,3},{4,36},{36... | collective-permute-start | bytes 417800 | tf_op jit(solution)/shard_map/ppermute | solution.py:298
  56.2 1.4 %other.7 = f32[136,256]{1,0:T(8,128)S(1)} custom-call(s32[16,8192]{1,0:T(8,128)S(1)} %bitcast.9, f8e4m3fn[288,2048]{1,0:T(32,128)(4,1)S(1)} %get-tuple-element.23.refs_0_, f8e4m3fn[288,2048]{1,0:T(32,128)(4,1)S(1)} %get-tuple-element.25.refs_1_, f8e4m3fn[288,4096]{1,0:T(32,128)(4,1)S(1)} %weights.1.refs_0_.refs_2_), custom_call_target="tpu_custom_call" | custom-call | flops 2000000000 | bytes 1000 | tf_op jit(solution)/shard_map/other/pallas_call | solution.py:247
  57.6 0.1 collective-permute-start.15
  57.7 0.0 collective-permute-done.10.refs_2_
  57.7 0.5 collective-permute-done.12.refs_3_
  58.2 0.8 %own.5 = f32[136,256]{1,0:T(8,128)S(1)} custom-call(s32[16,8192]{1,0:T(8,128)S(1)} %bitcast.10, f8e4m3fn[288,4096]{1,0:T(32,128)(4,1)S(1)} %weights.1.refs_0_.refs_2_, f32[4,136,256]{2,1,0:T(8,128)S(1)} %get-tuple-element.27.refs_1_, f32[136,256]{1,0:T(8,128)S(1)} %collective-permute-done.10.refs_2_, f32[136,256]{1,0:T(8,128)S(1)} %collective-permute-done.12.refs_3_), custom_call_target="tpu_custom_call" | custom-call | flops 5000000000 | bytes 1000 | tf_op jit(solution)/shard_map/own/pallas_call | solution.py:247
  59.0 2.7 %collective-permute-start.14 = (f32[136,256]{1,0:T(8,128)S(1)}, f32[136,256]{1,0:T(8,128)S(1)}, u32[]{:S(2)}, u32[]{:S(2)}) collective-permute-start(f32[136,256]{1,0:T(8,128)S(1)} %own.5), channel_id=1, source_target_pairs={{0,128},{64,192},{128,0},{192,64},{1,129},{65,193},{129,1},{193,65... | collective-permute-start | bytes 417800 | tf_op jit(solution)/shard_map/ppermute | solution.py:298
  61.7 0.0 collective-permute-done.15.refs_3_
  61.7 1.4 %own.7 = f32[136,256]{1,0:T(8,128)S(1)} custom-call(s32[16,8192]{1,0:T(8,128)S(1)} %bitcast.11, f8e4m3fn[288,2048]{1,0:T(32,128)(4,1)S(1)} %get-tuple-element.23.refs_0_, f8e4m3fn[288,2048]{1,0:T(32,128)(4,1)S(1)} %get-tuple-element.25.refs_1_, f8e4m3fn[288,4096]{1,0:T(32,128)(4,1)S(1)} %weights.1.refs_0_.refs_2_, f32[136,256]{1,0:T(8,128)S(1)} %collective-permute-done.15.refs_3_), custom_call_target="tpu_custom_call" | custom-call | flops 1000 | bytes 1000 | tf_op jit(solution)/shard_map/own/pallas_call | solution.py:247
  63.1 1.3 %collective-permute-start.16 = (f32[136,256]{1,0:T(8,128)S(1)}, f32[136,256]{1,0:T(8,128)S(1)}, u32[]{:S(2)}, u32[]{:S(2)}) collective-permute-start(f32[136,256]{1,0:T(8,128)S(1)} %own.7), channel_id=1, source_target_pairs={{0,64},{64,0},{128,192},{192,128},{1,65},{65,1},{129,193},{193,129... | collective-permute-start | bytes 417800 | tf_op jit(solution)/shard_map/ppermute | solution.py:298
  64.5 0.0 collective-permute-done.13.refs_3_
  64.5 1.4 %own.6.a_ref = f32[136,256]{1,0:T(8,128)S(1)} custom-call(s32[16,8192]{1,0:T(8,128)S(1)} %bitcast.12, f8e4m3fn[288,2048]{1,0:T(32,128)(4,1)S(1)} %get-tuple-element.23.refs_0_, f8e4m3fn[288,2048]{1,0:T(32,128)(4,1)S(1)} %get-tuple-element.25.refs_1_, f8e4m3fn[288,4096]{1,0:T(32,128)(4,1)S(1)} %weights.1.refs_0_.refs_2_, ...), custom_call_target="tpu_custom_call" | custom-call | flops 1000 | bytes 1000 | tf_op jit(solution)/shard_map/own/pallas_call | solution.py:247
  65.8 1.6 %collective-permute-done.14.b_ref = f32[136,256]{1,0:T(8,128)S(1)} collective-permute-done((f32[136,256]{1,0:T(8,128)S(1)}, f32[136,256]{1,0:T(8,128)S(1)}, u32[]{:S(2)}, u32[]{:S(2)}) %collective-permute-start.14) | collective-permute-done | bytes 139296 | tf_op jit(solution)/shard_map/ppermute | solution.py:298
  67.4 2.3 %collective-permute-done.16.b_ref = f32[136,256]{1,0:T(8,128)S(1)} collective-permute-done((f32[136,256]{1,0:T(8,128)S(1)}, f32[136,256]{1,0:T(8,128)S(1)}, u32[]{:S(2)}, u32[]{:S(2)}) %collective-permute-start.16) | collective-permute-done | bytes 139296 | tf_op jit(solution)/shard_map/ppermute | solution.py:298
  69.8 0.8 %finish.1 = f32[32,16,68]{2,1,0:T(8,128)} custom-call(f32[136,256]{1,0:T(8,128)S(1)} %add.30.a_ref, f32[136,256]{1,0:T(8,128)S(1)} %collective-permute-done.16.b_ref), custom_call_target="tpu_custom_call" | custom-call | tf_op jit(solution)/shard_map/finish/pallas_call | solution.py:289
  (4 shorter events, 0.1 us)
Async XLA Ops:
  0.0 0.7 %copy-start.1 = (s32[256,16]{0,1:T(8,128)S(1)}, s32[256,16]{0,1:T(8,128)}, u32[]{:S(2)}) copy-start(s32[256,16]{0,1:T(8,128)} %param.7) | copy-start | bytes 49156
  3.9 9.3 %collective-permute-start = (f32[272,128]{1,0:T(8,128)S(1)}, f32[272,128]{1,0:T(8,128)S(1)}, u32[]{:S(2)}, u32[]{:S(2)}) collective-permute-start(f32[272,128]{1,0:T(8,128)S(1)} %sketch.3), channel_id=1, source_target_pairs={{0,4},{2,6},{4,0},{6,2},{1,5},{3,7},{5,1},{7,3},{8,12},{10,14},{12... | collective-permute-start | bytes 417800 | tf_op jit(solution)/shard_map/ppermute | solution.py:298
  12.1 4.3 %collective-permute-start.1 = (f32[272,128]{1,0:T(8,128)S(1)}, f32[272,128]{1,0:T(8,128)S(1)}, u32[]{:S(2)}, u32[]{:S(2)}) collective-permute-start(f32[272,128]{1,0:T(8,128)S(1)} %get-tuple-element.21), channel_id=1, source_target_pairs={{0,2},{2,0},{4,6},{6,4},{1,3},{3,1},{5,7},{7,5},{8,10},{10,8},{12,... | collective-permute-start | bytes 417800 | tf_op jit(solution)/shard_map/ppermute | solution.py:298
  12.5 27.8 %copy-start = (s32[8192,16]{0,1:T(8,128)S(1)}, s32[8192,16]{0,1:T(8,128)}, u32[]{:S(2)}) copy-start(s32[8192,16]{0,1:T(8,128)} %param.8) | copy-start | bytes 1572868
  12.5 27.8 %copy-start.2 = (s32[8192]{0:T(1024)S(1)}, s32[8192]{0:T(1024)}, u32[]{:S(2)}) copy-start(s32[8192]{0:T(1024)} %param.9) | copy-start | bytes 98308
  12.5 5.1 %collective-permute-start.2 = (f32[272,128]{1,0:T(8,128)S(1)}, f32[272,128]{1,0:T(8,128)S(1)}, u32[]{:S(2)}, u32[]{:S(2)}) collective-permute-start(f32[272,128]{1,0:T(8,128)S(1)} %get-tuple-element.22), channel_id=1, source_target_pairs={{0,6},{2,4},{4,2},{6,0},{1,7},{3,5},{5,3},{7,1},{8,14},{10,12},{12... | collective-permute-start | bytes 417800 | tf_op jit(solution)/shard_map/ppermute | solution.py:298
  17.6 4.0 %collective-permute-start.4 = (f32[272,128]{1,0:T(8,128)S(1)}, f32[272,128]{1,0:T(8,128)S(1)}, u32[]{:S(2)}, u32[]{:S(2)}) collective-permute-start(f32[272,128]{1,0:T(8,128)S(1)} %add_add_fusion.1), channel_id=1, source_target_pairs={{0,8},{8,0},{16,24},{24,16},{1,9},{9,1},{17,25},{25,17},{2,10},{10... | collective-permute-start | bytes 417800 | tf_op jit(solution)/shard_map/ppermute | solution.py:298
  19.0 5.1 %collective-permute-start.5 = (f32[272,128]{1,0:T(8,128)S(1)}, f32[272,128]{1,0:T(8,128)S(1)}, u32[]{:S(2)}, u32[]{:S(2)}) collective-permute-start(f32[272,128]{1,0:T(8,128)S(1)} %add_add_fusion.1), channel_id=1, source_target_pairs={{0,24},{8,16},{16,8},{24,0},{1,25},{9,17},{17,9},{25,1},{2,26},{10... | collective-permute-start | bytes 417800 | tf_op jit(solution)/shard_map/ppermute | solution.py:298
  20.9 6.4 %collective-permute-start.3 = (f32[272,128]{1,0:T(8,128)S(1)}, f32[272,128]{1,0:T(8,128)S(1)}, u32[]{:S(2)}, u32[]{:S(2)}) collective-permute-start(f32[272,128]{1,0:T(8,128)S(1)} %add_add_fusion.1), channel_id=1, source_target_pairs={{0,16},{8,24},{16,0},{24,8},{1,17},{9,25},{17,1},{25,9},{2,18},{10... | collective-permute-start | bytes 417800 | tf_op jit(solution)/shard_map/ppermute | solution.py:298
  27.3 9.6 %collective-permute-start.6 = (f32[272,128]{1,0:T(8,128)S(1)}, f32[272,128]{1,0:T(8,128)S(1)}, u32[]{:S(2)}, u32[]{:S(2)}) collective-permute-start(f32[272,128]{1,0:T(8,128)S(1)} %add_add_fusion), channel_id=1, source_target_pairs={{0,1},{1,0},{2,3},{3,2},{4,5},{5,4},{6,7},{7,6},{8,9},{9,8},{10,11... | collective-permute-start | bytes 417800 | tf_op jit(solution)/shard_map/ppermute | solution.py:298
  36.9 4.8 %collective-permute-start.7 = (f32[272,128]{1,0:T(8,128)S(1)}, f32[272,128]{1,0:T(8,128)S(1)}, u32[]{:S(2)}, u32[]{:S(2)}) collective-permute-start(f32[272,128]{1,0:T(8,128)S(1)} %add.24.stats_ref), channel_id=1, source_target_pairs={{0,2},{2,0},{4,6},{6,4},{1,3},{3,1},{5,7},{7,5},{8,10},{10,8},{12,... | collective-permute-start | bytes 417800 | tf_op jit(solution)/shard_map/ppermute | solution.py:298
  37.4 5.7 %collective-permute-start.8 = (f32[272,128]{1,0:T(8,128)S(1)}, f32[272,128]{1,0:T(8,128)S(1)}, u32[]{:S(2)}, u32[]{:S(2)}) collective-permute-start(f32[272,128]{1,0:T(8,128)S(1)} %add.24.stats_ref), channel_id=1, source_target_pairs={{0,6},{2,4},{4,2},{6,0},{1,7},{3,5},{5,3},{7,1},{8,14},{10,12},{12... | collective-permute-start | bytes 417800 | tf_op jit(solution)/shard_map/ppermute | solution.py:298
  38.7 5.4 %collective-permute-start.9 = (f32[272,128]{1,0:T(8,128)S(1)}, f32[272,128]{1,0:T(8,128)S(1)}, u32[]{:S(2)}, u32[]{:S(2)}) collective-permute-start(f32[272,128]{1,0:T(8,128)S(1)} %add.24.stats_ref), channel_id=1, source_target_pairs={{0,4},{2,6},{4,0},{6,2},{1,5},{3,7},{5,1},{7,3},{8,12},{10,14},{12... | collective-permute-start | bytes 417800 | tf_op jit(solution)/shard_map/ppermute | solution.py:298
  45.5 7.0 %collective-permute-start.11 = (f32[136,256]{1,0:T(8,128)S(1)}, f32[136,256]{1,0:T(8,128)S(1)}, u32[]{:S(2)}, u32[]{:S(2)}) collective-permute-start(f32[136,256]{1,0:T(8,128)S(1)} %other.5), channel_id=1, source_target_pairs={{0,32},{32,0},{1,33},{33,1},{2,34},{34,2},{3,35},{35,3},{4,36},{36... | collective-permute-start | bytes 417800 | tf_op jit(solution)/shard_map/ppermute | solution.py:298
  52.2 5.5 %collective-permute-start.10 = (f32[136,256]{1,0:T(8,128)S(1)}, f32[136,256]{1,0:T(8,128)S(1)}, u32[]{:S(2)}, u32[]{:S(2)}) collective-permute-start(f32[136,256]{1,0:T(8,128)S(1)} %other.4), channel_id=1, source_target_pairs={{0,32},{32,0},{1,33},{33,1},{2,34},{34,2},{3,35},{35,3},{4,36},{36... | collective-permute-start | bytes 417800 | tf_op jit(solution)/shard_map/ppermute | solution.py:298
  53.2 5.0 %collective-permute-start.12 = (f32[136,256]{1,0:T(8,128)S(1)}, f32[136,256]{1,0:T(8,128)S(1)}, u32[]{:S(2)}, u32[]{:S(2)}) collective-permute-start(f32[136,256]{1,0:T(8,128)S(1)} %own.4), channel_id=1, source_target_pairs={{0,64},{64,0},{128,192},{192,128},{1,65},{65,1},{129,193},{193,129... | collective-permute-start | bytes 417800 | tf_op jit(solution)/shard_map/ppermute | solution.py:298
  55.5 9.0 %collective-permute-start.13 = (f32[136,256]{1,0:T(8,128)S(1)}, f32[136,256]{1,0:T(8,128)S(1)}, u32[]{:S(2)}, u32[]{:S(2)}) collective-permute-start(f32[136,256]{1,0:T(8,128)S(1)} %other.6), channel_id=1, source_target_pairs={{0,32},{32,0},{1,33},{33,1},{2,34},{34,2},{3,35},{35,3},{4,36},{36... | collective-permute-start | bytes 417800 | tf_op jit(solution)/shard_map/ppermute | solution.py:298
  57.6 4.1 %collective-permute-start.15 = (f32[136,256]{1,0:T(8,128)S(1)}, f32[136,256]{1,0:T(8,128)S(1)}, u32[]{:S(2)}, u32[]{:S(2)}) collective-permute-start(f32[136,256]{1,0:T(8,128)S(1)} %other.7), channel_id=1, source_target_pairs={{0,32},{32,0},{1,33},{33,1},{2,34},{34,2},{3,35},{35,3},{4,36},{36... | collective-permute-start | bytes 417800 | tf_op jit(solution)/shard_map/ppermute | solution.py:298
  59.0 8.4 %collective-permute-start.14 = (f32[136,256]{1,0:T(8,128)S(1)}, f32[136,256]{1,0:T(8,128)S(1)}, u32[]{:S(2)}, u32[]{:S(2)}) collective-permute-start(f32[136,256]{1,0:T(8,128)S(1)} %own.5), channel_id=1, source_target_pairs={{0,128},{64,192},{128,0},{192,64},{1,129},{65,193},{129,1},{193,65... | collective-permute-start | bytes 417800 | tf_op jit(solution)/shard_map/ppermute | solution.py:298
  63.1 6.6 %collective-permute-start.16 = (f32[136,256]{1,0:T(8,128)S(1)}, f32[136,256]{1,0:T(8,128)S(1)}, u32[]{:S(2)}, u32[]{:S(2)}) collective-permute-start(f32[136,256]{1,0:T(8,128)S(1)} %own.7), channel_id=1, source_target_pairs={{0,64},{64,0},{128,192},{192,128},{1,65},{65,1},{129,193},{193,129... | collective-permute-start | bytes 417800 | tf_op jit(solution)/shard_map/ppermute | solution.py:298

commit v8 on v7

--- a/solution.py
+++ b/solution.py
@@ -30,9 +30,11 @@
 CHUNK = 4 * SLAB
 HALF = OWN_BINS * FEATS // 2
 PART = (2 * LEAVES * (K + 1), HALF)
-EARLY = ((3, False), (3, True), (2, False), (2, True))
+EARLY = tuple((k, own) for k in (3, 2, 1) for own in (False, True))
+CUT = LEAVES * K
 MID_COST = 5_000_000_000
-COST = 2_000_000_000
+ADD_COSTS = (200_000_000, MID_COST)
+COST = 1000
 LAST = (3, 2)
 GROUP = 4
 SKETCH_VMEM = 51 << 20
@@ -232,47 +234,52 @@
     )(bins_t, stats, leaves, *before)
 
 
-def part_kernel(k, own, groups, bins_ref, *refs):
-    out_ref = refs[-1]
+def part_kernel(k, own, groups, outs, bins_ref, *refs):
     total = sum(
         count(block_bins(bins_ref, ks) - first_bin(k, own), ref[...]) for ks, ref in zip(groups, refs)
     )
     total = combine(total)
-    for ref in refs[len(groups) : -1]:
+    for ref in refs[len(groups) : -outs]:
         total += ref[EARLY.index((k, own))] if len(ref.shape) == 3 else ref[...]
-    out_ref[...] = total
-
-
-def part_call(k, own, bins_t, weights, *more, cost=1000):
-    return pl.pallas_call(
-        functools.partial(part_kernel, k, own, tuple(weights)),
+    if outs == 1:
+        refs[-1][...] = total
+    else:
+        refs[-2][...] = total[:CUT]
+        refs[-1][...] = total[CUT:]
+
+
+def part_call(k, own, bins_t, weights, *more, cut=False, cost=1000):
+    shapes = [(CUT, PART[1]), (PART[0] - CUT, PART[1])] if cut else [PART]
+    outs = pl.pallas_call(
+        functools.partial(part_kernel, k, own, tuple(weights), len(shapes)),
         in_specs=[pl.BlockSpec(memory_space=pltpu.VMEM)] * (1 + len(weights) + len(more)),
-        out_specs=pl.BlockSpec(memory_space=pltpu.VMEM),
-        out_shape=jax.ShapeDtypeStruct(PART, jnp.float32),
+        out_specs=[pl.BlockSpec(memory_space=pltpu.VMEM)] * len(shapes),
+        out_shape=[jax.ShapeDtypeStruct(shape, jnp.float32) for shape in shapes],
         compiler_params=pltpu.CompilerParams(vmem_limit_bytes=32 << 20),
         cost_estimate=pl.CostEstimate(flops=cost, bytes_accessed=1000, transcendentals=0),
         name="own" if own else "other",
     )(bins_t, *weights.values(), *more)
+    return outs if cut else outs[0]
 
 
 def add_kernel(a_ref, b_ref, out_ref):
     out_ref[...] = a_ref[...] + b_ref[...]
 
 
-def add_call(a, b):
+def add_call(a, b, cost=1000):
     return pl.pallas_call(
         add_kernel,
         in_specs=[pl.BlockSpec(memory_space=pltpu.VMEM)] * 2,
         out_specs=pl.BlockSpec(memory_space=pltpu.VMEM),
-        out_shape=jax.ShapeDtypeStruct(PART, jnp.float32),
+        out_shape=jax.ShapeDtypeStruct(a.shape, jnp.float32),
         compiler_params=pltpu.CompilerParams(vmem_limit_bytes=8 << 20),
-        cost_estimate=pl.CostEstimate(flops=MID_COST, bytes_accessed=1000, transcendentals=0),
+        cost_estimate=pl.CostEstimate(flops=cost, bytes_accessed=1000, transcendentals=0),
         name="add",
     )(a, b)
 
 
-def finish_kernel(a_ref, b_ref, out_ref):
-    total = a_ref[...] + b_ref[...]
+def finish_kernel(upper_ref, lower_ref, moved_ref, last_ref, out_ref):
+    total = jnp.concatenate([upper_ref[...], lower_ref[...] + last_ref[...]], axis=0) + moved_ref[...]
     for half in range(2):
         rows = []
         for e in range(LEAVES):
@@ -322,21 +329,21 @@
     rest = {LAST: weights}
     far = swap(part_call(3, False, bins_t, rest, start, cost=COST), "c", 1, 2)
     mid = part_call(2, False, bins_t, rest, start, cost=COST)
-    mid, start = lax.optimization_barrier((mid, start))
-    mid = swap(mid, "c", 1, 2)
-    part = part_call(3, True, bins_t, rest, start, far)
-    part, weights = lax.optimization_barrier((part, weights))
-    passed = swap(part, "zl", 1, 4)
+    near = part_call(1, False, bins_t, rest, start, cost=COST)
+    mid, near, start = lax.optimization_barrier((mid, near, start))
+    mid, near = swap(mid, "c", 1, 2), swap(near, "c", 1, 2)
+    upper, lower = part_call(3, True, bins_t, rest, start, far, cut=True)
+    upper, lower, start, weights = lax.optimization_barrier((upper, lower, start, weights))
+    passed = [swap(upper, "zl", 1, 4), swap(lower, "zl", 1, 4)]
+    rest = {LAST: weights}
+    moved1 = swap(part_call(1, True, bins_t, rest, start, near), "zl", 1, 4)
+    upper, lower = part_call(2, True, bins_t, rest, start, mid, cut=True)
+    upper, lower, weights = lax.optimization_barrier((upper, lower, weights))
     whole = {(0,): weights0, (1,): weights1, LAST: weights}
-    near = swap(part_call(1, False, bins_t, whole, cost=COST), "c", 1, 2)
+    moved2 = [swap(add_call(a, b, cost), "zl", 2, 4) for a, b, cost in zip((upper, lower), passed, ADD_COSTS)]
     home = swap(part_call(0, False, bins_t, whole, cost=COST), "c", 1, 2)
-    part = part_call(2, True, bins_t, rest, start, mid, passed, cost=MID_COST)
-    part, weights = lax.optimization_barrier((part, weights))
-    moved2 = swap(part, "zl", 2, 4)
-    whole = {(0,): weights0, (1,): weights1, LAST: weights}
-    moved1 = swap(part_call(1, True, bins_t, whole, near), "zl", 1, 4)
-    part = part_call(0, True, bins_t, whole, home)
-    return finish_call((add_call(part, moved2), moved1))
+    upper, lower = part_call(0, True, bins_t, whole, home, cut=True)
+    return finish_call((add_call(upper, moved2[0], MID_COST), lower, moved1, moved2[1]))
 
 
 def solution(mesh):

time: 70.8 us -> 72.5 us (1.024)
  starting transfers between devices: 31 us -> 31.9 us
  waiting for transfers between devices: 14.9 us -> 15.7 us
    pallas_call x2, Pallas kernels: 2.92 us -> 4.16 us  [block_call(): pl.pallas_call(functools.partial(block_kernel, k), in_specs=[pl.BlockSpec...]
    pallas_call x8, Pallas kernels: 8.57 us -> 7.4 us  [part_call(): pl.pallas_call(functools.partial(part_kernel, k, own, tuple(weights), len...]
    ppermute x17 -> x19, starting transfers between devices: 31 us -> 31.9 us  [swap(): return lax.ppermute(value, axis, [(i, i ^ bit) for i in range(size)])]
    ppermute x17 -> x19, waiting for transfers between devices: 14.9 us -> 15.7 us  [swap(): return lax.ppermute(value, axis, [(i, i ^ bit) for i in range(size)])]
  transfers between devices with their start and end apart: 17 -> 19, of which waited for: 10 -> 8; matrix products, arithmetic and copies ran while one was open for 0% -> 0% of each run, Pallas kernels for 26% -> 26%
where the time goes in v8:
time: 72.5 us; the launch traced here: 72.3 us
  starting transfers between devices  31.9 us (44%)
  Pallas kernels  23.8 us (33%)
  waiting for transfers between devices  15.7 us (22%)
    ppermute x19, starting transfers between devices, swap(): return lax.ppermute(value, axis, [(i, i ^ bit) for i in range(size)])  31.9 us
    ppermute x19, waiting for transfers between devices, swap(): return lax.ppermute(value, axis, [(i, i ^ bit) for i in range(size)])  15.7 us
    pallas_call x3, Pallas kernels, sketch_call(): pl.pallas_call(functools.partial(sketch_kernel, ks), in_specs=[pl.BlockSp...  10.8 us
    pallas_call x8, Pallas kernels, part_call(): pl.pallas_call(functools.partial(part_kernel, k, own, tuple(weights), len...  7.4 us
    pallas_call x2, Pallas kernels, block_call(): pl.pallas_call(functools.partial(block_kernel, k), in_specs=[pl.BlockSpec...  4.16 us
  transfers between devices with their start and end apart: 19, of which 8 were waited for; matrix products, arithmetic and copies ran while one was open for 0% of the time, Pallas kernels for 26%

profile of v8, /device:TPU:1, one launch (start us, length us, event | category | flops | bytes accessed | tf_op | source)
XLA Modules:
  0.0 72.3 jit_solution(6635783185447590614)
XLA Ops:
  0.0 0.0 copy-start.1
  0.0 0.7 copy-done.1
  0.7 3.2 %sketch.3 = f32[272,128]{1,0:T(8,128)S(1)} custom-call(bf16[8192,256]{1,0:T(8,128)(2,1)} %scores_ref.5, s32[8192,256]{1,0:T(8,128)} %targets_ref.5, s32[16,256]{1,0:T(8,128)S(1)} %bitcast.13), custom_call_target="tpu_custom_call" | custom-call | flops 100663296 | bytes 3145728 | tf_op jit(solution)/shard_map/sketch/pallas_call | solution.py:99
  3.9 3.7 %collective-permute-start = (f32[272,128]{1,0:T(8,128)S(1)}, f32[272,128]{1,0:T(8,128)S(1)}, u32[]{:S(2)}, u32[]{:S(2)}) collective-permute-start(f32[272,128]{1,0:T(8,128)S(1)} %sketch.3), channel_id=1, source_target_pairs={{0,4},{2,6},{4,0},{6,2},{1,5},{3,7},{5,1},{7,3},{8,12},{10,14},{12... | collective-permute-start | bytes 417800 | tf_op jit(solution)/shard_map/ppermute | solution.py:305
  7.5 4.5 %sketch.5 = (f32[272,128]{1,0:T(8,128)S(1)}, f32[272,128]{1,0:T(8,128)S(1)}) custom-call(bf16[8192,256]{1,0:T(8,128)(2,1)} %scores_ref.5, s32[8192,256]{1,0:T(8,128)} %targets_ref.5, s32[16,256]{1,0:T(8,128)S(1)} %bitcast.14), custom_call_target="tpu_custom_call" | custom-call | flops 201326592 | bytes 6291456 | tf_op jit(solution)/shard_map/sketch/pallas_call | solution.py:99
  12.1 0.4 collective-permute-start.1
  12.5 0.0 copy-start
  12.5 0.0 copy-start.2
  12.5 0.7 collective-permute-start.2
  13.1 0.0 collective-permute-done.refs_0_
  13.1 3.2 %sketch.4 = f32[272,128]{1,0:T(8,128)S(1)} custom-call(bf16[8192,256]{1,0:T(8,128)(2,1)} %scores_ref.5, s32[8192,256]{1,0:T(8,128)} %targets_ref.5, s32[16,256]{1,0:T(8,128)S(1)} %bitcast.15, f32[272,128]{1,0:T(8,128)S(1)} %collective-permute-done.refs_0_), custom_call_target="tpu_custom_call" | custom-call | flops 100663296 | bytes 3145728 | tf_op jit(solution)/shard_map/sketch/pallas_call | solution.py:99
  16.3 0.1 collective-permute-done.1
  16.4 1.2 %collective-permute-done.2 = f32[272,128]{1,0:T(8,128)S(1)} collective-permute-done((f32[272,128]{1,0:T(8,128)S(1)}, f32[272,128]{1,0:T(8,128)S(1)}, u32[]{:S(2)}, u32[]{:S(2)}) %collective-permute-start.2) | collective-permute-done | bytes 139296 | tf_op jit(solution)/shard_map/ppermute | solution.py:305
  17.6 1.4 %collective-permute-start.4 = (f32[272,128]{1,0:T(8,128)S(1)}, f32[272,128]{1,0:T(8,128)S(1)}, u32[]{:S(2)}, u32[]{:S(2)}) collective-permute-start(f32[272,128]{1,0:T(8,128)S(1)} %add_add_fusion.1), channel_id=1, source_target_pairs={{0,8},{8,0},{16,24},{24,16},{1,9},{9,1},{17,25},{25,17},{2,10},{10... | collective-permute-start | bytes 417800 | tf_op jit(solution)/shard_map/ppermute | solution.py:305
  19.0 1.9 %collective-permute-start.5 = (f32[272,128]{1,0:T(8,128)S(1)}, f32[272,128]{1,0:T(8,128)S(1)}, u32[]{:S(2)}, u32[]{:S(2)}) collective-permute-start(f32[272,128]{1,0:T(8,128)S(1)} %add_add_fusion.1), channel_id=1, source_target_pairs={{0,24},{8,16},{16,8},{24,0},{1,25},{9,17},{17,9},{25,1},{2,26},{10... | collective-permute-start | bytes 417800 | tf_op jit(solution)/shard_map/ppermute | solution.py:305
  20.9 0.7 collective-permute-start.3
  21.6 0.0 collective-permute-done.4
  21.6 2.5 %collective-permute-done.5 = f32[272,128]{1,0:T(8,128)S(1)} collective-permute-done((f32[272,128]{1,0:T(8,128)S(1)}, f32[272,128]{1,0:T(8,128)S(1)}, u32[]{:S(2)}, u32[]{:S(2)}) %collective-permute-start.5) | collective-permute-done | bytes 139296 | tf_op jit(solution)/shard_map/ppermute | solution.py:305
  24.1 3.1 %collective-permute-done.3 = f32[272,128]{1,0:T(8,128)S(1)} collective-permute-done((f32[272,128]{1,0:T(8,128)S(1)}, f32[272,128]{1,0:T(8,128)S(1)}, u32[]{:S(2)}, u32[]{:S(2)}) %collective-permute-start.3) | collective-permute-done | bytes 139296 | tf_op jit(solution)/shard_map/ppermute | solution.py:305
  27.3 7.0 %collective-permute-start.6 = (f32[272,128]{1,0:T(8,128)S(1)}, f32[272,128]{1,0:T(8,128)S(1)}, u32[]{:S(2)}, u32[]{:S(2)}) collective-permute-start(f32[272,128]{1,0:T(8,128)S(1)} %add_add_fusion), channel_id=1, source_target_pairs={{0,1},{1,0},{2,3},{3,2},{4,5},{5,4},{6,7},{7,6},{8,9},{9,8},{10,11... | collective-permute-start | bytes 417800 | tf_op jit(solution)/shard_map/ppermute | solution.py:305
  34.3 2.5 %collective-permute-done.6 = f32[272,128]{1,0:T(8,128)S(1)} collective-permute-done((f32[272,128]{1,0:T(8,128)S(1)}, f32[272,128]{1,0:T(8,128)S(1)}, u32[]{:S(2)}, u32[]{:S(2)}) %collective-permute-start.6) | collective-permute-done | bytes 139296 | tf_op jit(solution)/shard_map/ppermute | solution.py:305
  36.9 0.6 collective-permute-start.7
  37.4 1.3 %collective-permute-start.8 = (f32[272,128]{1,0:T(8,128)S(1)}, f32[272,128]{1,0:T(8,128)S(1)}, u32[]{:S(2)}, u32[]{:S(2)}) collective-permute-start(f32[272,128]{1,0:T(8,128)S(1)} %add.26.stats_ref), channel_id=1, source_target_pairs={{0,6},{2,4},{4,2},{6,0},{1,7},{3,5},{5,3},{7,1},{8,14},{10,12},{12... | collective-permute-start | bytes 417800 | tf_op jit(solution)/shard_map/ppermute | solution.py:305
  38.7 1.5 %collective-permute-start.9 = (f32[272,128]{1,0:T(8,128)S(1)}, f32[272,128]{1,0:T(8,128)S(1)}, u32[]{:S(2)}, u32[]{:S(2)}) collective-permute-start(f32[272,128]{1,0:T(8,128)S(1)} %add.26.stats_ref), channel_id=1, source_target_pairs={{0,4},{2,6},{4,0},{6,2},{1,5},{3,7},{5,1},{7,3},{8,12},{10,14},{12... | collective-permute-start | bytes 417800 | tf_op jit(solution)/shard_map/ppermute | solution.py:305
  40.2 0.0 copy-done
  40.2 0.0 copy-done.2
  40.2 2.1 %block.2 = (f32[6,136,256]{2,1,0:T(8,128)S(1)}, f8e4m3fn[288,2048]{1,0:T(32,128)(4,1)S(1)}) custom-call(s32[16,8192]{1,0:T(8,128)S(1)} %bitcast.3, f32[272,128]{1,0:T(8,128)S(1)} %add.26.stats_ref, s32[64,128]{1,0:T(8,128)S(1)} %bitcast.16), custom_call_target="tpu_custom_call" | custom-call | flops 5000000000 | bytes 1000000 | tf_op jit(solution)/shard_map/block/pallas_call | solution.py:223
  42.3 0.0 collective-permute-done.7.stats_ref
  42.3 2.1 %block.3 = (f32[6,136,256]{2,1,0:T(8,128)S(1)}, f8e4m3fn[288,2048]{1,0:T(32,128)(4,1)S(1)}) custom-call(s32[16,8192]{1,0:T(8,128)S(1)} %bitcast.4, f32[272,128]{1,0:T(8,128)S(1)} %collective-permute-done.7.stats_ref, s32[64,128]{1,0:T(8,128)S(1)} %bitcast.17, f32[6,136,256]{2,1,0:T(8,128)S(1)} %get-tuple-element.34.refs_0_), custom_call_target="tpu_custom_call" | custom-call | flops 5000000000 | bytes 1000000 | tf_op jit(solution)/shard_map/block/pallas_call | solution.py:223
  44.4 0.0 collective-permute-done.8.refs_0_
  44.4 0.0 collective-permute-done.9.refs_1_
  44.4 0.6 weights.1.refs_0_.refs_2_
  45.0 0.8 %other.6 = f32[136,256]{1,0:T(8,128)S(1)} custom-call(s32[16,8192]{1,0:T(8,128)S(1)} %bitcast.5, f8e4m3fn[288,4096]{1,0:T(32,128)(4,1)S(1)} %weights.1.refs_0_.refs_2_, f32[6,136,256]{2,1,0:T(8,128)S(1)} %get-tuple-element.41.refs_1_), custom_call_target="tpu_custom_call" | custom-call | flops 1000 | bytes 1000 | tf_op jit(solution)/shard_map/other/pallas_call | solution.py:253
  45.8 5.9 %collective-permute-start.10 = (f32[136,256]{1,0:T(8,128)S(1)}, f32[136,256]{1,0:T(8,128)S(1)}, u32[]{:S(2)}, u32[]{:S(2)}) collective-permute-start(f32[136,256]{1,0:T(8,128)S(1)} %other.6), channel_id=1, source_target_pairs={{0,32},{32,0},{1,33},{33,1},{2,34},{34,2},{3,35},{35,3},{4,36},{36... | collective-permute-start | bytes 417800 | tf_op jit(solution)/shard_map/ppermute | solution.py:305
  51.7 0.8 %other.4 = f32[136,256]{1,0:T(8,128)S(1)} custom-call(s32[16,8192]{1,0:T(8,128)S(1)} %bitcast.6, f8e4m3fn[288,4096]{1,0:T(32,128)(4,1)S(1)} %weights.1.refs_0_.refs_2_, f32[6,136,256]{2,1,0:T(8,128)S(1)} %get-tuple-element.41.refs_1_), custom_call_target="tpu_custom_call" | custom-call | flops 1000 | bytes 1000 | tf_op jit(solution)/shard_map/other/pallas_call | solution.py:253
  52.5 0.8 %other.5 = f32[136,256]{1,0:T(8,128)S(1)} custom-call(s32[16,8192]{1,0:T(8,128)S(1)} %bitcast.7, f8e4m3fn[288,4096]{1,0:T(32,128)(4,1)S(1)} %weights.1.refs_0_.refs_2_, f32[6,136,256]{2,1,0:T(8,128)S(1)} %get-tuple-element.41.refs_1_), custom_call_target="tpu_custom_call" | custom-call | flops 1000 | bytes 1000 | tf_op jit(solution)/shard_map/other/pallas_call | solution.py:253
  53.3 0.1 collective-permute-start.11
  53.4 0.5 collective-permute-start.15
  53.9 0.0 collective-permute-done.10.refs_2_
  53.9 0.8 %own.4 = (f32[64,256]{1,0:T(8,128)S(1)}, f32[72,256]{1,0:T(8,128)S(1)}) custom-call(s32[16,8192]{1,0:T(8,128)S(1)} %bitcast.8, f8e4m3fn[288,4096]{1,0:T(32,128)(4,1)S(1)} %weights.1.refs_0_.refs_2_, f32[6,136,256]{2,1,0:T(8,128)S(1)} %get-tuple-element.41.refs_1_, f32[136,256]{1,0:T(8,128)S(1)} %collective-permute-done.10.refs_2_), custom_call_target="tpu_custom_call" | custom-call | flops 1000 | bytes 1000 | tf_op jit(solution)/shard_map/own/pallas_call | solution.py:253
  54.6 0.8 %collective-permute-start.13 = (f32[64,256]{1,0:T(8,128)S(1)}, f32[64,256]{1,0:T(8,128)S(1)}, u32[]{:S(2)}, u32[]{:S(2)}) collective-permute-start(f32[64,256]{1,0:T(8,128)S(1)} %get-tuple-element.48), channel_id=1, source_target_pairs={{0,64},{64,0},{128,192},{192,128},{1,65},{65,1},{129,193},{193,129... | collective-permute-start | bytes 196616 | tf_op jit(solution)/shard_map/ppermute | solution.py:305
  55.4 0.8 %collective-permute-start.17 = (f32[72,256]{1,0:T(8,128)S(1)}, f32[72,256]{1,0:T(8,128)S(1)}, u32[]{:S(2)}, u32[]{:S(2)}) collective-permute-start(f32[72,256]{1,0:T(8,128)S(1)} %get-tuple-element.52), channel_id=1, source_target_pairs={{0,64},{64,0},{128,192},{192,128},{1,65},{65,1},{129,193},{193,129... | collective-permute-start | bytes 221192 | tf_op jit(solution)/shard_map/ppermute | solution.py:305
  56.2 0.0 collective-permute-done.11.refs_2_
  56.2 0.8 %own.5 = (f32[64,256]{1,0:T(8,128)S(1)}, f32[72,256]{1,0:T(8,128)S(1)}) custom-call(s32[16,8192]{1,0:T(8,128)S(1)} %bitcast.9, f8e4m3fn[288,4096]{1,0:T(32,128)(4,1)S(1)} %weights.1.refs_0_.refs_2_, f32[6,136,256]{2,1,0:T(8,128)S(1)} %get-tuple-element.41.refs_1_, f32[136,256]{1,0:T(8,128)S(1)} %collective-permute-done.11.refs_2_), custom_call_target="tpu_custom_call" | custom-call | flops 1000 | bytes 1000 | tf_op jit(solution)/shard_map/own/pallas_call | solution.py:253
  57.0 1.4 %other.7 = f32[136,256]{1,0:T(8,128)S(1)} custom-call(s32[16,8192]{1,0:T(8,128)S(1)} %bitcast.10, f8e4m3fn[288,2048]{1,0:T(32,128)(4,1)S(1)} %get-tuple-element.33.refs_0_, f8e4m3fn[288,2048]{1,0:T(32,128)(4,1)S(1)} %get-tuple-element.35.refs_1_, f8e4m3fn[288,4096]{1,0:T(32,128)(4,1)S(1)} %weights.1.refs_0_.refs_2_), custom_call_target="tpu_custom_call" | custom-call | flops 1000 | bytes 1000 | tf_op jit(solution)/shard_map/other/pallas_call | solution.py:253
  58.4 0.9 %collective-permute-start.12 = (f32[136,256]{1,0:T(8,128)S(1)}, f32[136,256]{1,0:T(8,128)S(1)}, u32[]{:S(2)}, u32[]{:S(2)}) collective-permute-start(f32[136,256]{1,0:T(8,128)S(1)} %other.7), channel_id=1, source_target_pairs={{0,32},{32,0},{1,33},{33,1},{2,34},{34,2},{3,35},{35,3},{4,36},{36... | collective-permute-start | bytes 417800 | tf_op jit(solution)/shard_map/ppermute | solution.py:305
  59.3 0.0 collective-permute-done.15.refs_2_
  59.3 0.8 %own.7 = f32[136,256]{1,0:T(8,128)S(1)} custom-call(s32[16,8192]{1,0:T(8,128)S(1)} %bitcast.11, f8e4m3fn[288,4096]{1,0:T(32,128)(4,1)S(1)} %weights.1.refs_0_.refs_2_, f32[6,136,256]{2,1,0:T(8,128)S(1)} %get-tuple-element.41.refs_1_, f32[136,256]{1,0:T(8,128)S(1)} %collective-permute-done.15.refs_2_), custom_call_target="tpu_custom_call" | custom-call | flops 1000 | bytes 1000 | tf_op jit(solution)/shard_map/own/pallas_call | solution.py:253
  60.1 0.8 %collective-permute-start.16 = (f32[136,256]{1,0:T(8,128)S(1)}, f32[136,256]{1,0:T(8,128)S(1)}, u32[]{:S(2)}, u32[]{:S(2)}) collective-permute-start(f32[136,256]{1,0:T(8,128)S(1)} %own.7), channel_id=1, source_target_pairs={{0,64},{64,0},{128,192},{192,128},{1,65},{65,1},{129,193},{193,129... | collective-permute-start | bytes 417800 | tf_op jit(solution)/shard_map/ppermute | solution.py:305
  60.9 0.0 collective-permute-done.13.b_ref
  60.9 2.8 %collective-permute-start.14 = (f32[64,256]{1,0:T(8,128)S(1)}, f32[64,256]{1,0:T(8,128)S(1)}, u32[]{:S(2)}, u32[]{:S(2)}) collective-permute-start(f32[64,256]{1,0:T(8,128)S(1)} %add.32), channel_id=1, source_target_pairs={{0,128},{64,192},{128,0},{192,64},{1,129},{65,193},{129,1},{193,65... | collective-permute-start | bytes 196616 | tf_op jit(solution)/shard_map/ppermute | solution.py:305
  63.8 0.0 collective-permute-done.17.b_ref
  63.8 0.1 collective-permute-start.18
  63.9 0.0 collective-permute-done.12.refs_3_
  63.9 1.4 %own.6 = (f32[64,256]{1,0:T(8,128)S(1)}, f32[72,256]{1,0:T(8,128)S(1)}) custom-call(s32[16,8192]{1,0:T(8,128)S(1)} %bitcast.12, f8e4m3fn[288,2048]{1,0:T(32,128)(4,1)S(1)} %get-tuple-element.33.refs_0_, f8e4m3fn[288,2048]{1,0:T(32,128)(4,1)S(1)} %get-tuple-element.35.refs_1_, f8e4m3fn[288,4096]{1,0:T(32,128)(4,1)S(1)} %weights.1.refs_0_.refs_2_, ...), custom_call_target="tpu_custom_call" | custom-call | flops 1000 | bytes 1000 | tf_op jit(solution)/shard_map/own/pallas_call | solution.py:253
  65.3 0.8 %collective-permute-done.14.b_ref = f32[64,256]{1,0:T(8,128)S(1)} collective-permute-done((f32[64,256]{1,0:T(8,128)S(1)}, f32[64,256]{1,0:T(8,128)S(1)}, u32[]{:S(2)}, u32[]{:S(2)}) %collective-permute-start.14) | collective-permute-done | bytes 65568 | tf_op jit(solution)/shard_map/ppermute | solution.py:305
  66.0 0.8 %collective-permute-done.16.moved_ref = f32[136,256]{1,0:T(8,128)S(1)} collective-permute-done((f32[136,256]{1,0:T(8,128)S(1)}, f32[136,256]{1,0:T(8,128)S(1)}, u32[]{:S(2)}, u32[]{:S(2)}) %collective-permute-start.16) | collective-permute-done | bytes 139296 | tf_op jit(solution)/shard_map/ppermute | solution.py:305
  66.9 4.6 %collective-permute-done.18.last_ref = f32[72,256]{1,0:T(8,128)S(1)} collective-permute-done((f32[72,256]{1,0:T(8,128)S(1)}, f32[72,256]{1,0:T(8,128)S(1)}, u32[]{:S(2)}, u32[]{:S(2)}) %collective-permute-start.18) | collective-permute-done | bytes 73760 | tf_op jit(solution)/shard_map/ppermute | solution.py:305
  71.5 0.8 %finish.1 = f32[32,16,68]{2,1,0:T(8,128)} custom-call(f32[64,256]{1,0:T(8,128)S(1)} %add.33.upper_ref, f32[72,256]{1,0:T(8,128)S(1)} %get-tuple-element.49.lower_ref, f32[136,256]{1,0:T(8,128)S(1)} %collective-permute-done.16.moved_ref, f32[72,256]{1,0:T(8,128)S(1)} %collective-permute-done.18.last_ref), custom_call_target="tpu_custom_call" | custom-call | tf_op jit(solution)/shard_map/finish/pallas_call | solution.py:296
  (6 shorter events, 0.1 us)
Async XLA Ops:
  0.0 0.7 copy-start.1
  3.9 9.3 %collective-permute-start = (f32[272,128]{1,0:T(8,128)S(1)}, f32[272,128]{1,0:T(8,128)S(1)}, u32[]{:S(2)}, u32[]{:S(2)}) collective-permute-start(f32[272,128]{1,0:T(8,128)S(1)} %sketch.3), channel_id=1, source_target_pairs={{0,4},{2,6},{4,0},{6,2},{1,5},{3,7},{5,1},{7,3},{8,12},{10,14},{12... | collective-permute-start | bytes 417800 | tf_op jit(solution)/shard_map/ppermute | solution.py:305
  12.1 4.3 %collective-permute-start.1 = (f32[272,128]{1,0:T(8,128)S(1)}, f32[272,128]{1,0:T(8,128)S(1)}, u32[]{:S(2)}, u32[]{:S(2)}) collective-permute-start(f32[272,128]{1,0:T(8,128)S(1)} %get-tuple-element.31), channel_id=1, source_target_pairs={{0,2},{2,0},{4,6},{6,4},{1,3},{3,1},{5,7},{7,5},{8,10},{10,8},{12,... | collective-permute-start | bytes 417800 | tf_op jit(solution)/shard_map/ppermute | solution.py:305
  12.5 27.8 %copy-start = (s32[8192,16]{0,1:T(8,128)S(1)}, s32[8192,16]{0,1:T(8,128)}, u32[]{:S(2)}) copy-start(s32[8192,16]{0,1:T(8,128)} %param.8) | copy-start | bytes 1572868
  12.5 27.8 %copy-start.2 = (s32[8192]{0:T(1024)S(1)}, s32[8192]{0:T(1024)}, u32[]{:S(2)}) copy-start(s32[8192]{0:T(1024)} %param.9) | copy-start | bytes 98308
  12.5 5.1 %collective-permute-start.2 = (f32[272,128]{1,0:T(8,128)S(1)}, f32[272,128]{1,0:T(8,128)S(1)}, u32[]{:S(2)}, u32[]{:S(2)}) collective-permute-start(f32[272,128]{1,0:T(8,128)S(1)} %get-tuple-element.32), channel_id=1, source_target_pairs={{0,6},{2,4},{4,2},{6,0},{1,7},{3,5},{5,3},{7,1},{8,14},{10,12},{12... | collective-permute-start | bytes 417800 | tf_op jit(solution)/shard_map/ppermute | solution.py:305
  17.6 4.0 %collective-permute-start.4 = (f32[272,128]{1,0:T(8,128)S(1)}, f32[272,128]{1,0:T(8,128)S(1)}, u32[]{:S(2)}, u32[]{:S(2)}) collective-permute-start(f32[272,128]{1,0:T(8,128)S(1)} %add_add_fusion.1), channel_id=1, source_target_pairs={{0,8},{8,0},{16,24},{24,16},{1,9},{9,1},{17,25},{25,17},{2,10},{10... | collective-permute-start | bytes 417800 | tf_op jit(solution)/shard_map/ppermute | solution.py:305
  19.0 5.1 %collective-permute-start.5 = (f32[272,128]{1,0:T(8,128)S(1)}, f32[272,128]{1,0:T(8,128)S(1)}, u32[]{:S(2)}, u32[]{:S(2)}) collective-permute-start(f32[272,128]{1,0:T(8,128)S(1)} %add_add_fusion.1), channel_id=1, source_target_pairs={{0,24},{8,16},{16,8},{24,0},{1,25},{9,17},{17,9},{25,1},{2,26},{10... | collective-permute-start | bytes 417800 | tf_op jit(solution)/shard_map/ppermute | solution.py:305
  20.9 6.4 %collective-permute-start.3 = (f32[272,128]{1,0:T(8,128)S(1)}, f32[272,128]{1,0:T(8,128)S(1)}, u32[]{:S(2)}, u32[]{:S(2)}) collective-permute-start(f32[272,128]{1,0:T(8,128)S(1)} %add_add_fusion.1), channel_id=1, source_target_pairs={{0,16},{8,24},{16,0},{24,8},{1,17},{9,25},{17,1},{25,9},{2,18},{10... | collective-permute-start | bytes 417800 | tf_op jit(solution)/shard_map/ppermute | solution.py:305
  27.3 9.6 %collective-permute-start.6 = (f32[272,128]{1,0:T(8,128)S(1)}, f32[272,128]{1,0:T(8,128)S(1)}, u32[]{:S(2)}, u32[]{:S(2)}) collective-permute-start(f32[272,128]{1,0:T(8,128)S(1)} %add_add_fusion), channel_id=1, source_target_pairs={{0,1},{1,0},{2,3},{3,2},{4,5},{5,4},{6,7},{7,6},{8,9},{9,8},{10,11... | collective-permute-start | bytes 417800 | tf_op jit(solution)/shard_map/ppermute | solution.py:305
  36.9 5.4 %collective-permute-start.7 = (f32[272,128]{1,0:T(8,128)S(1)}, f32[272,128]{1,0:T(8,128)S(1)}, u32[]{:S(2)}, u32[]{:S(2)}) collective-permute-start(f32[272,128]{1,0:T(8,128)S(1)} %add.26.stats_ref), channel_id=1, source_target_pairs={{0,2},{2,0},{4,6},{6,4},{1,3},{3,1},{5,7},{7,5},{8,10},{10,8},{12,... | collective-permute-start | bytes 417800 | tf_op jit(solution)/shard_map/ppermute | solution.py:305
  37.4 7.0 %collective-permute-start.8 = (f32[272,128]{1,0:T(8,128)S(1)}, f32[272,128]{1,0:T(8,128)S(1)}, u32[]{:S(2)}, u32[]{:S(2)}) collective-permute-start(f32[272,128]{1,0:T(8,128)S(1)} %add.26.stats_ref), channel_id=1, source_target_pairs={{0,6},{2,4},{4,2},{6,0},{1,7},{3,5},{5,3},{7,1},{8,14},{10,12},{12... | collective-permute-start | bytes 417800 | tf_op jit(solution)/shard_map/ppermute | solution.py:305
  38.7 5.7 %collective-permute-start.9 = (f32[272,128]{1,0:T(8,128)S(1)}, f32[272,128]{1,0:T(8,128)S(1)}, u32[]{:S(2)}, u32[]{:S(2)}) collective-permute-start(f32[272,128]{1,0:T(8,128)S(1)} %add.26.stats_ref), channel_id=1, source_target_pairs={{0,4},{2,6},{4,0},{6,2},{1,5},{3,7},{5,1},{7,3},{8,12},{10,14},{12... | collective-permute-start | bytes 417800 | tf_op jit(solution)/shard_map/ppermute | solution.py:305
  45.8 8.1 %collective-permute-start.10 = (f32[136,256]{1,0:T(8,128)S(1)}, f32[136,256]{1,0:T(8,128)S(1)}, u32[]{:S(2)}, u32[]{:S(2)}) collective-permute-start(f32[136,256]{1,0:T(8,128)S(1)} %other.6), channel_id=1, source_target_pairs={{0,32},{32,0},{1,33},{33,1},{2,34},{34,2},{3,35},{35,3},{4,36},{36... | collective-permute-start | bytes 417800 | tf_op jit(solution)/shard_map/ppermute | solution.py:305
  53.3 3.0 %collective-permute-start.11 = (f32[136,256]{1,0:T(8,128)S(1)}, f32[136,256]{1,0:T(8,128)S(1)}, u32[]{:S(2)}, u32[]{:S(2)}) collective-permute-start(f32[136,256]{1,0:T(8,128)S(1)} %other.4), channel_id=1, source_target_pairs={{0,32},{32,0},{1,33},{33,1},{2,34},{34,2},{3,35},{35,3},{4,36},{36... | collective-permute-start | bytes 417800 | tf_op jit(solution)/shard_map/ppermute | solution.py:305
  53.4 6.0 %collective-permute-start.15 = (f32[136,256]{1,0:T(8,128)S(1)}, f32[136,256]{1,0:T(8,128)S(1)}, u32[]{:S(2)}, u32[]{:S(2)}) collective-permute-start(f32[136,256]{1,0:T(8,128)S(1)} %other.5), channel_id=1, source_target_pairs={{0,32},{32,0},{1,33},{33,1},{2,34},{34,2},{3,35},{35,3},{4,36},{36... | collective-permute-start | bytes 417800 | tf_op jit(solution)/shard_map/ppermute | solution.py:305
  54.6 6.3 %collective-permute-start.13 = (f32[64,256]{1,0:T(8,128)S(1)}, f32[64,256]{1,0:T(8,128)S(1)}, u32[]{:S(2)}, u32[]{:S(2)}) collective-permute-start(f32[64,256]{1,0:T(8,128)S(1)} %get-tuple-element.48), channel_id=1, source_target_pairs={{0,64},{64,0},{128,192},{192,128},{1,65},{65,1},{129,193},{193,129... | collective-permute-start | bytes 196616 | tf_op jit(solution)/shard_map/ppermute | solution.py:305
  55.4 8.3 %collective-permute-start.17 = (f32[72,256]{1,0:T(8,128)S(1)}, f32[72,256]{1,0:T(8,128)S(1)}, u32[]{:S(2)}, u32[]{:S(2)}) collective-permute-start(f32[72,256]{1,0:T(8,128)S(1)} %get-tuple-element.52), channel_id=1, source_target_pairs={{0,64},{64,0},{128,192},{192,128},{1,65},{65,1},{129,193},{193,129... | collective-permute-start | bytes 221192 | tf_op jit(solution)/shard_map/ppermute | solution.py:305
  58.4 5.5 %collective-permute-start.12 = (f32[136,256]{1,0:T(8,128)S(1)}, f32[136,256]{1,0:T(8,128)S(1)}, u32[]{:S(2)}, u32[]{:S(2)}) collective-permute-start(f32[136,256]{1,0:T(8,128)S(1)} %other.7), channel_id=1, source_target_pairs={{0,32},{32,0},{1,33},{33,1},{2,34},{34,2},{3,35},{35,3},{4,36},{36... | collective-permute-start | bytes 417800 | tf_op jit(solution)/shard_map/ppermute | solution.py:305
  60.1 6.8 %collective-permute-start.16 = (f32[136,256]{1,0:T(8,128)S(1)}, f32[136,256]{1,0:T(8,128)S(1)}, u32[]{:S(2)}, u32[]{:S(2)}) collective-permute-start(f32[136,256]{1,0:T(8,128)S(1)} %own.7), channel_id=1, source_target_pairs={{0,64},{64,0},{128,192},{192,128},{1,65},{65,1},{129,193},{193,129... | collective-permute-start | bytes 417800 | tf_op jit(solution)/shard_map/ppermute | solution.py:305
  60.9 5.1 %collective-permute-start.14 = (f32[64,256]{1,0:T(8,128)S(1)}, f32[64,256]{1,0:T(8,128)S(1)}, u32[]{:S(2)}, u32[]{:S(2)}) collective-permute-start(f32[64,256]{1,0:T(8,128)S(1)} %add.32), channel_id=1, source_target_pairs={{0,128},{64,192},{128,0},{192,64},{1,129},{65,193},{129,1},{193,65... | collective-permute-start | bytes 196616 | tf_op jit(solution)/shard_map/ppermute | solution.py:305
  63.8 7.7 %collective-permute-start.18 = (f32[72,256]{1,0:T(8,128)S(1)}, f32[72,256]{1,0:T(8,128)S(1)}, u32[]{:S(2)}, u32[]{:S(2)}) collective-permute-start(f32[72,256]{1,0:T(8,128)S(1)} %add.34), channel_id=1, source_target_pairs={{0,128},{64,192},{128,0},{192,64},{1,129},{65,193},{129,1},{193,65... | collective-permute-start | bytes 221192 | tf_op jit(solution)/shard_map/ppermute | solution.py:305

commit v9 on v6

--- a/solution.py
+++ b/solution.py
@@ -32,7 +32,8 @@
 PART = (2 * LEAVES * (K + 1), HALF)
 ORDER = tuple((k, own) for k in (3, 2, 1, 0) for own in (False, True))
 OTHER_COST = 2_000_000_000
-HIST_COST = (1000, 1000, 5_000_000_000, 1000)
+HIST_COST = (1000, 1000, 1000, 1000)
+ADD_COST = 5_000_000_000
 LAST = (3, 2)
 GROUP = 4
 SKETCH_VMEM = 51 << 20
@@ -266,6 +267,22 @@
     )(bins_t, weights, start, swapped, *more)
 
 
+def add_kernel(a_ref, b_ref, out_ref):
+    out_ref[...] = a_ref[...] + b_ref[...]
+
+
+def add_call(a, b):
+    return pl.pallas_call(
+        add_kernel,
+        in_specs=[pl.BlockSpec(memory_space=pltpu.VMEM)] * 2,
+        out_specs=pl.BlockSpec(memory_space=pltpu.VMEM),
+        out_shape=jax.ShapeDtypeStruct(PART, jnp.float32),
+        compiler_params=pltpu.CompilerParams(vmem_limit_bytes=8 << 20),
+        cost_estimate=pl.CostEstimate(flops=ADD_COST, bytes_accessed=1000, transcendentals=0),
+        name="add",
+    )(a, b)
+
+
 def finish_kernel(a_ref, b_ref, out_ref):
     total = a_ref[...] + b_ref[...]
     for half in range(2):
@@ -315,16 +332,18 @@
     weights = weight_call(LAST, last, leaves2)
 
     far = swap(other_call((3,), bins_t, weights, start), "c", 1, 2)
-    mid = other_call((2, 1), bins_t, weights, start)
+    mid = other_call((2,), bins_t, weights, start)
     mid, start = lax.optimization_barrier((mid, start))
     mid = swap(mid, "c", 1, 2)
     part = hist_call(3, bins_t, weights, start, far, 0)
     part, start = lax.optimization_barrier((part, start))
     passed = swap(part, "zl", 1, 4)
-    near = swap(other_call((0,), bins_t, weights, start), "c", 1, 2)
-    moved1 = swap(hist_call(1, bins_t, weights, start, mid, 1), "zl", 1, 4)
-    moved2 = swap(hist_call(2, bins_t, weights, start, mid, 0, passed), "zl", 2, 4)
-    part = hist_call(0, bins_t, weights, start, near, 0, moved1)
+    near = swap(other_call((1,), bins_t, weights, start), "c", 1, 2)
+    part = hist_call(2, bins_t, weights, start, mid, 0)
+    moved1 = swap(hist_call(1, bins_t, weights, start, near, 0), "zl", 1, 4)
+    moved2 = swap(add_call(part, passed), "zl", 2, 4)
+    home = swap(other_call((0,), bins_t, weights, start), "c", 1, 2)
+    part = hist_call(0, bins_t, weights, start, home, 0, moved1)
     return finish_call((part, moved2))
 
 

time: 69.2 us -> 69.3 us (level)
  the two profiles are of different devices: /device:TPU:2 before, /device:TPU:32 now
where the time goes in v9:
time: 69.3 us; the launch traced here: 69.2 us
  starting transfers between devices  26.5 us (38%)
  Pallas kernels  23.9 us (34%)
  waiting for transfers between devices  17.8 us (26%)
  local copies, waits for them, and re-layouts  0.73 us (1%)
    ppermute x17, starting transfers between devices, swap(): return lax.ppermute(value, axis, [(i, i ^ bit) for i in range(size)])  26.5 us
    ppermute x17, waiting for transfers between devices, swap(): return lax.ppermute(value, axis, [(i, i ^ bit) for i in range(size)])  17.8 us
    pallas_call x3, Pallas kernels, sketch_call(): pl.pallas_call(functools.partial(sketch_kernel, ks), in_specs=[pl.BlockSp...  10.8 us
    pallas_call x2, Pallas kernels, block_call(): pl.pallas_call(functools.partial(block_kernel, k), in_specs=[pl.BlockSpec...  5.44 us
    pallas_call x4, Pallas kernels, other_call(): pl.pallas_call(functools.partial(other_kernel, ks), in_specs=[pl.BlockSpe...  3.1 us
    pallas_call x4, Pallas kernels, hist_call(): pl.pallas_call(functools.partial(hist_kernel, k, place), in_specs=[pl.Blo...  3.08 us
  transfers between devices with their start and end apart: 17, of which 8 were waited for; matrix products, arithmetic and copies ran while one was open for 0% of the time, Pallas kernels for 27%

profile of v9, /device:TPU:32, one launch (start us, length us, event | category | flops | bytes accessed | tf_op | source)
XLA Modules:
  0.0 69.2 jit_solution(12639338165634810835)
XLA Ops:
  0.0 0.0 copy-start.1
  0.0 0.7 %copy-done.1 = s32[256,16]{0,1:T(8,128)S(1)} copy-done((s32[256,16]{0,1:T(8,128)S(1)}, s32[256,16]{0,1:T(8,128)}, u32[]{:S(2)}) %copy-start.1) | copy-done | bytes 16408
  0.7 3.2 %sketch.3 = f32[272,128]{1,0:T(8,128)S(1)} custom-call(bf16[8192,256]{1,0:T(8,128)(2,1)} %scores_ref.5, s32[8192,256]{1,0:T(8,128)} %targets_ref.5, s32[16,256]{1,0:T(8,128)S(1)} %bitcast.13), custom_call_target="tpu_custom_call" | custom-call | flops 100663296 | bytes 3145728 | tf_op jit(solution)/shard_map/sketch/pallas_call | solution.py:98
  3.9 3.1 %collective-permute-start = (f32[272,128]{1,0:T(8,128)S(1)}, f32[272,128]{1,0:T(8,128)S(1)}, u32[]{:S(2)}, u32[]{:S(2)}) collective-permute-start(f32[272,128]{1,0:T(8,128)S(1)} %sketch.3), channel_id=1, source_target_pairs={{0,4},{2,6},{4,0},{6,2},{1,5},{3,7},{5,1},{7,3},{8,12},{10,14},{12... | collective-permute-start | bytes 417800 | tf_op jit(solution)/shard_map/ppermute | solution.py:310
  7.0 4.5 %sketch.5 = (f32[272,128]{1,0:T(8,128)S(1)}, f32[272,128]{1,0:T(8,128)S(1)}) custom-call(bf16[8192,256]{1,0:T(8,128)(2,1)} %scores_ref.5, s32[8192,256]{1,0:T(8,128)} %targets_ref.5, s32[16,256]{1,0:T(8,128)S(1)} %bitcast.14), custom_call_target="tpu_custom_call" | custom-call | flops 201326592 | bytes 6291456 | tf_op jit(solution)/shard_map/sketch/pallas_call | solution.py:98
  11.5 0.7 collective-permute-start.1
  12.2 0.6 collective-permute-start.2
  12.8 0.0 collective-permute-done.refs_0_
  12.8 3.2 %sketch.4 = f32[272,128]{1,0:T(8,128)S(1)} custom-call(bf16[8192,256]{1,0:T(8,128)(2,1)} %scores_ref.5, s32[8192,256]{1,0:T(8,128)} %targets_ref.5, s32[16,256]{1,0:T(8,128)S(1)} %bitcast.15, f32[272,128]{1,0:T(8,128)S(1)} %collective-permute-done.refs_0_), custom_call_target="tpu_custom_call" | custom-call | flops 100663296 | bytes 3145728 | tf_op jit(solution)/shard_map/sketch/pallas_call | solution.py:98
  16.0 0.0 copy-start
  16.0 0.0 copy-start.2
  16.0 0.7 collective-permute-done.1
  16.7 1.7 %collective-permute-done.2 = f32[272,128]{1,0:T(8,128)S(1)} collective-permute-done((f32[272,128]{1,0:T(8,128)S(1)}, f32[272,128]{1,0:T(8,128)S(1)}, u32[]{:S(2)}, u32[]{:S(2)}) %collective-permute-start.2) | collective-permute-done | bytes 139296 | tf_op jit(solution)/shard_map/ppermute | solution.py:310
  18.5 3.3 %collective-permute-start.3 = (f32[272,128]{1,0:T(8,128)S(1)}, f32[272,128]{1,0:T(8,128)S(1)}, u32[]{:S(2)}, u32[]{:S(2)}) collective-permute-start(f32[272,128]{1,0:T(8,128)S(1)} %add_add_fusion.1), channel_id=1, source_target_pairs={{0,16},{8,24},{16,0},{24,8},{1,17},{9,25},{17,1},{25,9},{2,18},{10... | collective-permute-start | bytes 417800 | tf_op jit(solution)/shard_map/ppermute | solution.py:310
  21.8 0.7 collective-permute-start.4
  22.4 0.4 collective-permute-start.5
  22.8 3.0 %collective-permute-done.3 = f32[272,128]{1,0:T(8,128)S(1)} collective-permute-done((f32[272,128]{1,0:T(8,128)S(1)}, f32[272,128]{1,0:T(8,128)S(1)}, u32[]{:S(2)}, u32[]{:S(2)}) %collective-permute-start.3) | collective-permute-done | bytes 139296 | tf_op jit(solution)/shard_map/ppermute | solution.py:310
  25.8 1.3 %collective-permute-done.4 = f32[272,128]{1,0:T(8,128)S(1)} collective-permute-done((f32[272,128]{1,0:T(8,128)S(1)}, f32[272,128]{1,0:T(8,128)S(1)}, u32[]{:S(2)}, u32[]{:S(2)}) %collective-permute-start.4) | collective-permute-done | bytes 139296 | tf_op jit(solution)/shard_map/ppermute | solution.py:310
  27.1 1.6 %collective-permute-done.5 = f32[272,128]{1,0:T(8,128)S(1)} collective-permute-done((f32[272,128]{1,0:T(8,128)S(1)}, f32[272,128]{1,0:T(8,128)S(1)}, u32[]{:S(2)}, u32[]{:S(2)}) %collective-permute-start.5) | collective-permute-done | bytes 139296 | tf_op jit(solution)/shard_map/ppermute | solution.py:310
  28.8 6.4 %collective-permute-start.6 = (f32[272,128]{1,0:T(8,128)S(1)}, f32[272,128]{1,0:T(8,128)S(1)}, u32[]{:S(2)}, u32[]{:S(2)}) collective-permute-start(f32[272,128]{1,0:T(8,128)S(1)} %add_add_fusion), channel_id=1, source_target_pairs={{0,1},{1,0},{2,3},{3,2},{4,5},{5,4},{6,7},{7,6},{8,9},{9,8},{10,11... | collective-permute-start | bytes 417800 | tf_op jit(solution)/shard_map/ppermute | solution.py:310
  35.1 3.8 %collective-permute-done.6 = f32[272,128]{1,0:T(8,128)S(1)} collective-permute-done((f32[272,128]{1,0:T(8,128)S(1)}, f32[272,128]{1,0:T(8,128)S(1)}, u32[]{:S(2)}, u32[]{:S(2)}) %collective-permute-start.6) | collective-permute-done | bytes 139296 | tf_op jit(solution)/shard_map/ppermute | solution.py:310
  38.9 0.5 collective-permute-start.9
  39.4 1.2 %collective-permute-start.7 = (f32[272,128]{1,0:T(8,128)S(1)}, f32[272,128]{1,0:T(8,128)S(1)}, u32[]{:S(2)}, u32[]{:S(2)}) collective-permute-start(f32[272,128]{1,0:T(8,128)S(1)} %add.24.stats_ref), channel_id=1, source_target_pairs={{0,6},{2,4},{4,2},{6,0},{1,7},{3,5},{5,3},{7,1},{8,14},{10,12},{12... | collective-permute-start | bytes 417800 | tf_op jit(solution)/shard_map/ppermute | solution.py:310
  40.6 2.5 %collective-permute-start.8 = (f32[272,128]{1,0:T(8,128)S(1)}, f32[272,128]{1,0:T(8,128)S(1)}, u32[]{:S(2)}, u32[]{:S(2)}) collective-permute-start(f32[272,128]{1,0:T(8,128)S(1)} %add.24.stats_ref), channel_id=1, source_target_pairs={{0,4},{2,6},{4,0},{6,2},{1,5},{3,7},{5,1},{7,3},{8,12},{10,14},{12... | collective-permute-start | bytes 417800 | tf_op jit(solution)/shard_map/ppermute | solution.py:310
  43.1 0.0 copy-done
  43.1 0.0 copy-done.2
  43.1 2.7 %block.2.refs_0_ = f32[8,136,256]{2,1,0:T(8,128)S(1)} custom-call(s32[16,8192]{1,0:T(8,128)S(1)} %bitcast.3, f32[272,128]{1,0:T(8,128)S(1)} %add.24.stats_ref, s32[64,128]{1,0:T(8,128)S(1)} %bitcast.16), custom_call_target="tpu_custom_call" | custom-call | flops 5000000000 | bytes 1000000 | tf_op jit(solution)/shard_map/block/pallas_call | solution.py:219
  45.8 0.0 collective-permute-done.9.stats_ref
  45.9 2.7 %block.3.start_ref = f32[8,136,256]{2,1,0:T(8,128)S(1)} custom-call(s32[16,8192]{1,0:T(8,128)S(1)} %bitcast.4, f32[272,128]{1,0:T(8,128)S(1)} %collective-permute-done.9.stats_ref, s32[64,128]{1,0:T(8,128)S(1)} %bitcast.17, f32[8,136,256]{2,1,0:T(8,128)S(1)} %block.2.refs_0_), custom_call_target="tpu_custom_call" | custom-call | flops 5000000000 | bytes 1000000 | tf_op jit(solution)/shard_map/block/pallas_call | solution.py:219
  48.6 0.0 collective-permute-done.7.refs_0_
  48.6 0.0 collective-permute-done.8.refs_1_
  48.6 0.6 weights.1.weights_ref
  49.2 0.8 %other.5 = f32[1,136,256]{2,1,0:T(8,128)S(1)} custom-call(s32[16,8192]{1,0:T(8,128)S(1)} %bitcast.5, f8e4m3fn[288,4096]{1,0:T(32,128)(4,1)S(1)} %weights.1.weights_ref, f32[8,136,256]{2,1,0:T(8,128)S(1)} %block.3.start_ref), custom_call_target="tpu_custom_call" | custom-call | flops 2000000000 | bytes 1000 | tf_op jit(solution)/shard_map/other/pallas_call | solution.py:238
  50.0 0.1 collective-permute-start.10
  50.1 0.8 %other.4 = f32[1,136,256]{2,1,0:T(8,128)S(1)} custom-call(s32[16,8192]{1,0:T(8,128)S(1)} %bitcast.6, f8e4m3fn[288,4096]{1,0:T(32,128)(4,1)S(1)} %weights.1.weights_ref, f32[8,136,256]{2,1,0:T(8,128)S(1)} %block.3.start_ref), custom_call_target="tpu_custom_call" | custom-call | flops 2000000000 | bytes 1000 | tf_op jit(solution)/shard_map/other/pallas_call | solution.py:238
  50.8 0.6 collective-permute-start.14
  51.4 0.0 collective-permute-done.10.swapped_ref
  51.4 0.8 %hist.4 = f32[136,256]{1,0:T(8,128)S(1)} custom-call(s32[16,8192]{1,0:T(8,128)S(1)} %bitcast.7, f8e4m3fn[288,4096]{1,0:T(32,128)(4,1)S(1)} %weights.1.weights_ref, f32[8,136,256]{2,1,0:T(8,128)S(1)} %block.3.start_ref, f32[1,136,256]{2,1,0:T(8,128)S(1)} %collective-permute-done.10.swapped_ref), custom_call_target="tpu_custom_call" | custom-call | flops 1000 | bytes 1000 | tf_op jit(solution)/shard_map/hist/pallas_call | solution.py:259
  52.2 1.5 %collective-permute-start.15 = (f32[136,256]{1,0:T(8,128)S(1)}, f32[136,256]{1,0:T(8,128)S(1)}, u32[]{:S(2)}, u32[]{:S(2)}) collective-permute-start(f32[136,256]{1,0:T(8,128)S(1)} %hist.4), channel_id=1, source_target_pairs={{0,64},{64,0},{128,192},{192,128},{1,65},{65,1},{129,193},{193,129... | collective-permute-start | bytes 417800 | tf_op jit(solution)/shard_map/ppermute | solution.py:310
  53.7 0.8 %other.7 = f32[1,136,256]{2,1,0:T(8,128)S(1)} custom-call(s32[16,8192]{1,0:T(8,128)S(1)} %bitcast.8, f8e4m3fn[288,4096]{1,0:T(32,128)(4,1)S(1)} %weights.1.weights_ref, f32[8,136,256]{2,1,0:T(8,128)S(1)} %block.3.start_ref), custom_call_target="tpu_custom_call" | custom-call | flops 2000000000 | bytes 1000 | tf_op jit(solution)/shard_map/other/pallas_call | solution.py:238
  54.4 0.1 collective-permute-start.12
  54.5 0.8 %other.6 = f32[1,136,256]{2,1,0:T(8,128)S(1)} custom-call(s32[16,8192]{1,0:T(8,128)S(1)} %bitcast.9, f8e4m3fn[288,4096]{1,0:T(32,128)(4,1)S(1)} %weights.1.weights_ref, f32[8,136,256]{2,1,0:T(8,128)S(1)} %block.3.start_ref), custom_call_target="tpu_custom_call" | custom-call | flops 2000000000 | bytes 1000 | tf_op jit(solution)/shard_map/other/pallas_call | solution.py:238
  55.3 0.8 %collective-permute-start.11 = (f32[1,136,256]{2,1,0:T(8,128)S(1)}, f32[1,136,256]{2,1,0:T(8,128)S(1)}, u32[]{:S(2)}, u32[]{:S(2)}) collective-permute-start(f32[1,136,256]{2,1,0:T(8,128)S(1)} %other.6), channel_id=1, source_target_pairs={{0,32},{32,0},{1,33},{33,1},{2,34},{34,2},{3,35},{35,3},{4,36},{36... | collective-permute-start | bytes 417800 | tf_op jit(solution)/shard_map/ppermute | solution.py:310
  56.1 0.0 collective-permute-done.14.swapped_ref
  56.1 0.8 %hist.7.a_ref = f32[136,256]{1,0:T(8,128)S(1)} custom-call(s32[16,8192]{1,0:T(8,128)S(1)} %bitcast.10, f8e4m3fn[288,4096]{1,0:T(32,128)(4,1)S(1)} %weights.1.weights_ref, f32[8,136,256]{2,1,0:T(8,128)S(1)} %block.3.start_ref, f32[1,136,256]{2,1,0:T(8,128)S(1)} %collective-permute-done.14.swapped_ref), custom_call_target="tpu_custom_call" | custom-call | flops 1000 | bytes 1000 | tf_op jit(solution)/shard_map/hist/pallas_call | solution.py:259
  56.9 0.0 collective-permute-done.12.swapped_ref
  56.9 0.8 %hist.5 = f32[136,256]{1,0:T(8,128)S(1)} custom-call(s32[16,8192]{1,0:T(8,128)S(1)} %bitcast.11, f8e4m3fn[288,4096]{1,0:T(32,128)(4,1)S(1)} %weights.1.weights_ref, f32[8,136,256]{2,1,0:T(8,128)S(1)} %block.3.start_ref, f32[1,136,256]{2,1,0:T(8,128)S(1)} %collective-permute-done.12.swapped_ref), custom_call_target="tpu_custom_call" | custom-call | flops 1000 | bytes 1000 | tf_op jit(solution)/shard_map/hist/pallas_call | solution.py:259
  57.7 0.7 %collective-permute-start.13 = (f32[136,256]{1,0:T(8,128)S(1)}, f32[136,256]{1,0:T(8,128)S(1)}, u32[]{:S(2)}, u32[]{:S(2)}) collective-permute-start(f32[136,256]{1,0:T(8,128)S(1)} %hist.5), channel_id=1, source_target_pairs={{0,64},{64,0},{128,192},{192,128},{1,65},{65,1},{129,193},{193,129... | collective-permute-start | bytes 417800 | tf_op jit(solution)/shard_map/ppermute | solution.py:310
  58.4 0.0 collective-permute-done.15.b_ref
  58.4 3.4 %collective-permute-start.16 = (f32[136,256]{1,0:T(8,128)S(1)}, f32[136,256]{1,0:T(8,128)S(1)}, u32[]{:S(2)}, u32[]{:S(2)}) collective-permute-start(f32[136,256]{1,0:T(8,128)S(1)} %add.30), channel_id=1, source_target_pairs={{0,128},{64,192},{128,0},{192,64},{1,129},{65,193},{129,1},{193,65... | collective-permute-start | bytes 417800 | tf_op jit(solution)/shard_map/ppermute | solution.py:310
  61.9 0.0 collective-permute-done.11.swapped_ref
  61.9 2.7 %collective-permute-done.13.refs_0_ = f32[136,256]{1,0:T(8,128)S(1)} collective-permute-done((f32[136,256]{1,0:T(8,128)S(1)}, f32[136,256]{1,0:T(8,128)S(1)}, u32[]{:S(2)}, u32[]{:S(2)}) %collective-permute-start.13) | collective-permute-done | bytes 139296 | tf_op jit(solution)/shard_map/ppermute | solution.py:310
  64.6 0.8 %hist.6.a_ref = f32[136,256]{1,0:T(8,128)S(1)} custom-call(s32[16,8192]{1,0:T(8,128)S(1)} %bitcast.12, f8e4m3fn[288,4096]{1,0:T(32,128)(4,1)S(1)} %weights.1.weights_ref, f32[8,136,256]{2,1,0:T(8,128)S(1)} %block.3.start_ref, f32[1,136,256]{2,1,0:T(8,128)S(1)} %collective-permute-done.11.swapped_ref, f32[136,256]{1,0:T(8,128)S(1)} %collective-permute-done.13.refs_0_), custom_call_target="tpu_custom_call" | custom-call | flops 1000 | bytes 1000 | tf_op jit(solution)/shard_map/hist/pallas_call | solution.py:259
  65.3 3.0 %collective-permute-done.16.b_ref = f32[136,256]{1,0:T(8,128)S(1)} collective-permute-done((f32[136,256]{1,0:T(8,128)S(1)}, f32[136,256]{1,0:T(8,128)S(1)}, u32[]{:S(2)}, u32[]{:S(2)}) %collective-permute-start.16) | collective-permute-done | bytes 139296 | tf_op jit(solution)/shard_map/ppermute | solution.py:310
  68.3 0.8 %finish.1 = f32[32,16,68]{2,1,0:T(8,128)} custom-call(f32[136,256]{1,0:T(8,128)S(1)} %hist.6.a_ref, f32[136,256]{1,0:T(8,128)S(1)} %collective-permute-done.16.b_ref), custom_call_target="tpu_custom_call" | custom-call | tf_op jit(solution)/shard_map/finish/pallas_call | solution.py:301
  (4 shorter events, 0.1 us)
Async XLA Ops:
  0.0 0.7 %copy-start.1 = (s32[256,16]{0,1:T(8,128)S(1)}, s32[256,16]{0,1:T(8,128)}, u32[]{:S(2)}) copy-start(s32[256,16]{0,1:T(8,128)} %param.7) | copy-start | bytes 49156
  3.9 9.0 %collective-permute-start = (f32[272,128]{1,0:T(8,128)S(1)}, f32[272,128]{1,0:T(8,128)S(1)}, u32[]{:S(2)}, u32[]{:S(2)}) collective-permute-start(f32[272,128]{1,0:T(8,128)S(1)} %sketch.3), channel_id=1, source_target_pairs={{0,4},{2,6},{4,0},{6,2},{1,5},{3,7},{5,1},{7,3},{8,12},{10,14},{12... | collective-permute-start | bytes 417800 | tf_op jit(solution)/shard_map/ppermute | solution.py:310
  11.5 5.2 %collective-permute-start.1 = (f32[272,128]{1,0:T(8,128)S(1)}, f32[272,128]{1,0:T(8,128)S(1)}, u32[]{:S(2)}, u32[]{:S(2)}) collective-permute-start(f32[272,128]{1,0:T(8,128)S(1)} %get-tuple-element.15), channel_id=1, source_target_pairs={{0,2},{2,0},{4,6},{6,4},{1,3},{3,1},{5,7},{7,5},{8,10},{10,8},{12,... | collective-permute-start | bytes 417800 | tf_op jit(solution)/shard_map/ppermute | solution.py:310
  12.2 6.3 %collective-permute-start.2 = (f32[272,128]{1,0:T(8,128)S(1)}, f32[272,128]{1,0:T(8,128)S(1)}, u32[]{:S(2)}, u32[]{:S(2)}) collective-permute-start(f32[272,128]{1,0:T(8,128)S(1)} %get-tuple-element.16), channel_id=1, source_target_pairs={{0,6},{2,4},{4,2},{6,0},{1,7},{3,5},{5,3},{7,1},{8,14},{10,12},{12... | collective-permute-start | bytes 417800 | tf_op jit(solution)/shard_map/ppermute | solution.py:310
  16.0 27.1 %copy-start = (s32[8192,16]{0,1:T(8,128)S(1)}, s32[8192,16]{0,1:T(8,128)}, u32[]{:S(2)}) copy-start(s32[8192,16]{0,1:T(8,128)} %param.8) | copy-start | bytes 1572868
  16.0 27.1 %copy-start.2 = (s32[8192]{0:T(1024)S(1)}, s32[8192]{0:T(1024)}, u32[]{:S(2)}) copy-start(s32[8192]{0:T(1024)} %param.9) | copy-start | bytes 98308
  18.5 7.3 %collective-permute-start.3 = (f32[272,128]{1,0:T(8,128)S(1)}, f32[272,128]{1,0:T(8,128)S(1)}, u32[]{:S(2)}, u32[]{:S(2)}) collective-permute-start(f32[272,128]{1,0:T(8,128)S(1)} %add_add_fusion.1), channel_id=1, source_target_pairs={{0,16},{8,24},{16,0},{24,8},{1,17},{9,25},{17,1},{25,9},{2,18},{10... | collective-permute-start | bytes 417800 | tf_op jit(solution)/shard_map/ppermute | solution.py:310
  21.8 5.3 %collective-permute-start.4 = (f32[272,128]{1,0:T(8,128)S(1)}, f32[272,128]{1,0:T(8,128)S(1)}, u32[]{:S(2)}, u32[]{:S(2)}) collective-permute-start(f32[272,128]{1,0:T(8,128)S(1)} %add_add_fusion.1), channel_id=1, source_target_pairs={{0,8},{8,0},{16,24},{24,16},{1,9},{9,1},{17,25},{25,17},{2,10},{10... | collective-permute-start | bytes 417800 | tf_op jit(solution)/shard_map/ppermute | solution.py:310
  22.4 6.3 %collective-permute-start.5 = (f32[272,128]{1,0:T(8,128)S(1)}, f32[272,128]{1,0:T(8,128)S(1)}, u32[]{:S(2)}, u32[]{:S(2)}) collective-permute-start(f32[272,128]{1,0:T(8,128)S(1)} %add_add_fusion.1), channel_id=1, source_target_pairs={{0,24},{8,16},{16,8},{24,0},{1,25},{9,17},{17,9},{25,1},{2,26},{10... | collective-permute-start | bytes 417800 | tf_op jit(solution)/shard_map/ppermute | solution.py:310
  28.8 10.2 %collective-permute-start.6 = (f32[272,128]{1,0:T(8,128)S(1)}, f32[272,128]{1,0:T(8,128)S(1)}, u32[]{:S(2)}, u32[]{:S(2)}) collective-permute-start(f32[272,128]{1,0:T(8,128)S(1)} %add_add_fusion), channel_id=1, source_target_pairs={{0,1},{1,0},{2,3},{3,2},{4,5},{5,4},{6,7},{7,6},{8,9},{9,8},{10,11... | collective-permute-start | bytes 417800 | tf_op jit(solution)/shard_map/ppermute | solution.py:310
  38.9 6.9 %collective-permute-start.9 = (f32[272,128]{1,0:T(8,128)S(1)}, f32[272,128]{1,0:T(8,128)S(1)}, u32[]{:S(2)}, u32[]{:S(2)}) collective-permute-start(f32[272,128]{1,0:T(8,128)S(1)} %add.24.stats_ref), channel_id=1, source_target_pairs={{0,2},{2,0},{4,6},{6,4},{1,3},{3,1},{5,7},{7,5},{8,10},{10,8},{12,... | collective-permute-start | bytes 417800 | tf_op jit(solution)/shard_map/ppermute | solution.py:310
  39.4 9.2 %collective-permute-start.7 = (f32[272,128]{1,0:T(8,128)S(1)}, f32[272,128]{1,0:T(8,128)S(1)}, u32[]{:S(2)}, u32[]{:S(2)}) collective-permute-start(f32[272,128]{1,0:T(8,128)S(1)} %add.24.stats_ref), channel_id=1, source_target_pairs={{0,6},{2,4},{4,2},{6,0},{1,7},{3,5},{5,3},{7,1},{8,14},{10,12},{12... | collective-permute-start | bytes 417800 | tf_op jit(solution)/shard_map/ppermute | solution.py:310
  40.6 8.0 %collective-permute-start.8 = (f32[272,128]{1,0:T(8,128)S(1)}, f32[272,128]{1,0:T(8,128)S(1)}, u32[]{:S(2)}, u32[]{:S(2)}) collective-permute-start(f32[272,128]{1,0:T(8,128)S(1)} %add.24.stats_ref), channel_id=1, source_target_pairs={{0,4},{2,6},{4,0},{6,2},{1,5},{3,7},{5,1},{7,3},{8,12},{10,14},{12... | collective-permute-start | bytes 417800 | tf_op jit(solution)/shard_map/ppermute | solution.py:310
  50.0 1.5 %collective-permute-start.10 = (f32[1,136,256]{2,1,0:T(8,128)S(1)}, f32[1,136,256]{2,1,0:T(8,128)S(1)}, u32[]{:S(2)}, u32[]{:S(2)}) collective-permute-start(f32[1,136,256]{2,1,0:T(8,128)S(1)} %other.5), channel_id=1, source_target_pairs={{0,32},{32,0},{1,33},{33,1},{2,34},{34,2},{3,35},{35,3},{4,36},{36... | collective-permute-start | bytes 417800 | tf_op jit(solution)/shard_map/ppermute | solution.py:310
  50.8 5.3 %collective-permute-start.14 = (f32[1,136,256]{2,1,0:T(8,128)S(1)}, f32[1,136,256]{2,1,0:T(8,128)S(1)}, u32[]{:S(2)}, u32[]{:S(2)}) collective-permute-start(f32[1,136,256]{2,1,0:T(8,128)S(1)} %other.4), channel_id=1, source_target_pairs={{0,32},{32,0},{1,33},{33,1},{2,34},{34,2},{3,35},{35,3},{4,36},{36... | collective-permute-start | bytes 417800 | tf_op jit(solution)/shard_map/ppermute | solution.py:310
  52.2 6.2 %collective-permute-start.15 = (f32[136,256]{1,0:T(8,128)S(1)}, f32[136,256]{1,0:T(8,128)S(1)}, u32[]{:S(2)}, u32[]{:S(2)}) collective-permute-start(f32[136,256]{1,0:T(8,128)S(1)} %hist.4), channel_id=1, source_target_pairs={{0,64},{64,0},{128,192},{192,128},{1,65},{65,1},{129,193},{193,129... | collective-permute-start | bytes 417800 | tf_op jit(solution)/shard_map/ppermute | solution.py:310
  54.4 2.5 %collective-permute-start.12 = (f32[1,136,256]{2,1,0:T(8,128)S(1)}, f32[1,136,256]{2,1,0:T(8,128)S(1)}, u32[]{:S(2)}, u32[]{:S(2)}) collective-permute-start(f32[1,136,256]{2,1,0:T(8,128)S(1)} %other.7), channel_id=1, source_target_pairs={{0,32},{32,0},{1,33},{33,1},{2,34},{34,2},{3,35},{35,3},{4,36},{36... | collective-permute-start | bytes 417800 | tf_op jit(solution)/shard_map/ppermute | solution.py:310
  55.3 6.5 %collective-permute-start.11 = (f32[1,136,256]{2,1,0:T(8,128)S(1)}, f32[1,136,256]{2,1,0:T(8,128)S(1)}, u32[]{:S(2)}, u32[]{:S(2)}) collective-permute-start(f32[1,136,256]{2,1,0:T(8,128)S(1)} %other.6), channel_id=1, source_target_pairs={{0,32},{32,0},{1,33},{33,1},{2,34},{34,2},{3,35},{35,3},{4,36},{36... | collective-permute-start | bytes 417800 | tf_op jit(solution)/shard_map/ppermute | solution.py:310
  57.7 6.9 %collective-permute-start.13 = (f32[136,256]{1,0:T(8,128)S(1)}, f32[136,256]{1,0:T(8,128)S(1)}, u32[]{:S(2)}, u32[]{:S(2)}) collective-permute-start(f32[136,256]{1,0:T(8,128)S(1)} %hist.5), channel_id=1, source_target_pairs={{0,64},{64,0},{128,192},{192,128},{1,65},{65,1},{129,193},{193,129... | collective-permute-start | bytes 417800 | tf_op jit(solution)/shard_map/ppermute | solution.py:310
  58.4 9.9 %collective-permute-start.16 = (f32[136,256]{1,0:T(8,128)S(1)}, f32[136,256]{1,0:T(8,128)S(1)}, u32[]{:S(2)}, u32[]{:S(2)}) collective-permute-start(f32[136,256]{1,0:T(8,128)S(1)} %add.30), channel_id=1, source_target_pairs={{0,128},{64,192},{128,0},{192,64},{1,129},{65,193},{129,1},{193,65... | collective-permute-start | bytes 417800 | tf_op jit(solution)/shard_map/ppermute | solution.py:310

commit v10 on v9

--- a/solution.py
+++ b/solution.py
@@ -271,14 +271,14 @@
     out_ref[...] = a_ref[...] + b_ref[...]
 
 
-def add_call(a, b):
+def add_call(a, b, cost):
     return pl.pallas_call(
         add_kernel,
         in_specs=[pl.BlockSpec(memory_space=pltpu.VMEM)] * 2,
         out_specs=pl.BlockSpec(memory_space=pltpu.VMEM),
         out_shape=jax.ShapeDtypeStruct(PART, jnp.float32),
         compiler_params=pltpu.CompilerParams(vmem_limit_bytes=8 << 20),
-        cost_estimate=pl.CostEstimate(flops=ADD_COST, bytes_accessed=1000, transcendentals=0),
+        cost_estimate=pl.CostEstimate(flops=cost, bytes_accessed=1000, transcendentals=0),
         name="add",
     )(a, b)
 
@@ -341,10 +341,10 @@
     near = swap(other_call((1,), bins_t, weights, start), "c", 1, 2)
     part = hist_call(2, bins_t, weights, start, mid, 0)
     moved1 = swap(hist_call(1, bins_t, weights, start, near, 0), "zl", 1, 4)
-    moved2 = swap(add_call(part, passed), "zl", 2, 4)
+    moved2 = swap(add_call(part, passed, ADD_COST), "zl", 2, 4)
     home = swap(other_call((0,), bins_t, weights, start), "c", 1, 2)
-    part = hist_call(0, bins_t, weights, start, home, 0, moved1)
-    return finish_call((part, moved2))
+    part = hist_call(0, bins_t, weights, start, home, 0)
+    return finish_call((add_call(part, moved1, ADD_COST), moved2))
 
 
 def solution(mesh):

time: 69.3 us -> 69.3 us (level)
  no operation moved by 1% of the time
where the time goes in v10:
time: 69.3 us; the launch traced here: 69.2 us
  starting transfers between devices  26.5 us (38%)
  Pallas kernels  23.9 us (34%)
  waiting for transfers between devices  17.8 us (26%)
  local copies, waits for them, and re-layouts  0.73 us (1%)
    ppermute x17, starting transfers between devices, swap(): return lax.ppermute(value, axis, [(i, i ^ bit) for i in range(size)])  26.5 us
    ppermute x17, waiting for transfers between devices, swap(): return lax.ppermute(value, axis, [(i, i ^ bit) for i in range(size)])  17.8 us
    pallas_call x3, Pallas kernels, sketch_call(): pl.pallas_call(functools.partial(sketch_kernel, ks), in_specs=[pl.BlockSp...  10.8 us
    pallas_call x2, Pallas kernels, block_call(): pl.pallas_call(functools.partial(block_kernel, k), in_specs=[pl.BlockSpec...  5.44 us
    pallas_call x4, Pallas kernels, other_call(): pl.pallas_call(functools.partial(other_kernel, ks), in_specs=[pl.BlockSpe...  3.1 us
    pallas_call x4, Pallas kernels, hist_call(): pl.pallas_call(functools.partial(hist_kernel, k, place), in_specs=[pl.Blo...  3.08 us
  transfers between devices with their start and end apart: 17, of which 8 were waited for; matrix products, arithmetic and copies ran while one was open for 0% of the time, Pallas kernels for 27%

profile of v10, /device:TPU:32, one launch (start us, length us, event | category | flops | bytes accessed | tf_op | source)
XLA Modules:
  0.0 69.2 jit_solution(10299511786839507461)
XLA Ops:
  0.0 0.0 copy-start.1
  0.0 0.7 %copy-done.1 = s32[256,16]{0,1:T(8,128)S(1)} copy-done((s32[256,16]{0,1:T(8,128)S(1)}, s32[256,16]{0,1:T(8,128)}, u32[]{:S(2)}) %copy-start.1) | copy-done | bytes 16408
  0.7 3.2 %sketch.3 = f32[272,128]{1,0:T(8,128)S(1)} custom-call(bf16[8192,256]{1,0:T(8,128)(2,1)} %scores_ref.5, s32[8192,256]{1,0:T(8,128)} %targets_ref.5, s32[16,256]{1,0:T(8,128)S(1)} %bitcast.13), custom_call_target="tpu_custom_call" | custom-call | flops 100663296 | bytes 3145728 | tf_op jit(solution)/shard_map/sketch/pallas_call | solution.py:98
  3.9 3.1 %collective-permute-start = (f32[272,128]{1,0:T(8,128)S(1)}, f32[272,128]{1,0:T(8,128)S(1)}, u32[]{:S(2)}, u32[]{:S(2)}) collective-permute-start(f32[272,128]{1,0:T(8,128)S(1)} %sketch.3), channel_id=1, source_target_pairs={{0,4},{2,6},{4,0},{6,2},{1,5},{3,7},{5,1},{7,3},{8,12},{10,14},{12... | collective-permute-start | bytes 417800 | tf_op jit(solution)/shard_map/ppermute | solution.py:310
  7.0 4.5 %sketch.5 = (f32[272,128]{1,0:T(8,128)S(1)}, f32[272,128]{1,0:T(8,128)S(1)}) custom-call(bf16[8192,256]{1,0:T(8,128)(2,1)} %scores_ref.5, s32[8192,256]{1,0:T(8,128)} %targets_ref.5, s32[16,256]{1,0:T(8,128)S(1)} %bitcast.14), custom_call_target="tpu_custom_call" | custom-call | flops 201326592 | bytes 6291456 | tf_op jit(solution)/shard_map/sketch/pallas_call | solution.py:98
  11.5 0.7 collective-permute-start.1
  12.2 0.6 collective-permute-start.2
  12.8 0.0 collective-permute-done.refs_0_
  12.8 3.2 %sketch.4 = f32[272,128]{1,0:T(8,128)S(1)} custom-call(bf16[8192,256]{1,0:T(8,128)(2,1)} %scores_ref.5, s32[8192,256]{1,0:T(8,128)} %targets_ref.5, s32[16,256]{1,0:T(8,128)S(1)} %bitcast.15, f32[272,128]{1,0:T(8,128)S(1)} %collective-permute-done.refs_0_), custom_call_target="tpu_custom_call" | custom-call | flops 100663296 | bytes 3145728 | tf_op jit(solution)/shard_map/sketch/pallas_call | solution.py:98
  16.0 0.0 copy-start
  16.0 0.0 copy-start.2
  16.0 0.7 collective-permute-done.1
  16.7 1.7 %collective-permute-done.2 = f32[272,128]{1,0:T(8,128)S(1)} collective-permute-done((f32[272,128]{1,0:T(8,128)S(1)}, f32[272,128]{1,0:T(8,128)S(1)}, u32[]{:S(2)}, u32[]{:S(2)}) %collective-permute-start.2) | collective-permute-done | bytes 139296 | tf_op jit(solution)/shard_map/ppermute | solution.py:310
  18.5 3.3 %collective-permute-start.3 = (f32[272,128]{1,0:T(8,128)S(1)}, f32[272,128]{1,0:T(8,128)S(1)}, u32[]{:S(2)}, u32[]{:S(2)}) collective-permute-start(f32[272,128]{1,0:T(8,128)S(1)} %add_add_fusion.1), channel_id=1, source_target_pairs={{0,16},{8,24},{16,0},{24,8},{1,17},{9,25},{17,1},{25,9},{2,18},{10... | collective-permute-start | bytes 417800 | tf_op jit(solution)/shard_map/ppermute | solution.py:310
  21.8 0.7 collective-permute-start.4
  22.4 0.4 collective-permute-start.5
  22.8 3.0 %collective-permute-done.3 = f32[272,128]{1,0:T(8,128)S(1)} collective-permute-done((f32[272,128]{1,0:T(8,128)S(1)}, f32[272,128]{1,0:T(8,128)S(1)}, u32[]{:S(2)}, u32[]{:S(2)}) %collective-permute-start.3) | collective-permute-done | bytes 139296 | tf_op jit(solution)/shard_map/ppermute | solution.py:310
  25.8 1.3 %collective-permute-done.4 = f32[272,128]{1,0:T(8,128)S(1)} collective-permute-done((f32[272,128]{1,0:T(8,128)S(1)}, f32[272,128]{1,0:T(8,128)S(1)}, u32[]{:S(2)}, u32[]{:S(2)}) %collective-permute-start.4) | collective-permute-done | bytes 139296 | tf_op jit(solution)/shard_map/ppermute | solution.py:310
  27.1 1.6 %collective-permute-done.5 = f32[272,128]{1,0:T(8,128)S(1)} collective-permute-done((f32[272,128]{1,0:T(8,128)S(1)}, f32[272,128]{1,0:T(8,128)S(1)}, u32[]{:S(2)}, u32[]{:S(2)}) %collective-permute-start.5) | collective-permute-done | bytes 139296 | tf_op jit(solution)/shard_map/ppermute | solution.py:310
  28.8 6.4 %collective-permute-start.6 = (f32[272,128]{1,0:T(8,128)S(1)}, f32[272,128]{1,0:T(8,128)S(1)}, u32[]{:S(2)}, u32[]{:S(2)}) collective-permute-start(f32[272,128]{1,0:T(8,128)S(1)} %add_add_fusion), channel_id=1, source_target_pairs={{0,1},{1,0},{2,3},{3,2},{4,5},{5,4},{6,7},{7,6},{8,9},{9,8},{10,11... | collective-permute-start | bytes 417800 | tf_op jit(solution)/shard_map/ppermute | solution.py:310
  35.1 3.8 %collective-permute-done.6 = f32[272,128]{1,0:T(8,128)S(1)} collective-permute-done((f32[272,128]{1,0:T(8,128)S(1)}, f32[272,128]{1,0:T(8,128)S(1)}, u32[]{:S(2)}, u32[]{:S(2)}) %collective-permute-start.6) | collective-permute-done | bytes 139296 | tf_op jit(solution)/shard_map/ppermute | solution.py:310
  38.9 0.5 collective-permute-start.9
  39.4 1.2 %collective-permute-start.7 = (f32[272,128]{1,0:T(8,128)S(1)}, f32[272,128]{1,0:T(8,128)S(1)}, u32[]{:S(2)}, u32[]{:S(2)}) collective-permute-start(f32[272,128]{1,0:T(8,128)S(1)} %add.25.stats_ref), channel_id=1, source_target_pairs={{0,6},{2,4},{4,2},{6,0},{1,7},{3,5},{5,3},{7,1},{8,14},{10,12},{12... | collective-permute-start | bytes 417800 | tf_op jit(solution)/shard_map/ppermute | solution.py:310
  40.6 2.5 %collective-permute-start.8 = (f32[272,128]{1,0:T(8,128)S(1)}, f32[272,128]{1,0:T(8,128)S(1)}, u32[]{:S(2)}, u32[]{:S(2)}) collective-permute-start(f32[272,128]{1,0:T(8,128)S(1)} %add.25.stats_ref), channel_id=1, source_target_pairs={{0,4},{2,6},{4,0},{6,2},{1,5},{3,7},{5,1},{7,3},{8,12},{10,14},{12... | collective-permute-start | bytes 417800 | tf_op jit(solution)/shard_map/ppermute | solution.py:310
  43.1 0.0 copy-done
  43.1 0.0 copy-done.2
  43.1 2.7 %block.2.refs_0_ = f32[8,136,256]{2,1,0:T(8,128)S(1)} custom-call(s32[16,8192]{1,0:T(8,128)S(1)} %bitcast.3, f32[272,128]{1,0:T(8,128)S(1)} %add.25.stats_ref, s32[64,128]{1,0:T(8,128)S(1)} %bitcast.16), custom_call_target="tpu_custom_call" | custom-call | flops 5000000000 | bytes 1000000 | tf_op jit(solution)/shard_map/block/pallas_call | solution.py:219
  45.8 0.0 collective-permute-done.9.stats_ref
  45.9 2.7 %block.3.start_ref = f32[8,136,256]{2,1,0:T(8,128)S(1)} custom-call(s32[16,8192]{1,0:T(8,128)S(1)} %bitcast.4, f32[272,128]{1,0:T(8,128)S(1)} %collective-permute-done.9.stats_ref, s32[64,128]{1,0:T(8,128)S(1)} %bitcast.17, f32[8,136,256]{2,1,0:T(8,128)S(1)} %block.2.refs_0_), custom_call_target="tpu_custom_call" | custom-call | flops 5000000000 | bytes 1000000 | tf_op jit(solution)/shard_map/block/pallas_call | solution.py:219
  48.6 0.0 collective-permute-done.7.refs_0_
  48.6 0.0 collective-permute-done.8.refs_1_
  48.6 0.6 weights.1.weights_ref
  49.2 0.8 %other.5 = f32[1,136,256]{2,1,0:T(8,128)S(1)} custom-call(s32[16,8192]{1,0:T(8,128)S(1)} %bitcast.5, f8e4m3fn[288,4096]{1,0:T(32,128)(4,1)S(1)} %weights.1.weights_ref, f32[8,136,256]{2,1,0:T(8,128)S(1)} %block.3.start_ref), custom_call_target="tpu_custom_call" | custom-call | flops 2000000000 | bytes 1000 | tf_op jit(solution)/shard_map/other/pallas_call | solution.py:238
  50.0 0.1 collective-permute-start.10
  50.1 0.8 %other.4 = f32[1,136,256]{2,1,0:T(8,128)S(1)} custom-call(s32[16,8192]{1,0:T(8,128)S(1)} %bitcast.6, f8e4m3fn[288,4096]{1,0:T(32,128)(4,1)S(1)} %weights.1.weights_ref, f32[8,136,256]{2,1,0:T(8,128)S(1)} %block.3.start_ref), custom_call_target="tpu_custom_call" | custom-call | flops 2000000000 | bytes 1000 | tf_op jit(solution)/shard_map/other/pallas_call | solution.py:238
  50.8 0.6 collective-permute-start.14
  51.4 0.0 collective-permute-done.10.swapped_ref
  51.4 0.8 %hist.4 = f32[136,256]{1,0:T(8,128)S(1)} custom-call(s32[16,8192]{1,0:T(8,128)S(1)} %bitcast.7, f8e4m3fn[288,4096]{1,0:T(32,128)(4,1)S(1)} %weights.1.weights_ref, f32[8,136,256]{2,1,0:T(8,128)S(1)} %block.3.start_ref, f32[1,136,256]{2,1,0:T(8,128)S(1)} %collective-permute-done.10.swapped_ref), custom_call_target="tpu_custom_call" | custom-call | flops 1000 | bytes 1000 | tf_op jit(solution)/shard_map/hist/pallas_call | solution.py:259
  52.2 1.5 %collective-permute-start.15 = (f32[136,256]{1,0:T(8,128)S(1)}, f32[136,256]{1,0:T(8,128)S(1)}, u32[]{:S(2)}, u32[]{:S(2)}) collective-permute-start(f32[136,256]{1,0:T(8,128)S(1)} %hist.4), channel_id=1, source_target_pairs={{0,64},{64,0},{128,192},{192,128},{1,65},{65,1},{129,193},{193,129... | collective-permute-start | bytes 417800 | tf_op jit(solution)/shard_map/ppermute | solution.py:310
  53.7 0.8 %other.7 = f32[1,136,256]{2,1,0:T(8,128)S(1)} custom-call(s32[16,8192]{1,0:T(8,128)S(1)} %bitcast.8, f8e4m3fn[288,4096]{1,0:T(32,128)(4,1)S(1)} %weights.1.weights_ref, f32[8,136,256]{2,1,0:T(8,128)S(1)} %block.3.start_ref), custom_call_target="tpu_custom_call" | custom-call | flops 2000000000 | bytes 1000 | tf_op jit(solution)/shard_map/other/pallas_call | solution.py:238
  54.4 0.1 collective-permute-start.12
  54.5 0.8 %other.6 = f32[1,136,256]{2,1,0:T(8,128)S(1)} custom-call(s32[16,8192]{1,0:T(8,128)S(1)} %bitcast.9, f8e4m3fn[288,4096]{1,0:T(32,128)(4,1)S(1)} %weights.1.weights_ref, f32[8,136,256]{2,1,0:T(8,128)S(1)} %block.3.start_ref), custom_call_target="tpu_custom_call" | custom-call | flops 2000000000 | bytes 1000 | tf_op jit(solution)/shard_map/other/pallas_call | solution.py:238
  55.3 0.8 %collective-permute-start.11 = (f32[1,136,256]{2,1,0:T(8,128)S(1)}, f32[1,136,256]{2,1,0:T(8,128)S(1)}, u32[]{:S(2)}, u32[]{:S(2)}) collective-permute-start(f32[1,136,256]{2,1,0:T(8,128)S(1)} %other.6), channel_id=1, source_target_pairs={{0,32},{32,0},{1,33},{33,1},{2,34},{34,2},{3,35},{35,3},{4,36},{36... | collective-permute-start | bytes 417800 | tf_op jit(solution)/shard_map/ppermute | solution.py:310
  56.1 0.0 collective-permute-done.14.swapped_ref
  56.1 0.8 %hist.7.a_ref = f32[136,256]{1,0:T(8,128)S(1)} custom-call(s32[16,8192]{1,0:T(8,128)S(1)} %bitcast.10, f8e4m3fn[288,4096]{1,0:T(32,128)(4,1)S(1)} %weights.1.weights_ref, f32[8,136,256]{2,1,0:T(8,128)S(1)} %block.3.start_ref, f32[1,136,256]{2,1,0:T(8,128)S(1)} %collective-permute-done.14.swapped_ref), custom_call_target="tpu_custom_call" | custom-call | flops 1000 | bytes 1000 | tf_op jit(solution)/shard_map/hist/pallas_call | solution.py:259
  56.9 0.0 collective-permute-done.12.swapped_ref
  56.9 0.8 %hist.6 = f32[136,256]{1,0:T(8,128)S(1)} custom-call(s32[16,8192]{1,0:T(8,128)S(1)} %bitcast.11, f8e4m3fn[288,4096]{1,0:T(32,128)(4,1)S(1)} %weights.1.weights_ref, f32[8,136,256]{2,1,0:T(8,128)S(1)} %block.3.start_ref, f32[1,136,256]{2,1,0:T(8,128)S(1)} %collective-permute-done.12.swapped_ref), custom_call_target="tpu_custom_call" | custom-call | flops 1000 | bytes 1000 | tf_op jit(solution)/shard_map/hist/pallas_call | solution.py:259
  57.7 0.7 %collective-permute-start.13 = (f32[136,256]{1,0:T(8,128)S(1)}, f32[136,256]{1,0:T(8,128)S(1)}, u32[]{:S(2)}, u32[]{:S(2)}) collective-permute-start(f32[136,256]{1,0:T(8,128)S(1)} %hist.6), channel_id=1, source_target_pairs={{0,64},{64,0},{128,192},{192,128},{1,65},{65,1},{129,193},{193,129... | collective-permute-start | bytes 417800 | tf_op jit(solution)/shard_map/ppermute | solution.py:310
  58.4 0.0 collective-permute-done.15.b_ref
  58.4 3.4 %collective-permute-start.16 = (f32[136,256]{1,0:T(8,128)S(1)}, f32[136,256]{1,0:T(8,128)S(1)}, u32[]{:S(2)}, u32[]{:S(2)}) collective-permute-start(f32[136,256]{1,0:T(8,128)S(1)} %add.32), channel_id=1, source_target_pairs={{0,128},{64,192},{128,0},{192,64},{1,129},{65,193},{129,1},{193,65... | collective-permute-start | bytes 417800 | tf_op jit(solution)/shard_map/ppermute | solution.py:310
  61.9 0.0 collective-permute-done.11.swapped_ref
  61.9 0.8 %hist.5.a_ref = f32[136,256]{1,0:T(8,128)S(1)} custom-call(s32[16,8192]{1,0:T(8,128)S(1)} %bitcast.12, f8e4m3fn[288,4096]{1,0:T(32,128)(4,1)S(1)} %weights.1.weights_ref, f32[8,136,256]{2,1,0:T(8,128)S(1)} %block.3.start_ref, f32[1,136,256]{2,1,0:T(8,128)S(1)} %collective-permute-done.11.swapped_ref), custom_call_target="tpu_custom_call" | custom-call | flops 1000 | bytes 1000 | tf_op jit(solution)/shard_map/hist/pallas_call | solution.py:259
  62.6 1.9 %collective-permute-done.13.b_ref = f32[136,256]{1,0:T(8,128)S(1)} collective-permute-done((f32[136,256]{1,0:T(8,128)S(1)}, f32[136,256]{1,0:T(8,128)S(1)}, u32[]{:S(2)}, u32[]{:S(2)}) %collective-permute-start.13) | collective-permute-done | bytes 139296 | tf_op jit(solution)/shard_map/ppermute | solution.py:310
  64.6 3.7 %collective-permute-done.16.b_ref = f32[136,256]{1,0:T(8,128)S(1)} collective-permute-done((f32[136,256]{1,0:T(8,128)S(1)}, f32[136,256]{1,0:T(8,128)S(1)}, u32[]{:S(2)}, u32[]{:S(2)}) %collective-permute-start.16) | collective-permute-done | bytes 139296 | tf_op jit(solution)/shard_map/ppermute | solution.py:310
  68.3 0.8 %finish.1 = f32[32,16,68]{2,1,0:T(8,128)} custom-call(f32[136,256]{1,0:T(8,128)S(1)} %add.31.a_ref, f32[136,256]{1,0:T(8,128)S(1)} %collective-permute-done.16.b_ref), custom_call_target="tpu_custom_call" | custom-call | tf_op jit(solution)/shard_map/finish/pallas_call | solution.py:301
  (5 shorter events, 0.1 us)
Async XLA Ops:
  0.0 0.7 %copy-start.1 = (s32[256,16]{0,1:T(8,128)S(1)}, s32[256,16]{0,1:T(8,128)}, u32[]{:S(2)}) copy-start(s32[256,16]{0,1:T(8,128)} %param.7) | copy-start | bytes 49156
  3.9 9.0 %collective-permute-start = (f32[272,128]{1,0:T(8,128)S(1)}, f32[272,128]{1,0:T(8,128)S(1)}, u32[]{:S(2)}, u32[]{:S(2)}) collective-permute-start(f32[272,128]{1,0:T(8,128)S(1)} %sketch.3), channel_id=1, source_target_pairs={{0,4},{2,6},{4,0},{6,2},{1,5},{3,7},{5,1},{7,3},{8,12},{10,14},{12... | collective-permute-start | bytes 417800 | tf_op jit(solution)/shard_map/ppermute | solution.py:310
  11.5 5.2 %collective-permute-start.1 = (f32[272,128]{1,0:T(8,128)S(1)}, f32[272,128]{1,0:T(8,128)S(1)}, u32[]{:S(2)}, u32[]{:S(2)}) collective-permute-start(f32[272,128]{1,0:T(8,128)S(1)} %get-tuple-element.15), channel_id=1, source_target_pairs={{0,2},{2,0},{4,6},{6,4},{1,3},{3,1},{5,7},{7,5},{8,10},{10,8},{12,... | collective-permute-start | bytes 417800 | tf_op jit(solution)/shard_map/ppermute | solution.py:310
  12.2 6.3 %collective-permute-start.2 = (f32[272,128]{1,0:T(8,128)S(1)}, f32[272,128]{1,0:T(8,128)S(1)}, u32[]{:S(2)}, u32[]{:S(2)}) collective-permute-start(f32[272,128]{1,0:T(8,128)S(1)} %get-tuple-element.16), channel_id=1, source_target_pairs={{0,6},{2,4},{4,2},{6,0},{1,7},{3,5},{5,3},{7,1},{8,14},{10,12},{12... | collective-permute-start | bytes 417800 | tf_op jit(solution)/shard_map/ppermute | solution.py:310
  16.0 27.1 %copy-start = (s32[8192,16]{0,1:T(8,128)S(1)}, s32[8192,16]{0,1:T(8,128)}, u32[]{:S(2)}) copy-start(s32[8192,16]{0,1:T(8,128)} %param.8) | copy-start | bytes 1572868
  16.0 27.1 %copy-start.2 = (s32[8192]{0:T(1024)S(1)}, s32[8192]{0:T(1024)}, u32[]{:S(2)}) copy-start(s32[8192]{0:T(1024)} %param.9) | copy-start | bytes 98308
  18.5 7.3 %collective-permute-start.3 = (f32[272,128]{1,0:T(8,128)S(1)}, f32[272,128]{1,0:T(8,128)S(1)}, u32[]{:S(2)}, u32[]{:S(2)}) collective-permute-start(f32[272,128]{1,0:T(8,128)S(1)} %add_add_fusion.1), channel_id=1, source_target_pairs={{0,16},{8,24},{16,0},{24,8},{1,17},{9,25},{17,1},{25,9},{2,18},{10... | collective-permute-start | bytes 417800 | tf_op jit(solution)/shard_map/ppermute | solution.py:310
  21.8 5.3 %collective-permute-start.4 = (f32[272,128]{1,0:T(8,128)S(1)}, f32[272,128]{1,0:T(8,128)S(1)}, u32[]{:S(2)}, u32[]{:S(2)}) collective-permute-start(f32[272,128]{1,0:T(8,128)S(1)} %add_add_fusion.1), channel_id=1, source_target_pairs={{0,8},{8,0},{16,24},{24,16},{1,9},{9,1},{17,25},{25,17},{2,10},{10... | collective-permute-start | bytes 417800 | tf_op jit(solution)/shard_map/ppermute | solution.py:310
  22.4 6.3 %collective-permute-start.5 = (f32[272,128]{1,0:T(8,128)S(1)}, f32[272,128]{1,0:T(8,128)S(1)}, u32[]{:S(2)}, u32[]{:S(2)}) collective-permute-start(f32[272,128]{1,0:T(8,128)S(1)} %add_add_fusion.1), channel_id=1, source_target_pairs={{0,24},{8,16},{16,8},{24,0},{1,25},{9,17},{17,9},{25,1},{2,26},{10... | collective-permute-start | bytes 417800 | tf_op jit(solution)/shard_map/ppermute | solution.py:310
  28.8 10.2 %collective-permute-start.6 = (f32[272,128]{1,0:T(8,128)S(1)}, f32[272,128]{1,0:T(8,128)S(1)}, u32[]{:S(2)}, u32[]{:S(2)}) collective-permute-start(f32[272,128]{1,0:T(8,128)S(1)} %add_add_fusion), channel_id=1, source_target_pairs={{0,1},{1,0},{2,3},{3,2},{4,5},{5,4},{6,7},{7,6},{8,9},{9,8},{10,11... | collective-permute-start | bytes 417800 | tf_op jit(solution)/shard_map/ppermute | solution.py:310
  38.9 6.9 %collective-permute-start.9 = (f32[272,128]{1,0:T(8,128)S(1)}, f32[272,128]{1,0:T(8,128)S(1)}, u32[]{:S(2)}, u32[]{:S(2)}) collective-permute-start(f32[272,128]{1,0:T(8,128)S(1)} %add.25.stats_ref), channel_id=1, source_target_pairs={{0,2},{2,0},{4,6},{6,4},{1,3},{3,1},{5,7},{7,5},{8,10},{10,8},{12,... | collective-permute-start | bytes 417800 | tf_op jit(solution)/shard_map/ppermute | solution.py:310
  39.4 9.2 %collective-permute-start.7 = (f32[272,128]{1,0:T(8,128)S(1)}, f32[272,128]{1,0:T(8,128)S(1)}, u32[]{:S(2)}, u32[]{:S(2)}) collective-permute-start(f32[272,128]{1,0:T(8,128)S(1)} %add.25.stats_ref), channel_id=1, source_target_pairs={{0,6},{2,4},{4,2},{6,0},{1,7},{3,5},{5,3},{7,1},{8,14},{10,12},{12... | collective-permute-start | bytes 417800 | tf_op jit(solution)/shard_map/ppermute | solution.py:310
  40.6 8.0 %collective-permute-start.8 = (f32[272,128]{1,0:T(8,128)S(1)}, f32[272,128]{1,0:T(8,128)S(1)}, u32[]{:S(2)}, u32[]{:S(2)}) collective-permute-start(f32[272,128]{1,0:T(8,128)S(1)} %add.25.stats_ref), channel_id=1, source_target_pairs={{0,4},{2,6},{4,0},{6,2},{1,5},{3,7},{5,1},{7,3},{8,12},{10,14},{12... | collective-permute-start | bytes 417800 | tf_op jit(solution)/shard_map/ppermute | solution.py:310
  50.0 1.5 %collective-permute-start.10 = (f32[1,136,256]{2,1,0:T(8,128)S(1)}, f32[1,136,256]{2,1,0:T(8,128)S(1)}, u32[]{:S(2)}, u32[]{:S(2)}) collective-permute-start(f32[1,136,256]{2,1,0:T(8,128)S(1)} %other.5), channel_id=1, source_target_pairs={{0,32},{32,0},{1,33},{33,1},{2,34},{34,2},{3,35},{35,3},{4,36},{36... | collective-permute-start | bytes 417800 | tf_op jit(solution)/shard_map/ppermute | solution.py:310
  50.8 5.3 %collective-permute-start.14 = (f32[1,136,256]{2,1,0:T(8,128)S(1)}, f32[1,136,256]{2,1,0:T(8,128)S(1)}, u32[]{:S(2)}, u32[]{:S(2)}) collective-permute-start(f32[1,136,256]{2,1,0:T(8,128)S(1)} %other.4), channel_id=1, source_target_pairs={{0,32},{32,0},{1,33},{33,1},{2,34},{34,2},{3,35},{35,3},{4,36},{36... | collective-permute-start | bytes 417800 | tf_op jit(solution)/shard_map/ppermute | solution.py:310
  52.2 6.2 %collective-permute-start.15 = (f32[136,256]{1,0:T(8,128)S(1)}, f32[136,256]{1,0:T(8,128)S(1)}, u32[]{:S(2)}, u32[]{:S(2)}) collective-permute-start(f32[136,256]{1,0:T(8,128)S(1)} %hist.4), channel_id=1, source_target_pairs={{0,64},{64,0},{128,192},{192,128},{1,65},{65,1},{129,193},{193,129... | collective-permute-start | bytes 417800 | tf_op jit(solution)/shard_map/ppermute | solution.py:310
  54.4 2.5 %collective-permute-start.12 = (f32[1,136,256]{2,1,0:T(8,128)S(1)}, f32[1,136,256]{2,1,0:T(8,128)S(1)}, u32[]{:S(2)}, u32[]{:S(2)}) collective-permute-start(f32[1,136,256]{2,1,0:T(8,128)S(1)} %other.7), channel_id=1, source_target_pairs={{0,32},{32,0},{1,33},{33,1},{2,34},{34,2},{3,35},{35,3},{4,36},{36... | collective-permute-start | bytes 417800 | tf_op jit(solution)/shard_map/ppermute | solution.py:310
  55.3 6.5 %collective-permute-start.11 = (f32[1,136,256]{2,1,0:T(8,128)S(1)}, f32[1,136,256]{2,1,0:T(8,128)S(1)}, u32[]{:S(2)}, u32[]{:S(2)}) collective-permute-start(f32[1,136,256]{2,1,0:T(8,128)S(1)} %other.6), channel_id=1, source_target_pairs={{0,32},{32,0},{1,33},{33,1},{2,34},{34,2},{3,35},{35,3},{4,36},{36... | collective-permute-start | bytes 417800 | tf_op jit(solution)/shard_map/ppermute | solution.py:310
  57.7 6.9 %collective-permute-start.13 = (f32[136,256]{1,0:T(8,128)S(1)}, f32[136,256]{1,0:T(8,128)S(1)}, u32[]{:S(2)}, u32[]{:S(2)}) collective-permute-start(f32[136,256]{1,0:T(8,128)S(1)} %hist.6), channel_id=1, source_target_pairs={{0,64},{64,0},{128,192},{192,128},{1,65},{65,1},{129,193},{193,129... | collective-permute-start | bytes 417800 | tf_op jit(solution)/shard_map/ppermute | solution.py:310
  58.4 9.9 %collective-permute-start.16 = (f32[136,256]{1,0:T(8,128)S(1)}, f32[136,256]{1,0:T(8,128)S(1)}, u32[]{:S(2)}, u32[]{:S(2)}) collective-permute-start(f32[136,256]{1,0:T(8,128)S(1)} %add.32), channel_id=1, source_target_pairs={{0,128},{64,192},{128,0},{192,64},{1,129},{65,193},{129,1},{193,65... | collective-permute-start | bytes 417800 | tf_op jit(solution)/shard_map/ppermute | solution.py:310

commit v11 on v10

--- a/solution.py
+++ b/solution.py
@@ -322,7 +322,7 @@
     arrived = [swap(part, "x", k, 4) for k, part in zip((1, 3), parts)]
     (mine,) = sketch_call((0,), scores, targets, signs_t, first)
     mine = mine + (arrived[0] + arrived[1])
-    arrived = [swap(mine, "y", k, 4) for k in (2, 1, 3)]
+    arrived = [swap(mine, "y", k, 4) for k in (1, 2, 3)]
     mine = (mine + arrived[0]) + (arrived[1] + arrived[2])
     mine = mine + swap(mine, "zh", 1, 2)
     first = swap(mine, "x", 1, 4)

time: 69.3 us -> 69.2 us (level)
  the two profiles are of different devices: /device:TPU:32 before, /device:TPU:1 now
where the time goes in v11:
time: 69.2 us; the launch traced here: 67.9 us
  starting transfers between devices  30.8 us (45%)
  Pallas kernels  23.9 us (35%)
  waiting for transfers between devices  12.2 us (18%)
  local copies, waits for them, and re-layouts  0.73 us (1%)
    ppermute x17, starting transfers between devices, swap(): return lax.ppermute(value, axis, [(i, i ^ bit) for i in range(size)])  30.8 us
    ppermute x17, waiting for transfers between devices, swap(): return lax.ppermute(value, axis, [(i, i ^ bit) for i in range(size)])  12.2 us
    pallas_call x3, Pallas kernels, sketch_call(): pl.pallas_call(functools.partial(sketch_kernel, ks), in_specs=[pl.BlockSp...  10.8 us
    pallas_call x2, Pallas kernels, block_call(): pl.pallas_call(functools.partial(block_kernel, k), in_specs=[pl.BlockSpec...  5.44 us
    pallas_call x4, Pallas kernels, hist_call(): pl.pallas_call(functools.partial(hist_kernel, k, place), in_specs=[pl.Blo...  3.09 us
    pallas_call x4, Pallas kernels, other_call(): pl.pallas_call(functools.partial(other_kernel, ks), in_specs=[pl.BlockSpe...  3.07 us
  transfers between devices with their start and end apart: 17, of which 7 were waited for; matrix products, arithmetic and copies ran while one was open for 0% of the time, Pallas kernels for 27%

profile of v11, /device:TPU:1, one launch (start us, length us, event | category | flops | bytes accessed | tf_op | source)
XLA Modules:
  0.0 67.9 jit_solution(10443972486163555271)
XLA Ops:
  0.0 0.0 copy-start.1
  0.0 0.7 %copy-done.1 = s32[256,16]{0,1:T(8,128)S(1)} copy-done((s32[256,16]{0,1:T(8,128)S(1)}, s32[256,16]{0,1:T(8,128)}, u32[]{:S(2)}) %copy-start.1) | copy-done | bytes 16408
  0.7 3.2 %sketch.3 = f32[272,128]{1,0:T(8,128)S(1)} custom-call(bf16[8192,256]{1,0:T(8,128)(2,1)} %scores_ref.5, s32[8192,256]{1,0:T(8,128)} %targets_ref.5, s32[16,256]{1,0:T(8,128)S(1)} %bitcast.13), custom_call_target="tpu_custom_call" | custom-call | flops 100663296 | bytes 3145728 | tf_op jit(solution)/shard_map/sketch/pallas_call | solution.py:98
  3.9 3.7 %collective-permute-start = (f32[272,128]{1,0:T(8,128)S(1)}, f32[272,128]{1,0:T(8,128)S(1)}, u32[]{:S(2)}, u32[]{:S(2)}) collective-permute-start(f32[272,128]{1,0:T(8,128)S(1)} %sketch.3), channel_id=1, source_target_pairs={{0,4},{2,6},{4,0},{6,2},{1,5},{3,7},{5,1},{7,3},{8,12},{10,14},{12... | collective-permute-start | bytes 417800 | tf_op jit(solution)/shard_map/ppermute | solution.py:310
  7.5 4.5 %sketch.5 = (f32[272,128]{1,0:T(8,128)S(1)}, f32[272,128]{1,0:T(8,128)S(1)}) custom-call(bf16[8192,256]{1,0:T(8,128)(2,1)} %scores_ref.5, s32[8192,256]{1,0:T(8,128)} %targets_ref.5, s32[16,256]{1,0:T(8,128)S(1)} %bitcast.14), custom_call_target="tpu_custom_call" | custom-call | flops 201326592 | bytes 6291456 | tf_op jit(solution)/shard_map/sketch/pallas_call | solution.py:98
  12.1 0.4 collective-permute-start.1
  12.5 0.6 collective-permute-start.2
  13.1 0.0 collective-permute-done.refs_0_
  13.1 3.2 %sketch.4 = f32[272,128]{1,0:T(8,128)S(1)} custom-call(bf16[8192,256]{1,0:T(8,128)(2,1)} %scores_ref.5, s32[8192,256]{1,0:T(8,128)} %targets_ref.5, s32[16,256]{1,0:T(8,128)S(1)} %bitcast.15, f32[272,128]{1,0:T(8,128)S(1)} %collective-permute-done.refs_0_), custom_call_target="tpu_custom_call" | custom-call | flops 100663296 | bytes 3145728 | tf_op jit(solution)/shard_map/sketch/pallas_call | solution.py:98
  16.3 0.0 copy-start
  16.3 0.0 copy-start.2
  16.3 0.1 collective-permute-done.1
  16.4 1.2 %collective-permute-done.2 = f32[272,128]{1,0:T(8,128)S(1)} collective-permute-done((f32[272,128]{1,0:T(8,128)S(1)}, f32[272,128]{1,0:T(8,128)S(1)}, u32[]{:S(2)}, u32[]{:S(2)}) %collective-permute-start.2) | collective-permute-done | bytes 139296 | tf_op jit(solution)/shard_map/ppermute | solution.py:310
  17.6 1.4 %collective-permute-start.3 = (f32[272,128]{1,0:T(8,128)S(1)}, f32[272,128]{1,0:T(8,128)S(1)}, u32[]{:S(2)}, u32[]{:S(2)}) collective-permute-start(f32[272,128]{1,0:T(8,128)S(1)} %add_add_fusion.1), channel_id=1, source_target_pairs={{0,8},{8,0},{16,24},{24,16},{1,9},{9,1},{17,25},{25,17},{2,10},{10... | collective-permute-start | bytes 417800 | tf_op jit(solution)/shard_map/ppermute | solution.py:310
  19.0 2.6 %collective-permute-start.4 = (f32[272,128]{1,0:T(8,128)S(1)}, f32[272,128]{1,0:T(8,128)S(1)}, u32[]{:S(2)}, u32[]{:S(2)}) collective-permute-start(f32[272,128]{1,0:T(8,128)S(1)} %add_add_fusion.1), channel_id=1, source_target_pairs={{0,16},{8,24},{16,0},{24,8},{1,17},{9,25},{17,1},{25,9},{2,18},{10... | collective-permute-start | bytes 417800 | tf_op jit(solution)/shard_map/ppermute | solution.py:310
  21.6 0.0 collective-permute-start.5
  21.6 0.0 collective-permute-done.3
  21.6 4.0 %collective-permute-done.4 = f32[272,128]{1,0:T(8,128)S(1)} collective-permute-done((f32[272,128]{1,0:T(8,128)S(1)}, f32[272,128]{1,0:T(8,128)S(1)}, u32[]{:S(2)}, u32[]{:S(2)}) %collective-permute-start.4) | collective-permute-done | bytes 139296 | tf_op jit(solution)/shard_map/ppermute | solution.py:310
  25.6 1.4 %collective-permute-done.5 = f32[272,128]{1,0:T(8,128)S(1)} collective-permute-done((f32[272,128]{1,0:T(8,128)S(1)}, f32[272,128]{1,0:T(8,128)S(1)}, u32[]{:S(2)}, u32[]{:S(2)}) %collective-permute-start.5) | collective-permute-done | bytes 139296 | tf_op jit(solution)/shard_map/ppermute | solution.py:310
  27.1 7.0 %collective-permute-start.6 = (f32[272,128]{1,0:T(8,128)S(1)}, f32[272,128]{1,0:T(8,128)S(1)}, u32[]{:S(2)}, u32[]{:S(2)}) collective-permute-start(f32[272,128]{1,0:T(8,128)S(1)} %add_add_fusion), channel_id=1, source_target_pairs={{0,1},{1,0},{2,3},{3,2},{4,5},{5,4},{6,7},{7,6},{8,9},{9,8},{10,11... | collective-permute-start | bytes 417800 | tf_op jit(solution)/shard_map/ppermute | solution.py:310
  34.1 2.5 %collective-permute-done.6 = f32[272,128]{1,0:T(8,128)S(1)} collective-permute-done((f32[272,128]{1,0:T(8,128)S(1)}, f32[272,128]{1,0:T(8,128)S(1)}, u32[]{:S(2)}, u32[]{:S(2)}) %collective-permute-start.6) | collective-permute-done | bytes 139296 | tf_op jit(solution)/shard_map/ppermute | solution.py:310
  36.6 0.7 collective-permute-start.9
  37.3 2.6 %collective-permute-start.7 = (f32[272,128]{1,0:T(8,128)S(1)}, f32[272,128]{1,0:T(8,128)S(1)}, u32[]{:S(2)}, u32[]{:S(2)}) collective-permute-start(f32[272,128]{1,0:T(8,128)S(1)} %add.25.stats_ref), channel_id=1, source_target_pairs={{0,6},{2,4},{4,2},{6,0},{1,7},{3,5},{5,3},{7,1},{8,14},{10,12},{12... | collective-permute-start | bytes 417800 | tf_op jit(solution)/shard_map/ppermute | solution.py:310
  39.9 0.8 %collective-permute-start.8 = (f32[272,128]{1,0:T(8,128)S(1)}, f32[272,128]{1,0:T(8,128)S(1)}, u32[]{:S(2)}, u32[]{:S(2)}) collective-permute-start(f32[272,128]{1,0:T(8,128)S(1)} %add.25.stats_ref), channel_id=1, source_target_pairs={{0,4},{2,6},{4,0},{6,2},{1,5},{3,7},{5,1},{7,3},{8,12},{10,14},{12... | collective-permute-start | bytes 417800 | tf_op jit(solution)/shard_map/ppermute | solution.py:310
  40.7 0.0 copy-done
  40.7 0.0 copy-done.2
  40.7 2.7 %block.2.refs_0_ = f32[8,136,256]{2,1,0:T(8,128)S(1)} custom-call(s32[16,8192]{1,0:T(8,128)S(1)} %bitcast.3, f32[272,128]{1,0:T(8,128)S(1)} %add.25.stats_ref, s32[64,128]{1,0:T(8,128)S(1)} %bitcast.16), custom_call_target="tpu_custom_call" | custom-call | flops 5000000000 | bytes 1000000 | tf_op jit(solution)/shard_map/block/pallas_call | solution.py:219
  43.4 0.0 collective-permute-done.9.stats_ref
  43.4 2.7 %block.3.start_ref = f32[8,136,256]{2,1,0:T(8,128)S(1)} custom-call(s32[16,8192]{1,0:T(8,128)S(1)} %bitcast.4, f32[272,128]{1,0:T(8,128)S(1)} %collective-permute-done.9.stats_ref, s32[64,128]{1,0:T(8,128)S(1)} %bitcast.17, f32[8,136,256]{2,1,0:T(8,128)S(1)} %block.2.refs_0_), custom_call_target="tpu_custom_call" | custom-call | flops 5000000000 | bytes 1000000 | tf_op jit(solution)/shard_map/block/pallas_call | solution.py:219
  46.2 0.0 collective-permute-done.7.refs_0_
  46.2 0.0 collective-permute-done.8.refs_1_
  46.2 0.6 weights.1.weights_ref
  46.8 0.8 %other.5 = f32[1,136,256]{2,1,0:T(8,128)S(1)} custom-call(s32[16,8192]{1,0:T(8,128)S(1)} %bitcast.5, f8e4m3fn[288,4096]{1,0:T(32,128)(4,1)S(1)} %weights.1.weights_ref, f32[8,136,256]{2,1,0:T(8,128)S(1)} %block.3.start_ref), custom_call_target="tpu_custom_call" | custom-call | flops 2000000000 | bytes 1000 | tf_op jit(solution)/shard_map/other/pallas_call | solution.py:238
  47.5 5.9 %collective-permute-start.10 = (f32[1,136,256]{2,1,0:T(8,128)S(1)}, f32[1,136,256]{2,1,0:T(8,128)S(1)}, u32[]{:S(2)}, u32[]{:S(2)}) collective-permute-start(f32[1,136,256]{2,1,0:T(8,128)S(1)} %other.5), channel_id=1, source_target_pairs={{0,32},{32,0},{1,33},{33,1},{2,34},{34,2},{3,35},{35,3},{4,36},{36... | collective-permute-start | bytes 417800 | tf_op jit(solution)/shard_map/ppermute | solution.py:310
  53.4 0.8 %other.4 = f32[1,136,256]{2,1,0:T(8,128)S(1)} custom-call(s32[16,8192]{1,0:T(8,128)S(1)} %bitcast.6, f8e4m3fn[288,4096]{1,0:T(32,128)(4,1)S(1)} %weights.1.weights_ref, f32[8,136,256]{2,1,0:T(8,128)S(1)} %block.3.start_ref), custom_call_target="tpu_custom_call" | custom-call | flops 2000000000 | bytes 1000 | tf_op jit(solution)/shard_map/other/pallas_call | solution.py:238
  54.2 0.1 collective-permute-start.14
  54.3 0.1 collective-permute-done.10.swapped_ref
  54.4 0.8 %hist.4 = f32[136,256]{1,0:T(8,128)S(1)} custom-call(s32[16,8192]{1,0:T(8,128)S(1)} %bitcast.7, f8e4m3fn[288,4096]{1,0:T(32,128)(4,1)S(1)} %weights.1.weights_ref, f32[8,136,256]{2,1,0:T(8,128)S(1)} %block.3.start_ref, f32[1,136,256]{2,1,0:T(8,128)S(1)} %collective-permute-done.10.swapped_ref), custom_call_target="tpu_custom_call" | custom-call | flops 1000 | bytes 1000 | tf_op jit(solution)/shard_map/hist/pallas_call | solution.py:259
  55.2 0.8 %collective-permute-start.15 = (f32[136,256]{1,0:T(8,128)S(1)}, f32[136,256]{1,0:T(8,128)S(1)}, u32[]{:S(2)}, u32[]{:S(2)}) collective-permute-start(f32[136,256]{1,0:T(8,128)S(1)} %hist.4), channel_id=1, source_target_pairs={{0,64},{64,0},{128,192},{192,128},{1,65},{65,1},{129,193},{193,129... | collective-permute-start | bytes 417800 | tf_op jit(solution)/shard_map/ppermute | solution.py:310
  56.0 0.8 %other.7 = f32[1,136,256]{2,1,0:T(8,128)S(1)} custom-call(s32[16,8192]{1,0:T(8,128)S(1)} %bitcast.8, f8e4m3fn[288,4096]{1,0:T(32,128)(4,1)S(1)} %weights.1.weights_ref, f32[8,136,256]{2,1,0:T(8,128)S(1)} %block.3.start_ref), custom_call_target="tpu_custom_call" | custom-call | flops 2000000000 | bytes 1000 | tf_op jit(solution)/shard_map/other/pallas_call | solution.py:238
  56.7 0.7 %collective-permute-start.12 = (f32[1,136,256]{2,1,0:T(8,128)S(1)}, f32[1,136,256]{2,1,0:T(8,128)S(1)}, u32[]{:S(2)}, u32[]{:S(2)}) collective-permute-start(f32[1,136,256]{2,1,0:T(8,128)S(1)} %other.7), channel_id=1, source_target_pairs={{0,32},{32,0},{1,33},{33,1},{2,34},{34,2},{3,35},{35,3},{4,36},{36... | collective-permute-start | bytes 417800 | tf_op jit(solution)/shard_map/ppermute | solution.py:310
  57.5 0.8 %other.6 = f32[1,136,256]{2,1,0:T(8,128)S(1)} custom-call(s32[16,8192]{1,0:T(8,128)S(1)} %bitcast.9, f8e4m3fn[288,4096]{1,0:T(32,128)(4,1)S(1)} %weights.1.weights_ref, f32[8,136,256]{2,1,0:T(8,128)S(1)} %block.3.start_ref), custom_call_target="tpu_custom_call" | custom-call | flops 2000000000 | bytes 1000 | tf_op jit(solution)/shard_map/other/pallas_call | solution.py:238
  58.2 0.3 collective-permute-start.11
  58.6 0.0 collective-permute-done.14.swapped_ref
  58.6 0.8 %hist.7.a_ref = f32[136,256]{1,0:T(8,128)S(1)} custom-call(s32[16,8192]{1,0:T(8,128)S(1)} %bitcast.10, f8e4m3fn[288,4096]{1,0:T(32,128)(4,1)S(1)} %weights.1.weights_ref, f32[8,136,256]{2,1,0:T(8,128)S(1)} %block.3.start_ref, f32[1,136,256]{2,1,0:T(8,128)S(1)} %collective-permute-done.14.swapped_ref), custom_call_target="tpu_custom_call" | custom-call | flops 1000 | bytes 1000 | tf_op jit(solution)/shard_map/hist/pallas_call | solution.py:259
  59.4 0.0 collective-permute-done.12.swapped_ref
  59.4 0.8 %hist.6 = f32[136,256]{1,0:T(8,128)S(1)} custom-call(s32[16,8192]{1,0:T(8,128)S(1)} %bitcast.11, f8e4m3fn[288,4096]{1,0:T(32,128)(4,1)S(1)} %weights.1.weights_ref, f32[8,136,256]{2,1,0:T(8,128)S(1)} %block.3.start_ref, f32[1,136,256]{2,1,0:T(8,128)S(1)} %collective-permute-done.12.swapped_ref), custom_call_target="tpu_custom_call" | custom-call | flops 1000 | bytes 1000 | tf_op jit(solution)/shard_map/hist/pallas_call | solution.py:259
  60.2 0.8 %collective-permute-start.13 = (f32[136,256]{1,0:T(8,128)S(1)}, f32[136,256]{1,0:T(8,128)S(1)}, u32[]{:S(2)}, u32[]{:S(2)}) collective-permute-start(f32[136,256]{1,0:T(8,128)S(1)} %hist.6), channel_id=1, source_target_pairs={{0,64},{64,0},{128,192},{192,128},{1,65},{65,1},{129,193},{193,129... | collective-permute-start | bytes 417800 | tf_op jit(solution)/shard_map/ppermute | solution.py:310
  61.0 0.0 collective-permute-done.15.b_ref
  61.0 2.3 %collective-permute-start.16 = (f32[136,256]{1,0:T(8,128)S(1)}, f32[136,256]{1,0:T(8,128)S(1)}, u32[]{:S(2)}, u32[]{:S(2)}) collective-permute-start(f32[136,256]{1,0:T(8,128)S(1)} %add.32), channel_id=1, source_target_pairs={{0,128},{64,192},{128,0},{192,64},{1,129},{65,193},{129,1},{193,65... | collective-permute-start | bytes 417800 | tf_op jit(solution)/shard_map/ppermute | solution.py:310
  63.3 0.0 collective-permute-done.11.swapped_ref
  63.4 0.8 %hist.5.a_ref = f32[136,256]{1,0:T(8,128)S(1)} custom-call(s32[16,8192]{1,0:T(8,128)S(1)} %bitcast.12, f8e4m3fn[288,4096]{1,0:T(32,128)(4,1)S(1)} %weights.1.weights_ref, f32[8,136,256]{2,1,0:T(8,128)S(1)} %block.3.start_ref, f32[1,136,256]{2,1,0:T(8,128)S(1)} %collective-permute-done.11.swapped_ref), custom_call_target="tpu_custom_call" | custom-call | flops 1000 | bytes 1000 | tf_op jit(solution)/shard_map/hist/pallas_call | solution.py:259
  64.1 2.9 %collective-permute-done.13.b_ref = f32[136,256]{1,0:T(8,128)S(1)} collective-permute-done((f32[136,256]{1,0:T(8,128)S(1)}, f32[136,256]{1,0:T(8,128)S(1)}, u32[]{:S(2)}, u32[]{:S(2)}) %collective-permute-start.13) | collective-permute-done | bytes 139296 | tf_op jit(solution)/shard_map/ppermute | solution.py:310
  67.0 0.0 collective-permute-done.16.b_ref
  67.0 0.8 %finish.1 = f32[32,16,68]{2,1,0:T(8,128)} custom-call(f32[136,256]{1,0:T(8,128)S(1)} %add.31.a_ref, f32[136,256]{1,0:T(8,128)S(1)} %collective-permute-done.16.b_ref), custom_call_target="tpu_custom_call" | custom-call | tf_op jit(solution)/shard_map/finish/pallas_call | solution.py:301
  (5 shorter events, 0.1 us)
Async XLA Ops:
  0.0 0.7 %copy-start.1 = (s32[256,16]{0,1:T(8,128)S(1)}, s32[256,16]{0,1:T(8,128)}, u32[]{:S(2)}) copy-start(s32[256,16]{0,1:T(8,128)} %param.7) | copy-start | bytes 49156
  3.9 9.2 %collective-permute-start = (f32[272,128]{1,0:T(8,128)S(1)}, f32[272,128]{1,0:T(8,128)S(1)}, u32[]{:S(2)}, u32[]{:S(2)}) collective-permute-start(f32[272,128]{1,0:T(8,128)S(1)} %sketch.3), channel_id=1, source_target_pairs={{0,4},{2,6},{4,0},{6,2},{1,5},{3,7},{5,1},{7,3},{8,12},{10,14},{12... | collective-permute-start | bytes 417800 | tf_op jit(solution)/shard_map/ppermute | solution.py:310
  12.1 4.3 %collective-permute-start.1 = (f32[272,128]{1,0:T(8,128)S(1)}, f32[272,128]{1,0:T(8,128)S(1)}, u32[]{:S(2)}, u32[]{:S(2)}) collective-permute-start(f32[272,128]{1,0:T(8,128)S(1)} %get-tuple-element.15), channel_id=1, source_target_pairs={{0,2},{2,0},{4,6},{6,4},{1,3},{3,1},{5,7},{7,5},{8,10},{10,8},{12,... | collective-permute-start | bytes 417800 | tf_op jit(solution)/shard_map/ppermute | solution.py:310
  12.5 5.1 %collective-permute-start.2 = (f32[272,128]{1,0:T(8,128)S(1)}, f32[272,128]{1,0:T(8,128)S(1)}, u32[]{:S(2)}, u32[]{:S(2)}) collective-permute-start(f32[272,128]{1,0:T(8,128)S(1)} %get-tuple-element.16), channel_id=1, source_target_pairs={{0,6},{2,4},{4,2},{6,0},{1,7},{3,5},{5,3},{7,1},{8,14},{10,12},{12... | collective-permute-start | bytes 417800 | tf_op jit(solution)/shard_map/ppermute | solution.py:310
  16.3 24.4 %copy-start = (s32[8192,16]{0,1:T(8,128)S(1)}, s32[8192,16]{0,1:T(8,128)}, u32[]{:S(2)}) copy-start(s32[8192,16]{0,1:T(8,128)} %param.8) | copy-start | bytes 1572868
  16.3 24.4 %copy-start.2 = (s32[8192]{0:T(1024)S(1)}, s32[8192]{0:T(1024)}, u32[]{:S(2)}) copy-start(s32[8192]{0:T(1024)} %param.9) | copy-start | bytes 98308
  17.6 4.0 %collective-permute-start.3 = (f32[272,128]{1,0:T(8,128)S(1)}, f32[272,128]{1,0:T(8,128)S(1)}, u32[]{:S(2)}, u32[]{:S(2)}) collective-permute-start(f32[272,128]{1,0:T(8,128)S(1)} %add_add_fusion.1), channel_id=1, source_target_pairs={{0,8},{8,0},{16,24},{24,16},{1,9},{9,1},{17,25},{25,17},{2,10},{10... | collective-permute-start | bytes 417800 | tf_op jit(solution)/shard_map/ppermute | solution.py:310
  19.0 6.6 %collective-permute-start.4 = (f32[272,128]{1,0:T(8,128)S(1)}, f32[272,128]{1,0:T(8,128)S(1)}, u32[]{:S(2)}, u32[]{:S(2)}) collective-permute-start(f32[272,128]{1,0:T(8,128)S(1)} %add_add_fusion.1), channel_id=1, source_target_pairs={{0,16},{8,24},{16,0},{24,8},{1,17},{9,25},{17,1},{25,9},{2,18},{10... | collective-permute-start | bytes 417800 | tf_op jit(solution)/shard_map/ppermute | solution.py:310
  21.6 5.4 %collective-permute-start.5 = (f32[272,128]{1,0:T(8,128)S(1)}, f32[272,128]{1,0:T(8,128)S(1)}, u32[]{:S(2)}, u32[]{:S(2)}) collective-permute-start(f32[272,128]{1,0:T(8,128)S(1)} %add_add_fusion.1), channel_id=1, source_target_pairs={{0,24},{8,16},{16,8},{24,0},{1,25},{9,17},{17,9},{25,1},{2,26},{10... | collective-permute-start | bytes 417800 | tf_op jit(solution)/shard_map/ppermute | solution.py:310
  27.1 9.5 %collective-permute-start.6 = (f32[272,128]{1,0:T(8,128)S(1)}, f32[272,128]{1,0:T(8,128)S(1)}, u32[]{:S(2)}, u32[]{:S(2)}) collective-permute-start(f32[272,128]{1,0:T(8,128)S(1)} %add_add_fusion), channel_id=1, source_target_pairs={{0,1},{1,0},{2,3},{3,2},{4,5},{5,4},{6,7},{7,6},{8,9},{9,8},{10,11... | collective-permute-start | bytes 417800 | tf_op jit(solution)/shard_map/ppermute | solution.py:310
  36.6 6.8 %collective-permute-start.9 = (f32[272,128]{1,0:T(8,128)S(1)}, f32[272,128]{1,0:T(8,128)S(1)}, u32[]{:S(2)}, u32[]{:S(2)}) collective-permute-start(f32[272,128]{1,0:T(8,128)S(1)} %add.25.stats_ref), channel_id=1, source_target_pairs={{0,2},{2,0},{4,6},{6,4},{1,3},{3,1},{5,7},{7,5},{8,10},{10,8},{12,... | collective-permute-start | bytes 417800 | tf_op jit(solution)/shard_map/ppermute | solution.py:310
  37.3 8.9 %collective-permute-start.7 = (f32[272,128]{1,0:T(8,128)S(1)}, f32[272,128]{1,0:T(8,128)S(1)}, u32[]{:S(2)}, u32[]{:S(2)}) collective-permute-start(f32[272,128]{1,0:T(8,128)S(1)} %add.25.stats_ref), channel_id=1, source_target_pairs={{0,6},{2,4},{4,2},{6,0},{1,7},{3,5},{5,3},{7,1},{8,14},{10,12},{12... | collective-permute-start | bytes 417800 | tf_op jit(solution)/shard_map/ppermute | solution.py:310
  39.9 6.3 %collective-permute-start.8 = (f32[272,128]{1,0:T(8,128)S(1)}, f32[272,128]{1,0:T(8,128)S(1)}, u32[]{:S(2)}, u32[]{:S(2)}) collective-permute-start(f32[272,128]{1,0:T(8,128)S(1)} %add.25.stats_ref), channel_id=1, source_target_pairs={{0,4},{2,6},{4,0},{6,2},{1,5},{3,7},{5,1},{7,3},{8,12},{10,14},{12... | collective-permute-start | bytes 417800 | tf_op jit(solution)/shard_map/ppermute | solution.py:310
  47.5 6.8 %collective-permute-start.10 = (f32[1,136,256]{2,1,0:T(8,128)S(1)}, f32[1,136,256]{2,1,0:T(8,128)S(1)}, u32[]{:S(2)}, u32[]{:S(2)}) collective-permute-start(f32[1,136,256]{2,1,0:T(8,128)S(1)} %other.5), channel_id=1, source_target_pairs={{0,32},{32,0},{1,33},{33,1},{2,34},{34,2},{3,35},{35,3},{4,36},{36... | collective-permute-start | bytes 417800 | tf_op jit(solution)/shard_map/ppermute | solution.py:310
  54.2 4.4 %collective-permute-start.14 = (f32[1,136,256]{2,1,0:T(8,128)S(1)}, f32[1,136,256]{2,1,0:T(8,128)S(1)}, u32[]{:S(2)}, u32[]{:S(2)}) collective-permute-start(f32[1,136,256]{2,1,0:T(8,128)S(1)} %other.4), channel_id=1, source_target_pairs={{0,32},{32,0},{1,33},{33,1},{2,34},{34,2},{3,35},{35,3},{4,36},{36... | collective-permute-start | bytes 417800 | tf_op jit(solution)/shard_map/ppermute | solution.py:310
  55.2 5.8 %collective-permute-start.15 = (f32[136,256]{1,0:T(8,128)S(1)}, f32[136,256]{1,0:T(8,128)S(1)}, u32[]{:S(2)}, u32[]{:S(2)}) collective-permute-start(f32[136,256]{1,0:T(8,128)S(1)} %hist.4), channel_id=1, source_target_pairs={{0,64},{64,0},{128,192},{192,128},{1,65},{65,1},{129,193},{193,129... | collective-permute-start | bytes 417800 | tf_op jit(solution)/shard_map/ppermute | solution.py:310
  56.7 2.6 %collective-permute-start.12 = (f32[1,136,256]{2,1,0:T(8,128)S(1)}, f32[1,136,256]{2,1,0:T(8,128)S(1)}, u32[]{:S(2)}, u32[]{:S(2)}) collective-permute-start(f32[1,136,256]{2,1,0:T(8,128)S(1)} %other.7), channel_id=1, source_target_pairs={{0,32},{32,0},{1,33},{33,1},{2,34},{34,2},{3,35},{35,3},{4,36},{36... | collective-permute-start | bytes 417800 | tf_op jit(solution)/shard_map/ppermute | solution.py:310
  58.2 5.1 %collective-permute-start.11 = (f32[1,136,256]{2,1,0:T(8,128)S(1)}, f32[1,136,256]{2,1,0:T(8,128)S(1)}, u32[]{:S(2)}, u32[]{:S(2)}) collective-permute-start(f32[1,136,256]{2,1,0:T(8,128)S(1)} %other.6), channel_id=1, source_target_pairs={{0,32},{32,0},{1,33},{33,1},{2,34},{34,2},{3,35},{35,3},{4,36},{36... | collective-permute-start | bytes 417800 | tf_op jit(solution)/shard_map/ppermute | solution.py:310
  60.2 6.8 %collective-permute-start.13 = (f32[136,256]{1,0:T(8,128)S(1)}, f32[136,256]{1,0:T(8,128)S(1)}, u32[]{:S(2)}, u32[]{:S(2)}) collective-permute-start(f32[136,256]{1,0:T(8,128)S(1)} %hist.6), channel_id=1, source_target_pairs={{0,64},{64,0},{128,192},{192,128},{1,65},{65,1},{129,193},{193,129... | collective-permute-start | bytes 417800 | tf_op jit(solution)/shard_map/ppermute | solution.py:310
  61.0 6.0 %collective-permute-start.16 = (f32[136,256]{1,0:T(8,128)S(1)}, f32[136,256]{1,0:T(8,128)S(1)}, u32[]{:S(2)}, u32[]{:S(2)}) collective-permute-start(f32[136,256]{1,0:T(8,128)S(1)} %add.32), channel_id=1, source_target_pairs={{0,128},{64,192},{128,0},{192,64},{1,129},{65,193},{129,1},{193,65... | collective-permute-start | bytes 417800 | tf_op jit(solution)/shard_map/ppermute | solution.py:310
